TPU v7x, 32 devices: a whole 2x2x4 slice. The times are simulated.
32 devices in a mesh: cuts: 2 (over y), gx: 4 (over z), gy: 2 (over x), ma: 2 (over core).
Axes of the slice: x: 2, y: 2, z: 4, core: 2. Of those that a mesh axis runs over, the one named last changes fastest.
Arguments:
- eigen_modes: bfloat16 [4, 32, 32, 2, 3, 512], P('cuts', 'gx', 'gy', None, None, 'ma'), parts along dimension 0, may hold values from -0.25 to 0.25
- links_first: bfloat16 [4, 3, 3, 32, 32, 2], P('cuts', None, None, 'gx', 'gy'), parts along dimension 0, may hold values from -2.5 to 2.5
- links_second: bfloat16 [4, 3, 3, 32, 32, 2], P('cuts', None, None, 'gx', 'gy'), parts along dimension 0, may hold values from -2.5 to 2.5
Outputs:
- elementals: float32 [4, 2, 512, 512], P('cuts', None, ('gx', 'gy'), 'ma'), parts along dimension 0
There are 2 independent parts, one for each index of `cuts`. A program takes and returns all parts, laid end to end along the dimension named above; each array names one. Nothing has to cross between parts.
All inputs are finite; a program needn't handle non-finite values.
Results may differ from a plain program's by a relative error of at most 0.0055.
Values may be sent and summed in bfloat16 or wider, within the bound.
No kernel may reach another device: no remote copies, remote signals or barrier semaphores. Data moves between devices by JAX's collectives and lax.ppermute only.
A program may use at most 64 MiB of HBM per device.

v0:
```python
import jax
import jax.numpy as jnp
import numpy as np
from jax import lax
from jax.experimental import pallas as pl
from jax.experimental.pallas import tpu as pltpu
from jax.sharding import PartitionSpec as P

VMEM_LIMIT = 16 * 1024 * 1024


def shifted(block, axis, distance):
    devices = range(lax.axis_size(axis))
    route = [((i - distance) % len(devices), i) for i in devices]
    return lax.ppermute(block, axis, route)


def call(body, out_shape, flops, operands, scratch=(), places=None):
    places = places or [pltpu.VMEM] * len(operands)
    return pl.pallas_call(
        body,
        out_shape=out_shape,
        in_specs=[pl.BlockSpec(memory_space=place) for place in places],
        scratch_shapes=scratch,
        cost_estimate=pl.CostEstimate(flops=flops // 2, bytes_accessed=0, transcendentals=0),
        compiler_params=pltpu.CompilerParams(vmem_limit_bytes=VMEM_LIMIT),
    )(*(pltpu.with_memory_space_constraint(a, place) for a, place in zip(operands, places)))


def dot(a, b):
    return jnp.dot(a, b, preferred_element_type=jnp.float32)


def iotas(shape):
    return (
        lax.broadcasted_iota(jnp.int32, shape, 0),
        lax.broadcasted_iota(jnp.int32, shape, 1),
    )


def place_of(x, planes):
    return planes - 2 if x == 0 else x if x == planes - 1 else x - 1


def lane_maps(parts, colours, planes, ys, zs, lanes):
    sites = ys * zs
    depth = parts * colours * sites
    row_size = parts * colours * zs
    lane = np.arange(lanes)
    inner = lane < depth
    past = (lane - depth) % row_size
    used = lane < depth + 2 * row_size
    part = np.where(inner, lane // (colours * sites), past // (colours * zs))
    colour = np.where(inner, lane // sites, past // zs) % colours
    z = np.where(inner, lane, past) % zs
    y = np.where(inner, lane % sites // zs, ys - 1)
    y_ahead = np.where(inner, lane % sites // zs, ys) - 1
    spread = y == np.arange(ys)[:, None]
    spread_ahead = y_ahead == np.arange(ys)[:, None]

    row = np.arange(parts * colours * colours * planes * zs)[:, None]
    row_z = row % zs
    row_x = row // zs % planes
    row_right = row // (zs * planes) % colours
    row_left = row // (zs * planes * colours) % colours
    row_part = row // (zs * planes * colours * colours)
    match_ahead = (row_z == z) & (row_right == colour) & used
    match_back = (row_z == z) & (row_left == colour) & used

    out = np.arange(parts * planes * 8)[:, None]
    field_part = out // (planes * 8)
    out_x = out // 8 % planes
    out_part = out % 8 // colours
    out_colour = out % 8 % colours
    source = (out_x == row_x.T) & (row_part.T == (out_part + field_part) % 2) & (out_part < parts)
    choose_ahead = source & (row_left.T == out_colour)
    choose_back = source & (row_right.T == out_colour)
    sign_ahead = np.where((field_part == 1) & (out_part == 0), -1.0, 1.0)
    sign_back = np.where((field_part == 0) & (out_part == 1), 1.0, -1.0)
    maps = (
        np.concatenate([spread, spread_ahead], axis=1), np.concatenate([match_ahead, match_back], axis=1),
        np.concatenate([choose_ahead * sign_ahead, choose_back * sign_back], axis=0),
        np.broadcast_to(part == 0, (8, lanes)),
    )
    return [np.pad(m, ((0, -len(m) % 8), (0, 2 * lanes - m.shape[1]))).astype(np.float32) for m in maps]


def coefficients(links_x, links_y, maps_ref, planes):
    lanes = maps_ref.shape[1] // 2
    ys = links_x.shape[1]
    count = links_x.shape[0]
    half = 2 * planes * 8
    wide = dot(jnp.concatenate([links_x, links_y], axis=0), maps_ref[:ys].astype(jnp.bfloat16))
    match = maps_ref[ys : ys + count]
    match_ahead, match_back = match[:, :lanes], match[:, lanes:]
    choose = maps_ref[ys + count : ys + count + 2 * half, :count].astype(jnp.bfloat16)
    first_part = maps_ref[ys + count + 2 * half : ys + count + 2 * half + 1, :lanes] > 0.5
    ahead = jnp.concatenate([wide[:count, :lanes] * match_ahead, wide[count:, lanes:] * match_ahead], axis=1)
    back = jnp.concatenate([wide[:count, :lanes] * match_back, wide[count:, :lanes] * match_back], axis=1)
    out = []
    for chosen in (
        dot(choose[:half], ahead.astype(jnp.bfloat16)), dot(choose[half:], back.astype(jnp.bfloat16))
    ):
        for start in (0, lanes):
            part = chosen[:, start : start + lanes]
            rows = jnp.where(first_part, part[: half // 2], part[half // 2 :])
            out.append(rows.reshape(planes, 8, lanes))
    return out


def plane_rows(ref, ys):
    parts, _, colours, zs, width = ref.shape
    return jnp.concatenate(
        [ref[p, :ys, c].reshape(ys * zs, width) for p in range(parts) for c in range(colours)],
        axis=0,
    )


def edges_kernel(
    raw_hbm, links_x_hbm, links_y_hbm, maps_hbm,
    first_ref, last_ref, raw_ref, links_x_ref, links_y_ref, maps_ref, arrived,
):
    parts, planes, ys, colours, zs, _ = raw_hbm.shape
    sources = (
        raw_hbm.at[:, planes - 1], raw_hbm.at[:, 0], links_x_hbm, links_y_hbm, maps_hbm, raw_hbm
    )
    targets = (last_ref.at[:, :ys], first_ref, links_x_ref, links_y_ref, maps_ref, raw_ref)
    copies = [
        pltpu.make_async_copy(source, target, arrived.at[i])
        for i, (source, target) in enumerate(zip(sources, targets))
    ]
    for copy in copies:
        copy.start()
    last_ref[:, ys:] = jnp.zeros((parts, colours) + last_ref.shape[2:], last_ref.dtype)
    copies[2].wait()
    last_ref[:, ys:, :, :, :ys] = links_x_ref[:, :, :, planes - 1]
    for copy in copies[:2] + copies[3:]:
        copy.wait()


def site_matrix(rows_and_masks, count):
    blocks = []
    for q in range(count):
        block = None
        for rows, mask in rows_and_masks:
            term = rows[q : q + 1] * mask
            block = term if block is None else block + term
        blocks.append(block.astype(jnp.bfloat16))
    return jnp.concatenate(blocks, axis=0)


def prepare_kernel(
    raw_ref, links_x_ref, links_y_ref, maps_ref,
    rows_ref, ends_ref, ahead_x_ref, back_x_ref, ahead_y_ref, back_y_ref,
):
    planes, depth, width = rows_ref.shape
    zs = raw_ref.shape[4]
    ys = raw_ref.shape[2]
    sites = ys * zs
    row_size = depth // sites * zs
    lanes = ahead_y_ref.shape[2]
    ahead_x, ahead_y, back_x, back_y = coefficients(
        links_x_ref[...].reshape(-1, ys), links_y_ref[...].reshape(-1, ys), maps_ref, planes
    )
    ahead_x_ref[...] = ahead_x
    back_x_ref[...] = back_x
    ahead_y_ref[...] = ahead_y
    back_y_ref[...] = back_y

    row, lane = iotas((2 * row_size, depth))
    spot = row % row_size
    wanted = (spot // zs) * sites + spot % zs + jnp.where(row < row_size, 0, sites - zs)
    ends = (lane == wanted).astype(jnp.bfloat16)
    filler = jnp.zeros((8, width - 128), jnp.float32)
    spare = ends_ref.shape[1] - 2 * row_size - 8
    for x in range(planes):
        plane = plane_rows(raw_ref.at[:, x], ys)
        rows_ref[place_of(x, planes)] = plane
        tail = jnp.concatenate([back_y[x, :, lanes - 128 :], filler], axis=1)
        pieces = [dot(ends, plane), tail]
        if spare:
            pieces.append(jnp.zeros((spare, width), jnp.float32))
        ends_ref[x] = jnp.concatenate(pieces, axis=0).astype(jnp.bfloat16)


def turn_kernel(raw_ref, rows_ref, turned_ref):
    planes, depth, width = rows_ref.shape
    for x in range(planes):
        rows_ref[place_of(x, planes)] = plane_rows(raw_ref.at[:, x], raw_ref.shape[2])
    turned_ref[...] = rows_ref[...].reshape(planes * depth, width).T


def move_plane(same, count, ahead, back, above, below):
    depth = same.shape[1]
    moved = dot(site_matrix([(ahead[:, :depth], same)], count), above)
    return (moved + dot(site_matrix([(back[:, :depth], same)], count), below)).astype(jnp.bfloat16)


def same_site(sites, depth):
    site, lane = iotas((sites, depth))
    return (lane % sites == site).astype(jnp.float32)


def set_right(right_ref, place, moved):
    depth, width = moved.shape
    half = depth // 2
    start = place * depth
    real, imag = moved[:half], moved[half:]
    right_ref[start : start + half, :width] = real
    right_ref[start : start + half, width:] = imag
    right_ref[start + half : start + depth, :width] = imag
    right_ref[start + half : start + depth, width:] = -real


def inner_kernel(sites, rows_ref, ahead_ref, back_ref, right_ref, turned_ref):
    planes, depth, width = rows_ref.shape
    same = same_site(sites, depth)
    for x in range(1, planes - 1):
        above = rows_ref[place_of(x + 1, planes)]
        below = rows_ref[place_of(x - 1, planes)]
        moved = move_plane(same, depth // sites, ahead_ref[x], back_ref[x - 1], above, below)
        set_right(right_ref, place_of(x, planes), moved)
    turned_ref[...] = rows_ref[...].reshape(planes * depth, width).T


def begin_first_kernel(own_ref, others_ref, right_ref, total_ref):
    inner = right_ref.shape[0]
    right = right_ref[...]
    total_ref[0] = dot(own_ref[:, :inner], right)
    for k in range(others_ref.shape[0]):
        total_ref[k + 1] = dot(others_ref[k, :, :inner], right)


def begin_second_kernel(lefts_ref, right_ref, total_ref):
    inner = right_ref.shape[0]
    right = right_ref[...]
    for k in range(lefts_ref.shape[0]):
        total_ref[k] = dot(lefts_ref[k, :, :inner], right)


def project(lefts, right, halved, begun_ref, keep_ref, send_ref, total_ref):
    my_bit = lax.bitwise_and(lax.axis_index("gy" if halved else "gx"), 1)
    my_modes = lax.axis_index("ma")
    for k, left in enumerate(lefts):
        total_ref[k] = begun_ref[k] + dot(left, right)
    groups, own_modes, _ = total_ref.shape
    parts, across_x, across_y, rows, width = keep_ref.shape

    def piece(index):
        start = index * rows
        group = lax.rem(start // own_modes + groups - my_modes, groups)
        begin = start % own_modes
        return total_ref[group, begin : begin + rows]

    for gx in range(across_x):
        for gy in range(across_y):
            if halved:
                base = gx * 2 * across_y + 2 * gy
                even, odd = piece(base), piece(base + 1)
            else:
                even, odd = piece(2 * gx * across_y + gy), piece((2 * gx + 1) * across_y + gy)
            keep = jnp.where(my_bit == 0, even, odd)
            send = jnp.where(my_bit == 0, odd, even).astype(send_ref.dtype)
            for p in range(parts):
                keep_ref[p, gx, gy] = keep[:, p * width : (p + 1) * width]
                send_ref[p, gx, gy] = send[:, p * width : (p + 1) * width]


def first_kernel(
    sites, rows_ref, high_ref, low_ref, ahead_ref, back_ref, past_maps_ref, own_ref, others_ref, begun_ref,
    keep_ref, send_ref, right_ref, total_ref,
):
    planes, depth, _ = rows_ref.shape
    same = same_site(sites, depth)
    count = depth // sites
    _, ys, colours, zs, _ = high_ref.shape
    links = low_ref[:, ys:, :, :, :ys].reshape(-1, ys)
    lanes = past_maps_ref.shape[1] // 2
    count = links.shape[0]
    spread = past_maps_ref[:ys, :lanes].astype(jnp.bfloat16)
    match = past_maps_ref[ys : ys + count, lanes:]
    start = past_maps_ref.shape[0] - 24
    choose = past_maps_ref[start : start + 16, :count].astype(jnp.bfloat16)
    past = dot(choose, (dot(links, spread) * match).astype(jnp.bfloat16))
    past = jnp.where(past_maps_ref[start + 16 : start + 17, :lanes] > 0.5, past[:8], past[8:])
    count = depth // sites
    above = rows_ref[place_of(1, planes)]
    set_right(right_ref, 0, move_plane(same, count, ahead_ref[0], past, above, plane_rows(low_ref, ys)))
    x = planes - 1
    below = rows_ref[place_of(x - 1, planes)]
    moved = move_plane(same, count, ahead_ref[x], back_ref[x - 1], plane_rows(high_ref, ys), below)
    set_right(right_ref, 1, moved)
    inner = (planes - 2) * depth
    lefts = [own_ref[:, inner:]] + [others_ref[k, :, inner:] for k in range(others_ref.shape[0])]
    project(lefts, right_ref[...], True, begun_ref, keep_ref, send_ref, total_ref)


def move_y_kernel(
    sites, zs, rows_ref, others_ref, near_ref, far_ref, ahead_ref, back_ref, turned_ref, field_ref
):
    planes, depth, width = rows_ref.shape
    groups = others_ref.shape[0] + 1
    row_size = depth // sites * zs
    reach = depth + near_ref.shape[1]
    head = back_ref.shape[2] - 128
    site, lane = iotas((sites, reach))
    inner = lane < depth
    upper = (lane >= depth) & (lane < depth + row_size)
    lower = (lane >= depth + row_size) & (lane < depth + 2 * row_size)
    lane_z = lane % zs
    to_next = (inner & (lane % sites == site + zs)) | (upper & (site == sites - zs + lane_z))
    to_last = (inner & (lane % sites == site - zs)) | (lower & (site == lane_z))
    to_next = jnp.where(to_next, -1.0, 0.0)
    to_last = jnp.where(to_last, -1.0, 0.0)
    _, lane = iotas((8, 128))
    for x in range(planes):
        past = near_ref[x, 2 * row_size : 2 * row_size + 8, :128].astype(jnp.float32)
        mixed = jnp.where(lane >= depth + row_size - head, past, back_ref[x, :, head:])
        back = jnp.concatenate([back_ref[x, :, :head], mixed], axis=1)[:, :reach]
        matrix = site_matrix([(ahead_ref[x, :, :reach], to_next), (back, to_last)], depth // sites)
        place = place_of(x, planes)
        column = jnp.concatenate([rows_ref[place], near_ref[x]], axis=0)
        field_ref[0, place] = dot(matrix, column).astype(jnp.bfloat16)
        for k in range(groups - 1):
            column = jnp.concatenate([others_ref[k, place], far_ref[k, x]], axis=0)
            field_ref[k + 1, place] = dot(matrix, column).astype(jnp.bfloat16)
    for k in range(groups):
        turned_ref[k] = field_ref[k].reshape(planes * depth, width).T


def second_kernel(lefts_ref, right_ref, begun_ref, keep_ref, send_ref, total_ref):
    inner = lefts_ref.shape[2] - right_ref.shape[0]
    lefts = [lefts_ref[k, :, inner:] for k in range(lefts_ref.shape[0])]
    project(lefts, right_ref[...], False, begun_ref, keep_ref, send_ref, total_ref)


def swap(block, axis, bit):
    return lax.ppermute(block, axis, [(i, i ^ (1 << bit)) for i in range(lax.axis_size(axis))])


def merge_kernel(dim, axis, bit, kept_ref, came_ref, keep_ref, send_ref):
    mine = lax.bitwise_and(lax.shift_right_logical(lax.axis_index(axis), bit), 1)
    for gx in range(keep_ref.shape[1]):
        for gy in range(keep_ref.shape[2]):
            pair = []
            for odd in range(2):
                at = (slice(None), 2 * gx + odd, gy) if dim == 1 else (slice(None), gx, 2 * gy + odd)
                pair.append(kept_ref[at] + came_ref[at].astype(jnp.float32))
            keep_ref[:, gx, gy] = jnp.where(mine == 0, pair[0], pair[1])
            send_ref[:, gx, gy] = jnp.where(mine == 0, pair[1], pair[0]).astype(send_ref.dtype)


def halve(kept, came, axis, bit):
    dim = ("gx", "gy").index(axis) + 1
    dims = kept.shape[:dim] + (kept.shape[dim] // 2,) + kept.shape[dim + 1 :]

    def merge(*refs):
        merge_kernel(dim, axis, bit, *refs)

    keep, send = call(
        merge, (pltpu.VMEM(dims, jnp.float32), pltpu.VMEM(dims, jnp.bfloat16)), kept.size, [kept, came]
    )
    return keep, swap(send, axis, bit)


def finish_kernel(*refs):
    out_ref = refs[-1]
    for d in range(out_ref.shape[0]):
        kept_ref, came_ref = refs[2 * d : 2 * d + 2]
        out_ref[d] = kept_ref[:, 0, 0] + came_ref[:, 0, 0].astype(jnp.float32)


def bits(axis):
    return range(lax.axis_size(axis).bit_length() - 1)


def local(eigen_modes, links_first, links_second):
    f32, bf16 = jnp.float32, jnp.bfloat16
    parts, planes, ys, zs, colours, width = eigen_modes.shape
    sites = ys * zs
    depth = parts * colours * sites
    row_size = parts * colours * zs
    edge = -(-(2 * row_size + 8) // 16) * 16
    lanes = -(-(depth + 2 * row_size) // 128) * 128
    across_x, across_y, groups = (lax.axis_size(a) for a in ("gx", "gy", "ma"))
    rows = groups * width // (across_x * across_y)
    inner_depth = (planes - 2) * depth
    raw = eigen_modes.transpose(0, 1, 2, 4, 3, 5)

    def shape(*dims, dtype=bf16):
        return pltpu.VMEM(dims, dtype)

    field_shape = shape(planes, depth, width)
    turned_shape = shape(width, planes * depth)
    total_shape = shape(groups, width, parts * width, dtype=f32)
    link_shape = shape(planes, 8, lanes, dtype=f32)
    total = pltpu.VMEM(total_shape.shape, f32)
    step_flops = 2 * planes * depth * depth * width
    project_flops = 2 * groups * width * planes * depth * parts * width

    raw_others = [shifted(raw, "ma", -step) for step in range(1, groups)]
    raw_links_x, raw_links_y = (a.transpose(0, 1, 2, 3, 5, 4) for a in (links_first, links_second))
    maps = jnp.asarray(np.concatenate(lane_maps(parts, colours, planes, ys, zs, lanes)))
    past_maps = jnp.asarray(np.concatenate(lane_maps(parts, colours, 1, ys, zs, lanes)))
    inputs = [raw, raw_links_x, raw_links_y, maps]
    first_plane, last_plane, *inputs = call(
        edges_kernel,
        (
            shape(parts, ys, colours, zs, width), shape(parts, ys + colours, colours, zs, width),
            *(shape(*a.shape, dtype=a.dtype) for a in inputs),
        ),
        0,
        inputs,
        [pltpu.SemaphoreType.DMA((6,))],
        [pltpu.HBM] * len(inputs),
    )
    low = shifted(last_plane, "gx", 1)
    high = shifted(first_plane, "gx", -1)
    field, ends, ahead_x, back_x, ahead_y, back_y = call(
        prepare_kernel,
        (field_shape, shape(planes, edge, width), link_shape, link_shape, link_shape, link_shape),
        0,
        inputs,
    )
    near = shifted(ends, "gy", 1)
    if across_y != 2:
        ahead_row = lax.broadcasted_iota(jnp.int32, ends.shape, 1) < row_size
        near = jnp.where(ahead_row, shifted(ends, "gy", -1), near)

    def inner(*refs):
        inner_kernel(sites, *refs)

    def first(*refs):
        first_kernel(sites, *refs)

    def move_y(*refs):
        move_y_kernel(sites, zs, *refs)

    right, own = call(
        inner, (shape(inner_depth, parts * width), turned_shape), 2 * step_flops, [field, ahead_x, back_x]
    )
    turned = [call(turn_kernel, (field_shape, turned_shape), step_flops // 4, [r]) for r in raw_others]
    fields = jnp.stack([t[0] for t in turned])
    others = jnp.stack([t[1] for t in turned])
    begun_first = call(begin_first_kernel, total_shape, project_flops, [own, others, right])
    keep_first, send_first, right_edge = call(
        first,
        (
            shape(parts, across_x, across_y // 2, rows, width, dtype=f32),
            shape(parts, across_x, across_y // 2, rows, width),
            shape(2 * depth, parts * width),
        ),
        project_flops,
        [field, high, low, ahead_x, back_x, past_maps, own, others, begun_first],
        [total],
    )
    near, right_edge = lax.optimization_barrier((near, right_edge))
    far = jnp.stack([shifted(near, "ma", -step) for step in range(1, groups)])
    lefts = call(
        move_y, shape(groups, width, planes * depth), 2 * step_flops,
        [field, fields, near, far, ahead_y, back_y],
        [pltpu.VMEM((groups,) + field_shape.shape, bf16)],
    )
    begun_second = call(begin_second_kernel, total_shape, project_flops, [lefts, right])
    keep_second, send_second = call(
        second_kernel,
        (
            shape(parts, across_x // 2, across_y, rows, width, dtype=f32),
            shape(parts, across_x // 2, across_y, rows, width),
        ),
        project_flops,
        [lefts, right_edge, begun_second],
        [total],
    )
    first_came = swap(send_first, "gy", 0)
    second_came = swap(send_second, "gx", 0)
    for bit in list(bits("gy"))[1:]:
        keep_first, first_came = halve(keep_first, first_came, "gy", bit)
    for bit in bits("gy"):
        keep_second, second_came = halve(keep_second, second_came, "gy", bit)
    for bit in bits("gx"):
        keep_first, first_came = halve(keep_first, first_came, "gx", bit)
    for bit in list(bits("gx"))[1:]:
        keep_second, second_came = halve(keep_second, second_came, "gx", bit)
    return call(
        finish_kernel, jax.ShapeDtypeStruct((2, parts, rows, width), f32), keep_first.size * 2,
        [keep_first, first_came, keep_second, second_came],
    )


def solution(mesh):
    return jax.shard_map(
        local,
        mesh=mesh,
        in_specs=(
            P("cuts", "gx", "gy", None, None, "ma"),
            P("cuts", None, None, "gx", "gy", None),
            P("cuts", None, None, "gx", "gy", None),
        ),
        out_specs=P("cuts", None, ("gx", "gy"), "ma"),
        check_vma=False,
    )
```

profile of v0, /device:TPU:0, one launch (start us, length us, event | category | flops | bytes accessed | tf_op | source)
XLA Modules:
  0.0 37.9 jit_solution(6555169884568446842)
XLA Ops:
  0.0 0.5 %collective-permute-start.2 = (bf16[2,8,16,3,2,256]{5,4,3,2,1,0:T(2,128)(2,1)}, bf16[2,8,16,3,2,256]{5,4,3,2,1,0:T(2,128)(2,1)S(1)}, u32[]{:S(2)}, u32[]{:S(2)}) collective-permute-start(bf16[2,8,16,3,2,256]{5,4,3,2,1,0:T(2,128)(2,1)} %bitcast.10), channel_id=1, source_target_pairs={{1,0},{0,1},{3,2},{2,3},{5,4},{4,5},{7,6},{6,7},{9,8},{8,9},{11,10... | collective-permute-start | bytes 2359304 | tf_op jit(solution)/shard_map/ppermute | solution.py:15
  0.5 1.7 %shard_map.55 = (bf16[2,16,3,2,256]{4,3,2,1,0:T(2,128)(2,1)S(1)}, bf16[2,19,3,2,256]{4,3,2,1,0:T(2,128)(2,1)S(1)}, bf16[2,8,16,3,2,256]{5,4,3,2,1,0:T(2,128)(2,1...) custom-call(bf16[2,8,16,3,2,256]{5,4,3,2,1,0:T(2,128)(2,1)} %bitcast, ...), custom_call_target="tpu_custom_call" | custom-call | tf_op jit(solution)/shard_map/pallas_call | solution.py:20
  2.2 2.6 %collective-permute-start.1 = (bf16[2,19,3,2,256]{4,3,2,1,0:T(2,128)(2,1)S(1)}, bf16[2,19,3,2,256]{4,3,2,1,0:T(2,128)(2,1)S(1)}, u32[]{:S(2)}, u32[]{:S(2)}) collective-permute-start(bf16[2,19,3,2,256]{4,3,2,1,0:T(2,128)(2,1)S(1)} %get-tuple-element.42), channel_id=1, source_target_pairs={{12,0},{0,4},{4,8},{8,12},{13,1},{1,5},{5,9},{9,13},{14,2},{2,6},{... | collective-permute-start | bytes 350216 | tf_op jit(solution)/shard_map/ppermute | solution.py:15
  4.8 2.1 %collective-permute-start = (bf16[2,16,3,2,256]{4,3,2,1,0:T(2,128)(2,1)S(1)}, bf16[2,16,3,2,256]{4,3,2,1,0:T(2,128)(2,1)S(1)}, u32[]{:S(2)}, u32[]{:S(2)}) collective-permute-start(bf16[2,16,3,2,256]{4,3,2,1,0:T(2,128)(2,1)S(1)} %get-tuple-element.41), channel_id=1, source_target_pairs={{4,0},{8,4},{12,8},{0,12},{5,1},{9,5},{13,9},{1,13},{6,2},{10,6},{... | collective-permute-start | bytes 294920 | tf_op jit(solution)/shard_map/ppermute | solution.py:15
  6.9 0.7 %shard_map.56 = (bf16[8,192,256]{2,1,0:T(8,128)(2,1)S(1)}, bf16[8,32,256]{2,1,0:T(8,128)(2,1)S(1)}, f32[8,8,256]{2,1,0:T(8,128)S(1)}, f32[8,8,256]{2,1,0:T(8,128...) custom-call(bf16[2,8,16,3,2,256]{5,4,3,2,1,0:T(2,128)(2,1)S(1)} %get-tuple-element.36.raw_ref, ...), custom_call_target="tpu_custom_call" | custom-call | tf_op jit(solution)/shard_map/pallas_call | solution.py:20
  7.6 1.7 %collective-permute-start.6 = (bf16[8,32,256]{2,1,0:T(8,128)(2,1)S(1)}, bf16[8,32,256]{2,1,0:T(8,128)(2,1)S(1)}, u32[]{:S(2)}, u32[]{:S(2)}) collective-permute-start(bf16[8,32,256]{2,1,0:T(8,128)(2,1)S(1)} %get-tuple-element.55), channel_id=1, source_target_pairs={{2,0},{0,2},{3,1},{1,3},{6,4},{4,6},{7,5},{5,7},{10,8},{8,10},{11,... | collective-permute-start | bytes 393224 | tf_op jit(solution)/shard_map/ppermute | solution.py:15
  9.3 0.5 %shard_map.57 = (bf16[1152,512]{1,0:T(8,128)(2,1)S(1)}, bf16[256,1536]{1,0:T(8,128)(2,1)S(1)}) custom-call(bf16[8,192,256]{2,1,0:T(8,128)(2,1)S(1)} %get-tuple-element.40.refs_0_, f32[8,8,256]{2,1,0:T(8,128)S(1)} %get-tuple-element.43.refs_1_.refs_3_, f32[8,8,256]{2,1,0:T(8,128)S(1)} %get-tuple-element.44.refs_2_.refs_4_), custom_call_target="tpu_custom_call" | custom-call | flops 150994944 | tf_op jit(solution)/shard_map/pallas_call | solution.py:20
  9.8 0.0 collective-permute-done.2.raw_ref
  9.8 0.3 shard_map.58
  10.1 0.0 copy-start
  10.1 0.8 %shard_map.59.refs_8_ = f32[2,256,512]{2,1,0:T(8,128)S(1)} custom-call(bf16[256,1536]{1,0:T(8,128)(2,1)S(1)} %get-tuple-element.45.own_ref.refs_6_, bf16[1,256,1536]{2,1,0:T(8,128)(2,1)S(1)} %bitcast.6, bf16[1152,512]{1,0:T(8,128)(2,1)S(1)} %get-tuple-element.47.right_ref), custom_call_target="tpu_custom_call" | custom-call | flops 402653184 | tf_op jit(solution)/shard_map/pallas_call | solution.py:20
  11.0 1.3 %collective-permute-done.refs_1_ = bf16[2,16,3,2,256]{4,3,2,1,0:T(2,128)(2,1)S(1)} collective-permute-done((bf16[2,16,3,2,256]{4,3,2,1,0:T(2,128)(2,1)S(1)}, bf16[2,16,3,2,256]{4,3,2,1,0:T(2,128)(2,1)S(1)}, u32[]{:S(2)}, u32[]{:S(2)}) %collective-permute-start) | collective-permute-done | bytes 98336 | tf_op jit(solution)/shard_map/ppermute | solution.py:15
  12.2 0.0 collective-permute-done.1.refs_2_
  12.2 0.0 copy-done
  12.2 1.0 %shard_map.60 = (f32[2,4,1,64,256]{4,3,2,1,0:T(8,128)S(1)}, bf16[2,4,1,64,256]{4,3,2,1,0:T(8,128)(2,1)S(1)}, bf16[384,512]{1,0:T(8,128)(2,1)S(1)}) custom-call(bf16[8,192,256]{2,1,0:T(8,128)(2,1)S(1)} %get-tuple-element.40.refs_0_, bf16[2,16,3,2,256]{4,3,2,1,0:T(2,128)(2,1)S(1)} %collective-permute-done.refs_1_, ...), custom_call_target="tpu_custom_call" | custom-call | flops 402653184 | tf_op jit(solution)/shard_map/pallas_call | solution.py:20
  13.2 0.1 collective-permute-done.6.refs_2_
  13.3 0.0 collective-permute-start.7
  13.3 1.6 %collective-permute-start.3 = (bf16[2,4,1,64,256]{4,3,2,1,0:T(8,128)(2,1)S(1)}, bf16[2,4,1,64,256]{4,3,2,1,0:T(8,128)(2,1)S(1)}, u32[]{:S(2)}, u32[]{:S(2)}) collective-permute-start(bf16[2,4,1,64,256]{4,3,2,1,0:T(8,128)(2,1)S(1)} %get-tuple-element.49), channel_id=1, source_target_pairs={{0,2},{2,0},{1,3},{3,1},{4,6},{6,4},{5,7},{7,5},{8,10},{10,8},{9,1... | collective-permute-start | bytes 786440 | tf_op jit(solution)/shard_map/ppermute | solution.py:338
  14.9 0.0 collective-permute-done.7
  14.9 0.7 %shard_map.63.lefts_ref = bf16[2,256,1536]{2,1,0:T(8,128)(2,1)S(1)} custom-call(bf16[8,192,256]{2,1,0:T(8,128)(2,1)S(1)} %get-tuple-element.40.refs_0_, bf16[1,8,192,256]{3,2,1,0:T(8,128)(2,1)S(1)} %bitcast.8, bf16[8,32,256]{2,1,0:T(8,128)(2,1)S(1)} %collective-permute-done.6.refs_2_, bf16[1,8,32,256]{3,2,1,0:T(8,128)(2,1)S(1)} %bitcast.9, ...), custom_call_target="tpu_custom_call" | custom-call | flops 150994944 | tf_op jit(solution)/shard_map/pallas_call | solution.py:20
  15.5 0.8 %shard_map.64.begun_ref = f32[2,256,512]{2,1,0:T(8,128)S(1)} custom-call(bf16[2,256,1536]{2,1,0:T(8,128)(2,1)S(1)} %shard_map.63.lefts_ref, bf16[1152,512]{1,0:T(8,128)(2,1)S(1)} %get-tuple-element.47.right_ref), custom_call_target="tpu_custom_call" | custom-call | flops 402653184 | tf_op jit(solution)/shard_map/pallas_call | solution.py:20
  16.4 0.5 %shard_map.65 = (f32[2,2,2,64,256]{4,3,2,1,0:T(8,128)S(1)}, bf16[2,2,2,64,256]{4,3,2,1,0:T(8,128)(2,1)S(1)}) custom-call(bf16[2,256,1536]{2,1,0:T(8,128)(2,1)S(1)} %shard_map.63.lefts_ref, bf16[384,512]{1,0:T(8,128)(2,1)S(1)} %get-tuple-element.60.right_ref, f32[2,256,512]{2,1,0:T(8,128)S(1)} %shard_map.64.begun_ref), custom_call_target="tpu_custom_call" | custom-call | flops 402653184 | tf_op jit(solution)/shard_map/pallas_call | solution.py:20
  16.9 1.2 %collective-permute-start.8 = (bf16[2,2,2,64,256]{4,3,2,1,0:T(8,128)(2,1)S(1)}, bf16[2,2,2,64,256]{4,3,2,1,0:T(8,128)(2,1)S(1)}, u32[]{:S(2)}, u32[]{:S(2)}) collective-permute-start(bf16[2,2,2,64,256]{4,3,2,1,0:T(8,128)(2,1)S(1)} %get-tuple-element.62), channel_id=1, source_target_pairs={{0,4},{4,0},{8,12},{12,8},{1,5},{5,1},{9,13},{13,9},{2,6},{6,2},{1... | collective-permute-start | bytes 786440 | tf_op jit(solution)/shard_map/ppermute | solution.py:338
  18.1 4.0 %collective-permute-done.3.refs_1_ = bf16[2,4,1,64,256]{4,3,2,1,0:T(8,128)(2,1)S(1)} collective-permute-done((bf16[2,4,1,64,256]{4,3,2,1,0:T(8,128)(2,1)S(1)}, bf16[2,4,1,64,256]{4,3,2,1,0:T(8,128)(2,1)S(1)}, u32[]{:S(2)}, u32[]{:S(2)}) %collective-permute-start.3) | collective-permute-done | bytes 262176 | tf_op jit(solution)/shard_map/ppermute | solution.py:338
  22.0 0.1 shard_map.61
  22.1 1.2 %collective-permute-start.4 = (bf16[2,2,1,64,256]{4,3,2,1,0:T(8,128)(2,1)S(1)}, bf16[2,2,1,64,256]{4,3,2,1,0:T(8,128)(2,1)S(1)}, u32[]{:S(2)}, u32[]{:S(2)}) collective-permute-start(bf16[2,2,1,64,256]{4,3,2,1,0:T(8,128)(2,1)S(1)} %get-tuple-element.51), channel_id=1, source_target_pairs={{0,4},{4,0},{8,12},{12,8},{1,5},{5,1},{9,13},{13,9},{2,6},{6,2},{1... | collective-permute-start | bytes 393224 | tf_op jit(solution)/shard_map/ppermute | solution.py:338
  23.3 2.8 %collective-permute-done.8.refs_1_ = bf16[2,2,2,64,256]{4,3,2,1,0:T(8,128)(2,1)S(1)} collective-permute-done((bf16[2,2,2,64,256]{4,3,2,1,0:T(8,128)(2,1)S(1)}, bf16[2,2,2,64,256]{4,3,2,1,0:T(8,128)(2,1)S(1)}, u32[]{:S(2)}, u32[]{:S(2)}) %collective-permute-start.8) | collective-permute-done | bytes 262176 | tf_op jit(solution)/shard_map/ppermute | solution.py:338
  26.1 0.1 shard_map.66
  26.2 1.1 %collective-permute-start.9 = (bf16[2,2,1,64,256]{4,3,2,1,0:T(8,128)(2,1)S(1)}, bf16[2,2,1,64,256]{4,3,2,1,0:T(8,128)(2,1)S(1)}, u32[]{:S(2)}, u32[]{:S(2)}) collective-permute-start(bf16[2,2,1,64,256]{4,3,2,1,0:T(8,128)(2,1)S(1)} %get-tuple-element.64), channel_id=1, source_target_pairs={{0,2},{2,0},{1,3},{3,1},{4,6},{6,4},{5,7},{7,5},{8,10},{10,8},{9,1... | collective-permute-start | bytes 393224 | tf_op jit(solution)/shard_map/ppermute | solution.py:338
  27.3 0.8 %collective-permute-done.4.refs_1_ = bf16[2,2,1,64,256]{4,3,2,1,0:T(8,128)(2,1)S(1)} collective-permute-done((bf16[2,2,1,64,256]{4,3,2,1,0:T(8,128)(2,1)S(1)}, bf16[2,2,1,64,256]{4,3,2,1,0:T(8,128)(2,1)S(1)}, u32[]{:S(2)}, u32[]{:S(2)}) %collective-permute-start.4) | collective-permute-done | bytes 131104 | tf_op jit(solution)/shard_map/ppermute | solution.py:338
  28.2 1.3 %collective-permute-start.5 = (bf16[2,1,1,64,256]{4,3,2,1,0:T(8,128)(2,1)S(1)}, bf16[2,1,1,64,256]{4,3,2,1,0:T(8,128)(2,1)S(1)}, u32[]{:S(2)}, u32[]{:S(2)}) collective-permute-start(bf16[2,1,1,64,256]{4,3,2,1,0:T(8,128)(2,1)S(1)} %get-tuple-element.53), channel_id=1, source_target_pairs={{0,8},{4,12},{8,0},{12,4},{1,9},{5,13},{9,1},{13,5},{2,10},{6,14},... | collective-permute-start | bytes 196616 | tf_op jit(solution)/shard_map/ppermute | solution.py:338
  29.5 1.7 %collective-permute-done.9.refs_1_ = bf16[2,2,1,64,256]{4,3,2,1,0:T(8,128)(2,1)S(1)} collective-permute-done((bf16[2,2,1,64,256]{4,3,2,1,0:T(8,128)(2,1)S(1)}, bf16[2,2,1,64,256]{4,3,2,1,0:T(8,128)(2,1)S(1)}, u32[]{:S(2)}, u32[]{:S(2)}) %collective-permute-start.9) | collective-permute-done | bytes 131104 | tf_op jit(solution)/shard_map/ppermute | solution.py:338
  31.2 1.4 %collective-permute-start.10 = (bf16[2,1,1,64,256]{4,3,2,1,0:T(8,128)(2,1)S(1)}, bf16[2,1,1,64,256]{4,3,2,1,0:T(8,128)(2,1)S(1)}, u32[]{:S(2)}, u32[]{:S(2)}) collective-permute-start(bf16[2,1,1,64,256]{4,3,2,1,0:T(8,128)(2,1)S(1)} %get-tuple-element.66), channel_id=1, source_target_pairs={{0,8},{4,12},{8,0},{12,4},{1,9},{5,13},{9,1},{13,5},{2,10},{6,14},... | collective-permute-start | bytes 196616 | tf_op jit(solution)/shard_map/ppermute | solution.py:338
  32.6 2.7 %collective-permute-done.5.refs_1_ = bf16[2,1,1,64,256]{4,3,2,1,0:T(8,128)(2,1)S(1)} collective-permute-done((bf16[2,1,1,64,256]{4,3,2,1,0:T(8,128)(2,1)S(1)}, bf16[2,1,1,64,256]{4,3,2,1,0:T(8,128)(2,1)S(1)}, u32[]{:S(2)}, u32[]{:S(2)}) %collective-permute-start.5) | collective-permute-done | bytes 65568 | tf_op jit(solution)/shard_map/ppermute | solution.py:338
  35.3 1.9 %collective-permute-done.10.refs_3_ = bf16[2,1,1,64,256]{4,3,2,1,0:T(8,128)(2,1)S(1)} collective-permute-done((bf16[2,1,1,64,256]{4,3,2,1,0:T(8,128)(2,1)S(1)}, bf16[2,1,1,64,256]{4,3,2,1,0:T(8,128)(2,1)S(1)}, u32[]{:S(2)}, u32[]{:S(2)}) %collective-permute-start.10) | collective-permute-done | bytes 65568 | tf_op jit(solution)/shard_map/ppermute | solution.py:338
  37.2 0.7 %shard_map.68 = f32[2,2,64,256]{3,2,1,0:T(8,128)} custom-call(f32[2,1,1,64,256]{4,3,2,1,0:T(8,128)S(1)} %get-tuple-element.52.refs_0_, bf16[2,1,1,64,256]{4,3,2,1,0:T(8,128)(2,1)S(1)} %collective-permute-done.5.refs_1_, f32[2,1,1,64,256]{4,3,2,1,0:T(8,128)S(1)} %get-tuple-element.65.refs_2_, bf16[2,1,1,64,256]{4,3,2,1,0:T(8,128)(2,1)S(1)} %collective-permute-done.10.refs_3_), custom_call_target="tpu_custom_call" | custom-call | flops 32768 | tf_op jit(solution)/shard_map/pallas_call | solution.py:20
  (2 shorter events, 0.1 us)
Async XLA Ops:
  0.0 9.8 %collective-permute-start.2 = (bf16[2,8,16,3,2,256]{5,4,3,2,1,0:T(2,128)(2,1)}, bf16[2,8,16,3,2,256]{5,4,3,2,1,0:T(2,128)(2,1)S(1)}, u32[]{:S(2)}, u32[]{:S(2)}) collective-permute-start(bf16[2,8,16,3,2,256]{5,4,3,2,1,0:T(2,128)(2,1)} %bitcast.10), channel_id=1, source_target_pairs={{1,0},{0,1},{3,2},{2,3},{5,4},{4,5},{7,6},{6,7},{9,8},{8,9},{11,10... | collective-permute-start | bytes 2359304 | tf_op jit(solution)/shard_map/ppermute | solution.py:15
  2.2 10.1 %collective-permute-start.1 = (bf16[2,19,3,2,256]{4,3,2,1,0:T(2,128)(2,1)S(1)}, bf16[2,19,3,2,256]{4,3,2,1,0:T(2,128)(2,1)S(1)}, u32[]{:S(2)}, u32[]{:S(2)}) collective-permute-start(bf16[2,19,3,2,256]{4,3,2,1,0:T(2,128)(2,1)S(1)} %get-tuple-element.42), channel_id=1, source_target_pairs={{12,0},{0,4},{4,8},{8,12},{13,1},{1,5},{5,9},{9,13},{14,2},{2,6},{... | collective-permute-start | bytes 350216 | tf_op jit(solution)/shard_map/ppermute | solution.py:15
  4.8 7.4 %collective-permute-start = (bf16[2,16,3,2,256]{4,3,2,1,0:T(2,128)(2,1)S(1)}, bf16[2,16,3,2,256]{4,3,2,1,0:T(2,128)(2,1)S(1)}, u32[]{:S(2)}, u32[]{:S(2)}) collective-permute-start(bf16[2,16,3,2,256]{4,3,2,1,0:T(2,128)(2,1)S(1)} %get-tuple-element.41), channel_id=1, source_target_pairs={{4,0},{8,4},{12,8},{0,12},{5,1},{9,5},{13,9},{1,13},{6,2},{10,6},{... | collective-permute-start | bytes 294920 | tf_op jit(solution)/shard_map/ppermute | solution.py:15
  7.6 5.6 %collective-permute-start.6 = (bf16[8,32,256]{2,1,0:T(8,128)(2,1)S(1)}, bf16[8,32,256]{2,1,0:T(8,128)(2,1)S(1)}, u32[]{:S(2)}, u32[]{:S(2)}) collective-permute-start(bf16[8,32,256]{2,1,0:T(8,128)(2,1)S(1)} %get-tuple-element.55), channel_id=1, source_target_pairs={{2,0},{0,2},{3,1},{1,3},{6,4},{4,6},{7,5},{5,7},{10,8},{8,10},{11,... | collective-permute-start | bytes 393224 | tf_op jit(solution)/shard_map/ppermute | solution.py:15
  10.1 2.1 %copy-start = (f32[96,512]{1,0:T(8,128)S(1)}, f32[96,512]{1,0:T(8,128)}, u32[]{:S(2)}) copy-start(f32[96,512]{1,0:T(8,128)} %constant.5.clone.refs_5_) | copy-start | bytes 589828
  13.3 1.6 %collective-permute-start.7 = (bf16[8,32,256]{2,1,0:T(8,128)(2,1)S(1)}, bf16[8,32,256]{2,1,0:T(8,128)(2,1)S(1)}, u32[]{:S(2)}, u32[]{:S(2)}) collective-permute-start(bf16[8,32,256]{2,1,0:T(8,128)(2,1)S(1)} %collective-permute-done.6.refs_2_), channel_id=1, source_target_pairs={{1,0},{0,1},{3,2},{2,3},{5,4},{4,5},{7,6},{6,7},{9,8},{8,9},{11,10... | collective-permute-start | bytes 393224 | tf_op jit(solution)/shard_map/ppermute | solution.py:15
  13.3 8.7 %collective-permute-start.3 = (bf16[2,4,1,64,256]{4,3,2,1,0:T(8,128)(2,1)S(1)}, bf16[2,4,1,64,256]{4,3,2,1,0:T(8,128)(2,1)S(1)}, u32[]{:S(2)}, u32[]{:S(2)}) collective-permute-start(bf16[2,4,1,64,256]{4,3,2,1,0:T(8,128)(2,1)S(1)} %get-tuple-element.49), channel_id=1, source_target_pairs={{0,2},{2,0},{1,3},{3,1},{4,6},{6,4},{5,7},{7,5},{8,10},{10,8},{9,1... | collective-permute-start | bytes 786440 | tf_op jit(solution)/shard_map/ppermute | solution.py:338
  16.9 9.2 %collective-permute-start.8 = (bf16[2,2,2,64,256]{4,3,2,1,0:T(8,128)(2,1)S(1)}, bf16[2,2,2,64,256]{4,3,2,1,0:T(8,128)(2,1)S(1)}, u32[]{:S(2)}, u32[]{:S(2)}) collective-permute-start(bf16[2,2,2,64,256]{4,3,2,1,0:T(8,128)(2,1)S(1)} %get-tuple-element.62), channel_id=1, source_target_pairs={{0,4},{4,0},{8,12},{12,8},{1,5},{5,1},{9,13},{13,9},{2,6},{6,2},{1... | collective-permute-start | bytes 786440 | tf_op jit(solution)/shard_map/ppermute | solution.py:338
  22.1 6.1 %collective-permute-start.4 = (bf16[2,2,1,64,256]{4,3,2,1,0:T(8,128)(2,1)S(1)}, bf16[2,2,1,64,256]{4,3,2,1,0:T(8,128)(2,1)S(1)}, u32[]{:S(2)}, u32[]{:S(2)}) collective-permute-start(bf16[2,2,1,64,256]{4,3,2,1,0:T(8,128)(2,1)S(1)} %get-tuple-element.51), channel_id=1, source_target_pairs={{0,4},{4,0},{8,12},{12,8},{1,5},{5,1},{9,13},{13,9},{2,6},{6,2},{1... | collective-permute-start | bytes 393224 | tf_op jit(solution)/shard_map/ppermute | solution.py:338
  26.2 5.0 %collective-permute-start.9 = (bf16[2,2,1,64,256]{4,3,2,1,0:T(8,128)(2,1)S(1)}, bf16[2,2,1,64,256]{4,3,2,1,0:T(8,128)(2,1)S(1)}, u32[]{:S(2)}, u32[]{:S(2)}) collective-permute-start(bf16[2,2,1,64,256]{4,3,2,1,0:T(8,128)(2,1)S(1)} %get-tuple-element.64), channel_id=1, source_target_pairs={{0,2},{2,0},{1,3},{3,1},{4,6},{6,4},{5,7},{7,5},{8,10},{10,8},{9,1... | collective-permute-start | bytes 393224 | tf_op jit(solution)/shard_map/ppermute | solution.py:338
  28.2 7.1 %collective-permute-start.5 = (bf16[2,1,1,64,256]{4,3,2,1,0:T(8,128)(2,1)S(1)}, bf16[2,1,1,64,256]{4,3,2,1,0:T(8,128)(2,1)S(1)}, u32[]{:S(2)}, u32[]{:S(2)}) collective-permute-start(bf16[2,1,1,64,256]{4,3,2,1,0:T(8,128)(2,1)S(1)} %get-tuple-element.53), channel_id=1, source_target_pairs={{0,8},{4,12},{8,0},{12,4},{1,9},{5,13},{9,1},{13,5},{2,10},{6,14},... | collective-permute-start | bytes 196616 | tf_op jit(solution)/shard_map/ppermute | solution.py:338
  31.2 5.9 %collective-permute-start.10 = (bf16[2,1,1,64,256]{4,3,2,1,0:T(8,128)(2,1)S(1)}, bf16[2,1,1,64,256]{4,3,2,1,0:T(8,128)(2,1)S(1)}, u32[]{:S(2)}, u32[]{:S(2)}) collective-permute-start(bf16[2,1,1,64,256]{4,3,2,1,0:T(8,128)(2,1)S(1)} %get-tuple-element.66), channel_id=1, source_target_pairs={{0,8},{4,12},{8,0},{12,4},{1,9},{5,13},{9,1},{13,5},{2,10},{6,14},... | collective-permute-start | bytes 196616 | tf_op jit(solution)/shard_map/ppermute | solution.py:338
where the time goes:
time: 38 us; the launch traced here: 37.9 us
  waiting for transfers between devices  15.2 us (40%)
  starting transfers between devices  14.6 us (38%)
  Pallas kernels  7.97 us (21%)
    ppermute x6, waiting for transfers between devices, swap(): lax.ppermute(block, axis, [(i, i ^ 1 << bit) for i in range(lax.axis_size...  13.8 us
    pallas_call x14, Pallas kernels, call(): pl.pallas_call(body, out_shape=out_shape, in_specs=[pl.BlockSpec(memory_s...  7.97 us
    ppermute x6, starting transfers between devices, swap(): lax.ppermute(block, axis, [(i, i ^ 1 << bit) for i in range(lax.axis_size...  7.78 us
    ppermute x5, starting transfers between devices, shifted(): return lax.ppermute(block, axis, route)  6.85 us
    ppermute x5, waiting for transfers between devices, shifted(): return lax.ppermute(block, axis, route)  1.35 us
  transfers between devices with their start and end apart: 11, of which 8 were waited for; matrix products, arithmetic and copies ran while one was open for 0% of the time, Pallas kernels for 19%

commit v1 on v0

--- a/solution.py
+++ b/solution.py
@@ -238,38 +238,55 @@
         total_ref[k] = dot(lefts_ref[k, :, :inner], right)
 
 
-def project(lefts, right, halved, begun_ref, keep_ref, send_ref, total_ref):
-    my_bit = lax.bitwise_and(lax.axis_index("gy" if halved else "gx"), 1)
-    my_modes = lax.axis_index("ma")
+def bits(axis):
+    return range(lax.axis_size(axis).bit_length() - 1)
+
+
+def my_bit(axis, bit):
+    return lax.bitwise_and(lax.shift_right_logical(lax.axis_index(axis), bit), 1)
+
+
+def project(lefts, right, begun_ref, steps, refs, total_ref):
     for k, left in enumerate(lefts):
         total_ref[k] = begun_ref[k] + dot(left, right)
     groups, own_modes, _ = total_ref.shape
-    parts, across_x, across_y, rows, width = keep_ref.shape
-
-    def piece(index):
-        start = index * rows
+    my_modes = lax.axis_index("ma")
+    top = my_bit("gx", bits("gx")[-1])
+    across_x, across_y = lax.axis_size("gx"), lax.axis_size("gy")
+    rows, width = refs[0].shape[3:]
+
+    def piece(gx, gy):
+        start = (gx * across_y + gy) * rows
         group = lax.rem(start // own_modes + groups - my_modes, groups)
         begin = start % own_modes
         return total_ref[group, begin : begin + rows]
 
-    for gx in range(across_x):
-        for gy in range(across_y):
-            if halved:
-                base = gx * 2 * across_y + 2 * gy
-                even, odd = piece(base), piece(base + 1)
-            else:
-                even, odd = piece(2 * gx * across_y + gy), piece((2 * gx + 1) * across_y + gy)
-            keep = jnp.where(my_bit == 0, even, odd)
-            send = jnp.where(my_bit == 0, odd, even).astype(send_ref.dtype)
-            for p in range(parts):
-                keep_ref[p, gx, gy] = keep[:, p * width : (p + 1) * width]
-                send_ref[p, gx, gy] = send[:, p * width : (p + 1) * width]
+    for kind, axis in enumerate(steps):
+        keep_ref, send_ref = refs[2 * kind : 2 * kind + 2]
+        mine = my_bit(axis, 0)
+        half = lax.bitwise_xor(top, 1 - kind)
+
+        def chosen(gx, gy):
+            return jnp.where(half == 0, piece(gx, gy), piece(gx + across_x // 2, gy))
+
+        for gx in range(keep_ref.shape[1]):
+            for gy in range(keep_ref.shape[2]):
+                if axis == "gx":
+                    even, odd = chosen(2 * gx, gy), chosen(2 * gx + 1, gy)
+                else:
+                    even, odd = chosen(gx, 2 * gy), chosen(gx, 2 * gy + 1)
+                keep = jnp.where(mine == 0, even, odd)
+                send = jnp.where(mine == 0, odd, even).astype(send_ref.dtype)
+                for p in range(keep_ref.shape[0]):
+                    keep_ref[p, gx, gy] = keep[:, p * width : (p + 1) * width]
+                    send_ref[p, gx, gy] = send[:, p * width : (p + 1) * width]
 
 
 def first_kernel(
-    sites, rows_ref, high_ref, low_ref, ahead_ref, back_ref, past_maps_ref, own_ref, others_ref, begun_ref,
-    keep_ref, send_ref, right_ref, total_ref,
+    sites, steps, rows_ref, high_ref, low_ref, ahead_ref, back_ref, past_maps_ref, own_ref, others_ref, begun_ref,
+    *refs,
 ):
+    *refs, right_ref, total_ref = refs
     planes, depth, _ = rows_ref.shape
     same = same_site(sites, depth)
     count = depth // sites
@@ -292,7 +309,7 @@
     set_right(right_ref, 1, moved)
     inner = (planes - 2) * depth
     lefts = [own_ref[:, inner:]] + [others_ref[k, :, inner:] for k in range(others_ref.shape[0])]
-    project(lefts, right_ref[...], True, begun_ref, keep_ref, send_ref, total_ref)
+    project(lefts, right_ref[...], begun_ref, steps, refs, total_ref)
 
 
 def move_y_kernel(
@@ -328,50 +345,69 @@
         turned_ref[k] = field_ref[k].reshape(planes * depth, width).T
 
 
-def second_kernel(lefts_ref, right_ref, begun_ref, keep_ref, send_ref, total_ref):
+def second_kernel(steps, lefts_ref, right_ref, begun_ref, *refs):
+    *refs, total_ref = refs
     inner = lefts_ref.shape[2] - right_ref.shape[0]
     lefts = [lefts_ref[k, :, inner:] for k in range(lefts_ref.shape[0])]
-    project(lefts, right_ref[...], False, begun_ref, keep_ref, send_ref, total_ref)
+    project(lefts, right_ref[...], begun_ref, steps, refs, total_ref)
 
 
 def swap(block, axis, bit):
     return lax.ppermute(block, axis, [(i, i ^ (1 << bit)) for i in range(lax.axis_size(axis))])
 
 
-def merge_kernel(dim, axis, bit, kept_ref, came_ref, keep_ref, send_ref):
-    mine = lax.bitwise_and(lax.shift_right_logical(lax.axis_index(axis), bit), 1)
+def merge_kernel(axis, bit, kept_ref, came_ref, keep_ref, send_ref):
+    mine = my_bit(axis, bit)
     for gx in range(keep_ref.shape[1]):
         for gy in range(keep_ref.shape[2]):
             pair = []
             for odd in range(2):
-                at = (slice(None), 2 * gx + odd, gy) if dim == 1 else (slice(None), gx, 2 * gy + odd)
+                at = (slice(None), 2 * gx + odd, gy) if axis == "gx" else (slice(None), gx, 2 * gy + odd)
                 pair.append(kept_ref[at] + came_ref[at].astype(jnp.float32))
             keep_ref[:, gx, gy] = jnp.where(mine == 0, pair[0], pair[1])
             send_ref[:, gx, gy] = jnp.where(mine == 0, pair[1], pair[0]).astype(send_ref.dtype)
 
 
-def halve(kept, came, axis, bit):
-    dim = ("gx", "gy").index(axis) + 1
-    dims = kept.shape[:dim] + (kept.shape[dim] // 2,) + kept.shape[dim + 1 :]
-
-    def merge(*refs):
-        merge_kernel(dim, axis, bit, *refs)
-
-    keep, send = call(
-        merge, (pltpu.VMEM(dims, jnp.float32), pltpu.VMEM(dims, jnp.bfloat16)), kept.size, [kept, came]
-    )
-    return keep, swap(send, axis, bit)
+def sum_kernel(kept_ref, came_ref, send_ref):
+    send_ref[...] = (kept_ref[...] + came_ref[...].astype(jnp.float32)).astype(send_ref.dtype)
 
 
 def finish_kernel(*refs):
     out_ref = refs[-1]
     for d in range(out_ref.shape[0]):
-        kept_ref, came_ref = refs[2 * d : 2 * d + 2]
-        out_ref[d] = kept_ref[:, 0, 0] + came_ref[:, 0, 0].astype(jnp.float32)
-
-
-def bits(axis):
-    return range(lax.axis_size(axis).bit_length() - 1)
+        kept_ref, came_ref, crossed_ref = refs[3 * d : 3 * d + 3]
+        total = kept_ref[:, 0, 0] + came_ref[:, 0, 0].astype(jnp.float32)
+        out_ref[d] = total + crossed_ref[:, 0, 0].astype(jnp.float32)
+
+
+class Reduction:
+    def __init__(self, kept, sent, axis):
+        *low, self.top = [("gx", bit) for bit in bits("gx")]
+        across = [("gy", bit) for bit in bits("gy")]
+        self.steps = across + low[1:] if axis == "gx" else across[1:] + low
+        self.kept, self.came = kept, swap(sent, axis, 0)
+
+    def halve(self, after):
+        (axis, bit), *self.steps = self.steps
+        dim = ("gx", "gy").index(axis) + 1
+        shape = self.kept.shape
+        shape = shape[:dim] + (shape[dim] // 2,) + shape[dim + 1 :]
+
+        def merge(*refs):
+            merge_kernel(axis, bit, *refs)
+
+        self.came, _ = lax.optimization_barrier((self.came, after))
+        self.kept, sent = call(
+            merge, (pltpu.VMEM(shape, jnp.float32), pltpu.VMEM(shape, jnp.bfloat16)), 0, [self.kept, self.came]
+        )
+        self.came = swap(sent, axis, bit)
+        return self.kept
+
+    def cross(self, after):
+        self.came, _ = lax.optimization_barrier((self.came, after))
+        sent = call(sum_kernel, pltpu.VMEM(self.kept.shape, jnp.bfloat16), 0, [self.kept, self.came])
+        self.came = swap(sent, *self.top)
+        return sent
 
 
 def local(eigen_modes, links_first, links_second):
@@ -427,11 +463,23 @@
         ahead_row = lax.broadcasted_iota(jnp.int32, ends.shape, 1) < row_size
         near = jnp.where(ahead_row, shifted(ends, "gy", -1), near)
 
+    first_steps, second_steps = ("gx", "gx"), ("gy", "gx")
+
+    def split(steps):
+        shapes = []
+        for axis in steps:
+            dims = (across_x // 4, across_y) if axis == "gx" else (across_x // 2, across_y // 2)
+            shapes += [shape(parts, *dims, rows, width, dtype=dtype) for dtype in (f32, bf16)]
+        return shapes
+
     def inner(*refs):
         inner_kernel(sites, *refs)
 
     def first(*refs):
-        first_kernel(sites, *refs)
+        first_kernel(sites, first_steps, *refs)
+
+    def second(*refs):
+        second_kernel(second_steps, *refs)
 
     def move_y(*refs):
         move_y_kernel(sites, zs, *refs)
@@ -443,13 +491,9 @@
     fields = jnp.stack([t[0] for t in turned])
     others = jnp.stack([t[1] for t in turned])
     begun_first = call(begin_first_kernel, total_shape, project_flops, [own, others, right])
-    keep_first, send_first, right_edge = call(
+    *parts_first, right_edge = call(
         first,
-        (
-            shape(parts, across_x, across_y // 2, rows, width, dtype=f32),
-            shape(parts, across_x, across_y // 2, rows, width),
-            shape(2 * depth, parts * width),
-        ),
+        (*split(first_steps), shape(2 * depth, parts * width)),
         project_flops,
         [field, high, low, ahead_x, back_x, past_maps, own, others, begun_first],
         [total],
@@ -462,30 +506,31 @@
         [pltpu.VMEM((groups,) + field_shape.shape, bf16)],
     )
     begun_second = call(begin_second_kernel, total_shape, project_flops, [lefts, right])
-    keep_second, send_second = call(
-        second_kernel,
-        (
-            shape(parts, across_x // 2, across_y, rows, width, dtype=f32),
-            shape(parts, across_x // 2, across_y, rows, width),
-        ),
-        project_flops,
-        [lefts, right_edge, begun_second],
-        [total],
-    )
-    first_came = swap(send_first, "gy", 0)
-    second_came = swap(send_second, "gx", 0)
-    for bit in list(bits("gy"))[1:]:
-        keep_first, first_came = halve(keep_first, first_came, "gy", bit)
-    for bit in bits("gy"):
-        keep_second, second_came = halve(keep_second, second_came, "gy", bit)
-    for bit in bits("gx"):
-        keep_first, first_came = halve(keep_first, first_came, "gx", bit)
-    for bit in list(bits("gx"))[1:]:
-        keep_second, second_came = halve(keep_second, second_came, "gx", bit)
-    return call(
-        finish_kernel, jax.ShapeDtypeStruct((2, parts, rows, width), f32), keep_first.size * 2,
-        [keep_first, first_came, keep_second, second_came],
-    )
+    parts_second = call(
+        second, split(second_steps), project_flops, [lefts, right_edge, begun_second], [total]
+    )
+    crossing, staying = (
+        [
+            Reduction(*parts_first[k : k + 2], first_steps[k // 2]),
+            Reduction(*parts_second[k : k + 2], second_steps[k // 2]),
+        ]
+        for k in (0, 2)
+    )
+    after = parts_second[0]
+    while any(r.steps for r in crossing):
+        for r in crossing:
+            if r.steps:
+                after = r.halve(after)
+    for r in crossing:
+        after = r.cross(after)
+    while any(r.steps for r in staying):
+        for r in staying:
+            if r.steps:
+                after = r.halve(after)
+    sums = []
+    for stay, cross in zip(staying, crossing):
+        sums += [stay.kept, stay.came, cross.came]
+    return call(finish_kernel, jax.ShapeDtypeStruct((2, parts, rows, width), f32), 0, sums)
 
 
 def solution(mesh):

time: 38 us -> 37.5 us (0.987)
  waiting for transfers between devices: 15.2 us -> 10.3 us
  starting transfers between devices: 14.6 us -> 18.8 us
    ppermute x6 -> x10, waiting for transfers between devices: 13.8 us -> 8.85 us  [swap(): lax.ppermute(block, axis, [(i, i ^ 1 << bit) for i in range(lax.axis_size...]
    ppermute x6 -> x10, starting transfers between devices: 7.78 us -> 11.9 us  [swap(): lax.ppermute(block, axis, [(i, i ^ 1 << bit) for i in range(lax.axis_size...]
    pallas_call x14 -> x16, Pallas kernels: 7.97 us -> 8.03 us  [call(): pl.pallas_call(body, out_shape=out_shape, in_specs=[pl.BlockSpec(memory_s...]
  transfers between devices with their start and end apart: 11 -> 15, of which waited for: 8 -> 8; matrix products, arithmetic and copies ran while one was open for 0% -> 0% of each run, Pallas kernels for 19% -> 20%
where the time goes in v1:
time: 37.5 us; the launch traced here: 37.3 us
  starting transfers between devices  18.8 us (50%)
  waiting for transfers between devices  10.3 us (27%)
  Pallas kernels  8.03 us (21%)
    ppermute x10, starting transfers between devices, swap(): lax.ppermute(block, axis, [(i, i ^ 1 << bit) for i in range(lax.axis_size...  11.9 us
    ppermute x10, waiting for transfers between devices, swap(): lax.ppermute(block, axis, [(i, i ^ 1 << bit) for i in range(lax.axis_size...  8.85 us
    pallas_call x16, Pallas kernels, call(): pl.pallas_call(body, out_shape=out_shape, in_specs=[pl.BlockSpec(memory_s...  8.03 us
    ppermute x5, starting transfers between devices, shifted(): return lax.ppermute(block, axis, route)  6.88 us
    ppermute x5, waiting for transfers between devices, shifted(): return lax.ppermute(block, axis, route)  1.46 us
  transfers between devices with their start and end apart: 15, of which 8 were waited for; matrix products, arithmetic and copies ran while one was open for 0% of the time, Pallas kernels for 20%

profile of v1, /device:TPU:0, one launch (start us, length us, event | category | flops | bytes accessed | tf_op | source)
XLA Modules:
  0.0 37.3 jit_solution(157228544961194970)
XLA Ops:
  0.0 0.5 %collective-permute-start.2 = (bf16[2,8,16,3,2,256]{5,4,3,2,1,0:T(2,128)(2,1)}, bf16[2,8,16,3,2,256]{5,4,3,2,1,0:T(2,128)(2,1)S(1)}, u32[]{:S(2)}, u32[]{:S(2)}) collective-permute-start(bf16[2,8,16,3,2,256]{5,4,3,2,1,0:T(2,128)(2,1)} %bitcast.10), channel_id=1, source_target_pairs={{1,0},{0,1},{3,2},{2,3},{5,4},{4,5},{7,6},{6,7},{9,8},{8,9},{11,10... | collective-permute-start | bytes 2359304 | tf_op jit(solution)/shard_map/ppermute | solution.py:15
  0.5 1.7 %shard_map.55 = (bf16[2,16,3,2,256]{4,3,2,1,0:T(2,128)(2,1)S(1)}, bf16[2,19,3,2,256]{4,3,2,1,0:T(2,128)(2,1)S(1)}, bf16[2,8,16,3,2,256]{5,4,3,2,1,0:T(2,128)(2,1...) custom-call(bf16[2,8,16,3,2,256]{5,4,3,2,1,0:T(2,128)(2,1)} %bitcast, ...), custom_call_target="tpu_custom_call" | custom-call | tf_op jit(solution)/shard_map/pallas_call | solution.py:20
  2.2 2.6 %collective-permute-start.1 = (bf16[2,19,3,2,256]{4,3,2,1,0:T(2,128)(2,1)S(1)}, bf16[2,19,3,2,256]{4,3,2,1,0:T(2,128)(2,1)S(1)}, u32[]{:S(2)}, u32[]{:S(2)}) collective-permute-start(bf16[2,19,3,2,256]{4,3,2,1,0:T(2,128)(2,1)S(1)} %get-tuple-element.52), channel_id=1, source_target_pairs={{12,0},{0,4},{4,8},{8,12},{13,1},{1,5},{5,9},{9,13},{14,2},{2,6},{... | collective-permute-start | bytes 350216 | tf_op jit(solution)/shard_map/ppermute | solution.py:15
  4.8 2.1 %collective-permute-start = (bf16[2,16,3,2,256]{4,3,2,1,0:T(2,128)(2,1)S(1)}, bf16[2,16,3,2,256]{4,3,2,1,0:T(2,128)(2,1)S(1)}, u32[]{:S(2)}, u32[]{:S(2)}) collective-permute-start(bf16[2,16,3,2,256]{4,3,2,1,0:T(2,128)(2,1)S(1)} %get-tuple-element.51), channel_id=1, source_target_pairs={{4,0},{8,4},{12,8},{0,12},{5,1},{9,5},{13,9},{1,13},{6,2},{10,6},{... | collective-permute-start | bytes 294920 | tf_op jit(solution)/shard_map/ppermute | solution.py:15
  6.9 0.7 %shard_map.56 = (bf16[8,192,256]{2,1,0:T(8,128)(2,1)S(1)}, bf16[8,32,256]{2,1,0:T(8,128)(2,1)S(1)}, f32[8,8,256]{2,1,0:T(8,128)S(1)}, f32[8,8,256]{2,1,0:T(8,128...) custom-call(bf16[2,8,16,3,2,256]{5,4,3,2,1,0:T(2,128)(2,1)S(1)} %get-tuple-element.46.raw_ref, ...), custom_call_target="tpu_custom_call" | custom-call | tf_op jit(solution)/shard_map/pallas_call | solution.py:20
  7.6 1.7 %collective-permute-start.4 = (bf16[8,32,256]{2,1,0:T(8,128)(2,1)S(1)}, bf16[8,32,256]{2,1,0:T(8,128)(2,1)S(1)}, u32[]{:S(2)}, u32[]{:S(2)}) collective-permute-start(bf16[8,32,256]{2,1,0:T(8,128)(2,1)S(1)} %get-tuple-element.61), channel_id=1, source_target_pairs={{2,0},{0,2},{3,1},{1,3},{6,4},{4,6},{7,5},{5,7},{10,8},{8,10},{11,... | collective-permute-start | bytes 393224 | tf_op jit(solution)/shard_map/ppermute | solution.py:15
  9.3 0.5 %shard_map.57 = (bf16[1152,512]{1,0:T(8,128)(2,1)S(1)}, bf16[256,1536]{1,0:T(8,128)(2,1)S(1)}) custom-call(bf16[8,192,256]{2,1,0:T(8,128)(2,1)S(1)} %get-tuple-element.50.refs_0_, f32[8,8,256]{2,1,0:T(8,128)S(1)} %get-tuple-element.53.refs_1_.refs_3_, f32[8,8,256]{2,1,0:T(8,128)S(1)} %get-tuple-element.54.refs_2_.refs_4_), custom_call_target="tpu_custom_call" | custom-call | flops 150994944 | tf_op jit(solution)/shard_map/pallas_call | solution.py:20
  9.8 0.0 collective-permute-done.2.raw_ref
  9.8 0.3 shard_map.58
  10.1 0.0 copy-start
  10.1 0.8 %shard_map.59.refs_8_ = f32[2,256,512]{2,1,0:T(8,128)S(1)} custom-call(bf16[256,1536]{1,0:T(8,128)(2,1)S(1)} %get-tuple-element.55.own_ref.refs_6_, bf16[1,256,1536]{2,1,0:T(8,128)(2,1)S(1)} %bitcast.6, bf16[1152,512]{1,0:T(8,128)(2,1)S(1)} %get-tuple-element.57.right_ref), custom_call_target="tpu_custom_call" | custom-call | flops 402653184 | tf_op jit(solution)/shard_map/pallas_call | solution.py:20
  11.0 1.3 %collective-permute-done.refs_1_ = bf16[2,16,3,2,256]{4,3,2,1,0:T(2,128)(2,1)S(1)} collective-permute-done((bf16[2,16,3,2,256]{4,3,2,1,0:T(2,128)(2,1)S(1)}, bf16[2,16,3,2,256]{4,3,2,1,0:T(2,128)(2,1)S(1)}, u32[]{:S(2)}, u32[]{:S(2)}) %collective-permute-start) | collective-permute-done | bytes 98336 | tf_op jit(solution)/shard_map/ppermute | solution.py:15
  12.2 0.0 collective-permute-done.1.refs_2_
  12.2 0.0 copy-done
  12.2 1.0 %shard_map.60 = (f32[2,1,2,64,256]{4,3,2,1,0:T(8,128)S(1)}, bf16[2,1,2,64,256]{4,3,2,1,0:T(8,128)(2,1)S(1)}, f32[2,1,2,64,256]{4,3,2,1,0:T(8,128)S(1)}, bf16[2,1...) custom-call(bf16[8,192,256]{2,1,0:T(8,128)(2,1)S(1)} %get-tuple-element.50.refs_0_, ...), custom_call_target="tpu_custom_call" | custom-call | flops 402653184 | tf_op jit(solution)/shard_map/pallas_call | solution.py:20
  13.2 0.0 collective-permute-done.4.refs_2_
  13.3 0.0 collective-permute-start.5
  13.3 1.2 %collective-permute-start.7 = (bf16[2,1,2,64,256]{4,3,2,1,0:T(8,128)(2,1)S(1)}, bf16[2,1,2,64,256]{4,3,2,1,0:T(8,128)(2,1)S(1)}, u32[]{:S(2)}, u32[]{:S(2)}) collective-permute-start(bf16[2,1,2,64,256]{4,3,2,1,0:T(8,128)(2,1)S(1)} %get-tuple-element.70), channel_id=1, source_target_pairs={{0,4},{4,0},{8,12},{12,8},{1,5},{5,1},{9,13},{13,9},{2,6},{6,2},{1... | collective-permute-start | bytes 393224 | tf_op jit(solution)/shard_map/ppermute | solution.py:356
  14.5 0.1 collective-permute-done.5
  14.7 0.7 %shard_map.61.lefts_ref.refs_0_ = bf16[2,256,1536]{2,1,0:T(8,128)(2,1)S(1)} custom-call(bf16[8,192,256]{2,1,0:T(8,128)(2,1)S(1)} %get-tuple-element.50.refs_0_, bf16[1,8,192,256]{3,2,1,0:T(8,128)(2,1)S(1)} %bitcast.8, bf16[8,32,256]{2,1,0:T(8,128)(2,1)S(1)} %collective-permute-done.4.refs_2_, bf16[1,8,32,256]{3,2,1,0:T(8,128)(2,1)S(1)} %bitcast.9, ...), custom_call_target="tpu_custom_call" | custom-call | flops 150994944 | tf_op jit(solution)/shard_map/pallas_call | solution.py:20
  15.3 0.8 %shard_map.62.refs_2_ = f32[2,256,512]{2,1,0:T(8,128)S(1)} custom-call(bf16[2,256,1536]{2,1,0:T(8,128)(2,1)S(1)} %shard_map.61.lefts_ref.refs_0_, bf16[1152,512]{1,0:T(8,128)(2,1)S(1)} %get-tuple-element.57.right_ref), custom_call_target="tpu_custom_call" | custom-call | flops 402653184 | tf_op jit(solution)/shard_map/pallas_call | solution.py:20
  16.2 0.6 %shard_map.63 = (f32[2,2,1,64,256]{4,3,2,1,0:T(8,128)S(1)}, bf16[2,2,1,64,256]{4,3,2,1,0:T(8,128)(2,1)S(1)}, f32[2,1,2,64,256]{4,3,2,1,0:T(8,128)S(1)}, bf16[2,1,2,64,256]{4,3,2,1,0:T(8,128)(2,1)S(1)}) custom-call(bf16[2,256,1536]{2,1,0:T(8,128)(2,1)S(1)} %shard_map.61.lefts_ref.refs_0_, bf16[384,512]{1,0:T(8,128)(2,1)S(1)} %get-tuple-element.66.refs_1_, ...), custom_call_target="tpu_custom_call" | custom-call | flops 402653184 | tf_op jit(solution)/shard_map/pallas_call | solution.py:20
  16.7 1.6 %collective-permute-start.6 = (bf16[2,2,1,64,256]{4,3,2,1,0:T(8,128)(2,1)S(1)}, bf16[2,2,1,64,256]{4,3,2,1,0:T(8,128)(2,1)S(1)}, u32[]{:S(2)}, u32[]{:S(2)}) collective-permute-start(bf16[2,2,1,64,256]{4,3,2,1,0:T(8,128)(2,1)S(1)} %get-tuple-element.68), channel_id=1, source_target_pairs={{0,2},{2,0},{1,3},{3,1},{4,6},{6,4},{5,7},{7,5},{8,10},{10,8},{9,1... | collective-permute-start | bytes 393224 | tf_op jit(solution)/shard_map/ppermute | solution.py:356
  18.3 1.1 %collective-permute-start.3 = (bf16[2,1,2,64,256]{4,3,2,1,0:T(8,128)(2,1)S(1)}, bf16[2,1,2,64,256]{4,3,2,1,0:T(8,128)(2,1)S(1)}, u32[]{:S(2)}, u32[]{:S(2)}) collective-permute-start(bf16[2,1,2,64,256]{4,3,2,1,0:T(8,128)(2,1)S(1)} %get-tuple-element.59), channel_id=1, source_target_pairs={{0,4},{4,0},{8,12},{12,8},{1,5},{5,1},{9,13},{13,9},{2,6},{6,2},{1... | collective-permute-start | bytes 393224 | tf_op jit(solution)/shard_map/ppermute | solution.py:356
  19.4 0.9 %collective-permute-start.12 = (bf16[2,1,2,64,256]{4,3,2,1,0:T(8,128)(2,1)S(1)}, bf16[2,1,2,64,256]{4,3,2,1,0:T(8,128)(2,1)S(1)}, u32[]{:S(2)}, u32[]{:S(2)}) collective-permute-start(bf16[2,1,2,64,256]{4,3,2,1,0:T(8,128)(2,1)S(1)} %get-tuple-element.83), channel_id=1, source_target_pairs={{0,4},{4,0},{8,12},{12,8},{1,5},{5,1},{9,13},{13,9},{2,6},{6,2},{1... | collective-permute-start | bytes 393224 | tf_op jit(solution)/shard_map/ppermute | solution.py:356
  20.3 0.0 collective-permute-done.7.refs_1_
  20.4 0.6 %collective-permute-start.9 = (bf16[2,1,1,64,256]{4,3,2,1,0:T(8,128)(2,1)S(1)}, bf16[2,1,1,64,256]{4,3,2,1,0:T(8,128)(2,1)S(1)}, u32[]{:S(2)}, u32[]{:S(2)}) collective-permute-start(bf16[2,1,1,64,256]{4,3,2,1,0:T(8,128)(2,1)S(1)} %get-tuple-element.76), channel_id=1, source_target_pairs={{0,2},{2,0},{1,3},{3,1},{4,6},{6,4},{5,7},{7,5},{8,10},{10,8},{9,1... | collective-permute-start | bytes 196616 | tf_op jit(solution)/shard_map/ppermute | solution.py:356
  21.0 1.4 %collective-permute-done.6.refs_1_ = bf16[2,2,1,64,256]{4,3,2,1,0:T(8,128)(2,1)S(1)} collective-permute-done((bf16[2,2,1,64,256]{4,3,2,1,0:T(8,128)(2,1)S(1)}, bf16[2,2,1,64,256]{4,3,2,1,0:T(8,128)(2,1)S(1)}, u32[]{:S(2)}, u32[]{:S(2)}) %collective-permute-start.6) | collective-permute-done | bytes 131104 | tf_op jit(solution)/shard_map/ppermute | solution.py:356
  22.4 1.2 %collective-permute-start.8 = (bf16[2,1,1,64,256]{4,3,2,1,0:T(8,128)(2,1)S(1)}, bf16[2,1,1,64,256]{4,3,2,1,0:T(8,128)(2,1)S(1)}, u32[]{:S(2)}, u32[]{:S(2)}) collective-permute-start(bf16[2,1,1,64,256]{4,3,2,1,0:T(8,128)(2,1)S(1)} %get-tuple-element.75), channel_id=1, source_target_pairs={{0,4},{4,0},{8,12},{12,8},{1,5},{5,1},{9,13},{13,9},{2,6},{6,2},{1... | collective-permute-start | bytes 196616 | tf_op jit(solution)/shard_map/ppermute | solution.py:356
  23.6 1.1 %collective-permute-done.9.came_ref = bf16[2,1,1,64,256]{4,3,2,1,0:T(8,128)(2,1)S(1)} collective-permute-done((bf16[2,1,1,64,256]{4,3,2,1,0:T(8,128)(2,1)S(1)}, bf16[2,1,1,64,256]{4,3,2,1,0:T(8,128)(2,1)S(1)}, u32[]{:S(2)}, u32[]{:S(2)}) %collective-permute-start.9) | collective-permute-done | bytes 65568 | tf_op jit(solution)/shard_map/ppermute | solution.py:356
  24.7 1.7 %collective-permute-start.11 = (bf16[2,1,1,64,256]{4,3,2,1,0:T(8,128)(2,1)S(1)}, bf16[2,1,1,64,256]{4,3,2,1,0:T(8,128)(2,1)S(1)}, u32[]{:S(2)}, u32[]{:S(2)}) collective-permute-start(bf16[2,1,1,64,256]{4,3,2,1,0:T(8,128)(2,1)S(1)} %shard_map.66), channel_id=1, source_target_pairs={{0,8},{4,12},{8,0},{12,4},{1,9},{5,13},{9,1},{13,5},{2,10},{6,14},... | collective-permute-start | bytes 196616 | tf_op jit(solution)/shard_map/ppermute | solution.py:356
  26.4 2.1 %collective-permute-done.8.came_ref = bf16[2,1,1,64,256]{4,3,2,1,0:T(8,128)(2,1)S(1)} collective-permute-done((bf16[2,1,1,64,256]{4,3,2,1,0:T(8,128)(2,1)S(1)}, bf16[2,1,1,64,256]{4,3,2,1,0:T(8,128)(2,1)S(1)}, u32[]{:S(2)}, u32[]{:S(2)}) %collective-permute-start.8) | collective-permute-done | bytes 65568 | tf_op jit(solution)/shard_map/ppermute | solution.py:356
  28.5 0.0 collective-permute-done.3.refs_1_
  28.6 0.0 collective-permute-done.12.refs_1_
  28.6 1.2 %collective-permute-start.13 = (bf16[2,1,1,64,256]{4,3,2,1,0:T(8,128)(2,1)S(1)}, bf16[2,1,1,64,256]{4,3,2,1,0:T(8,128)(2,1)S(1)}, u32[]{:S(2)}, u32[]{:S(2)}) collective-permute-start(bf16[2,1,1,64,256]{4,3,2,1,0:T(8,128)(2,1)S(1)} %get-tuple-element.86), channel_id=1, source_target_pairs={{0,2},{2,0},{1,3},{3,1},{4,6},{6,4},{5,7},{7,5},{8,10},{10,8},{9,1... | collective-permute-start | bytes 196616 | tf_op jit(solution)/shard_map/ppermute | solution.py:356
  29.8 0.9 %collective-permute-start.10 = (bf16[2,1,1,64,256]{4,3,2,1,0:T(8,128)(2,1)S(1)}, bf16[2,1,1,64,256]{4,3,2,1,0:T(8,128)(2,1)S(1)}, u32[]{:S(2)}, u32[]{:S(2)}) collective-permute-start(bf16[2,1,1,64,256]{4,3,2,1,0:T(8,128)(2,1)S(1)} %get-tuple-element.81), channel_id=1, source_target_pairs={{0,2},{2,0},{1,3},{3,1},{4,6},{6,4},{5,7},{7,5},{8,10},{10,8},{9,1... | collective-permute-start | bytes 196616 | tf_op jit(solution)/shard_map/ppermute | solution.py:356
  30.7 1.6 %collective-permute-start.14 = (bf16[2,1,1,64,256]{4,3,2,1,0:T(8,128)(2,1)S(1)}, bf16[2,1,1,64,256]{4,3,2,1,0:T(8,128)(2,1)S(1)}, u32[]{:S(2)}, u32[]{:S(2)}) collective-permute-start(bf16[2,1,1,64,256]{4,3,2,1,0:T(8,128)(2,1)S(1)} %shard_map.67), channel_id=1, source_target_pairs={{0,8},{4,12},{8,0},{12,4},{1,9},{5,13},{9,1},{13,5},{2,10},{6,14},... | collective-permute-start | bytes 196616 | tf_op jit(solution)/shard_map/ppermute | solution.py:356
  32.3 0.0 collective-permute-done.11.refs_2_
  32.3 0.6 %collective-permute-done.13.refs_4_ = bf16[2,1,1,64,256]{4,3,2,1,0:T(8,128)(2,1)S(1)} collective-permute-done((bf16[2,1,1,64,256]{4,3,2,1,0:T(8,128)(2,1)S(1)}, bf16[2,1,1,64,256]{4,3,2,1,0:T(8,128)(2,1)S(1)}, u32[]{:S(2)}, u32[]{:S(2)}) %collective-permute-start.13) | collective-permute-done | bytes 65568 | tf_op jit(solution)/shard_map/ppermute | solution.py:356
  33.0 1.1 %collective-permute-done.10.refs_1_ = bf16[2,1,1,64,256]{4,3,2,1,0:T(8,128)(2,1)S(1)} collective-permute-done((bf16[2,1,1,64,256]{4,3,2,1,0:T(8,128)(2,1)S(1)}, bf16[2,1,1,64,256]{4,3,2,1,0:T(8,128)(2,1)S(1)}, u32[]{:S(2)}, u32[]{:S(2)}) %collective-permute-start.10) | collective-permute-done | bytes 65568 | tf_op jit(solution)/shard_map/ppermute | solution.py:356
  34.1 2.5 %collective-permute-done.14.refs_5_ = bf16[2,1,1,64,256]{4,3,2,1,0:T(8,128)(2,1)S(1)} collective-permute-done((bf16[2,1,1,64,256]{4,3,2,1,0:T(8,128)(2,1)S(1)}, bf16[2,1,1,64,256]{4,3,2,1,0:T(8,128)(2,1)S(1)}, u32[]{:S(2)}, u32[]{:S(2)}) %collective-permute-start.14) | collective-permute-done | bytes 65568 | tf_op jit(solution)/shard_map/ppermute | solution.py:356
  36.6 0.7 %shard_map.70 = f32[2,2,64,256]{3,2,1,0:T(8,128)} custom-call(f32[2,1,1,64,256]{4,3,2,1,0:T(8,128)S(1)} %get-tuple-element.80.refs_0_, bf16[2,1,1,64,256]{4,3,2,1,0:T(8,128)(2,1)S(1)} %collective-permute-done.10.refs_1_, bf16[2,1,1,64,256]{4,3,2,1,0:T(8,128)(2,1)S(1)} %collective-permute-done.11.refs_2_, ...), custom_call_target="tpu_custom_call" | custom-call | tf_op jit(solution)/shard_map/pallas_call | solution.py:20
  (6 shorter events, 0.2 us)
Async XLA Ops:
  0.0 9.8 %collective-permute-start.2 = (bf16[2,8,16,3,2,256]{5,4,3,2,1,0:T(2,128)(2,1)}, bf16[2,8,16,3,2,256]{5,4,3,2,1,0:T(2,128)(2,1)S(1)}, u32[]{:S(2)}, u32[]{:S(2)}) collective-permute-start(bf16[2,8,16,3,2,256]{5,4,3,2,1,0:T(2,128)(2,1)} %bitcast.10), channel_id=1, source_target_pairs={{1,0},{0,1},{3,2},{2,3},{5,4},{4,5},{7,6},{6,7},{9,8},{8,9},{11,10... | collective-permute-start | bytes 2359304 | tf_op jit(solution)/shard_map/ppermute | solution.py:15
  2.2 10.1 %collective-permute-start.1 = (bf16[2,19,3,2,256]{4,3,2,1,0:T(2,128)(2,1)S(1)}, bf16[2,19,3,2,256]{4,3,2,1,0:T(2,128)(2,1)S(1)}, u32[]{:S(2)}, u32[]{:S(2)}) collective-permute-start(bf16[2,19,3,2,256]{4,3,2,1,0:T(2,128)(2,1)S(1)} %get-tuple-element.52), channel_id=1, source_target_pairs={{12,0},{0,4},{4,8},{8,12},{13,1},{1,5},{5,9},{9,13},{14,2},{2,6},{... | collective-permute-start | bytes 350216 | tf_op jit(solution)/shard_map/ppermute | solution.py:15
  4.8 7.4 %collective-permute-start = (bf16[2,16,3,2,256]{4,3,2,1,0:T(2,128)(2,1)S(1)}, bf16[2,16,3,2,256]{4,3,2,1,0:T(2,128)(2,1)S(1)}, u32[]{:S(2)}, u32[]{:S(2)}) collective-permute-start(bf16[2,16,3,2,256]{4,3,2,1,0:T(2,128)(2,1)S(1)} %get-tuple-element.51), channel_id=1, source_target_pairs={{4,0},{8,4},{12,8},{0,12},{5,1},{9,5},{13,9},{1,13},{6,2},{10,6},{... | collective-permute-start | bytes 294920 | tf_op jit(solution)/shard_map/ppermute | solution.py:15
  7.6 5.6 %collective-permute-start.4 = (bf16[8,32,256]{2,1,0:T(8,128)(2,1)S(1)}, bf16[8,32,256]{2,1,0:T(8,128)(2,1)S(1)}, u32[]{:S(2)}, u32[]{:S(2)}) collective-permute-start(bf16[8,32,256]{2,1,0:T(8,128)(2,1)S(1)} %get-tuple-element.61), channel_id=1, source_target_pairs={{2,0},{0,2},{3,1},{1,3},{6,4},{4,6},{7,5},{5,7},{10,8},{8,10},{11,... | collective-permute-start | bytes 393224 | tf_op jit(solution)/shard_map/ppermute | solution.py:15
  10.1 2.1 %copy-start = (f32[96,512]{1,0:T(8,128)S(1)}, f32[96,512]{1,0:T(8,128)}, u32[]{:S(2)}) copy-start(f32[96,512]{1,0:T(8,128)} %constant.5.clone.refs_5_) | copy-start | bytes 589828
  13.3 1.4 %collective-permute-start.5 = (bf16[8,32,256]{2,1,0:T(8,128)(2,1)S(1)}, bf16[8,32,256]{2,1,0:T(8,128)(2,1)S(1)}, u32[]{:S(2)}, u32[]{:S(2)}) collective-permute-start(bf16[8,32,256]{2,1,0:T(8,128)(2,1)S(1)} %collective-permute-done.4.refs_2_), channel_id=1, source_target_pairs={{1,0},{0,1},{3,2},{2,3},{5,4},{4,5},{7,6},{6,7},{9,8},{8,9},{11,10... | collective-permute-start | bytes 393224 | tf_op jit(solution)/shard_map/ppermute | solution.py:15
  13.3 7.0 %collective-permute-start.7 = (bf16[2,1,2,64,256]{4,3,2,1,0:T(8,128)(2,1)S(1)}, bf16[2,1,2,64,256]{4,3,2,1,0:T(8,128)(2,1)S(1)}, u32[]{:S(2)}, u32[]{:S(2)}) collective-permute-start(bf16[2,1,2,64,256]{4,3,2,1,0:T(8,128)(2,1)S(1)} %get-tuple-element.70), channel_id=1, source_target_pairs={{0,4},{4,0},{8,12},{12,8},{1,5},{5,1},{9,13},{13,9},{2,6},{6,2},{1... | collective-permute-start | bytes 393224 | tf_op jit(solution)/shard_map/ppermute | solution.py:356
  16.7 5.6 %collective-permute-start.6 = (bf16[2,2,1,64,256]{4,3,2,1,0:T(8,128)(2,1)S(1)}, bf16[2,2,1,64,256]{4,3,2,1,0:T(8,128)(2,1)S(1)}, u32[]{:S(2)}, u32[]{:S(2)}) collective-permute-start(bf16[2,2,1,64,256]{4,3,2,1,0:T(8,128)(2,1)S(1)} %get-tuple-element.68), channel_id=1, source_target_pairs={{0,2},{2,0},{1,3},{3,1},{4,6},{6,4},{5,7},{7,5},{8,10},{10,8},{9,1... | collective-permute-start | bytes 393224 | tf_op jit(solution)/shard_map/ppermute | solution.py:356
  18.3 10.2 %collective-permute-start.3 = (bf16[2,1,2,64,256]{4,3,2,1,0:T(8,128)(2,1)S(1)}, bf16[2,1,2,64,256]{4,3,2,1,0:T(8,128)(2,1)S(1)}, u32[]{:S(2)}, u32[]{:S(2)}) collective-permute-start(bf16[2,1,2,64,256]{4,3,2,1,0:T(8,128)(2,1)S(1)} %get-tuple-element.59), channel_id=1, source_target_pairs={{0,4},{4,0},{8,12},{12,8},{1,5},{5,1},{9,13},{13,9},{2,6},{6,2},{1... | collective-permute-start | bytes 393224 | tf_op jit(solution)/shard_map/ppermute | solution.py:356
  19.4 9.1 %collective-permute-start.12 = (bf16[2,1,2,64,256]{4,3,2,1,0:T(8,128)(2,1)S(1)}, bf16[2,1,2,64,256]{4,3,2,1,0:T(8,128)(2,1)S(1)}, u32[]{:S(2)}, u32[]{:S(2)}) collective-permute-start(bf16[2,1,2,64,256]{4,3,2,1,0:T(8,128)(2,1)S(1)} %get-tuple-element.83), channel_id=1, source_target_pairs={{0,4},{4,0},{8,12},{12,8},{1,5},{5,1},{9,13},{13,9},{2,6},{6,2},{1... | collective-permute-start | bytes 393224 | tf_op jit(solution)/shard_map/ppermute | solution.py:356
  20.4 4.3 %collective-permute-start.9 = (bf16[2,1,1,64,256]{4,3,2,1,0:T(8,128)(2,1)S(1)}, bf16[2,1,1,64,256]{4,3,2,1,0:T(8,128)(2,1)S(1)}, u32[]{:S(2)}, u32[]{:S(2)}) collective-permute-start(bf16[2,1,1,64,256]{4,3,2,1,0:T(8,128)(2,1)S(1)} %get-tuple-element.76), channel_id=1, source_target_pairs={{0,2},{2,0},{1,3},{3,1},{4,6},{6,4},{5,7},{7,5},{8,10},{10,8},{9,1... | collective-permute-start | bytes 196616 | tf_op jit(solution)/shard_map/ppermute | solution.py:356
  22.4 6.1 %collective-permute-start.8 = (bf16[2,1,1,64,256]{4,3,2,1,0:T(8,128)(2,1)S(1)}, bf16[2,1,1,64,256]{4,3,2,1,0:T(8,128)(2,1)S(1)}, u32[]{:S(2)}, u32[]{:S(2)}) collective-permute-start(bf16[2,1,1,64,256]{4,3,2,1,0:T(8,128)(2,1)S(1)} %get-tuple-element.75), channel_id=1, source_target_pairs={{0,4},{4,0},{8,12},{12,8},{1,5},{5,1},{9,13},{13,9},{2,6},{6,2},{1... | collective-permute-start | bytes 196616 | tf_op jit(solution)/shard_map/ppermute | solution.py:356
  24.7 7.6 %collective-permute-start.11 = (bf16[2,1,1,64,256]{4,3,2,1,0:T(8,128)(2,1)S(1)}, bf16[2,1,1,64,256]{4,3,2,1,0:T(8,128)(2,1)S(1)}, u32[]{:S(2)}, u32[]{:S(2)}) collective-permute-start(bf16[2,1,1,64,256]{4,3,2,1,0:T(8,128)(2,1)S(1)} %shard_map.66), channel_id=1, source_target_pairs={{0,8},{4,12},{8,0},{12,4},{1,9},{5,13},{9,1},{13,5},{2,10},{6,14},... | collective-permute-start | bytes 196616 | tf_op jit(solution)/shard_map/ppermute | solution.py:356
  28.6 4.3 %collective-permute-start.13 = (bf16[2,1,1,64,256]{4,3,2,1,0:T(8,128)(2,1)S(1)}, bf16[2,1,1,64,256]{4,3,2,1,0:T(8,128)(2,1)S(1)}, u32[]{:S(2)}, u32[]{:S(2)}) collective-permute-start(bf16[2,1,1,64,256]{4,3,2,1,0:T(8,128)(2,1)S(1)} %get-tuple-element.86), channel_id=1, source_target_pairs={{0,2},{2,0},{1,3},{3,1},{4,6},{6,4},{5,7},{7,5},{8,10},{10,8},{9,1... | collective-permute-start | bytes 196616 | tf_op jit(solution)/shard_map/ppermute | solution.py:356
  29.8 4.3 %collective-permute-start.10 = (bf16[2,1,1,64,256]{4,3,2,1,0:T(8,128)(2,1)S(1)}, bf16[2,1,1,64,256]{4,3,2,1,0:T(8,128)(2,1)S(1)}, u32[]{:S(2)}, u32[]{:S(2)}) collective-permute-start(bf16[2,1,1,64,256]{4,3,2,1,0:T(8,128)(2,1)S(1)} %get-tuple-element.81), channel_id=1, source_target_pairs={{0,2},{2,0},{1,3},{3,1},{4,6},{6,4},{5,7},{7,5},{8,10},{10,8},{9,1... | collective-permute-start | bytes 196616 | tf_op jit(solution)/shard_map/ppermute | solution.py:356
  30.7 5.9 %collective-permute-start.14 = (bf16[2,1,1,64,256]{4,3,2,1,0:T(8,128)(2,1)S(1)}, bf16[2,1,1,64,256]{4,3,2,1,0:T(8,128)(2,1)S(1)}, u32[]{:S(2)}, u32[]{:S(2)}) collective-permute-start(bf16[2,1,1,64,256]{4,3,2,1,0:T(8,128)(2,1)S(1)} %shard_map.67), channel_id=1, source_target_pairs={{0,8},{4,12},{8,0},{12,4},{1,9},{5,13},{9,1},{13,5},{2,10},{6,14},... | collective-permute-start | bytes 196616 | tf_op jit(solution)/shard_map/ppermute | solution.py:356

commit v2 on v1

--- a/solution.py
+++ b/solution.py
@@ -118,13 +118,11 @@
 
 def edges_kernel(
     raw_hbm, links_x_hbm, links_y_hbm, maps_hbm,
-    first_ref, last_ref, raw_ref, links_x_ref, links_y_ref, maps_ref, arrived,
+    first_ref, last_ref, links_x_ref, links_y_ref, maps_ref, arrived,
 ):
     parts, planes, ys, colours, zs, _ = raw_hbm.shape
-    sources = (
-        raw_hbm.at[:, planes - 1], raw_hbm.at[:, 0], links_x_hbm, links_y_hbm, maps_hbm, raw_hbm
-    )
-    targets = (last_ref.at[:, :ys], first_ref, links_x_ref, links_y_ref, maps_ref, raw_ref)
+    sources = (raw_hbm.at[:, planes - 1], raw_hbm.at[:, 0], links_x_hbm, links_y_hbm, maps_hbm)
+    targets = (last_ref.at[:, :ys], first_ref, links_x_ref, links_y_ref, maps_ref)
     copies = [
         pltpu.make_async_copy(source, target, arrived.at[i])
         for i, (source, target) in enumerate(zip(sources, targets))
@@ -150,9 +148,11 @@
 
 
 def prepare_kernel(
-    raw_ref, links_x_ref, links_y_ref, maps_ref,
-    rows_ref, ends_ref, ahead_x_ref, back_x_ref, ahead_y_ref, back_y_ref,
+    raw_hbm, links_x_ref, links_y_ref, maps_ref,
+    rows_ref, ends_ref, ahead_x_ref, back_x_ref, ahead_y_ref, back_y_ref, raw_ref, arrived,
 ):
+    copy = pltpu.make_async_copy(raw_hbm, raw_ref, arrived)
+    copy.start()
     planes, depth, width = rows_ref.shape
     zs = raw_ref.shape[4]
     ys = raw_ref.shape[2]
@@ -173,6 +173,7 @@
     ends = (lane == wanted).astype(jnp.bfloat16)
     filler = jnp.zeros((8, width - 128), jnp.float32)
     spare = ends_ref.shape[1] - 2 * row_size - 8
+    copy.wait()
     for x in range(planes):
         plane = plane_rows(raw_ref.at[:, x], ys)
         rows_ref[place_of(x, planes)] = plane
@@ -387,7 +388,7 @@
         self.steps = across + low[1:] if axis == "gx" else across[1:] + low
         self.kept, self.came = kept, swap(sent, axis, 0)
 
-    def halve(self, after):
+    def halve(self, after, weight=0):
         (axis, bit), *self.steps = self.steps
         dim = ("gx", "gy").index(axis) + 1
         shape = self.kept.shape
@@ -398,7 +399,7 @@
 
         self.came, _ = lax.optimization_barrier((self.came, after))
         self.kept, sent = call(
-            merge, (pltpu.VMEM(shape, jnp.float32), pltpu.VMEM(shape, jnp.bfloat16)), 0, [self.kept, self.came]
+            merge, (pltpu.VMEM(shape, jnp.float32), pltpu.VMEM(shape, jnp.bfloat16)), weight, [self.kept, self.came]
         )
         self.came = swap(sent, axis, bit)
         return self.kept
@@ -443,11 +444,11 @@
         edges_kernel,
         (
             shape(parts, ys, colours, zs, width), shape(parts, ys + colours, colours, zs, width),
-            *(shape(*a.shape, dtype=a.dtype) for a in inputs),
+            *(shape(*a.shape, dtype=a.dtype) for a in inputs[1:]),
         ),
         0,
         inputs,
-        [pltpu.SemaphoreType.DMA((6,))],
+        [pltpu.SemaphoreType.DMA((5,))],
         [pltpu.HBM] * len(inputs),
     )
     low = shifted(last_plane, "gx", 1)
@@ -456,14 +457,16 @@
         prepare_kernel,
         (field_shape, shape(planes, edge, width), link_shape, link_shape, link_shape, link_shape),
         0,
-        inputs,
+        [raw] + inputs,
+        [pltpu.VMEM(raw.shape, bf16), pltpu.SemaphoreType.DMA],
+        [pltpu.HBM] + [pltpu.VMEM] * len(inputs),
     )
     near = shifted(ends, "gy", 1)
     if across_y != 2:
         ahead_row = lax.broadcasted_iota(jnp.int32, ends.shape, 1) < row_size
         near = jnp.where(ahead_row, shifted(ends, "gy", -1), near)
 
-    first_steps, second_steps = ("gx", "gx"), ("gy", "gx")
+    first_steps, second_steps = ("gx", "gy"), ("gy", "gx")
 
     def split(steps):
         shapes = []
@@ -509,24 +512,25 @@
     parts_second = call(
         second, split(second_steps), project_flops, [lefts, right_edge, begun_second], [total]
     )
-    crossing, staying = (
-        [
-            Reduction(*parts_first[k : k + 2], first_steps[k // 2]),
-            Reduction(*parts_second[k : k + 2], second_steps[k // 2]),
-        ]
-        for k in (0, 2)
-    )
-    after = parts_second[0]
+    crossing = [
+        Reduction(*parts_first[:2], first_steps[0]), Reduction(*parts_second[:2], second_steps[0])
+    ]
+    after = crossing[0].halve(parts_second[0])
+    kept, sent = parts_first[2:]
+    sent, _ = lax.optimization_barrier((sent, after))
+    staying = [Reduction(kept, sent, first_steps[1]), Reduction(*parts_second[2:], second_steps[1])]
+    after = crossing[1].halve(after)
     while any(r.steps for r in crossing):
         for r in crossing:
             if r.steps:
                 after = r.halve(after)
     for r in crossing:
         after = r.cross(after)
+    weights = (0, 4 * project_flops)
     while any(r.steps for r in staying):
-        for r in staying:
+        for r in staying[::-1]:
             if r.steps:
-                after = r.halve(after)
+                after = r.halve(after, weights[r is staying[1]])
     sums = []
     for stay, cross in zip(staying, crossing):
         sums += [stay.kept, stay.came, cross.came]

time: 37.5 us -> 36.5 us (0.973)
  waiting for transfers between devices: 10.3 us -> 9.12 us
  Pallas kernels: 8.03 us -> 8.58 us
    ppermute x10, waiting for transfers between devices: 8.85 us -> 6.86 us  [swap(): lax.ppermute(block, axis, [(i, i ^ 1 << bit) for i in range(lax.axis_size...]
    ppermute x5, waiting for transfers between devices: 1.46 us -> 2.26 us  [shifted(): return lax.ppermute(block, axis, route)]
    pallas_call x16, Pallas kernels: 8.03 us -> 8.58 us  [call(): pl.pallas_call(body, out_shape=out_shape, in_specs=[pl.BlockSpec(memory_s...]
    ppermute x10, starting transfers between devices: 11.9 us -> 11.6 us  [swap(): lax.ppermute(block, axis, [(i, i ^ 1 << bit) for i in range(lax.axis_size...]
  transfers between devices with their start and end apart: 15 -> 15, of which waited for: 8 -> 9; matrix products, arithmetic and copies ran while one was open for 0% -> 0% of each run, Pallas kernels for 20% -> 22%
where the time goes in v2:
time: 36.5 us; the launch traced here: 36.3 us
  starting transfers between devices  18.5 us (51%)
  waiting for transfers between devices  9.12 us (25%)
  Pallas kernels  8.58 us (24%)
    ppermute x10, starting transfers between devices, swap(): lax.ppermute(block, axis, [(i, i ^ 1 << bit) for i in range(lax.axis_size...  11.6 us
    pallas_call x16, Pallas kernels, call(): pl.pallas_call(body, out_shape=out_shape, in_specs=[pl.BlockSpec(memory_s...  8.58 us
    ppermute x5, starting transfers between devices, shifted(): return lax.ppermute(block, axis, route)  6.89 us
    ppermute x10, waiting for transfers between devices, swap(): lax.ppermute(block, axis, [(i, i ^ 1 << bit) for i in range(lax.axis_size...  6.86 us
    ppermute x5, waiting for transfers between devices, shifted(): return lax.ppermute(block, axis, route)  2.26 us
  transfers between devices with their start and end apart: 15, of which 9 were waited for; matrix products, arithmetic and copies ran while one was open for 0% of the time, Pallas kernels for 22%

profile of v2, /device:TPU:0, one launch (start us, length us, event | category | flops | bytes accessed | tf_op | source)
XLA Modules:
  0.0 36.3 jit_solution(7576739535980987524)
XLA Ops:
  0.0 0.5 %collective-permute-start.2 = (bf16[2,8,16,3,2,256]{5,4,3,2,1,0:T(2,128)(2,1)}, bf16[2,8,16,3,2,256]{5,4,3,2,1,0:T(2,128)(2,1)S(1)}, u32[]{:S(2)}, u32[]{:S(2)}) collective-permute-start(bf16[2,8,16,3,2,256]{5,4,3,2,1,0:T(2,128)(2,1)} %bitcast.10), channel_id=1, source_target_pairs={{1,0},{0,1},{3,2},{2,3},{5,4},{4,5},{7,6},{6,7},{9,8},{8,9},{11,10... | collective-permute-start | bytes 2359304 | tf_op jit(solution)/shard_map/ppermute | solution.py:15
  0.5 1.5 %shard_map.55 = (bf16[2,16,3,2,256]{4,3,2,1,0:T(2,128)(2,1)S(1)}, bf16[2,19,3,2,256]{4,3,2,1,0:T(2,128)(2,1)S(1)}, bf16[2,3,3,8,2,16]{5,4,3,2,1,0:T(2,128)(2,1)S...) custom-call(bf16[2,8,16,3,2,256]{5,4,3,2,1,0:T(2,128)(2,1)} %bitcast.11, ...), custom_call_target="tpu_custom_call" | custom-call | tf_op jit(solution)/shard_map/pallas_call | solution.py:20
  2.0 2.6 %collective-permute-start.1 = (bf16[2,19,3,2,256]{4,3,2,1,0:T(2,128)(2,1)S(1)}, bf16[2,19,3,2,256]{4,3,2,1,0:T(2,128)(2,1)S(1)}, u32[]{:S(2)}, u32[]{:S(2)}) collective-permute-start(bf16[2,19,3,2,256]{4,3,2,1,0:T(2,128)(2,1)S(1)} %get-tuple-element.51), channel_id=1, source_target_pairs={{12,0},{0,4},{4,8},{8,12},{13,1},{1,5},{5,9},{9,13},{14,2},{2,6},{... | collective-permute-start | bytes 350216 | tf_op jit(solution)/shard_map/ppermute | solution.py:15
  4.6 2.1 %collective-permute-start = (bf16[2,16,3,2,256]{4,3,2,1,0:T(2,128)(2,1)S(1)}, bf16[2,16,3,2,256]{4,3,2,1,0:T(2,128)(2,1)S(1)}, u32[]{:S(2)}, u32[]{:S(2)}) collective-permute-start(bf16[2,16,3,2,256]{4,3,2,1,0:T(2,128)(2,1)S(1)} %get-tuple-element.50), channel_id=1, source_target_pairs={{4,0},{8,4},{12,8},{0,12},{5,1},{9,5},{13,9},{1,13},{6,2},{10,6},{... | collective-permute-start | bytes 294920 | tf_op jit(solution)/shard_map/ppermute | solution.py:15
  6.7 1.5 %shard_map.56 = (bf16[8,192,256]{2,1,0:T(8,128)(2,1)S(1)}, bf16[8,32,256]{2,1,0:T(8,128)(2,1)S(1)}, f32[8,8,256]{2,1,0:T(8,128)S(1)}, f32[8,8,256]{2,1,0:T(8,128...) custom-call(bf16[2,8,16,3,2,256]{5,4,3,2,1,0:T(2,128)(2,1)} %bitcast.12, ...), custom_call_target="tpu_custom_call" | custom-call | tf_op jit(solution)/shard_map/pallas_call | solution.py:20
  8.2 1.7 %collective-permute-start.4 = (bf16[8,32,256]{2,1,0:T(8,128)(2,1)S(1)}, bf16[8,32,256]{2,1,0:T(8,128)(2,1)S(1)}, u32[]{:S(2)}, u32[]{:S(2)}) collective-permute-start(bf16[8,32,256]{2,1,0:T(8,128)(2,1)S(1)} %get-tuple-element.62), channel_id=1, source_target_pairs={{2,0},{0,2},{3,1},{1,3},{6,4},{4,6},{7,5},{5,7},{10,8},{8,10},{11,... | collective-permute-start | bytes 393224 | tf_op jit(solution)/shard_map/ppermute | solution.py:15
  9.9 0.5 %shard_map.57 = (bf16[1152,512]{1,0:T(8,128)(2,1)S(1)}, bf16[256,1536]{1,0:T(8,128)(2,1)S(1)}) custom-call(bf16[8,192,256]{2,1,0:T(8,128)(2,1)S(1)} %get-tuple-element.49.refs_0_, f32[8,8,256]{2,1,0:T(8,128)S(1)} %get-tuple-element.52.refs_1_.refs_3_, f32[8,8,256]{2,1,0:T(8,128)S(1)} %get-tuple-element.53.refs_2_.refs_4_), custom_call_target="tpu_custom_call" | custom-call | flops 150994944 | tf_op jit(solution)/shard_map/pallas_call | solution.py:20
  10.4 0.0 collective-permute-done.2.raw_ref
  10.4 0.3 shard_map.58
  10.7 0.0 copy-start
  10.7 0.8 %shard_map.59.refs_8_ = f32[2,256,512]{2,1,0:T(8,128)S(1)} custom-call(bf16[256,1536]{1,0:T(8,128)(2,1)S(1)} %get-tuple-element.54.own_ref.refs_6_, bf16[1,256,1536]{2,1,0:T(8,128)(2,1)S(1)} %bitcast.6, bf16[1152,512]{1,0:T(8,128)(2,1)S(1)} %get-tuple-element.56.right_ref), custom_call_target="tpu_custom_call" | custom-call | flops 402653184 | tf_op jit(solution)/shard_map/pallas_call | solution.py:20
  11.6 0.4 %collective-permute-done.refs_1_ = bf16[2,16,3,2,256]{4,3,2,1,0:T(2,128)(2,1)S(1)} collective-permute-done((bf16[2,16,3,2,256]{4,3,2,1,0:T(2,128)(2,1)S(1)}, bf16[2,16,3,2,256]{4,3,2,1,0:T(2,128)(2,1)S(1)}, u32[]{:S(2)}, u32[]{:S(2)}) %collective-permute-start) | collective-permute-done | bytes 98336 | tf_op jit(solution)/shard_map/ppermute | solution.py:15
  12.0 0.0 collective-permute-done.1.refs_2_
  12.0 0.0 copy-done
  12.0 1.0 %shard_map.60 = (f32[2,1,2,64,256]{4,3,2,1,0:T(8,128)S(1)}, bf16[2,1,2,64,256]{4,3,2,1,0:T(8,128)(2,1)S(1)}, f32[2,2,1,64,256]{4,3,2,1,0:T(8,128)S(1)}, bf16[2,2...) custom-call(bf16[8,192,256]{2,1,0:T(8,128)(2,1)S(1)} %get-tuple-element.49.refs_0_, ...), custom_call_target="tpu_custom_call" | custom-call | flops 402653184 | tf_op jit(solution)/shard_map/pallas_call | solution.py:20
  13.0 0.9 %collective-permute-done.4.refs_2_ = bf16[8,32,256]{2,1,0:T(8,128)(2,1)S(1)} collective-permute-done((bf16[8,32,256]{2,1,0:T(8,128)(2,1)S(1)}, bf16[8,32,256]{2,1,0:T(8,128)(2,1)S(1)}, u32[]{:S(2)}, u32[]{:S(2)}) %collective-permute-start.4) | collective-permute-done | bytes 131104 | tf_op jit(solution)/shard_map/ppermute | solution.py:15
  13.9 0.0 collective-permute-start.5
  13.9 0.4 %collective-permute-start.3 = (bf16[2,1,2,64,256]{4,3,2,1,0:T(8,128)(2,1)S(1)}, bf16[2,1,2,64,256]{4,3,2,1,0:T(8,128)(2,1)S(1)}, u32[]{:S(2)}, u32[]{:S(2)}) collective-permute-start(bf16[2,1,2,64,256]{4,3,2,1,0:T(8,128)(2,1)S(1)} %get-tuple-element.60), channel_id=1, source_target_pairs={{0,4},{4,0},{8,12},{12,8},{1,5},{5,1},{9,13},{13,9},{2,6},{6,2},{1... | collective-permute-start | bytes 393224 | tf_op jit(solution)/shard_map/ppermute | solution.py:357
  14.3 0.9 %collective-permute-done.5 = bf16[8,32,256]{2,1,0:T(8,128)(2,1)S(1)} collective-permute-done((bf16[8,32,256]{2,1,0:T(8,128)(2,1)S(1)}, bf16[8,32,256]{2,1,0:T(8,128)(2,1)S(1)}, u32[]{:S(2)}, u32[]{:S(2)}) %collective-permute-start.5) | collective-permute-done | bytes 131104 | tf_op jit(solution)/shard_map/ppermute | solution.py:15
  15.2 0.7 %shard_map.61.lefts_ref.refs_0_ = bf16[2,256,1536]{2,1,0:T(8,128)(2,1)S(1)} custom-call(bf16[8,192,256]{2,1,0:T(8,128)(2,1)S(1)} %get-tuple-element.49.refs_0_, bf16[1,8,192,256]{3,2,1,0:T(8,128)(2,1)S(1)} %bitcast.8, bf16[8,32,256]{2,1,0:T(8,128)(2,1)S(1)} %collective-permute-done.4.refs_2_, bf16[1,8,32,256]{3,2,1,0:T(8,128)(2,1)S(1)} %bitcast.9, ...), custom_call_target="tpu_custom_call" | custom-call | flops 150994944 | tf_op jit(solution)/shard_map/pallas_call | solution.py:20
  15.9 0.8 %shard_map.62.refs_2_ = f32[2,256,512]{2,1,0:T(8,128)S(1)} custom-call(bf16[2,256,1536]{2,1,0:T(8,128)(2,1)S(1)} %shard_map.61.lefts_ref.refs_0_, bf16[1152,512]{1,0:T(8,128)(2,1)S(1)} %get-tuple-element.56.right_ref), custom_call_target="tpu_custom_call" | custom-call | flops 402653184 | tf_op jit(solution)/shard_map/pallas_call | solution.py:20
  16.8 0.6 %shard_map.63 = (f32[2,2,1,64,256]{4,3,2,1,0:T(8,128)S(1)}, bf16[2,2,1,64,256]{4,3,2,1,0:T(8,128)(2,1)S(1)}, f32[2,1,2,64,256]{4,3,2,1,0:T(8,128)S(1)}, bf16[2,1,2,64,256]{4,3,2,1,0:T(8,128)(2,1)S(1)}) custom-call(bf16[2,256,1536]{2,1,0:T(8,128)(2,1)S(1)} %shard_map.61.lefts_ref.refs_0_, bf16[384,512]{1,0:T(8,128)(2,1)S(1)} %get-tuple-element.67.refs_1_, ...), custom_call_target="tpu_custom_call" | custom-call | flops 402653184 | tf_op jit(solution)/shard_map/pallas_call | solution.py:20
  17.3 1.6 %collective-permute-start.8 = (bf16[2,2,1,64,256]{4,3,2,1,0:T(8,128)(2,1)S(1)}, bf16[2,2,1,64,256]{4,3,2,1,0:T(8,128)(2,1)S(1)}, u32[]{:S(2)}, u32[]{:S(2)}) collective-permute-start(bf16[2,2,1,64,256]{4,3,2,1,0:T(8,128)(2,1)S(1)} %get-tuple-element.74), channel_id=1, source_target_pairs={{0,2},{2,0},{1,3},{3,1},{4,6},{6,4},{5,7},{7,5},{8,10},{10,8},{9,1... | collective-permute-start | bytes 393224 | tf_op jit(solution)/shard_map/ppermute | solution.py:357
  18.9 0.7 %collective-permute-start.7 = (bf16[2,1,2,64,256]{4,3,2,1,0:T(8,128)(2,1)S(1)}, bf16[2,1,2,64,256]{4,3,2,1,0:T(8,128)(2,1)S(1)}, u32[]{:S(2)}, u32[]{:S(2)}) collective-permute-start(bf16[2,1,2,64,256]{4,3,2,1,0:T(8,128)(2,1)S(1)} %get-tuple-element.73), channel_id=1, source_target_pairs={{0,4},{4,0},{8,12},{12,8},{1,5},{5,1},{9,13},{13,9},{2,6},{6,2},{1... | collective-permute-start | bytes 393224 | tf_op jit(solution)/shard_map/ppermute | solution.py:357
  19.6 0.2 collective-permute-done.3.refs_1_
  19.8 1.6 %collective-permute-start.10 = (bf16[2,1,1,64,256]{4,3,2,1,0:T(8,128)(2,1)S(1)}, bf16[2,1,1,64,256]{4,3,2,1,0:T(8,128)(2,1)S(1)}, u32[]{:S(2)}, u32[]{:S(2)}) collective-permute-start(bf16[2,1,1,64,256]{4,3,2,1,0:T(8,128)(2,1)S(1)} %get-tuple-element.78), channel_id=1, source_target_pairs={{0,2},{2,0},{1,3},{3,1},{4,6},{6,4},{5,7},{7,5},{8,10},{10,8},{9,1... | collective-permute-start | bytes 196616 | tf_op jit(solution)/shard_map/ppermute | solution.py:357
  21.4 2.2 %collective-permute-done.8.refs_1_ = bf16[2,2,1,64,256]{4,3,2,1,0:T(8,128)(2,1)S(1)} collective-permute-done((bf16[2,2,1,64,256]{4,3,2,1,0:T(8,128)(2,1)S(1)}, bf16[2,2,1,64,256]{4,3,2,1,0:T(8,128)(2,1)S(1)}, u32[]{:S(2)}, u32[]{:S(2)}) %collective-permute-start.8) | collective-permute-done | bytes 131104 | tf_op jit(solution)/shard_map/ppermute | solution.py:357
  23.6 0.6 %collective-permute-start.9 = (bf16[2,1,1,64,256]{4,3,2,1,0:T(8,128)(2,1)S(1)}, bf16[2,1,1,64,256]{4,3,2,1,0:T(8,128)(2,1)S(1)}, u32[]{:S(2)}, u32[]{:S(2)}) collective-permute-start(bf16[2,1,1,64,256]{4,3,2,1,0:T(8,128)(2,1)S(1)} %get-tuple-element.77), channel_id=1, source_target_pairs={{0,4},{4,0},{8,12},{12,8},{1,5},{5,1},{9,13},{13,9},{2,6},{6,2},{1... | collective-permute-start | bytes 196616 | tf_op jit(solution)/shard_map/ppermute | solution.py:357
  24.2 1.8 %collective-permute-start.6 = (bf16[2,2,1,64,256]{4,3,2,1,0:T(8,128)(2,1)S(1)}, bf16[2,2,1,64,256]{4,3,2,1,0:T(8,128)(2,1)S(1)}, u32[]{:S(2)}, u32[]{:S(2)}) collective-permute-start(bf16[2,2,1,64,256]{4,3,2,1,0:T(8,128)(2,1)S(1)} %get-tuple-element.71), channel_id=1, source_target_pairs={{0,2},{2,0},{1,3},{3,1},{4,6},{6,4},{5,7},{7,5},{8,10},{10,8},{9,1... | collective-permute-start | bytes 393224 | tf_op jit(solution)/shard_map/ppermute | solution.py:357
  26.0 0.0 collective-permute-done.10.came_ref
  26.0 1.5 %collective-permute-start.12 = (bf16[2,1,1,64,256]{4,3,2,1,0:T(8,128)(2,1)S(1)}, bf16[2,1,1,64,256]{4,3,2,1,0:T(8,128)(2,1)S(1)}, u32[]{:S(2)}, u32[]{:S(2)}) collective-permute-start(bf16[2,1,1,64,256]{4,3,2,1,0:T(8,128)(2,1)S(1)} %shard_map.66), channel_id=1, source_target_pairs={{0,8},{4,12},{8,0},{12,4},{1,9},{5,13},{9,1},{13,5},{2,10},{6,14},... | collective-permute-start | bytes 196616 | tf_op jit(solution)/shard_map/ppermute | solution.py:357
  27.5 1.1 %collective-permute-done.9.came_ref = bf16[2,1,1,64,256]{4,3,2,1,0:T(8,128)(2,1)S(1)} collective-permute-done((bf16[2,1,1,64,256]{4,3,2,1,0:T(8,128)(2,1)S(1)}, bf16[2,1,1,64,256]{4,3,2,1,0:T(8,128)(2,1)S(1)}, u32[]{:S(2)}, u32[]{:S(2)}) %collective-permute-start.9) | collective-permute-done | bytes 65568 | tf_op jit(solution)/shard_map/ppermute | solution.py:357
  28.7 0.4 %collective-permute-start.14 = (bf16[2,1,1,64,256]{4,3,2,1,0:T(8,128)(2,1)S(1)}, bf16[2,1,1,64,256]{4,3,2,1,0:T(8,128)(2,1)S(1)}, u32[]{:S(2)}, u32[]{:S(2)}) collective-permute-start(bf16[2,1,1,64,256]{4,3,2,1,0:T(8,128)(2,1)S(1)} %shard_map.67), channel_id=1, source_target_pairs={{0,8},{4,12},{8,0},{12,4},{1,9},{5,13},{9,1},{13,5},{2,10},{6,14},... | collective-permute-start | bytes 196616 | tf_op jit(solution)/shard_map/ppermute | solution.py:357
  29.1 0.0 collective-permute-done.7.refs_1_
  29.1 2.0 %collective-permute-start.13 = (bf16[2,1,1,64,256]{4,3,2,1,0:T(8,128)(2,1)S(1)}, bf16[2,1,1,64,256]{4,3,2,1,0:T(8,128)(2,1)S(1)}, u32[]{:S(2)}, u32[]{:S(2)}) collective-permute-start(bf16[2,1,1,64,256]{4,3,2,1,0:T(8,128)(2,1)S(1)} %get-tuple-element.86), channel_id=1, source_target_pairs={{0,2},{2,0},{1,3},{3,1},{4,6},{6,4},{5,7},{7,5},{8,10},{10,8},{9,1... | collective-permute-start | bytes 196616 | tf_op jit(solution)/shard_map/ppermute | solution.py:357
  31.2 0.0 collective-permute-done.6.refs_1_
  31.2 1.1 %collective-permute-start.11 = (bf16[2,1,1,64,256]{4,3,2,1,0:T(8,128)(2,1)S(1)}, bf16[2,1,1,64,256]{4,3,2,1,0:T(8,128)(2,1)S(1)}, u32[]{:S(2)}, u32[]{:S(2)}) collective-permute-start(bf16[2,1,1,64,256]{4,3,2,1,0:T(8,128)(2,1)S(1)} %get-tuple-element.85), channel_id=1, source_target_pairs={{0,4},{4,0},{8,12},{12,8},{1,5},{5,1},{9,13},{13,9},{2,6},{6,2},{1... | collective-permute-start | bytes 196616 | tf_op jit(solution)/shard_map/ppermute | solution.py:357
  32.3 0.0 collective-permute-done.12.refs_2_
  32.3 1.2 %collective-permute-done.13.refs_4_ = bf16[2,1,1,64,256]{4,3,2,1,0:T(8,128)(2,1)S(1)} collective-permute-done((bf16[2,1,1,64,256]{4,3,2,1,0:T(8,128)(2,1)S(1)}, bf16[2,1,1,64,256]{4,3,2,1,0:T(8,128)(2,1)S(1)}, u32[]{:S(2)}, u32[]{:S(2)}) %collective-permute-start.13) | collective-permute-done | bytes 65568 | tf_op jit(solution)/shard_map/ppermute | solution.py:357
  33.5 0.8 %collective-permute-done.14.refs_5_ = bf16[2,1,1,64,256]{4,3,2,1,0:T(8,128)(2,1)S(1)} collective-permute-done((bf16[2,1,1,64,256]{4,3,2,1,0:T(8,128)(2,1)S(1)}, bf16[2,1,1,64,256]{4,3,2,1,0:T(8,128)(2,1)S(1)}, u32[]{:S(2)}, u32[]{:S(2)}) %collective-permute-start.14) | collective-permute-done | bytes 65568 | tf_op jit(solution)/shard_map/ppermute | solution.py:357
  34.3 1.3 %collective-permute-done.11.refs_1_ = bf16[2,1,1,64,256]{4,3,2,1,0:T(8,128)(2,1)S(1)} collective-permute-done((bf16[2,1,1,64,256]{4,3,2,1,0:T(8,128)(2,1)S(1)}, bf16[2,1,1,64,256]{4,3,2,1,0:T(8,128)(2,1)S(1)}, u32[]{:S(2)}, u32[]{:S(2)}) %collective-permute-start.11) | collective-permute-done | bytes 65568 | tf_op jit(solution)/shard_map/ppermute | solution.py:357
  35.5 0.7 %shard_map.70 = f32[2,2,64,256]{3,2,1,0:T(8,128)} custom-call(f32[2,1,1,64,256]{4,3,2,1,0:T(8,128)S(1)} %get-tuple-element.84.refs_0_, bf16[2,1,1,64,256]{4,3,2,1,0:T(8,128)(2,1)S(1)} %collective-permute-done.11.refs_1_, bf16[2,1,1,64,256]{4,3,2,1,0:T(8,128)(2,1)S(1)} %collective-permute-done.12.refs_2_, ...), custom_call_target="tpu_custom_call" | custom-call | tf_op jit(solution)/shard_map/pallas_call | solution.py:20
  (6 shorter events, 0.2 us)
Async XLA Ops:
  0.0 10.4 %collective-permute-start.2 = (bf16[2,8,16,3,2,256]{5,4,3,2,1,0:T(2,128)(2,1)}, bf16[2,8,16,3,2,256]{5,4,3,2,1,0:T(2,128)(2,1)S(1)}, u32[]{:S(2)}, u32[]{:S(2)}) collective-permute-start(bf16[2,8,16,3,2,256]{5,4,3,2,1,0:T(2,128)(2,1)} %bitcast.10), channel_id=1, source_target_pairs={{1,0},{0,1},{3,2},{2,3},{5,4},{4,5},{7,6},{6,7},{9,8},{8,9},{11,10... | collective-permute-start | bytes 2359304 | tf_op jit(solution)/shard_map/ppermute | solution.py:15
  2.0 10.1 %collective-permute-start.1 = (bf16[2,19,3,2,256]{4,3,2,1,0:T(2,128)(2,1)S(1)}, bf16[2,19,3,2,256]{4,3,2,1,0:T(2,128)(2,1)S(1)}, u32[]{:S(2)}, u32[]{:S(2)}) collective-permute-start(bf16[2,19,3,2,256]{4,3,2,1,0:T(2,128)(2,1)S(1)} %get-tuple-element.51), channel_id=1, source_target_pairs={{12,0},{0,4},{4,8},{8,12},{13,1},{1,5},{5,9},{9,13},{14,2},{2,6},{... | collective-permute-start | bytes 350216 | tf_op jit(solution)/shard_map/ppermute | solution.py:15
  4.6 7.4 %collective-permute-start = (bf16[2,16,3,2,256]{4,3,2,1,0:T(2,128)(2,1)S(1)}, bf16[2,16,3,2,256]{4,3,2,1,0:T(2,128)(2,1)S(1)}, u32[]{:S(2)}, u32[]{:S(2)}) collective-permute-start(bf16[2,16,3,2,256]{4,3,2,1,0:T(2,128)(2,1)S(1)} %get-tuple-element.50), channel_id=1, source_target_pairs={{4,0},{8,4},{12,8},{0,12},{5,1},{9,5},{13,9},{1,13},{6,2},{10,6},{... | collective-permute-start | bytes 294920 | tf_op jit(solution)/shard_map/ppermute | solution.py:15
  8.2 5.7 %collective-permute-start.4 = (bf16[8,32,256]{2,1,0:T(8,128)(2,1)S(1)}, bf16[8,32,256]{2,1,0:T(8,128)(2,1)S(1)}, u32[]{:S(2)}, u32[]{:S(2)}) collective-permute-start(bf16[8,32,256]{2,1,0:T(8,128)(2,1)S(1)} %get-tuple-element.62), channel_id=1, source_target_pairs={{2,0},{0,2},{3,1},{1,3},{6,4},{4,6},{7,5},{5,7},{10,8},{8,10},{11,... | collective-permute-start | bytes 393224 | tf_op jit(solution)/shard_map/ppermute | solution.py:15
  10.7 1.3 %copy-start = (f32[96,512]{1,0:T(8,128)S(1)}, f32[96,512]{1,0:T(8,128)}, u32[]{:S(2)}) copy-start(f32[96,512]{1,0:T(8,128)} %constant.5.clone.refs_5_) | copy-start | bytes 589828
  13.9 1.3 %collective-permute-start.5 = (bf16[8,32,256]{2,1,0:T(8,128)(2,1)S(1)}, bf16[8,32,256]{2,1,0:T(8,128)(2,1)S(1)}, u32[]{:S(2)}, u32[]{:S(2)}) collective-permute-start(bf16[8,32,256]{2,1,0:T(8,128)(2,1)S(1)} %collective-permute-done.4.refs_2_), channel_id=1, source_target_pairs={{1,0},{0,1},{3,2},{2,3},{5,4},{4,5},{7,6},{6,7},{9,8},{8,9},{11,10... | collective-permute-start | bytes 393224 | tf_op jit(solution)/shard_map/ppermute | solution.py:15
  13.9 5.9 %collective-permute-start.3 = (bf16[2,1,2,64,256]{4,3,2,1,0:T(8,128)(2,1)S(1)}, bf16[2,1,2,64,256]{4,3,2,1,0:T(8,128)(2,1)S(1)}, u32[]{:S(2)}, u32[]{:S(2)}) collective-permute-start(bf16[2,1,2,64,256]{4,3,2,1,0:T(8,128)(2,1)S(1)} %get-tuple-element.60), channel_id=1, source_target_pairs={{0,4},{4,0},{8,12},{12,8},{1,5},{5,1},{9,13},{13,9},{2,6},{6,2},{1... | collective-permute-start | bytes 393224 | tf_op jit(solution)/shard_map/ppermute | solution.py:357
  17.3 6.3 %collective-permute-start.8 = (bf16[2,2,1,64,256]{4,3,2,1,0:T(8,128)(2,1)S(1)}, bf16[2,2,1,64,256]{4,3,2,1,0:T(8,128)(2,1)S(1)}, u32[]{:S(2)}, u32[]{:S(2)}) collective-permute-start(bf16[2,2,1,64,256]{4,3,2,1,0:T(8,128)(2,1)S(1)} %get-tuple-element.74), channel_id=1, source_target_pairs={{0,2},{2,0},{1,3},{3,1},{4,6},{6,4},{5,7},{7,5},{8,10},{10,8},{9,1... | collective-permute-start | bytes 393224 | tf_op jit(solution)/shard_map/ppermute | solution.py:357
  18.9 10.2 %collective-permute-start.7 = (bf16[2,1,2,64,256]{4,3,2,1,0:T(8,128)(2,1)S(1)}, bf16[2,1,2,64,256]{4,3,2,1,0:T(8,128)(2,1)S(1)}, u32[]{:S(2)}, u32[]{:S(2)}) collective-permute-start(bf16[2,1,2,64,256]{4,3,2,1,0:T(8,128)(2,1)S(1)} %get-tuple-element.73), channel_id=1, source_target_pairs={{0,4},{4,0},{8,12},{12,8},{1,5},{5,1},{9,13},{13,9},{2,6},{6,2},{1... | collective-permute-start | bytes 393224 | tf_op jit(solution)/shard_map/ppermute | solution.py:357
  19.8 6.2 %collective-permute-start.10 = (bf16[2,1,1,64,256]{4,3,2,1,0:T(8,128)(2,1)S(1)}, bf16[2,1,1,64,256]{4,3,2,1,0:T(8,128)(2,1)S(1)}, u32[]{:S(2)}, u32[]{:S(2)}) collective-permute-start(bf16[2,1,1,64,256]{4,3,2,1,0:T(8,128)(2,1)S(1)} %get-tuple-element.78), channel_id=1, source_target_pairs={{0,2},{2,0},{1,3},{3,1},{4,6},{6,4},{5,7},{7,5},{8,10},{10,8},{9,1... | collective-permute-start | bytes 196616 | tf_op jit(solution)/shard_map/ppermute | solution.py:357
  23.6 5.0 %collective-permute-start.9 = (bf16[2,1,1,64,256]{4,3,2,1,0:T(8,128)(2,1)S(1)}, bf16[2,1,1,64,256]{4,3,2,1,0:T(8,128)(2,1)S(1)}, u32[]{:S(2)}, u32[]{:S(2)}) collective-permute-start(bf16[2,1,1,64,256]{4,3,2,1,0:T(8,128)(2,1)S(1)} %get-tuple-element.77), channel_id=1, source_target_pairs={{0,4},{4,0},{8,12},{12,8},{1,5},{5,1},{9,13},{13,9},{2,6},{6,2},{1... | collective-permute-start | bytes 196616 | tf_op jit(solution)/shard_map/ppermute | solution.py:357
  24.2 6.9 %collective-permute-start.6 = (bf16[2,2,1,64,256]{4,3,2,1,0:T(8,128)(2,1)S(1)}, bf16[2,2,1,64,256]{4,3,2,1,0:T(8,128)(2,1)S(1)}, u32[]{:S(2)}, u32[]{:S(2)}) collective-permute-start(bf16[2,2,1,64,256]{4,3,2,1,0:T(8,128)(2,1)S(1)} %get-tuple-element.71), channel_id=1, source_target_pairs={{0,2},{2,0},{1,3},{3,1},{4,6},{6,4},{5,7},{7,5},{8,10},{10,8},{9,1... | collective-permute-start | bytes 393224 | tf_op jit(solution)/shard_map/ppermute | solution.py:357
  26.0 6.2 %collective-permute-start.12 = (bf16[2,1,1,64,256]{4,3,2,1,0:T(8,128)(2,1)S(1)}, bf16[2,1,1,64,256]{4,3,2,1,0:T(8,128)(2,1)S(1)}, u32[]{:S(2)}, u32[]{:S(2)}) collective-permute-start(bf16[2,1,1,64,256]{4,3,2,1,0:T(8,128)(2,1)S(1)} %shard_map.66), channel_id=1, source_target_pairs={{0,8},{4,12},{8,0},{12,4},{1,9},{5,13},{9,1},{13,5},{2,10},{6,14},... | collective-permute-start | bytes 196616 | tf_op jit(solution)/shard_map/ppermute | solution.py:357
  28.7 5.6 %collective-permute-start.14 = (bf16[2,1,1,64,256]{4,3,2,1,0:T(8,128)(2,1)S(1)}, bf16[2,1,1,64,256]{4,3,2,1,0:T(8,128)(2,1)S(1)}, u32[]{:S(2)}, u32[]{:S(2)}) collective-permute-start(bf16[2,1,1,64,256]{4,3,2,1,0:T(8,128)(2,1)S(1)} %shard_map.67), channel_id=1, source_target_pairs={{0,8},{4,12},{8,0},{12,4},{1,9},{5,13},{9,1},{13,5},{2,10},{6,14},... | collective-permute-start | bytes 196616 | tf_op jit(solution)/shard_map/ppermute | solution.py:357
  29.1 4.3 %collective-permute-start.13 = (bf16[2,1,1,64,256]{4,3,2,1,0:T(8,128)(2,1)S(1)}, bf16[2,1,1,64,256]{4,3,2,1,0:T(8,128)(2,1)S(1)}, u32[]{:S(2)}, u32[]{:S(2)}) collective-permute-start(bf16[2,1,1,64,256]{4,3,2,1,0:T(8,128)(2,1)S(1)} %get-tuple-element.86), channel_id=1, source_target_pairs={{0,2},{2,0},{1,3},{3,1},{4,6},{6,4},{5,7},{7,5},{8,10},{10,8},{9,1... | collective-permute-start | bytes 196616 | tf_op jit(solution)/shard_map/ppermute | solution.py:357
  31.2 4.3 %collective-permute-start.11 = (bf16[2,1,1,64,256]{4,3,2,1,0:T(8,128)(2,1)S(1)}, bf16[2,1,1,64,256]{4,3,2,1,0:T(8,128)(2,1)S(1)}, u32[]{:S(2)}, u32[]{:S(2)}) collective-permute-start(bf16[2,1,1,64,256]{4,3,2,1,0:T(8,128)(2,1)S(1)} %get-tuple-element.85), channel_id=1, source_target_pairs={{0,4},{4,0},{8,12},{12,8},{1,5},{5,1},{9,13},{13,9},{2,6},{6,2},{1... | collective-permute-start | bytes 196616 | tf_op jit(solution)/shard_map/ppermute | solution.py:357

commit v3 on v2

--- a/solution.py
+++ b/solution.py
@@ -1,6 +1,5 @@
 import jax
 import jax.numpy as jnp
-import numpy as np
 from jax import lax
 from jax.experimental import pallas as pl
 from jax.experimental.pallas import tpu as pltpu
@@ -42,47 +41,70 @@
     return planes - 2 if x == 0 else x if x == planes - 1 else x - 1
 
 
-def lane_maps(parts, colours, planes, ys, zs, lanes):
+def map_rows(parts, colours, planes, ys, zs):
+    match = ys
+    choose = match + -(-parts * colours * colours * planes * zs // 8) * 8
+    first_part = choose + 2 * parts * planes * 8
+    return match, choose, first_part, first_part + 8
+
+
+def write_maps(ref, parts, colours, planes, ys, zs):
+    lanes = ref.shape[1] // 2
     sites = ys * zs
     depth = parts * colours * sites
     row_size = parts * colours * zs
-    lane = np.arange(lanes)
+    match, choose, first_part, _ = map_rows(parts, colours, planes, ys, zs)
+
+    def ones(mask):
+        return jnp.where(mask, 1.0, 0.0)
+
+    def column(count):
+        return lax.broadcasted_iota(jnp.int32, (count, 1), 0)
+
+    def line(count):
+        return lax.broadcasted_iota(jnp.int32, (1, count), 1)
+
+    lane = line(lanes)
     inner = lane < depth
-    past = (lane - depth) % row_size
+    past = lax.rem(jnp.maximum(lane - depth, 0), row_size)
     used = lane < depth + 2 * row_size
-    part = np.where(inner, lane // (colours * sites), past // (colours * zs))
-    colour = np.where(inner, lane // sites, past // zs) % colours
-    z = np.where(inner, lane, past) % zs
-    y = np.where(inner, lane % sites // zs, ys - 1)
-    y_ahead = np.where(inner, lane % sites // zs, ys) - 1
-    spread = y == np.arange(ys)[:, None]
-    spread_ahead = y_ahead == np.arange(ys)[:, None]
-
-    row = np.arange(parts * colours * colours * planes * zs)[:, None]
-    row_z = row % zs
-    row_x = row // zs % planes
-    row_right = row // (zs * planes) % colours
-    row_left = row // (zs * planes * colours) % colours
-    row_part = row // (zs * planes * colours * colours)
-    match_ahead = (row_z == z) & (row_right == colour) & used
-    match_back = (row_z == z) & (row_left == colour) & used
-
-    out = np.arange(parts * planes * 8)[:, None]
-    field_part = out // (planes * 8)
-    out_x = out // 8 % planes
-    out_part = out % 8 // colours
-    out_colour = out % 8 % colours
-    source = (out_x == row_x.T) & (row_part.T == (out_part + field_part) % 2) & (out_part < parts)
-    choose_ahead = source & (row_left.T == out_colour)
-    choose_back = source & (row_right.T == out_colour)
-    sign_ahead = np.where((field_part == 1) & (out_part == 0), -1.0, 1.0)
-    sign_back = np.where((field_part == 0) & (out_part == 1), 1.0, -1.0)
-    maps = (
-        np.concatenate([spread, spread_ahead], axis=1), np.concatenate([match_ahead, match_back], axis=1),
-        np.concatenate([choose_ahead * sign_ahead, choose_back * sign_back], axis=0),
-        np.broadcast_to(part == 0, (8, lanes)),
-    )
-    return [np.pad(m, ((0, -len(m) % 8), (0, 2 * lanes - m.shape[1]))).astype(np.float32) for m in maps]
+    part = jnp.where(inner, lax.div(lane, colours * sites), lax.div(past, colours * zs))
+    colour = lax.rem(jnp.where(inner, lax.div(lane, sites), lax.div(past, zs)), colours)
+    z = lax.rem(jnp.where(inner, lane, past), zs)
+    y = lax.div(lax.rem(lane, sites), zs)
+    ref[:ys, :lanes] = ones(column(ys) == jnp.where(inner, y, ys - 1))
+    ref[:ys, lanes:] = ones(column(ys) == jnp.where(inner, y, ys) - 1)
+
+    count = parts * colours * colours * planes * zs
+
+    def link(index):
+        x = lax.rem(lax.div(index, zs), planes)
+        right = lax.rem(lax.div(index, zs * planes), colours)
+        left = lax.rem(lax.div(index, zs * planes * colours), colours)
+        return x, right, left, lax.div(index, zs * planes * colours * colours)
+
+    row = column(count)
+    _, right, left, _ = link(row)
+    row_z = lax.rem(row, zs)
+    key = jnp.where(used, colour * zs + z, -1)
+    ref[match : match + count, :lanes] = ones(right * zs + row_z == key)
+    ref[match : match + count, lanes:] = ones(left * zs + row_z == key)
+
+    out = column(parts * planes * 8)
+    field_part = lax.div(out, planes * 8)
+    out_x = lax.rem(lax.div(out, 8), planes)
+    out_part = lax.div(lax.rem(out, 8), colours)
+    out_colour = lax.rem(lax.rem(out, 8), colours)
+    x, right, left, source_part = link(line(count))
+    source = source_part * planes + x
+    wanted = jnp.where(out_part < parts, lax.rem(out_part + field_part, 2) * planes + out_x, -1)
+    sign_ahead = jnp.where((field_part == 1) & (out_part == 0), -1.0, 1.0)
+    sign_back = jnp.where((field_part == 0) & (out_part == 1), 1.0, -1.0)
+    half = parts * planes * 8
+    for start, end, sign in ((choose, left, sign_ahead), (choose + half, right, sign_back)):
+        hit = source * colours + end == wanted * colours + jnp.where(wanted < 0, -1, out_colour)
+        ref[start : start + half, :count] = jnp.where(hit, sign, 0.0)
+    ref[first_part:, :lanes] = jnp.broadcast_to(ones(part == 0), (8, lanes))
 
 
 def coefficients(links_x, links_y, maps_ref, planes):
@@ -117,12 +139,12 @@
 
 
 def edges_kernel(
-    raw_hbm, links_x_hbm, links_y_hbm, maps_hbm,
-    first_ref, last_ref, links_x_ref, links_y_ref, maps_ref, arrived,
+    raw_hbm, links_x_hbm, links_y_hbm,
+    first_ref, last_ref, raw_ref, links_x_ref, links_y_ref, maps_ref, past_maps_ref, arrived,
 ):
     parts, planes, ys, colours, zs, _ = raw_hbm.shape
-    sources = (raw_hbm.at[:, planes - 1], raw_hbm.at[:, 0], links_x_hbm, links_y_hbm, maps_hbm)
-    targets = (last_ref.at[:, :ys], first_ref, links_x_ref, links_y_ref, maps_ref)
+    sources = (raw_hbm.at[:, planes - 1], raw_hbm.at[:, 0], links_x_hbm, links_y_hbm, raw_hbm)
+    targets = (last_ref.at[:, :ys], first_ref, links_x_ref, links_y_ref, raw_ref)
     copies = [
         pltpu.make_async_copy(source, target, arrived.at[i])
         for i, (source, target) in enumerate(zip(sources, targets))
@@ -130,6 +152,8 @@
     for copy in copies:
         copy.start()
     last_ref[:, ys:] = jnp.zeros((parts, colours) + last_ref.shape[2:], last_ref.dtype)
+    write_maps(maps_ref, parts, colours, planes, ys, zs)
+    write_maps(past_maps_ref, parts, colours, 1, ys, zs)
     copies[2].wait()
     last_ref[:, ys:, :, :, :ys] = links_x_ref[:, :, :, planes - 1]
     for copy in copies[:2] + copies[3:]:
@@ -148,11 +172,9 @@
 
 
 def prepare_kernel(
-    raw_hbm, links_x_ref, links_y_ref, maps_ref,
-    rows_ref, ends_ref, ahead_x_ref, back_x_ref, ahead_y_ref, back_y_ref, raw_ref, arrived,
+    raw_ref, links_x_ref, links_y_ref, maps_ref,
+    rows_ref, ends_ref, ahead_x_ref, back_x_ref, ahead_y_ref, back_y_ref,
 ):
-    copy = pltpu.make_async_copy(raw_hbm, raw_ref, arrived)
-    copy.start()
     planes, depth, width = rows_ref.shape
     zs = raw_ref.shape[4]
     ys = raw_ref.shape[2]
@@ -173,7 +195,6 @@
     ends = (lane == wanted).astype(jnp.bfloat16)
     filler = jnp.zeros((8, width - 128), jnp.float32)
     spare = ends_ref.shape[1] - 2 * row_size - 8
-    copy.wait()
     for x in range(planes):
         plane = plane_rows(raw_ref.at[:, x], ys)
         rows_ref[place_of(x, planes)] = plane
@@ -331,6 +352,7 @@
     to_next = jnp.where(to_next, -1.0, 0.0)
     to_last = jnp.where(to_last, -1.0, 0.0)
     _, lane = iotas((8, 128))
+    spare = jnp.zeros((near_ref.shape[1] - far_ref.shape[2], width), far_ref.dtype)
     for x in range(planes):
         past = near_ref[x, 2 * row_size : 2 * row_size + 8, :128].astype(jnp.float32)
         mixed = jnp.where(lane >= depth + row_size - head, past, back_ref[x, :, head:])
@@ -340,7 +362,7 @@
         column = jnp.concatenate([rows_ref[place], near_ref[x]], axis=0)
         field_ref[0, place] = dot(matrix, column).astype(jnp.bfloat16)
         for k in range(groups - 1):
-            column = jnp.concatenate([others_ref[k, place], far_ref[k, x]], axis=0)
+            column = jnp.concatenate([others_ref[k, place], far_ref[k, x], spare], axis=0)
             field_ref[k + 1, place] = dot(matrix, column).astype(jnp.bfloat16)
     for k in range(groups):
         turned_ref[k] = field_ref[k].reshape(planes * depth, width).T
@@ -437,14 +459,14 @@
 
     raw_others = [shifted(raw, "ma", -step) for step in range(1, groups)]
     raw_links_x, raw_links_y = (a.transpose(0, 1, 2, 3, 5, 4) for a in (links_first, links_second))
-    maps = jnp.asarray(np.concatenate(lane_maps(parts, colours, planes, ys, zs, lanes)))
-    past_maps = jnp.asarray(np.concatenate(lane_maps(parts, colours, 1, ys, zs, lanes)))
-    inputs = [raw, raw_links_x, raw_links_y, maps]
-    first_plane, last_plane, *inputs = call(
+    inputs = [raw, raw_links_x, raw_links_y]
+    first_plane, last_plane, *inputs, past_maps = call(
         edges_kernel,
         (
             shape(parts, ys, colours, zs, width), shape(parts, ys + colours, colours, zs, width),
-            *(shape(*a.shape, dtype=a.dtype) for a in inputs[1:]),
+            *(shape(*a.shape) for a in inputs),
+            shape(map_rows(parts, colours, planes, ys, zs)[-1], 2 * lanes, dtype=f32),
+            shape(map_rows(parts, colours, 1, ys, zs)[-1], 2 * lanes, dtype=f32),
         ),
         0,
         inputs,
@@ -457,9 +479,7 @@
         prepare_kernel,
         (field_shape, shape(planes, edge, width), link_shape, link_shape, link_shape, link_shape),
         0,
-        [raw] + inputs,
-        [pltpu.VMEM(raw.shape, bf16), pltpu.SemaphoreType.DMA],
-        [pltpu.HBM] + [pltpu.VMEM] * len(inputs),
+        inputs,
     )
     near = shifted(ends, "gy", 1)
     if across_y != 2:
@@ -502,7 +522,8 @@
         [total],
     )
     near, right_edge = lax.optimization_barrier((near, right_edge))
-    far = jnp.stack([shifted(near, "ma", -step) for step in range(1, groups)])
+    near_rows = near[:, : 2 * row_size]
+    far = jnp.stack([shifted(near_rows, "ma", -step) for step in range(1, groups)])
     lefts = call(
         move_y, shape(groups, width, planes * depth), 2 * step_flops,
         [field, fields, near, far, ahead_y, back_y],

time: 36.5 us -> 35.9 us (0.984)
  starting transfers between devices: 18.5 us -> 21.5 us
  waiting for transfers between devices: 9.12 us -> 6.38 us
  Pallas kernels: 8.58 us -> 7.69 us
    ppermute x10, starting transfers between devices: 11.6 us -> 14.6 us  [swap(): lax.ppermute(block, axis, [(i, i ^ 1 << bit) for i in range(lax.axis_size...]
    ppermute x10, waiting for transfers between devices: 6.86 us -> 4.92 us  [swap(): lax.ppermute(block, axis, [(i, i ^ 1 << bit) for i in range(lax.axis_size...]
    pallas_call x16, Pallas kernels: 8.58 us -> 7.69 us  [call(): pl.pallas_call(body, out_shape=out_shape, in_specs=[pl.BlockSpec(memory_s...]
    ppermute x5, waiting for transfers between devices: 2.26 us -> 1.46 us  [shifted(): return lax.ppermute(block, axis, route)]
  transfers between devices with their start and end apart: 15 -> 15, of which waited for: 9 -> 5; matrix products, arithmetic and copies ran while one was open for 0% -> 0% of each run, Pallas kernels for 22% -> 19%
where the time goes in v3:
time: 35.9 us; the launch traced here: 35.7 us
  starting transfers between devices  21.5 us (60%)
  Pallas kernels  7.69 us (21%)
  waiting for transfers between devices  6.38 us (18%)
    ppermute x10, starting transfers between devices, swap(): lax.ppermute(block, axis, [(i, i ^ 1 << bit) for i in range(lax.axis_size...  14.6 us
    pallas_call x16, Pallas kernels, call(): pl.pallas_call(body, out_shape=out_shape, in_specs=[pl.BlockSpec(memory_s...  7.69 us
    ppermute x5, starting transfers between devices, shifted(): return lax.ppermute(block, axis, route)  6.9 us
    ppermute x10, waiting for transfers between devices, swap(): lax.ppermute(block, axis, [(i, i ^ 1 << bit) for i in range(lax.axis_size...  4.92 us
    ppermute x5, waiting for transfers between devices, shifted(): return lax.ppermute(block, axis, route)  1.46 us
  transfers between devices with their start and end apart: 15, of which 5 were waited for; matrix products, arithmetic and copies ran while one was open for 0% of the time, Pallas kernels for 19%

profile of v3, /device:TPU:0, one launch (start us, length us, event | category | flops | bytes accessed | tf_op | source)
XLA Modules:
  0.0 35.7 jit_solution(7414851164808727533)
XLA Ops:
  0.0 0.5 %collective-permute-start.2 = (bf16[2,8,16,3,2,256]{5,4,3,2,1,0:T(2,128)(2,1)}, bf16[2,8,16,3,2,256]{5,4,3,2,1,0:T(2,128)(2,1)S(1)}, u32[]{:S(2)}, u32[]{:S(2)}) collective-permute-start(bf16[2,8,16,3,2,256]{5,4,3,2,1,0:T(2,128)(2,1)} %bitcast.10), channel_id=1, source_target_pairs={{1,0},{0,1},{3,2},{2,3},{5,4},{4,5},{7,6},{6,7},{9,8},{8,9},{11,10... | collective-permute-start | bytes 2359304 | tf_op jit(solution)/shard_map/ppermute | solution.py:14
  0.5 1.4 %shard_map.37 = (bf16[2,16,3,2,256]{4,3,2,1,0:T(2,128)(2,1)S(1)}, bf16[2,19,3,2,256]{4,3,2,1,0:T(2,128)(2,1)S(1)}, bf16[2,8,16,3,2,256]{5,4,3,2,1,0:T(2,128)(2,1...) custom-call(bf16[2,8,16,3,2,256]{5,4,3,2,1,0:T(2,128)(2,1)} %bitcast, ...), custom_call_target="tpu_custom_call" | custom-call | tf_op jit(solution)/shard_map/pallas_call | solution.py:19
  1.8 2.6 %collective-permute-start.1 = (bf16[2,19,3,2,256]{4,3,2,1,0:T(2,128)(2,1)S(1)}, bf16[2,19,3,2,256]{4,3,2,1,0:T(2,128)(2,1)S(1)}, u32[]{:S(2)}, u32[]{:S(2)}) collective-permute-start(bf16[2,19,3,2,256]{4,3,2,1,0:T(2,128)(2,1)S(1)} %get-tuple-element.54), channel_id=1, source_target_pairs={{12,0},{0,4},{4,8},{8,12},{13,1},{1,5},{5,9},{9,13},{14,2},{2,6},{... | collective-permute-start | bytes 350216 | tf_op jit(solution)/shard_map/ppermute | solution.py:14
  4.4 2.1 %collective-permute-start = (bf16[2,16,3,2,256]{4,3,2,1,0:T(2,128)(2,1)S(1)}, bf16[2,16,3,2,256]{4,3,2,1,0:T(2,128)(2,1)S(1)}, u32[]{:S(2)}, u32[]{:S(2)}) collective-permute-start(bf16[2,16,3,2,256]{4,3,2,1,0:T(2,128)(2,1)S(1)} %get-tuple-element.53), channel_id=1, source_target_pairs={{4,0},{8,4},{12,8},{0,12},{5,1},{9,5},{13,9},{1,13},{6,2},{10,6},{... | collective-permute-start | bytes 294920 | tf_op jit(solution)/shard_map/ppermute | solution.py:14
  6.5 0.8 %shard_map.38 = (bf16[8,192,256]{2,1,0:T(8,128)(2,1)S(1)}, bf16[8,32,256]{2,1,0:T(8,128)(2,1)S(1)}, f32[8,8,256]{2,1,0:T(8,128)S(1)}, f32[8,8,256]{2,1,0:T(8,128...) custom-call(bf16[2,8,16,3,2,256]{5,4,3,2,1,0:T(2,128)(2,1)S(1)} %get-tuple-element.48.raw_ref, ...), custom_call_target="tpu_custom_call" | custom-call | tf_op jit(solution)/shard_map/pallas_call | solution.py:19
  7.3 1.7 %collective-permute-start.4 = (bf16[8,32,256]{2,1,0:T(8,128)(2,1)S(1)}, bf16[8,32,256]{2,1,0:T(8,128)(2,1)S(1)}, u32[]{:S(2)}, u32[]{:S(2)}) collective-permute-start(bf16[8,32,256]{2,1,0:T(8,128)(2,1)S(1)} %get-tuple-element.66), channel_id=1, source_target_pairs={{2,0},{0,2},{3,1},{1,3},{6,4},{4,6},{7,5},{5,7},{10,8},{8,10},{11,... | collective-permute-start | bytes 393224 | tf_op jit(solution)/shard_map/ppermute | solution.py:14
  8.9 0.5 %shard_map.39 = (bf16[1152,512]{1,0:T(8,128)(2,1)S(1)}, bf16[256,1536]{1,0:T(8,128)(2,1)S(1)}) custom-call(bf16[8,192,256]{2,1,0:T(8,128)(2,1)S(1)} %get-tuple-element.52.refs_0_, f32[8,8,256]{2,1,0:T(8,128)S(1)} %get-tuple-element.55.refs_1_.refs_3_, f32[8,8,256]{2,1,0:T(8,128)S(1)} %get-tuple-element.56.refs_2_.refs_4_), custom_call_target="tpu_custom_call" | custom-call | flops 150994944 | tf_op jit(solution)/shard_map/pallas_call | solution.py:19
  9.4 0.0 collective-permute-done.2.raw_ref
  9.4 0.3 shard_map.40
  9.7 0.8 %shard_map.41.refs_8_ = f32[2,256,512]{2,1,0:T(8,128)S(1)} custom-call(bf16[256,1536]{1,0:T(8,128)(2,1)S(1)} %get-tuple-element.58.own_ref.refs_6_, bf16[1,256,1536]{2,1,0:T(8,128)(2,1)S(1)} %bitcast.6, bf16[1152,512]{1,0:T(8,128)(2,1)S(1)} %get-tuple-element.60.right_ref), custom_call_target="tpu_custom_call" | custom-call | flops 402653184 | tf_op jit(solution)/shard_map/pallas_call | solution.py:19
  10.6 1.3 %collective-permute-done.refs_1_ = bf16[2,16,3,2,256]{4,3,2,1,0:T(2,128)(2,1)S(1)} collective-permute-done((bf16[2,16,3,2,256]{4,3,2,1,0:T(2,128)(2,1)S(1)}, bf16[2,16,3,2,256]{4,3,2,1,0:T(2,128)(2,1)S(1)}, u32[]{:S(2)}, u32[]{:S(2)}) %collective-permute-start) | collective-permute-done | bytes 98336 | tf_op jit(solution)/shard_map/ppermute | solution.py:14
  11.9 0.0 collective-permute-done.1.refs_2_
  11.9 1.0 %shard_map.42 = (f32[2,1,2,64,256]{4,3,2,1,0:T(8,128)S(1)}, bf16[2,1,2,64,256]{4,3,2,1,0:T(8,128)(2,1)S(1)}, f32[2,2,1,64,256]{4,3,2,1,0:T(8,128)S(1)}, bf16[2,2...) custom-call(bf16[8,192,256]{2,1,0:T(8,128)(2,1)S(1)} %get-tuple-element.52.refs_0_, ...), custom_call_target="tpu_custom_call" | custom-call | flops 402653184 | tf_op jit(solution)/shard_map/pallas_call | solution.py:19
  12.9 0.0 collective-permute-done.4.refs_2_
  12.9 0.1 collective-permute-start.5
  13.0 1.2 %collective-permute-start.3 = (bf16[2,1,2,64,256]{4,3,2,1,0:T(8,128)(2,1)S(1)}, bf16[2,1,2,64,256]{4,3,2,1,0:T(8,128)(2,1)S(1)}, u32[]{:S(2)}, u32[]{:S(2)}) collective-permute-start(bf16[2,1,2,64,256]{4,3,2,1,0:T(8,128)(2,1)S(1)} %get-tuple-element.64), channel_id=1, source_target_pairs={{0,4},{4,0},{8,12},{12,8},{1,5},{5,1},{9,13},{13,9},{2,6},{6,2},{1... | collective-permute-start | bytes 393224 | tf_op jit(solution)/shard_map/ppermute | solution.py:379
  14.2 0.1 collective-permute-done.5
  14.3 0.7 %shard_map.43.lefts_ref.refs_0_ = bf16[2,256,1536]{2,1,0:T(8,128)(2,1)S(1)} custom-call(bf16[8,192,256]{2,1,0:T(8,128)(2,1)S(1)} %get-tuple-element.52.refs_0_, bf16[1,8,192,256]{3,2,1,0:T(8,128)(2,1)S(1)} %bitcast.8, bf16[8,32,256]{2,1,0:T(8,128)(2,1)S(1)} %collective-permute-done.4.refs_2_, bf16[1,8,24,256]{3,2,1,0:T(8,128)(2,1)S(1)} %bitcast.9, ...), custom_call_target="tpu_custom_call" | custom-call | flops 150994944 | tf_op jit(solution)/shard_map/pallas_call | solution.py:19
  15.0 0.8 %shard_map.44.refs_2_ = f32[2,256,512]{2,1,0:T(8,128)S(1)} custom-call(bf16[2,256,1536]{2,1,0:T(8,128)(2,1)S(1)} %shard_map.43.lefts_ref.refs_0_, bf16[1152,512]{1,0:T(8,128)(2,1)S(1)} %get-tuple-element.60.right_ref), custom_call_target="tpu_custom_call" | custom-call | flops 402653184 | tf_op jit(solution)/shard_map/pallas_call | solution.py:19
  15.8 0.6 %shard_map.45 = (f32[2,2,1,64,256]{4,3,2,1,0:T(8,128)S(1)}, bf16[2,2,1,64,256]{4,3,2,1,0:T(8,128)(2,1)S(1)}, f32[2,1,2,64,256]{4,3,2,1,0:T(8,128)S(1)}, bf16[2,1,2,64,256]{4,3,2,1,0:T(8,128)(2,1)S(1)}) custom-call(bf16[2,256,1536]{2,1,0:T(8,128)(2,1)S(1)} %shard_map.43.lefts_ref.refs_0_, bf16[384,512]{1,0:T(8,128)(2,1)S(1)} %get-tuple-element.71.refs_1_, ...), custom_call_target="tpu_custom_call" | custom-call | flops 402653184 | tf_op jit(solution)/shard_map/pallas_call | solution.py:19
  16.4 1.6 %collective-permute-start.8 = (bf16[2,2,1,64,256]{4,3,2,1,0:T(8,128)(2,1)S(1)}, bf16[2,2,1,64,256]{4,3,2,1,0:T(8,128)(2,1)S(1)}, u32[]{:S(2)}, u32[]{:S(2)}) collective-permute-start(bf16[2,2,1,64,256]{4,3,2,1,0:T(8,128)(2,1)S(1)} %get-tuple-element.78), channel_id=1, source_target_pairs={{0,2},{2,0},{1,3},{3,1},{4,6},{6,4},{5,7},{7,5},{8,10},{10,8},{9,1... | collective-permute-start | bytes 393224 | tf_op jit(solution)/shard_map/ppermute | solution.py:379
  17.9 1.1 %collective-permute-start.7 = (bf16[2,1,2,64,256]{4,3,2,1,0:T(8,128)(2,1)S(1)}, bf16[2,1,2,64,256]{4,3,2,1,0:T(8,128)(2,1)S(1)}, u32[]{:S(2)}, u32[]{:S(2)}) collective-permute-start(bf16[2,1,2,64,256]{4,3,2,1,0:T(8,128)(2,1)S(1)} %get-tuple-element.77), channel_id=1, source_target_pairs={{0,4},{4,0},{8,12},{12,8},{1,5},{5,1},{9,13},{13,9},{2,6},{6,2},{1... | collective-permute-start | bytes 393224 | tf_op jit(solution)/shard_map/ppermute | solution.py:379
  19.1 0.0 collective-permute-done.3.refs_1_
  19.1 1.4 %collective-permute-start.10 = (bf16[2,1,1,64,256]{4,3,2,1,0:T(8,128)(2,1)S(1)}, bf16[2,1,1,64,256]{4,3,2,1,0:T(8,128)(2,1)S(1)}, u32[]{:S(2)}, u32[]{:S(2)}) collective-permute-start(bf16[2,1,1,64,256]{4,3,2,1,0:T(8,128)(2,1)S(1)} %get-tuple-element.82), channel_id=1, source_target_pairs={{0,2},{2,0},{1,3},{3,1},{4,6},{6,4},{5,7},{7,5},{8,10},{10,8},{9,1... | collective-permute-start | bytes 196616 | tf_op jit(solution)/shard_map/ppermute | solution.py:379
  20.5 2.1 %collective-permute-done.8.refs_1_ = bf16[2,2,1,64,256]{4,3,2,1,0:T(8,128)(2,1)S(1)} collective-permute-done((bf16[2,2,1,64,256]{4,3,2,1,0:T(8,128)(2,1)S(1)}, bf16[2,2,1,64,256]{4,3,2,1,0:T(8,128)(2,1)S(1)}, u32[]{:S(2)}, u32[]{:S(2)}) %collective-permute-start.8) | collective-permute-done | bytes 131104 | tf_op jit(solution)/shard_map/ppermute | solution.py:379
  22.7 1.2 %collective-permute-start.9 = (bf16[2,1,1,64,256]{4,3,2,1,0:T(8,128)(2,1)S(1)}, bf16[2,1,1,64,256]{4,3,2,1,0:T(8,128)(2,1)S(1)}, u32[]{:S(2)}, u32[]{:S(2)}) collective-permute-start(bf16[2,1,1,64,256]{4,3,2,1,0:T(8,128)(2,1)S(1)} %get-tuple-element.81), channel_id=1, source_target_pairs={{0,4},{4,0},{8,12},{12,8},{1,5},{5,1},{9,13},{13,9},{2,6},{6,2},{1... | collective-permute-start | bytes 196616 | tf_op jit(solution)/shard_map/ppermute | solution.py:379
  23.9 1.5 %collective-permute-start.6 = (bf16[2,2,1,64,256]{4,3,2,1,0:T(8,128)(2,1)S(1)}, bf16[2,2,1,64,256]{4,3,2,1,0:T(8,128)(2,1)S(1)}, u32[]{:S(2)}, u32[]{:S(2)}) collective-permute-start(bf16[2,2,1,64,256]{4,3,2,1,0:T(8,128)(2,1)S(1)} %get-tuple-element.75), channel_id=1, source_target_pairs={{0,2},{2,0},{1,3},{3,1},{4,6},{6,4},{5,7},{7,5},{8,10},{10,8},{9,1... | collective-permute-start | bytes 393224 | tf_op jit(solution)/shard_map/ppermute | solution.py:379
  25.4 0.0 collective-permute-done.10.came_ref
  25.4 1.8 %collective-permute-start.12 = (bf16[2,1,1,64,256]{4,3,2,1,0:T(8,128)(2,1)S(1)}, bf16[2,1,1,64,256]{4,3,2,1,0:T(8,128)(2,1)S(1)}, u32[]{:S(2)}, u32[]{:S(2)}) collective-permute-start(bf16[2,1,1,64,256]{4,3,2,1,0:T(8,128)(2,1)S(1)} %shard_map.48), channel_id=1, source_target_pairs={{0,8},{4,12},{8,0},{12,4},{1,9},{5,13},{9,1},{13,5},{2,10},{6,14},... | collective-permute-start | bytes 196616 | tf_op jit(solution)/shard_map/ppermute | solution.py:379
  27.2 0.0 collective-permute-done.9.came_ref
  27.2 1.9 %collective-permute-start.14 = (bf16[2,1,1,64,256]{4,3,2,1,0:T(8,128)(2,1)S(1)}, bf16[2,1,1,64,256]{4,3,2,1,0:T(8,128)(2,1)S(1)}, u32[]{:S(2)}, u32[]{:S(2)}) collective-permute-start(bf16[2,1,1,64,256]{4,3,2,1,0:T(8,128)(2,1)S(1)} %shard_map.49), channel_id=1, source_target_pairs={{0,8},{4,12},{8,0},{12,4},{1,9},{5,13},{9,1},{13,5},{2,10},{6,14},... | collective-permute-start | bytes 196616 | tf_op jit(solution)/shard_map/ppermute | solution.py:379
  29.1 0.0 collective-permute-done.7.refs_1_
  29.2 1.5 %collective-permute-start.13 = (bf16[2,1,1,64,256]{4,3,2,1,0:T(8,128)(2,1)S(1)}, bf16[2,1,1,64,256]{4,3,2,1,0:T(8,128)(2,1)S(1)}, u32[]{:S(2)}, u32[]{:S(2)}) collective-permute-start(bf16[2,1,1,64,256]{4,3,2,1,0:T(8,128)(2,1)S(1)} %get-tuple-element.90), channel_id=1, source_target_pairs={{0,2},{2,0},{1,3},{3,1},{4,6},{6,4},{5,7},{7,5},{8,10},{10,8},{9,1... | collective-permute-start | bytes 196616 | tf_op jit(solution)/shard_map/ppermute | solution.py:379
  30.6 0.0 collective-permute-done.6.refs_1_
  30.7 1.5 %collective-permute-start.11 = (bf16[2,1,1,64,256]{4,3,2,1,0:T(8,128)(2,1)S(1)}, bf16[2,1,1,64,256]{4,3,2,1,0:T(8,128)(2,1)S(1)}, u32[]{:S(2)}, u32[]{:S(2)}) collective-permute-start(bf16[2,1,1,64,256]{4,3,2,1,0:T(8,128)(2,1)S(1)} %get-tuple-element.89), channel_id=1, source_target_pairs={{0,4},{4,0},{8,12},{12,8},{1,5},{5,1},{9,13},{13,9},{2,6},{6,2},{1... | collective-permute-start | bytes 196616 | tf_op jit(solution)/shard_map/ppermute | solution.py:379
  32.2 0.0 collective-permute-done.12.refs_2_
  32.2 1.3 %collective-permute-done.13.refs_4_ = bf16[2,1,1,64,256]{4,3,2,1,0:T(8,128)(2,1)S(1)} collective-permute-done((bf16[2,1,1,64,256]{4,3,2,1,0:T(8,128)(2,1)S(1)}, bf16[2,1,1,64,256]{4,3,2,1,0:T(8,128)(2,1)S(1)}, u32[]{:S(2)}, u32[]{:S(2)}) %collective-permute-start.13) | collective-permute-done | bytes 65568 | tf_op jit(solution)/shard_map/ppermute | solution.py:379
  33.5 0.0 collective-permute-done.14.refs_5_
  33.5 1.5 %collective-permute-done.11.refs_1_ = bf16[2,1,1,64,256]{4,3,2,1,0:T(8,128)(2,1)S(1)} collective-permute-done((bf16[2,1,1,64,256]{4,3,2,1,0:T(8,128)(2,1)S(1)}, bf16[2,1,1,64,256]{4,3,2,1,0:T(8,128)(2,1)S(1)}, u32[]{:S(2)}, u32[]{:S(2)}) %collective-permute-start.11) | collective-permute-done | bytes 65568 | tf_op jit(solution)/shard_map/ppermute | solution.py:379
  35.0 0.7 %shard_map.52 = f32[2,2,64,256]{3,2,1,0:T(8,128)} custom-call(f32[2,1,1,64,256]{4,3,2,1,0:T(8,128)S(1)} %get-tuple-element.88.refs_0_, bf16[2,1,1,64,256]{4,3,2,1,0:T(8,128)(2,1)S(1)} %collective-permute-done.11.refs_1_, bf16[2,1,1,64,256]{4,3,2,1,0:T(8,128)(2,1)S(1)} %collective-permute-done.12.refs_2_, ...), custom_call_target="tpu_custom_call" | custom-call | tf_op jit(solution)/shard_map/pallas_call | solution.py:19
  (7 shorter events, 0.2 us)
Async XLA Ops:
  0.0 9.4 %collective-permute-start.2 = (bf16[2,8,16,3,2,256]{5,4,3,2,1,0:T(2,128)(2,1)}, bf16[2,8,16,3,2,256]{5,4,3,2,1,0:T(2,128)(2,1)S(1)}, u32[]{:S(2)}, u32[]{:S(2)}) collective-permute-start(bf16[2,8,16,3,2,256]{5,4,3,2,1,0:T(2,128)(2,1)} %bitcast.10), channel_id=1, source_target_pairs={{1,0},{0,1},{3,2},{2,3},{5,4},{4,5},{7,6},{6,7},{9,8},{8,9},{11,10... | collective-permute-start | bytes 2359304 | tf_op jit(solution)/shard_map/ppermute | solution.py:14
  1.8 10.1 %collective-permute-start.1 = (bf16[2,19,3,2,256]{4,3,2,1,0:T(2,128)(2,1)S(1)}, bf16[2,19,3,2,256]{4,3,2,1,0:T(2,128)(2,1)S(1)}, u32[]{:S(2)}, u32[]{:S(2)}) collective-permute-start(bf16[2,19,3,2,256]{4,3,2,1,0:T(2,128)(2,1)S(1)} %get-tuple-element.54), channel_id=1, source_target_pairs={{12,0},{0,4},{4,8},{8,12},{13,1},{1,5},{5,9},{9,13},{14,2},{2,6},{... | collective-permute-start | bytes 350216 | tf_op jit(solution)/shard_map/ppermute | solution.py:14
  4.4 7.4 %collective-permute-start = (bf16[2,16,3,2,256]{4,3,2,1,0:T(2,128)(2,1)S(1)}, bf16[2,16,3,2,256]{4,3,2,1,0:T(2,128)(2,1)S(1)}, u32[]{:S(2)}, u32[]{:S(2)}) collective-permute-start(bf16[2,16,3,2,256]{4,3,2,1,0:T(2,128)(2,1)S(1)} %get-tuple-element.53), channel_id=1, source_target_pairs={{4,0},{8,4},{12,8},{0,12},{5,1},{9,5},{13,9},{1,13},{6,2},{10,6},{... | collective-permute-start | bytes 294920 | tf_op jit(solution)/shard_map/ppermute | solution.py:14
  7.3 5.6 %collective-permute-start.4 = (bf16[8,32,256]{2,1,0:T(8,128)(2,1)S(1)}, bf16[8,32,256]{2,1,0:T(8,128)(2,1)S(1)}, u32[]{:S(2)}, u32[]{:S(2)}) collective-permute-start(bf16[8,32,256]{2,1,0:T(8,128)(2,1)S(1)} %get-tuple-element.66), channel_id=1, source_target_pairs={{2,0},{0,2},{3,1},{1,3},{6,4},{4,6},{7,5},{5,7},{10,8},{8,10},{11,... | collective-permute-start | bytes 393224 | tf_op jit(solution)/shard_map/ppermute | solution.py:14
  12.9 1.4 %collective-permute-start.5 = (bf16[8,24,256]{2,1,0:T(8,128)(2,1)S(1)}, bf16[8,24,256]{2,1,0:T(8,128)(2,1)S(1)}, u32[]{:S(2)}, u32[]{:S(2)}) collective-permute-start(bf16[8,24,256]{2,1,0:T(8,128)(2,1)S(1)} %slice.3), channel_id=1, source_target_pairs={{1,0},{0,1},{3,2},{2,3},{5,4},{4,5},{7,6},{6,7},{9,8},{8,9},{11,10... | collective-permute-start | bytes 294920 | tf_op jit(solution)/shard_map/ppermute | solution.py:14
  13.0 6.0 %collective-permute-start.3 = (bf16[2,1,2,64,256]{4,3,2,1,0:T(8,128)(2,1)S(1)}, bf16[2,1,2,64,256]{4,3,2,1,0:T(8,128)(2,1)S(1)}, u32[]{:S(2)}, u32[]{:S(2)}) collective-permute-start(bf16[2,1,2,64,256]{4,3,2,1,0:T(8,128)(2,1)S(1)} %get-tuple-element.64), channel_id=1, source_target_pairs={{0,4},{4,0},{8,12},{12,8},{1,5},{5,1},{9,13},{13,9},{2,6},{6,2},{1... | collective-permute-start | bytes 393224 | tf_op jit(solution)/shard_map/ppermute | solution.py:379
  16.4 6.2 %collective-permute-start.8 = (bf16[2,2,1,64,256]{4,3,2,1,0:T(8,128)(2,1)S(1)}, bf16[2,2,1,64,256]{4,3,2,1,0:T(8,128)(2,1)S(1)}, u32[]{:S(2)}, u32[]{:S(2)}) collective-permute-start(bf16[2,2,1,64,256]{4,3,2,1,0:T(8,128)(2,1)S(1)} %get-tuple-element.78), channel_id=1, source_target_pairs={{0,2},{2,0},{1,3},{3,1},{4,6},{6,4},{5,7},{7,5},{8,10},{10,8},{9,1... | collective-permute-start | bytes 393224 | tf_op jit(solution)/shard_map/ppermute | solution.py:379
  17.9 11.2 %collective-permute-start.7 = (bf16[2,1,2,64,256]{4,3,2,1,0:T(8,128)(2,1)S(1)}, bf16[2,1,2,64,256]{4,3,2,1,0:T(8,128)(2,1)S(1)}, u32[]{:S(2)}, u32[]{:S(2)}) collective-permute-start(bf16[2,1,2,64,256]{4,3,2,1,0:T(8,128)(2,1)S(1)} %get-tuple-element.77), channel_id=1, source_target_pairs={{0,4},{4,0},{8,12},{12,8},{1,5},{5,1},{9,13},{13,9},{2,6},{6,2},{1... | collective-permute-start | bytes 393224 | tf_op jit(solution)/shard_map/ppermute | solution.py:379
  19.1 6.3 %collective-permute-start.10 = (bf16[2,1,1,64,256]{4,3,2,1,0:T(8,128)(2,1)S(1)}, bf16[2,1,1,64,256]{4,3,2,1,0:T(8,128)(2,1)S(1)}, u32[]{:S(2)}, u32[]{:S(2)}) collective-permute-start(bf16[2,1,1,64,256]{4,3,2,1,0:T(8,128)(2,1)S(1)} %get-tuple-element.82), channel_id=1, source_target_pairs={{0,2},{2,0},{1,3},{3,1},{4,6},{6,4},{5,7},{7,5},{8,10},{10,8},{9,1... | collective-permute-start | bytes 196616 | tf_op jit(solution)/shard_map/ppermute | solution.py:379
  22.7 4.5 %collective-permute-start.9 = (bf16[2,1,1,64,256]{4,3,2,1,0:T(8,128)(2,1)S(1)}, bf16[2,1,1,64,256]{4,3,2,1,0:T(8,128)(2,1)S(1)}, u32[]{:S(2)}, u32[]{:S(2)}) collective-permute-start(bf16[2,1,1,64,256]{4,3,2,1,0:T(8,128)(2,1)S(1)} %get-tuple-element.81), channel_id=1, source_target_pairs={{0,4},{4,0},{8,12},{12,8},{1,5},{5,1},{9,13},{13,9},{2,6},{6,2},{1... | collective-permute-start | bytes 196616 | tf_op jit(solution)/shard_map/ppermute | solution.py:379
  23.9 6.7 %collective-permute-start.6 = (bf16[2,2,1,64,256]{4,3,2,1,0:T(8,128)(2,1)S(1)}, bf16[2,2,1,64,256]{4,3,2,1,0:T(8,128)(2,1)S(1)}, u32[]{:S(2)}, u32[]{:S(2)}) collective-permute-start(bf16[2,2,1,64,256]{4,3,2,1,0:T(8,128)(2,1)S(1)} %get-tuple-element.75), channel_id=1, source_target_pairs={{0,2},{2,0},{1,3},{3,1},{4,6},{6,4},{5,7},{7,5},{8,10},{10,8},{9,1... | collective-permute-start | bytes 393224 | tf_op jit(solution)/shard_map/ppermute | solution.py:379
  25.4 6.8 %collective-permute-start.12 = (bf16[2,1,1,64,256]{4,3,2,1,0:T(8,128)(2,1)S(1)}, bf16[2,1,1,64,256]{4,3,2,1,0:T(8,128)(2,1)S(1)}, u32[]{:S(2)}, u32[]{:S(2)}) collective-permute-start(bf16[2,1,1,64,256]{4,3,2,1,0:T(8,128)(2,1)S(1)} %shard_map.48), channel_id=1, source_target_pairs={{0,8},{4,12},{8,0},{12,4},{1,9},{5,13},{9,1},{13,5},{2,10},{6,14},... | collective-permute-start | bytes 196616 | tf_op jit(solution)/shard_map/ppermute | solution.py:379
  27.2 6.2 %collective-permute-start.14 = (bf16[2,1,1,64,256]{4,3,2,1,0:T(8,128)(2,1)S(1)}, bf16[2,1,1,64,256]{4,3,2,1,0:T(8,128)(2,1)S(1)}, u32[]{:S(2)}, u32[]{:S(2)}) collective-permute-start(bf16[2,1,1,64,256]{4,3,2,1,0:T(8,128)(2,1)S(1)} %shard_map.49), channel_id=1, source_target_pairs={{0,8},{4,12},{8,0},{12,4},{1,9},{5,13},{9,1},{13,5},{2,10},{6,14},... | collective-permute-start | bytes 196616 | tf_op jit(solution)/shard_map/ppermute | solution.py:379
  29.2 4.3 %collective-permute-start.13 = (bf16[2,1,1,64,256]{4,3,2,1,0:T(8,128)(2,1)S(1)}, bf16[2,1,1,64,256]{4,3,2,1,0:T(8,128)(2,1)S(1)}, u32[]{:S(2)}, u32[]{:S(2)}) collective-permute-start(bf16[2,1,1,64,256]{4,3,2,1,0:T(8,128)(2,1)S(1)} %get-tuple-element.90), channel_id=1, source_target_pairs={{0,2},{2,0},{1,3},{3,1},{4,6},{6,4},{5,7},{7,5},{8,10},{10,8},{9,1... | collective-permute-start | bytes 196616 | tf_op jit(solution)/shard_map/ppermute | solution.py:379
  30.7 4.3 %collective-permute-start.11 = (bf16[2,1,1,64,256]{4,3,2,1,0:T(8,128)(2,1)S(1)}, bf16[2,1,1,64,256]{4,3,2,1,0:T(8,128)(2,1)S(1)}, u32[]{:S(2)}, u32[]{:S(2)}) collective-permute-start(bf16[2,1,1,64,256]{4,3,2,1,0:T(8,128)(2,1)S(1)} %get-tuple-element.89), channel_id=1, source_target_pairs={{0,4},{4,0},{8,12},{12,8},{1,5},{5,1},{9,13},{13,9},{2,6},{6,2},{1... | collective-permute-start | bytes 196616 | tf_op jit(solution)/shard_map/ppermute | solution.py:379

commit v4 on v3

--- a/solution.py
+++ b/solution.py
@@ -264,18 +264,34 @@
     return range(lax.axis_size(axis).bit_length() - 1)
 
 
+def steps():
+    one = [("gx", bit) for bit in bits("gx")[:-1]]
+    two = [("gy", bit) for bit in bits("gy")]
+    both = min(len(one), len(two))
+    pairs = [pair for ends in zip(one, two) for pair in (ends, ends[::-1])]
+    return pairs + [(step, step) for step in one[both:] + two[both:]]
+
+
 def my_bit(axis, bit):
     return lax.bitwise_and(lax.shift_right_logical(lax.axis_index(axis), bit), 1)
 
 
-def project(lefts, right, begun_ref, steps, refs, total_ref):
-    for k, left in enumerate(lefts):
-        total_ref[k] = begun_ref[k] + dot(left, right)
+def my_side(step):
+    even, odd = (my_bit(*way) for way in step)
+    return jnp.where(my_bit("ma", 0) == 0, even, odd)
+
+
+def project(terms, begun_ref, keep_refs, send_refs, total_ref):
+    for k, term in enumerate(terms):
+        total_ref[k] = begun_ref[k] + term
     groups, own_modes, _ = total_ref.shape
     my_modes = lax.axis_index("ma")
+    odd_core = my_bit("ma", 0)
     top = my_bit("gx", bits("gx")[-1])
     across_x, across_y = lax.axis_size("gx"), lax.axis_size("gy")
-    rows, width = refs[0].shape[3:]
+    parts, count, rows, width = keep_refs[0].shape
+    plan = steps()
+    mine = my_side(plan[0])
 
     def piece(gx, gy):
         start = (gx * across_y + gy) * rows
@@ -283,29 +299,35 @@
         begin = start % own_modes
         return total_ref[group, begin : begin + rows]
 
-    for kind, axis in enumerate(steps):
-        keep_ref, send_ref = refs[2 * kind : 2 * kind + 2]
-        mine = my_bit(axis, 0)
+    for kind in range(2):
         half = lax.bitwise_xor(top, 1 - kind)
 
         def chosen(gx, gy):
             return jnp.where(half == 0, piece(gx, gy), piece(gx + across_x // 2, gy))
 
-        for gx in range(keep_ref.shape[1]):
-            for gy in range(keep_ref.shape[2]):
-                if axis == "gx":
-                    even, odd = chosen(2 * gx, gy), chosen(2 * gx + 1, gy)
-                else:
-                    even, odd = chosen(gx, 2 * gy), chosen(gx, 2 * gy + 1)
-                keep = jnp.where(mine == 0, even, odd)
-                send = jnp.where(mine == 0, odd, even).astype(send_ref.dtype)
-                for p in range(keep_ref.shape[0]):
-                    keep_ref[p, gx, gy] = keep[:, p * width : (p + 1) * width]
-                    send_ref[p, gx, gy] = send[:, p * width : (p + 1) * width]
+        def at(index):
+            places = []
+            for core in range(2):
+                place = {"gx": 0, "gy": 0}
+                for k, step in enumerate(plan):
+                    axis, bit = step[core]
+                    place[axis] |= (index >> (len(plan) - 1 - k) & 1) << bit
+                places.append((place["gx"], place["gy"]))
+            if places[0] == places[1]:
+                return chosen(*places[0])
+            return jnp.where(odd_core == 0, chosen(*places[0]), chosen(*places[1]))
+
+        for index in range(count):
+            low, high = at(index), at(index + count)
+            keep = jnp.where(mine == 0, low, high)
+            send = jnp.where(mine == 0, high, low).astype(jnp.bfloat16)
+            for p in range(parts):
+                keep_refs[kind][p, index] = keep[:, p * width : (p + 1) * width]
+                send_refs[kind][p, index] = send[:, p * width : (p + 1) * width]
 
 
 def first_kernel(
-    sites, steps, rows_ref, high_ref, low_ref, ahead_ref, back_ref, past_maps_ref, own_ref, others_ref, begun_ref,
+    sites, rows_ref, high_ref, low_ref, ahead_ref, back_ref, past_maps_ref, own_ref, others_ref, begun_ref,
     *refs,
 ):
     *refs, right_ref, total_ref = refs
@@ -331,7 +353,9 @@
     set_right(right_ref, 1, moved)
     inner = (planes - 2) * depth
     lefts = [own_ref[:, inner:]] + [others_ref[k, :, inner:] for k in range(others_ref.shape[0])]
-    project(lefts, right_ref[...], begun_ref, steps, refs, total_ref)
+    terms = [dot(left, right_ref[...]) for left in lefts]
+    keep_other, keep_own, send_ref = refs
+    project(terms, begun_ref, (keep_other, keep_own), (send_ref.at[0], send_ref.at[1]), total_ref)
 
 
 def move_y_kernel(
@@ -368,69 +392,63 @@
         turned_ref[k] = field_ref[k].reshape(planes * depth, width).T
 
 
-def second_kernel(steps, lefts_ref, right_ref, begun_ref, *refs):
+def second_kernel(lefts_ref, right_ref, begun_ref, *refs):
     *refs, total_ref = refs
     inner = lefts_ref.shape[2] - right_ref.shape[0]
     lefts = [lefts_ref[k, :, inner:] for k in range(lefts_ref.shape[0])]
-    project(lefts, right_ref[...], begun_ref, steps, refs, total_ref)
-
-
-def swap(block, axis, bit):
-    return lax.ppermute(block, axis, [(i, i ^ (1 << bit)) for i in range(lax.axis_size(axis))])
-
-
-def merge_kernel(axis, bit, kept_ref, came_ref, keep_ref, send_ref):
-    mine = my_bit(axis, bit)
-    for gx in range(keep_ref.shape[1]):
-        for gy in range(keep_ref.shape[2]):
-            pair = []
-            for odd in range(2):
-                at = (slice(None), 2 * gx + odd, gy) if axis == "gx" else (slice(None), gx, 2 * gy + odd)
-                pair.append(kept_ref[at] + came_ref[at].astype(jnp.float32))
-            keep_ref[:, gx, gy] = jnp.where(mine == 0, pair[0], pair[1])
-            send_ref[:, gx, gy] = jnp.where(mine == 0, pair[1], pair[0]).astype(send_ref.dtype)
+    terms = [dot(left, right_ref[...]) for left in lefts]
+    project(terms, begun_ref, refs[:2], refs[2:], total_ref)
+
+
+def exchange(block, step):
+    axes = ("gx", "gy", "ma")
+    sizes = [lax.axis_size(axis) for axis in axes]
+    route = []
+    for source in range(sizes[0] * sizes[1] * sizes[2]):
+        where = [source // (sizes[1] * sizes[2]), source // sizes[2] % sizes[1], source % sizes[2]]
+        axis, bit = step[where[2] % 2]
+        where[axes.index(axis)] ^= 1 << bit
+        route.append((source, (where[0] * sizes[1] + where[1]) * sizes[2] + where[2]))
+    return lax.ppermute(block, axes, route)
+
+
+def halve(sums, step, weight=0):
+    parts = sum(kept.shape[0] for kept, _, _ in sums)
+    count, rows, width = sums[0][0].shape[1:]
+    dims = (parts, count // 2, rows, width)
+
+    def merge(*refs):
+        *refs, keep_ref, send_ref = refs
+        mine = my_side(step)
+        start = 0
+        for k, (_, _, which) in enumerate(sums):
+            kept_ref, came_ref = refs[2 * k : 2 * k + 2]
+            came_ref = came_ref if which is None else came_ref.at[which]
+            end = start + kept_ref.shape[0]
+            for index in range(count // 2):
+                low, high = (
+                    kept_ref[:, at] + came_ref[:, at].astype(jnp.float32) for at in (index, index + count // 2)
+                )
+                keep_ref[start:end, index] = jnp.where(mine == 0, low, high)
+                send_ref[start:end, index] = jnp.where(mine == 0, high, low).astype(send_ref.dtype)
+            start = end
+
+    operands = [a for kept, came, _ in sums for a in (kept, came)]
+    keep, send = call(merge, (pltpu.VMEM(dims, jnp.float32), pltpu.VMEM(dims, jnp.bfloat16)), weight, operands)
+    return keep, exchange(send, step)
 
 
 def sum_kernel(kept_ref, came_ref, send_ref):
     send_ref[...] = (kept_ref[...] + came_ref[...].astype(jnp.float32)).astype(send_ref.dtype)
 
 
-def finish_kernel(*refs):
-    out_ref = refs[-1]
-    for d in range(out_ref.shape[0]):
-        kept_ref, came_ref, crossed_ref = refs[3 * d : 3 * d + 3]
-        total = kept_ref[:, 0, 0] + came_ref[:, 0, 0].astype(jnp.float32)
-        out_ref[d] = total + crossed_ref[:, 0, 0].astype(jnp.float32)
-
-
-class Reduction:
-    def __init__(self, kept, sent, axis):
-        *low, self.top = [("gx", bit) for bit in bits("gx")]
-        across = [("gy", bit) for bit in bits("gy")]
-        self.steps = across + low[1:] if axis == "gx" else across[1:] + low
-        self.kept, self.came = kept, swap(sent, axis, 0)
-
-    def halve(self, after, weight=0):
-        (axis, bit), *self.steps = self.steps
-        dim = ("gx", "gy").index(axis) + 1
-        shape = self.kept.shape
-        shape = shape[:dim] + (shape[dim] // 2,) + shape[dim + 1 :]
-
-        def merge(*refs):
-            merge_kernel(axis, bit, *refs)
-
-        self.came, _ = lax.optimization_barrier((self.came, after))
-        self.kept, sent = call(
-            merge, (pltpu.VMEM(shape, jnp.float32), pltpu.VMEM(shape, jnp.bfloat16)), weight, [self.kept, self.came]
-        )
-        self.came = swap(sent, axis, bit)
-        return self.kept
-
-    def cross(self, after):
-        self.came, _ = lax.optimization_barrier((self.came, after))
-        sent = call(sum_kernel, pltpu.VMEM(self.kept.shape, jnp.bfloat16), 0, [self.kept, self.came])
-        self.came = swap(sent, *self.top)
-        return sent
+def finish_kernel(kept_ref, came_ref, *refs):
+    *crossed_refs, out_ref = refs
+    parts = out_ref.shape[1]
+    for d, crossed_ref in enumerate(crossed_refs):
+        own = slice(d * parts, (d + 1) * parts)
+        total = kept_ref[own, 0] + came_ref[own, 0].astype(jnp.float32)
+        out_ref[d] = total + crossed_ref[:, 0].astype(jnp.float32)
 
 
 def local(eigen_modes, links_first, links_second):
@@ -486,23 +504,16 @@
         ahead_row = lax.broadcasted_iota(jnp.int32, ends.shape, 1) < row_size
         near = jnp.where(ahead_row, shifted(ends, "gy", -1), near)
 
-    first_steps, second_steps = ("gx", "gy"), ("gy", "gx")
-
-    def split(steps):
-        shapes = []
-        for axis in steps:
-            dims = (across_x // 4, across_y) if axis == "gx" else (across_x // 2, across_y // 2)
-            shapes += [shape(parts, *dims, rows, width, dtype=dtype) for dtype in (f32, bf16)]
-        return shapes
+    plan = steps()
+    top = ("gx", bits("gx")[-1])
+    pieces = across_x * across_y // 4
+    kept_shape = shape(parts, pieces, rows, width, dtype=f32)
 
     def inner(*refs):
         inner_kernel(sites, *refs)
 
     def first(*refs):
-        first_kernel(sites, first_steps, *refs)
-
-    def second(*refs):
-        second_kernel(second_steps, *refs)
+        first_kernel(sites, *refs)
 
     def move_y(*refs):
         move_y_kernel(sites, zs, *refs)
@@ -514,9 +525,9 @@
     fields = jnp.stack([t[0] for t in turned])
     others = jnp.stack([t[1] for t in turned])
     begun_first = call(begin_first_kernel, total_shape, project_flops, [own, others, right])
-    *parts_first, right_edge = call(
+    kept_first, own_first, sent_first, right_edge = call(
         first,
-        (*split(first_steps), shape(2 * depth, parts * width)),
+        (kept_shape, kept_shape, shape(2, parts, pieces, rows, width), shape(2 * depth, parts * width)),
         project_flops,
         [field, high, low, ahead_x, back_x, past_maps, own, others, begun_first],
         [total],
@@ -530,32 +541,34 @@
         [pltpu.VMEM((groups,) + field_shape.shape, bf16)],
     )
     begun_second = call(begin_second_kernel, total_shape, project_flops, [lefts, right])
-    parts_second = call(
-        second, split(second_steps), project_flops, [lefts, right_edge, begun_second], [total]
-    )
-    crossing = [
-        Reduction(*parts_first[:2], first_steps[0]), Reduction(*parts_second[:2], second_steps[0])
-    ]
-    after = crossing[0].halve(parts_second[0])
-    kept, sent = parts_first[2:]
-    sent, _ = lax.optimization_barrier((sent, after))
-    staying = [Reduction(kept, sent, first_steps[1]), Reduction(*parts_second[2:], second_steps[1])]
-    after = crossing[1].halve(after)
-    while any(r.steps for r in crossing):
-        for r in crossing:
-            if r.steps:
-                after = r.halve(after)
-    for r in crossing:
-        after = r.cross(after)
-    weights = (0, 4 * project_flops)
-    while any(r.steps for r in staying):
-        for r in staying[::-1]:
-            if r.steps:
-                after = r.halve(after, weights[r is staying[1]])
-    sums = []
-    for stay, cross in zip(staying, crossing):
-        sums += [stay.kept, stay.came, cross.came]
-    return call(finish_kernel, jax.ShapeDtypeStruct((2, parts, rows, width), f32), 0, sums)
+    sent_shape = shape(parts, pieces, rows, width)
+    kept_second, own_second, sent_second, sent_own = call(
+        second_kernel, (kept_shape, kept_shape, sent_shape, sent_shape), project_flops,
+        [lefts, right_edge, begun_second], [total],
+    )
+    came_first = exchange(sent_first, plan[0])
+    crossing = [(kept_first, came_first, 0), (kept_second, exchange(sent_second, plan[0]), None)]
+    staying = [(own_first, came_first, 1), (own_second, exchange(sent_own, plan[0]), None)]
+    after = kept_second
+    for step in plan[1:]:
+        for d, (kept, came, which) in enumerate(crossing):
+            came, after = lax.optimization_barrier((came, after))
+            kept, came = halve([(kept, came, which)], step)
+            crossing[d], after = (kept, came, None), kept
+    crossed = []
+    for kept, came, _ in crossing:
+        came, after = lax.optimization_barrier((came, after))
+        after = call(sum_kernel, pltpu.VMEM(kept.shape, bf16), 0, [kept, came])
+        crossed.append(exchange(after, (top, top)))
+    for step in plan[1:]:
+        kept, came, which = staying[-1]
+        came, after = lax.optimization_barrier((came, after))
+        kept, came = halve(staying[:-1] + [(kept, came, which)], step)
+        staying, after = [(kept, came, None)], kept
+    kept, came, _ = staying[0]
+    return call(
+        finish_kernel, jax.ShapeDtypeStruct((2, parts, rows, width), f32), 0, [kept, came, *crossed]
+    )
 
 
 def solution(mesh):

time: 35.9 us -> 35.2 us (0.981)
  starting transfers between devices: 21.5 us -> 17.8 us
  waiting for transfers between devices: 6.38 us -> 9.44 us
    ppermute x10 -> x8, starting transfers between devices: 14.6 us -> 10.9 us  [exchange(): return lax.ppermute(block, axes, route)]
    ppermute x10 -> x8, waiting for transfers between devices: 4.92 us -> 8.01 us  [exchange(): return lax.ppermute(block, axes, route)]
    pallas_call x16 -> x15, Pallas kernels: 7.69 us -> 7.72 us  [call(): pl.pallas_call(body, out_shape=out_shape, in_specs=[pl.BlockSpec(memory_s...]
  transfers between devices with their start and end apart: 15 -> 13, of which waited for: 5 -> 8; matrix products, arithmetic and copies ran while one was open for 0% -> 0% of each run, Pallas kernels for 19% -> 20%
where the time goes in v4:
time: 35.2 us; the launch traced here: 35.1 us
  starting transfers between devices  17.8 us (51%)
  waiting for transfers between devices  9.44 us (27%)
  Pallas kernels  7.72 us (22%)
    ppermute x8, starting transfers between devices, exchange(): return lax.ppermute(block, axes, route)  10.9 us
    ppermute x8, waiting for transfers between devices, exchange(): return lax.ppermute(block, axes, route)  8.01 us
    pallas_call x15, Pallas kernels, call(): pl.pallas_call(body, out_shape=out_shape, in_specs=[pl.BlockSpec(memory_s...  7.72 us
    ppermute x5, starting transfers between devices, shifted(): return lax.ppermute(block, axis, route)  6.9 us
    ppermute x5, waiting for transfers between devices, shifted(): return lax.ppermute(block, axis, route)  1.43 us
  transfers between devices with their start and end apart: 13, of which 8 were waited for; matrix products, arithmetic and copies ran while one was open for 0% of the time, Pallas kernels for 20%

profile of v4, /device:TPU:0, one launch (start us, length us, event | category | flops | bytes accessed | tf_op | source)
XLA Modules:
  0.0 35.1 jit_solution(16422073489314353107)
XLA Ops:
  0.0 0.5 %collective-permute-start.2 = (bf16[2,8,16,3,2,256]{5,4,3,2,1,0:T(2,128)(2,1)}, bf16[2,8,16,3,2,256]{5,4,3,2,1,0:T(2,128)(2,1)S(1)}, u32[]{:S(2)}, u32[]{:S(2)}) collective-permute-start(bf16[2,8,16,3,2,256]{5,4,3,2,1,0:T(2,128)(2,1)} %bitcast.10), channel_id=1, source_target_pairs={{1,0},{0,1},{3,2},{2,3},{5,4},{4,5},{7,6},{6,7},{9,8},{8,9},{11,10... | collective-permute-start | bytes 2359304 | tf_op jit(solution)/shard_map/ppermute | solution.py:14
  0.5 1.4 %shard_map.37 = (bf16[2,16,3,2,256]{4,3,2,1,0:T(2,128)(2,1)S(1)}, bf16[2,19,3,2,256]{4,3,2,1,0:T(2,128)(2,1)S(1)}, bf16[2,8,16,3,2,256]{5,4,3,2,1,0:T(2,128)(2,1...) custom-call(bf16[2,8,16,3,2,256]{5,4,3,2,1,0:T(2,128)(2,1)} %bitcast, ...), custom_call_target="tpu_custom_call" | custom-call | tf_op jit(solution)/shard_map/pallas_call | solution.py:19
  1.8 2.6 %collective-permute-start.1 = (bf16[2,19,3,2,256]{4,3,2,1,0:T(2,128)(2,1)S(1)}, bf16[2,19,3,2,256]{4,3,2,1,0:T(2,128)(2,1)S(1)}, u32[]{:S(2)}, u32[]{:S(2)}) collective-permute-start(bf16[2,19,3,2,256]{4,3,2,1,0:T(2,128)(2,1)S(1)} %get-tuple-element.49), channel_id=1, source_target_pairs={{12,0},{0,4},{4,8},{8,12},{13,1},{1,5},{5,9},{9,13},{14,2},{2,6},{... | collective-permute-start | bytes 350216 | tf_op jit(solution)/shard_map/ppermute | solution.py:14
  4.4 2.1 %collective-permute-start = (bf16[2,16,3,2,256]{4,3,2,1,0:T(2,128)(2,1)S(1)}, bf16[2,16,3,2,256]{4,3,2,1,0:T(2,128)(2,1)S(1)}, u32[]{:S(2)}, u32[]{:S(2)}) collective-permute-start(bf16[2,16,3,2,256]{4,3,2,1,0:T(2,128)(2,1)S(1)} %get-tuple-element.48), channel_id=1, source_target_pairs={{4,0},{8,4},{12,8},{0,12},{5,1},{9,5},{13,9},{1,13},{6,2},{10,6},{... | collective-permute-start | bytes 294920 | tf_op jit(solution)/shard_map/ppermute | solution.py:14
  6.5 0.8 %shard_map.38 = (bf16[8,192,256]{2,1,0:T(8,128)(2,1)S(1)}, bf16[8,32,256]{2,1,0:T(8,128)(2,1)S(1)}, f32[8,8,256]{2,1,0:T(8,128)S(1)}, f32[8,8,256]{2,1,0:T(8,128...) custom-call(bf16[2,8,16,3,2,256]{5,4,3,2,1,0:T(2,128)(2,1)S(1)} %get-tuple-element.43.raw_ref, ...), custom_call_target="tpu_custom_call" | custom-call | tf_op jit(solution)/shard_map/pallas_call | solution.py:19
  7.3 1.7 %collective-permute-start.4 = (bf16[8,32,256]{2,1,0:T(8,128)(2,1)S(1)}, bf16[8,32,256]{2,1,0:T(8,128)(2,1)S(1)}, u32[]{:S(2)}, u32[]{:S(2)}) collective-permute-start(bf16[8,32,256]{2,1,0:T(8,128)(2,1)S(1)} %get-tuple-element.59), channel_id=1, source_target_pairs={{2,0},{0,2},{3,1},{1,3},{6,4},{4,6},{7,5},{5,7},{10,8},{8,10},{11,... | collective-permute-start | bytes 393224 | tf_op jit(solution)/shard_map/ppermute | solution.py:14
  8.9 0.5 %shard_map.39 = (bf16[1152,512]{1,0:T(8,128)(2,1)S(1)}, bf16[256,1536]{1,0:T(8,128)(2,1)S(1)}) custom-call(bf16[8,192,256]{2,1,0:T(8,128)(2,1)S(1)} %get-tuple-element.47.refs_0_, f32[8,8,256]{2,1,0:T(8,128)S(1)} %get-tuple-element.50.refs_1_.refs_3_, f32[8,8,256]{2,1,0:T(8,128)S(1)} %get-tuple-element.51.refs_2_.refs_4_), custom_call_target="tpu_custom_call" | custom-call | flops 150994944 | tf_op jit(solution)/shard_map/pallas_call | solution.py:19
  9.4 0.0 collective-permute-done.2.raw_ref
  9.4 0.3 shard_map.40
  9.7 0.8 %shard_map.41.refs_8_ = f32[2,256,512]{2,1,0:T(8,128)S(1)} custom-call(bf16[256,1536]{1,0:T(8,128)(2,1)S(1)} %get-tuple-element.53.own_ref.refs_6_, bf16[1,256,1536]{2,1,0:T(8,128)(2,1)S(1)} %bitcast.6, bf16[1152,512]{1,0:T(8,128)(2,1)S(1)} %get-tuple-element.55.right_ref), custom_call_target="tpu_custom_call" | custom-call | flops 402653184 | tf_op jit(solution)/shard_map/pallas_call | solution.py:19
  10.6 1.3 %collective-permute-done.refs_1_ = bf16[2,16,3,2,256]{4,3,2,1,0:T(2,128)(2,1)S(1)} collective-permute-done((bf16[2,16,3,2,256]{4,3,2,1,0:T(2,128)(2,1)S(1)}, bf16[2,16,3,2,256]{4,3,2,1,0:T(2,128)(2,1)S(1)}, u32[]{:S(2)}, u32[]{:S(2)}) %collective-permute-start) | collective-permute-done | bytes 98336 | tf_op jit(solution)/shard_map/ppermute | solution.py:14
  11.9 0.0 collective-permute-done.1.refs_2_
  11.9 1.0 %shard_map.42 = (f32[2,2,64,256]{3,2,1,0:T(8,128)S(1)}, f32[2,2,64,256]{3,2,1,0:T(8,128)S(1)}, bf16[2,2,2,64,256]{4,3,2,1,0:T(8,128)(2,1)S(1)}, bf16[384,512]{1,0:T(8,128)(2,1)S(1)}) custom-call(bf16[8,192,256]{2,1,0:T(8,128)(2,1)S(1)} %get-tuple-element.47.refs_0_, bf16[2,16,3,2,256]{4,3,2,1,0:T(2,128)(2,1)S(1)} %collective-permute-done.refs_1_, ...), custom_call_target="tpu_custom_call" | custom-call | flops 402653184 | tf_op jit(solution)/shard_map/pallas_call | solution.py:19
  12.9 0.0 collective-permute-done.4.refs_2_
  12.9 0.1 collective-permute-start.5
  13.0 1.2 %collective-permute-start.3 = (bf16[2,2,2,64,256]{4,3,2,1,0:T(8,128)(2,1)S(1)}, bf16[2,2,2,64,256]{4,3,2,1,0:T(8,128)(2,1)S(1)}, u32[]{:S(2)}, u32[]{:S(2)}) collective-permute-start(bf16[2,2,2,64,256]{4,3,2,1,0:T(8,128)(2,1)S(1)} %get-tuple-element.57), channel_id=1, source_target_pairs={{0,4},{1,3},{2,6},{3,1},{4,0},{5,7},{6,2},{7,5},{8,12},{9,11},{10,... | collective-permute-start | bytes 786440 | tf_op jit(solution)/shard_map/ppermute | solution.py:412
  14.2 0.1 collective-permute-done.5
  14.3 0.7 %shard_map.43.lefts_ref = bf16[2,256,1536]{2,1,0:T(8,128)(2,1)S(1)} custom-call(bf16[8,192,256]{2,1,0:T(8,128)(2,1)S(1)} %get-tuple-element.47.refs_0_, bf16[1,8,192,256]{3,2,1,0:T(8,128)(2,1)S(1)} %bitcast.8, bf16[8,32,256]{2,1,0:T(8,128)(2,1)S(1)} %collective-permute-done.4.refs_2_, bf16[1,8,24,256]{3,2,1,0:T(8,128)(2,1)S(1)} %bitcast.9, ...), custom_call_target="tpu_custom_call" | custom-call | flops 150994944 | tf_op jit(solution)/shard_map/pallas_call | solution.py:19
  15.0 0.8 %shard_map.44.begun_ref = f32[2,256,512]{2,1,0:T(8,128)S(1)} custom-call(bf16[2,256,1536]{2,1,0:T(8,128)(2,1)S(1)} %shard_map.43.lefts_ref, bf16[1152,512]{1,0:T(8,128)(2,1)S(1)} %get-tuple-element.55.right_ref), custom_call_target="tpu_custom_call" | custom-call | flops 402653184 | tf_op jit(solution)/shard_map/pallas_call | solution.py:19
  15.8 0.6 %shard_map.45 = (f32[2,2,64,256]{3,2,1,0:T(8,128)S(1)}, f32[2,2,64,256]{3,2,1,0:T(8,128)S(1)}, bf16[2,2,64,256]{3,2,1,0:T(8,128)(2,1)S(1)}, bf16[2,2,64,256]{3,2,1,0:T(8,128)(2,1)S(1)}) custom-call(bf16[2,256,1536]{2,1,0:T(8,128)(2,1)S(1)} %shard_map.43.lefts_ref, bf16[384,512]{1,0:T(8,128)(2,1)S(1)} %get-tuple-element.64.right_ref, ...), custom_call_target="tpu_custom_call" | custom-call | flops 402653184 | tf_op jit(solution)/shard_map/pallas_call | solution.py:19
  16.4 1.2 %collective-permute-start.7 = (bf16[2,2,64,256]{3,2,1,0:T(8,128)(2,1)S(1)}, bf16[2,2,64,256]{3,2,1,0:T(8,128)(2,1)S(1)}, u32[]{:S(2)}, u32[]{:S(2)}) collective-permute-start(bf16[2,2,64,256]{3,2,1,0:T(8,128)(2,1)S(1)} %get-tuple-element.68), channel_id=1, source_target_pairs={{0,4},{1,3},{2,6},{3,1},{4,0},{5,7},{6,2},{7,5},{8,12},{9,11},{10,... | collective-permute-start | bytes 393224 | tf_op jit(solution)/shard_map/ppermute | solution.py:412
  17.6 0.9 %collective-permute-start.6 = (bf16[2,2,64,256]{3,2,1,0:T(8,128)(2,1)S(1)}, bf16[2,2,64,256]{3,2,1,0:T(8,128)(2,1)S(1)}, u32[]{:S(2)}, u32[]{:S(2)}) collective-permute-start(bf16[2,2,64,256]{3,2,1,0:T(8,128)(2,1)S(1)} %get-tuple-element.66), channel_id=1, source_target_pairs={{0,4},{1,3},{2,6},{3,1},{4,0},{5,7},{6,2},{7,5},{8,12},{9,11},{10,... | collective-permute-start | bytes 393224 | tf_op jit(solution)/shard_map/ppermute | solution.py:412
  18.5 0.9 %collective-permute-done.3.refs_1_ = bf16[2,2,2,64,256]{4,3,2,1,0:T(8,128)(2,1)S(1)} collective-permute-done((bf16[2,2,2,64,256]{4,3,2,1,0:T(8,128)(2,1)S(1)}, bf16[2,2,2,64,256]{4,3,2,1,0:T(8,128)(2,1)S(1)}, u32[]{:S(2)}, u32[]{:S(2)}) %collective-permute-start.3) | collective-permute-done | bytes 262176 | tf_op jit(solution)/shard_map/ppermute | solution.py:412
  19.5 1.6 %collective-permute-start.9 = (bf16[2,1,64,256]{3,2,1,0:T(8,128)(2,1)S(1)}, bf16[2,1,64,256]{3,2,1,0:T(8,128)(2,1)S(1)}, u32[]{:S(2)}, u32[]{:S(2)}) collective-permute-start(bf16[2,1,64,256]{3,2,1,0:T(8,128)(2,1)S(1)} %get-tuple-element.75), channel_id=1, source_target_pairs={{0,2},{1,5},{2,0},{3,7},{4,6},{5,1},{6,4},{7,3},{8,10},{9,13},{10,... | collective-permute-start | bytes 196616 | tf_op jit(solution)/shard_map/ppermute | solution.py:412
  21.1 0.4 %collective-permute-done.7.refs_1_ = bf16[2,2,64,256]{3,2,1,0:T(8,128)(2,1)S(1)} collective-permute-done((bf16[2,2,64,256]{3,2,1,0:T(8,128)(2,1)S(1)}, bf16[2,2,64,256]{3,2,1,0:T(8,128)(2,1)S(1)}, u32[]{:S(2)}, u32[]{:S(2)}) %collective-permute-start.7) | collective-permute-done | bytes 131104 | tf_op jit(solution)/shard_map/ppermute | solution.py:412
  21.5 1.6 %collective-permute-start.8 = (bf16[2,1,64,256]{3,2,1,0:T(8,128)(2,1)S(1)}, bf16[2,1,64,256]{3,2,1,0:T(8,128)(2,1)S(1)}, u32[]{:S(2)}, u32[]{:S(2)}) collective-permute-start(bf16[2,1,64,256]{3,2,1,0:T(8,128)(2,1)S(1)} %get-tuple-element.74), channel_id=1, source_target_pairs={{0,2},{1,5},{2,0},{3,7},{4,6},{5,1},{6,4},{7,3},{8,10},{9,13},{10,... | collective-permute-start | bytes 196616 | tf_op jit(solution)/shard_map/ppermute | solution.py:412
  23.0 0.8 %collective-permute-done.9.came_ref = bf16[2,1,64,256]{3,2,1,0:T(8,128)(2,1)S(1)} collective-permute-done((bf16[2,1,64,256]{3,2,1,0:T(8,128)(2,1)S(1)}, bf16[2,1,64,256]{3,2,1,0:T(8,128)(2,1)S(1)}, u32[]{:S(2)}, u32[]{:S(2)}) %collective-permute-start.9) | collective-permute-done | bytes 65568 | tf_op jit(solution)/shard_map/ppermute | solution.py:412
  23.8 2.0 %collective-permute-done.8.came_ref = bf16[2,1,64,256]{3,2,1,0:T(8,128)(2,1)S(1)} collective-permute-done((bf16[2,1,64,256]{3,2,1,0:T(8,128)(2,1)S(1)}, bf16[2,1,64,256]{3,2,1,0:T(8,128)(2,1)S(1)}, u32[]{:S(2)}, u32[]{:S(2)}) %collective-permute-start.8) | collective-permute-done | bytes 65568 | tf_op jit(solution)/shard_map/ppermute | solution.py:412
  25.8 0.0 collective-permute-done.6.refs_3_
  25.9 0.1 shard_map.50
  25.9 1.6 %collective-permute-start.10 = (bf16[4,1,64,256]{3,2,1,0:T(8,128)(2,1)S(1)}, bf16[4,1,64,256]{3,2,1,0:T(8,128)(2,1)S(1)}, u32[]{:S(2)}, u32[]{:S(2)}) collective-permute-start(bf16[4,1,64,256]{3,2,1,0:T(8,128)(2,1)S(1)} %get-tuple-element.80), channel_id=1, source_target_pairs={{0,2},{1,5},{2,0},{3,7},{4,6},{5,1},{6,4},{7,3},{8,10},{9,13},{10,... | collective-permute-start | bytes 393224 | tf_op jit(solution)/shard_map/ppermute | solution.py:412
  27.5 1.7 %collective-permute-start.12 = (bf16[2,1,64,256]{3,2,1,0:T(8,128)(2,1)S(1)}, bf16[2,1,64,256]{3,2,1,0:T(8,128)(2,1)S(1)}, u32[]{:S(2)}, u32[]{:S(2)}) collective-permute-start(bf16[2,1,64,256]{3,2,1,0:T(8,128)(2,1)S(1)} %shard_map.49), channel_id=1, source_target_pairs={{0,8},{1,9},{2,10},{3,11},{4,12},{5,13},{6,14},{7,15},{8,0},{9,1},... | collective-permute-start | bytes 196616 | tf_op jit(solution)/shard_map/ppermute | solution.py:412
  29.1 1.3 %collective-permute-start.11 = (bf16[2,1,64,256]{3,2,1,0:T(8,128)(2,1)S(1)}, bf16[2,1,64,256]{3,2,1,0:T(8,128)(2,1)S(1)}, u32[]{:S(2)}, u32[]{:S(2)}) collective-permute-start(bf16[2,1,64,256]{3,2,1,0:T(8,128)(2,1)S(1)} %shard_map.48), channel_id=1, source_target_pairs={{0,8},{1,9},{2,10},{3,11},{4,12},{5,13},{6,14},{7,15},{8,0},{9,1},... | collective-permute-start | bytes 196616 | tf_op jit(solution)/shard_map/ppermute | solution.py:412
  30.4 2.9 %collective-permute-done.12.refs_1_ = bf16[2,1,64,256]{3,2,1,0:T(8,128)(2,1)S(1)} collective-permute-done((bf16[2,1,64,256]{3,2,1,0:T(8,128)(2,1)S(1)}, bf16[2,1,64,256]{3,2,1,0:T(8,128)(2,1)S(1)}, u32[]{:S(2)}, u32[]{:S(2)}) %collective-permute-start.12) | collective-permute-done | bytes 65568 | tf_op jit(solution)/shard_map/ppermute | solution.py:412
  33.3 1.0 %collective-permute-done.11.refs_0_ = bf16[2,1,64,256]{3,2,1,0:T(8,128)(2,1)S(1)} collective-permute-done((bf16[2,1,64,256]{3,2,1,0:T(8,128)(2,1)S(1)}, bf16[2,1,64,256]{3,2,1,0:T(8,128)(2,1)S(1)}, u32[]{:S(2)}, u32[]{:S(2)}) %collective-permute-start.11) | collective-permute-done | bytes 65568 | tf_op jit(solution)/shard_map/ppermute | solution.py:412
  34.3 0.0 collective-permute-done.10.came_ref
  34.3 0.7 %shard_map.51 = f32[2,2,64,256]{3,2,1,0:T(8,128)} custom-call(f32[4,1,64,256]{3,2,1,0:T(8,128)S(1)} %get-tuple-element.79.kept_ref, bf16[4,1,64,256]{3,2,1,0:T(8,128)(2,1)S(1)} %collective-permute-done.10.came_ref, bf16[2,1,64,256]{3,2,1,0:T(8,128)(2,1)S(1)} %collective-permute-done.11.refs_0_, bf16[2,1,64,256]{3,2,1,0:T(8,128)(2,1)S(1)} %collective-permute-done.12.refs_1_), custom_call_target="tpu_custom_call" | custom-call | tf_op jit(solution)/shard_map/pallas_call | solution.py:19
  (5 shorter events, 0.1 us)
Async XLA Ops:
  0.0 9.4 %collective-permute-start.2 = (bf16[2,8,16,3,2,256]{5,4,3,2,1,0:T(2,128)(2,1)}, bf16[2,8,16,3,2,256]{5,4,3,2,1,0:T(2,128)(2,1)S(1)}, u32[]{:S(2)}, u32[]{:S(2)}) collective-permute-start(bf16[2,8,16,3,2,256]{5,4,3,2,1,0:T(2,128)(2,1)} %bitcast.10), channel_id=1, source_target_pairs={{1,0},{0,1},{3,2},{2,3},{5,4},{4,5},{7,6},{6,7},{9,8},{8,9},{11,10... | collective-permute-start | bytes 2359304 | tf_op jit(solution)/shard_map/ppermute | solution.py:14
  1.8 10.1 %collective-permute-start.1 = (bf16[2,19,3,2,256]{4,3,2,1,0:T(2,128)(2,1)S(1)}, bf16[2,19,3,2,256]{4,3,2,1,0:T(2,128)(2,1)S(1)}, u32[]{:S(2)}, u32[]{:S(2)}) collective-permute-start(bf16[2,19,3,2,256]{4,3,2,1,0:T(2,128)(2,1)S(1)} %get-tuple-element.49), channel_id=1, source_target_pairs={{12,0},{0,4},{4,8},{8,12},{13,1},{1,5},{5,9},{9,13},{14,2},{2,6},{... | collective-permute-start | bytes 350216 | tf_op jit(solution)/shard_map/ppermute | solution.py:14
  4.4 7.4 %collective-permute-start = (bf16[2,16,3,2,256]{4,3,2,1,0:T(2,128)(2,1)S(1)}, bf16[2,16,3,2,256]{4,3,2,1,0:T(2,128)(2,1)S(1)}, u32[]{:S(2)}, u32[]{:S(2)}) collective-permute-start(bf16[2,16,3,2,256]{4,3,2,1,0:T(2,128)(2,1)S(1)} %get-tuple-element.48), channel_id=1, source_target_pairs={{4,0},{8,4},{12,8},{0,12},{5,1},{9,5},{13,9},{1,13},{6,2},{10,6},{... | collective-permute-start | bytes 294920 | tf_op jit(solution)/shard_map/ppermute | solution.py:14
  7.3 5.6 %collective-permute-start.4 = (bf16[8,32,256]{2,1,0:T(8,128)(2,1)S(1)}, bf16[8,32,256]{2,1,0:T(8,128)(2,1)S(1)}, u32[]{:S(2)}, u32[]{:S(2)}) collective-permute-start(bf16[8,32,256]{2,1,0:T(8,128)(2,1)S(1)} %get-tuple-element.59), channel_id=1, source_target_pairs={{2,0},{0,2},{3,1},{1,3},{6,4},{4,6},{7,5},{5,7},{10,8},{8,10},{11,... | collective-permute-start | bytes 393224 | tf_op jit(solution)/shard_map/ppermute | solution.py:14
  12.9 1.4 %collective-permute-start.5 = (bf16[8,24,256]{2,1,0:T(8,128)(2,1)S(1)}, bf16[8,24,256]{2,1,0:T(8,128)(2,1)S(1)}, u32[]{:S(2)}, u32[]{:S(2)}) collective-permute-start(bf16[8,24,256]{2,1,0:T(8,128)(2,1)S(1)} %slice.3), channel_id=1, source_target_pairs={{1,0},{0,1},{3,2},{2,3},{5,4},{4,5},{7,6},{6,7},{9,8},{8,9},{11,10... | collective-permute-start | bytes 294920 | tf_op jit(solution)/shard_map/ppermute | solution.py:14
  13.0 6.4 %collective-permute-start.3 = (bf16[2,2,2,64,256]{4,3,2,1,0:T(8,128)(2,1)S(1)}, bf16[2,2,2,64,256]{4,3,2,1,0:T(8,128)(2,1)S(1)}, u32[]{:S(2)}, u32[]{:S(2)}) collective-permute-start(bf16[2,2,2,64,256]{4,3,2,1,0:T(8,128)(2,1)S(1)} %get-tuple-element.57), channel_id=1, source_target_pairs={{0,4},{1,3},{2,6},{3,1},{4,0},{5,7},{6,2},{7,5},{8,12},{9,11},{10,... | collective-permute-start | bytes 786440 | tf_op jit(solution)/shard_map/ppermute | solution.py:412
  16.4 5.0 %collective-permute-start.7 = (bf16[2,2,64,256]{3,2,1,0:T(8,128)(2,1)S(1)}, bf16[2,2,64,256]{3,2,1,0:T(8,128)(2,1)S(1)}, u32[]{:S(2)}, u32[]{:S(2)}) collective-permute-start(bf16[2,2,64,256]{3,2,1,0:T(8,128)(2,1)S(1)} %get-tuple-element.68), channel_id=1, source_target_pairs={{0,4},{1,3},{2,6},{3,1},{4,0},{5,7},{6,2},{7,5},{8,12},{9,11},{10,... | collective-permute-start | bytes 393224 | tf_op jit(solution)/shard_map/ppermute | solution.py:412
  17.6 8.3 %collective-permute-start.6 = (bf16[2,2,64,256]{3,2,1,0:T(8,128)(2,1)S(1)}, bf16[2,2,64,256]{3,2,1,0:T(8,128)(2,1)S(1)}, u32[]{:S(2)}, u32[]{:S(2)}) collective-permute-start(bf16[2,2,64,256]{3,2,1,0:T(8,128)(2,1)S(1)} %get-tuple-element.66), channel_id=1, source_target_pairs={{0,4},{1,3},{2,6},{3,1},{4,0},{5,7},{6,2},{7,5},{8,12},{9,11},{10,... | collective-permute-start | bytes 393224 | tf_op jit(solution)/shard_map/ppermute | solution.py:412
  19.5 4.3 %collective-permute-start.9 = (bf16[2,1,64,256]{3,2,1,0:T(8,128)(2,1)S(1)}, bf16[2,1,64,256]{3,2,1,0:T(8,128)(2,1)S(1)}, u32[]{:S(2)}, u32[]{:S(2)}) collective-permute-start(bf16[2,1,64,256]{3,2,1,0:T(8,128)(2,1)S(1)} %get-tuple-element.75), channel_id=1, source_target_pairs={{0,2},{1,5},{2,0},{3,7},{4,6},{5,1},{6,4},{7,3},{8,10},{9,13},{10,... | collective-permute-start | bytes 196616 | tf_op jit(solution)/shard_map/ppermute | solution.py:412
  21.5 4.3 %collective-permute-start.8 = (bf16[2,1,64,256]{3,2,1,0:T(8,128)(2,1)S(1)}, bf16[2,1,64,256]{3,2,1,0:T(8,128)(2,1)S(1)}, u32[]{:S(2)}, u32[]{:S(2)}) collective-permute-start(bf16[2,1,64,256]{3,2,1,0:T(8,128)(2,1)S(1)} %get-tuple-element.74), channel_id=1, source_target_pairs={{0,2},{1,5},{2,0},{3,7},{4,6},{5,1},{6,4},{7,3},{8,10},{9,13},{10,... | collective-permute-start | bytes 196616 | tf_op jit(solution)/shard_map/ppermute | solution.py:412
  25.9 8.4 %collective-permute-start.10 = (bf16[4,1,64,256]{3,2,1,0:T(8,128)(2,1)S(1)}, bf16[4,1,64,256]{3,2,1,0:T(8,128)(2,1)S(1)}, u32[]{:S(2)}, u32[]{:S(2)}) collective-permute-start(bf16[4,1,64,256]{3,2,1,0:T(8,128)(2,1)S(1)} %get-tuple-element.80), channel_id=1, source_target_pairs={{0,2},{1,5},{2,0},{3,7},{4,6},{5,1},{6,4},{7,3},{8,10},{9,13},{10,... | collective-permute-start | bytes 393224 | tf_op jit(solution)/shard_map/ppermute | solution.py:412
  27.5 5.9 %collective-permute-start.12 = (bf16[2,1,64,256]{3,2,1,0:T(8,128)(2,1)S(1)}, bf16[2,1,64,256]{3,2,1,0:T(8,128)(2,1)S(1)}, u32[]{:S(2)}, u32[]{:S(2)}) collective-permute-start(bf16[2,1,64,256]{3,2,1,0:T(8,128)(2,1)S(1)} %shard_map.49), channel_id=1, source_target_pairs={{0,8},{1,9},{2,10},{3,11},{4,12},{5,13},{6,14},{7,15},{8,0},{9,1},... | collective-permute-start | bytes 196616 | tf_op jit(solution)/shard_map/ppermute | solution.py:412
  29.1 5.2 %collective-permute-start.11 = (bf16[2,1,64,256]{3,2,1,0:T(8,128)(2,1)S(1)}, bf16[2,1,64,256]{3,2,1,0:T(8,128)(2,1)S(1)}, u32[]{:S(2)}, u32[]{:S(2)}) collective-permute-start(bf16[2,1,64,256]{3,2,1,0:T(8,128)(2,1)S(1)} %shard_map.48), channel_id=1, source_target_pairs={{0,8},{1,9},{2,10},{3,11},{4,12},{5,13},{6,14},{7,15},{8,0},{9,1},... | collective-permute-start | bytes 196616 | tf_op jit(solution)/shard_map/ppermute | solution.py:412

commit v5 on v4

--- a/solution.py
+++ b/solution.py
@@ -442,13 +442,16 @@
     send_ref[...] = (kept_ref[...] + came_ref[...].astype(jnp.float32)).astype(send_ref.dtype)
 
 
-def finish_kernel(kept_ref, came_ref, *refs):
-    *crossed_refs, out_ref = refs
+def cross_kernel(start, kept_ref, crossed_ref, out_ref):
+    kept = kept_ref[start : start + out_ref.shape[0]]
+    out_ref[...] = kept + crossed_ref[...].astype(jnp.float32)
+
+
+def finish_kernel(came_ref, *refs):
+    *kept_refs, out_ref = refs
     parts = out_ref.shape[1]
-    for d, crossed_ref in enumerate(crossed_refs):
-        own = slice(d * parts, (d + 1) * parts)
-        total = kept_ref[own, 0] + came_ref[own, 0].astype(jnp.float32)
-        out_ref[d] = total + crossed_ref[:, 0].astype(jnp.float32)
+    for d, kept_ref in enumerate(kept_refs):
+        out_ref[d] = kept_ref[:, 0] + came_ref[d * parts : (d + 1) * parts, 0].astype(jnp.float32)
 
 
 def local(eigen_modes, links_first, links_second):
@@ -566,8 +569,18 @@
         kept, came = halve(staying[:-1] + [(kept, came, which)], step)
         staying, after = [(kept, came, None)], kept
     kept, came, _ = staying[0]
+    totals = []
+    for d, block in enumerate(crossed):
+
+        def cross(*refs, start=d * parts):
+            cross_kernel(start, *refs)
+
+        block, after = lax.optimization_barrier((block, after))
+        after = call(cross, shape(*block.shape, dtype=f32), 4 * project_flops, [kept, block])
+        totals.append(after)
+    came, after = lax.optimization_barrier((came, after))
     return call(
-        finish_kernel, jax.ShapeDtypeStruct((2, parts, rows, width), f32), 0, [kept, came, *crossed]
+        finish_kernel, jax.ShapeDtypeStruct((2, parts, rows, width), f32), 0, [came, *totals]
     )
 
 

time: 35.2 us -> 35.5 us (level)
  starting transfers between devices: 17.8 us -> 18.4 us
  waiting for transfers between devices: 9.44 us -> 9.02 us
    ppermute x8, waiting for transfers between devices: 8.01 us -> 6.43 us  [exchange(): return lax.ppermute(block, axes, route)]
    ppermute x5, waiting for transfers between devices: 1.43 us -> 2.59 us  [shifted(): return lax.ppermute(block, axis, route)]
    ppermute x8, starting transfers between devices: 10.9 us -> 11.5 us  [exchange(): return lax.ppermute(block, axes, route)]
    pallas_call x15 -> x17, Pallas kernels: 7.72 us -> 7.73 us  [call(): pl.pallas_call(body, out_shape=out_shape, in_specs=[pl.BlockSpec(memory_s...]
  transfers between devices with their start and end apart: 13 -> 13, of which waited for: 8 -> 7; matrix products, arithmetic and copies ran while one was open for 0% -> 0% of each run, Pallas kernels for 20% -> 20%
where the time goes in v5:
time: 35.5 us; the launch traced here: 35.3 us
  starting transfers between devices  18.4 us (52%)
  waiting for transfers between devices  9.02 us (25%)
  Pallas kernels  7.73 us (22%)
    ppermute x8, starting transfers between devices, exchange(): return lax.ppermute(block, axes, route)  11.5 us
    pallas_call x17, Pallas kernels, call(): pl.pallas_call(body, out_shape=out_shape, in_specs=[pl.BlockSpec(memory_s...  7.73 us
    ppermute x5, starting transfers between devices, shifted(): return lax.ppermute(block, axis, route)  6.9 us
    ppermute x8, waiting for transfers between devices, exchange(): return lax.ppermute(block, axes, route)  6.43 us
    ppermute x5, waiting for transfers between devices, shifted(): return lax.ppermute(block, axis, route)  2.59 us
  transfers between devices with their start and end apart: 13, of which 7 were waited for; matrix products, arithmetic and copies ran while one was open for 0% of the time, Pallas kernels for 20%

profile of v5, /device:TPU:0, one launch (start us, length us, event | category | flops | bytes accessed | tf_op | source)
XLA Modules:
  0.0 35.3 jit_solution(177171977600718891)
XLA Ops:
  0.0 0.5 %collective-permute-start.2 = (bf16[2,8,16,3,2,256]{5,4,3,2,1,0:T(2,128)(2,1)}, bf16[2,8,16,3,2,256]{5,4,3,2,1,0:T(2,128)(2,1)S(1)}, u32[]{:S(2)}, u32[]{:S(2)}) collective-permute-start(bf16[2,8,16,3,2,256]{5,4,3,2,1,0:T(2,128)(2,1)} %bitcast.10), channel_id=1, source_target_pairs={{1,0},{0,1},{3,2},{2,3},{5,4},{4,5},{7,6},{6,7},{9,8},{8,9},{11,10... | collective-permute-start | bytes 2359304 | tf_op jit(solution)/shard_map/ppermute | solution.py:14
  0.5 1.4 %shard_map.37 = (bf16[2,16,3,2,256]{4,3,2,1,0:T(2,128)(2,1)S(1)}, bf16[2,19,3,2,256]{4,3,2,1,0:T(2,128)(2,1)S(1)}, bf16[2,8,16,3,2,256]{5,4,3,2,1,0:T(2,128)(2,1...) custom-call(bf16[2,8,16,3,2,256]{5,4,3,2,1,0:T(2,128)(2,1)} %bitcast, ...), custom_call_target="tpu_custom_call" | custom-call | tf_op jit(solution)/shard_map/pallas_call | solution.py:19
  1.8 2.6 %collective-permute-start.1 = (bf16[2,19,3,2,256]{4,3,2,1,0:T(2,128)(2,1)S(1)}, bf16[2,19,3,2,256]{4,3,2,1,0:T(2,128)(2,1)S(1)}, u32[]{:S(2)}, u32[]{:S(2)}) collective-permute-start(bf16[2,19,3,2,256]{4,3,2,1,0:T(2,128)(2,1)S(1)} %get-tuple-element.52), channel_id=1, source_target_pairs={{12,0},{0,4},{4,8},{8,12},{13,1},{1,5},{5,9},{9,13},{14,2},{2,6},{... | collective-permute-start | bytes 350216 | tf_op jit(solution)/shard_map/ppermute | solution.py:14
  4.4 2.1 %collective-permute-start = (bf16[2,16,3,2,256]{4,3,2,1,0:T(2,128)(2,1)S(1)}, bf16[2,16,3,2,256]{4,3,2,1,0:T(2,128)(2,1)S(1)}, u32[]{:S(2)}, u32[]{:S(2)}) collective-permute-start(bf16[2,16,3,2,256]{4,3,2,1,0:T(2,128)(2,1)S(1)} %get-tuple-element.51), channel_id=1, source_target_pairs={{4,0},{8,4},{12,8},{0,12},{5,1},{9,5},{13,9},{1,13},{6,2},{10,6},{... | collective-permute-start | bytes 294920 | tf_op jit(solution)/shard_map/ppermute | solution.py:14
  6.5 0.8 %shard_map.38 = (bf16[8,192,256]{2,1,0:T(8,128)(2,1)S(1)}, bf16[8,32,256]{2,1,0:T(8,128)(2,1)S(1)}, f32[8,8,256]{2,1,0:T(8,128)S(1)}, f32[8,8,256]{2,1,0:T(8,128...) custom-call(bf16[2,8,16,3,2,256]{5,4,3,2,1,0:T(2,128)(2,1)S(1)} %get-tuple-element.46.raw_ref, ...), custom_call_target="tpu_custom_call" | custom-call | tf_op jit(solution)/shard_map/pallas_call | solution.py:19
  7.3 1.7 %collective-permute-start.4 = (bf16[8,32,256]{2,1,0:T(8,128)(2,1)S(1)}, bf16[8,32,256]{2,1,0:T(8,128)(2,1)S(1)}, u32[]{:S(2)}, u32[]{:S(2)}) collective-permute-start(bf16[8,32,256]{2,1,0:T(8,128)(2,1)S(1)} %get-tuple-element.62), channel_id=1, source_target_pairs={{2,0},{0,2},{3,1},{1,3},{6,4},{4,6},{7,5},{5,7},{10,8},{8,10},{11,... | collective-permute-start | bytes 393224 | tf_op jit(solution)/shard_map/ppermute | solution.py:14
  8.9 0.5 %shard_map.39 = (bf16[1152,512]{1,0:T(8,128)(2,1)S(1)}, bf16[256,1536]{1,0:T(8,128)(2,1)S(1)}) custom-call(bf16[8,192,256]{2,1,0:T(8,128)(2,1)S(1)} %get-tuple-element.50.refs_0_, f32[8,8,256]{2,1,0:T(8,128)S(1)} %get-tuple-element.53.refs_1_.refs_3_, f32[8,8,256]{2,1,0:T(8,128)S(1)} %get-tuple-element.54.refs_2_.refs_4_), custom_call_target="tpu_custom_call" | custom-call | flops 150994944 | tf_op jit(solution)/shard_map/pallas_call | solution.py:19
  9.4 0.0 collective-permute-done.2.raw_ref
  9.4 0.3 shard_map.40
  9.7 0.8 %shard_map.41.refs_8_ = f32[2,256,512]{2,1,0:T(8,128)S(1)} custom-call(bf16[256,1536]{1,0:T(8,128)(2,1)S(1)} %get-tuple-element.56.own_ref.refs_6_, bf16[1,256,1536]{2,1,0:T(8,128)(2,1)S(1)} %bitcast.6, bf16[1152,512]{1,0:T(8,128)(2,1)S(1)} %get-tuple-element.58.right_ref), custom_call_target="tpu_custom_call" | custom-call | flops 402653184 | tf_op jit(solution)/shard_map/pallas_call | solution.py:19
  10.6 1.3 %collective-permute-done.refs_1_ = bf16[2,16,3,2,256]{4,3,2,1,0:T(2,128)(2,1)S(1)} collective-permute-done((bf16[2,16,3,2,256]{4,3,2,1,0:T(2,128)(2,1)S(1)}, bf16[2,16,3,2,256]{4,3,2,1,0:T(2,128)(2,1)S(1)}, u32[]{:S(2)}, u32[]{:S(2)}) %collective-permute-start) | collective-permute-done | bytes 98336 | tf_op jit(solution)/shard_map/ppermute | solution.py:14
  11.9 0.0 collective-permute-done.1.refs_2_
  11.9 1.0 %shard_map.42 = (f32[2,2,64,256]{3,2,1,0:T(8,128)S(1)}, f32[2,2,64,256]{3,2,1,0:T(8,128)S(1)}, bf16[2,2,2,64,256]{4,3,2,1,0:T(8,128)(2,1)S(1)}, bf16[384,512]{1,0:T(8,128)(2,1)S(1)}) custom-call(bf16[8,192,256]{2,1,0:T(8,128)(2,1)S(1)} %get-tuple-element.50.refs_0_, bf16[2,16,3,2,256]{4,3,2,1,0:T(2,128)(2,1)S(1)} %collective-permute-done.refs_1_, ...), custom_call_target="tpu_custom_call" | custom-call | flops 402653184 | tf_op jit(solution)/shard_map/pallas_call | solution.py:19
  12.9 1.2 %collective-permute-start.3 = (bf16[2,2,2,64,256]{4,3,2,1,0:T(8,128)(2,1)S(1)}, bf16[2,2,2,64,256]{4,3,2,1,0:T(8,128)(2,1)S(1)}, u32[]{:S(2)}, u32[]{:S(2)}) collective-permute-start(bf16[2,2,2,64,256]{4,3,2,1,0:T(8,128)(2,1)S(1)} %get-tuple-element.60), channel_id=1, source_target_pairs={{0,4},{1,3},{2,6},{3,1},{4,0},{5,7},{6,2},{7,5},{8,12},{9,11},{10,... | collective-permute-start | bytes 786440 | tf_op jit(solution)/shard_map/ppermute | solution.py:412
  14.1 0.0 collective-permute-done.4.refs_2_
  14.1 0.1 collective-permute-start.5
  14.2 1.3 %collective-permute-done.5 = bf16[8,24,256]{2,1,0:T(8,128)(2,1)S(1)} collective-permute-done((bf16[8,24,256]{2,1,0:T(8,128)(2,1)S(1)}, bf16[8,24,256]{2,1,0:T(8,128)(2,1)S(1)}, u32[]{:S(2)}, u32[]{:S(2)}) %collective-permute-start.5) | collective-permute-done | bytes 98336 | tf_op jit(solution)/shard_map/ppermute | solution.py:14
  15.5 0.7 %shard_map.43.lefts_ref = bf16[2,256,1536]{2,1,0:T(8,128)(2,1)S(1)} custom-call(bf16[8,192,256]{2,1,0:T(8,128)(2,1)S(1)} %get-tuple-element.50.refs_0_, bf16[1,8,192,256]{3,2,1,0:T(8,128)(2,1)S(1)} %bitcast.8, bf16[8,32,256]{2,1,0:T(8,128)(2,1)S(1)} %collective-permute-done.4.refs_2_, bf16[1,8,24,256]{3,2,1,0:T(8,128)(2,1)S(1)} %bitcast.9, ...), custom_call_target="tpu_custom_call" | custom-call | flops 150994944 | tf_op jit(solution)/shard_map/pallas_call | solution.py:19
  16.2 0.8 %shard_map.44.begun_ref = f32[2,256,512]{2,1,0:T(8,128)S(1)} custom-call(bf16[2,256,1536]{2,1,0:T(8,128)(2,1)S(1)} %shard_map.43.lefts_ref, bf16[1152,512]{1,0:T(8,128)(2,1)S(1)} %get-tuple-element.58.right_ref), custom_call_target="tpu_custom_call" | custom-call | flops 402653184 | tf_op jit(solution)/shard_map/pallas_call | solution.py:19
  17.0 0.6 %shard_map.45 = (f32[2,2,64,256]{3,2,1,0:T(8,128)S(1)}, f32[2,2,64,256]{3,2,1,0:T(8,128)S(1)}, bf16[2,2,64,256]{3,2,1,0:T(8,128)(2,1)S(1)}, bf16[2,2,64,256]{3,2,1,0:T(8,128)(2,1)S(1)}) custom-call(bf16[2,256,1536]{2,1,0:T(8,128)(2,1)S(1)} %shard_map.43.lefts_ref, bf16[384,512]{1,0:T(8,128)(2,1)S(1)} %get-tuple-element.67.right_ref, ...), custom_call_target="tpu_custom_call" | custom-call | flops 402653184 | tf_op jit(solution)/shard_map/pallas_call | solution.py:19
  17.6 1.0 %collective-permute-start.7 = (bf16[2,2,64,256]{3,2,1,0:T(8,128)(2,1)S(1)}, bf16[2,2,64,256]{3,2,1,0:T(8,128)(2,1)S(1)}, u32[]{:S(2)}, u32[]{:S(2)}) collective-permute-start(bf16[2,2,64,256]{3,2,1,0:T(8,128)(2,1)S(1)} %get-tuple-element.71), channel_id=1, source_target_pairs={{0,4},{1,3},{2,6},{3,1},{4,0},{5,7},{6,2},{7,5},{8,12},{9,11},{10,... | collective-permute-start | bytes 393224 | tf_op jit(solution)/shard_map/ppermute | solution.py:412
  18.5 1.1 %collective-permute-start.6 = (bf16[2,2,64,256]{3,2,1,0:T(8,128)(2,1)S(1)}, bf16[2,2,64,256]{3,2,1,0:T(8,128)(2,1)S(1)}, u32[]{:S(2)}, u32[]{:S(2)}) collective-permute-start(bf16[2,2,64,256]{3,2,1,0:T(8,128)(2,1)S(1)} %get-tuple-element.69), channel_id=1, source_target_pairs={{0,4},{1,3},{2,6},{3,1},{4,0},{5,7},{6,2},{7,5},{8,12},{9,11},{10,... | collective-permute-start | bytes 393224 | tf_op jit(solution)/shard_map/ppermute | solution.py:412
  19.7 0.0 collective-permute-done.3.refs_1_
  19.7 1.6 %collective-permute-start.9 = (bf16[2,1,64,256]{3,2,1,0:T(8,128)(2,1)S(1)}, bf16[2,1,64,256]{3,2,1,0:T(8,128)(2,1)S(1)}, u32[]{:S(2)}, u32[]{:S(2)}) collective-permute-start(bf16[2,1,64,256]{3,2,1,0:T(8,128)(2,1)S(1)} %get-tuple-element.78), channel_id=1, source_target_pairs={{0,2},{1,5},{2,0},{3,7},{4,6},{5,1},{6,4},{7,3},{8,10},{9,13},{10,... | collective-permute-start | bytes 196616 | tf_op jit(solution)/shard_map/ppermute | solution.py:412
  21.3 2.0 %collective-permute-done.7.refs_1_ = bf16[2,2,64,256]{3,2,1,0:T(8,128)(2,1)S(1)} collective-permute-done((bf16[2,2,64,256]{3,2,1,0:T(8,128)(2,1)S(1)}, bf16[2,2,64,256]{3,2,1,0:T(8,128)(2,1)S(1)}, u32[]{:S(2)}, u32[]{:S(2)}) %collective-permute-start.7) | collective-permute-done | bytes 131104 | tf_op jit(solution)/shard_map/ppermute | solution.py:412
  23.3 1.5 %collective-permute-start.8 = (bf16[2,1,64,256]{3,2,1,0:T(8,128)(2,1)S(1)}, bf16[2,1,64,256]{3,2,1,0:T(8,128)(2,1)S(1)}, u32[]{:S(2)}, u32[]{:S(2)}) collective-permute-start(bf16[2,1,64,256]{3,2,1,0:T(8,128)(2,1)S(1)} %get-tuple-element.77), channel_id=1, source_target_pairs={{0,2},{1,5},{2,0},{3,7},{4,6},{5,1},{6,4},{7,3},{8,10},{9,13},{10,... | collective-permute-start | bytes 196616 | tf_op jit(solution)/shard_map/ppermute | solution.py:412
  24.9 0.0 collective-permute-done.9.came_ref
  24.9 1.8 %collective-permute-start.12 = (bf16[2,1,64,256]{3,2,1,0:T(8,128)(2,1)S(1)}, bf16[2,1,64,256]{3,2,1,0:T(8,128)(2,1)S(1)}, u32[]{:S(2)}, u32[]{:S(2)}) collective-permute-start(bf16[2,1,64,256]{3,2,1,0:T(8,128)(2,1)S(1)} %shard_map.48), channel_id=1, source_target_pairs={{0,8},{1,9},{2,10},{3,11},{4,12},{5,13},{6,14},{7,15},{8,0},{9,1},... | collective-permute-start | bytes 196616 | tf_op jit(solution)/shard_map/ppermute | solution.py:412
  26.7 1.0 %collective-permute-done.8.came_ref = bf16[2,1,64,256]{3,2,1,0:T(8,128)(2,1)S(1)} collective-permute-done((bf16[2,1,64,256]{3,2,1,0:T(8,128)(2,1)S(1)}, bf16[2,1,64,256]{3,2,1,0:T(8,128)(2,1)S(1)}, u32[]{:S(2)}, u32[]{:S(2)}) %collective-permute-start.8) | collective-permute-done | bytes 65568 | tf_op jit(solution)/shard_map/ppermute | solution.py:412
  27.7 1.8 %collective-permute-start.11 = (bf16[2,1,64,256]{3,2,1,0:T(8,128)(2,1)S(1)}, bf16[2,1,64,256]{3,2,1,0:T(8,128)(2,1)S(1)}, u32[]{:S(2)}, u32[]{:S(2)}) collective-permute-start(bf16[2,1,64,256]{3,2,1,0:T(8,128)(2,1)S(1)} %shard_map.49), channel_id=1, source_target_pairs={{0,8},{1,9},{2,10},{3,11},{4,12},{5,13},{6,14},{7,15},{8,0},{9,1},... | collective-permute-start | bytes 196616 | tf_op jit(solution)/shard_map/ppermute | solution.py:412
  29.5 0.0 collective-permute-done.6.refs_3_
  29.5 0.1 shard_map.50
  29.6 1.6 %collective-permute-start.10 = (bf16[4,1,64,256]{3,2,1,0:T(8,128)(2,1)S(1)}, bf16[4,1,64,256]{3,2,1,0:T(8,128)(2,1)S(1)}, u32[]{:S(2)}, u32[]{:S(2)}) collective-permute-start(bf16[4,1,64,256]{3,2,1,0:T(8,128)(2,1)S(1)} %get-tuple-element.82), channel_id=1, source_target_pairs={{0,2},{1,5},{2,0},{3,7},{4,6},{5,1},{6,4},{7,3},{8,10},{9,13},{10,... | collective-permute-start | bytes 393224 | tf_op jit(solution)/shard_map/ppermute | solution.py:412
  31.1 0.6 %collective-permute-done.12.refs_1_ = bf16[2,1,64,256]{3,2,1,0:T(8,128)(2,1)S(1)} collective-permute-done((bf16[2,1,64,256]{3,2,1,0:T(8,128)(2,1)S(1)}, bf16[2,1,64,256]{3,2,1,0:T(8,128)(2,1)S(1)}, u32[]{:S(2)}, u32[]{:S(2)}) %collective-permute-start.12) | collective-permute-done | bytes 65568 | tf_op jit(solution)/shard_map/ppermute | solution.py:412
  31.8 1.9 %collective-permute-done.11.refs_1_ = bf16[2,1,64,256]{3,2,1,0:T(8,128)(2,1)S(1)} collective-permute-done((bf16[2,1,64,256]{3,2,1,0:T(8,128)(2,1)S(1)}, bf16[2,1,64,256]{3,2,1,0:T(8,128)(2,1)S(1)}, u32[]{:S(2)}, u32[]{:S(2)}) %collective-permute-start.11) | collective-permute-done | bytes 65568 | tf_op jit(solution)/shard_map/ppermute | solution.py:412
  33.6 0.9 %collective-permute-done.10.came_ref = bf16[4,1,64,256]{3,2,1,0:T(8,128)(2,1)S(1)} collective-permute-done((bf16[4,1,64,256]{3,2,1,0:T(8,128)(2,1)S(1)}, bf16[4,1,64,256]{3,2,1,0:T(8,128)(2,1)S(1)}, u32[]{:S(2)}, u32[]{:S(2)}) %collective-permute-start.10) | collective-permute-done | bytes 131104 | tf_op jit(solution)/shard_map/ppermute | solution.py:412
  34.6 0.7 %shard_map.53 = f32[2,2,64,256]{3,2,1,0:T(8,128)} custom-call(bf16[4,1,64,256]{3,2,1,0:T(8,128)(2,1)S(1)} %collective-permute-done.10.came_ref, f32[2,1,64,256]{3,2,1,0:T(8,128)S(1)} %shard_map.51.refs_0_, f32[2,1,64,256]{3,2,1,0:T(8,128)S(1)} %shard_map.52.refs_1_), custom_call_target="tpu_custom_call" | custom-call | tf_op jit(solution)/shard_map/pallas_call | solution.py:19
  (7 shorter events, 0.1 us)
Async XLA Ops:
  0.0 9.4 %collective-permute-start.2 = (bf16[2,8,16,3,2,256]{5,4,3,2,1,0:T(2,128)(2,1)}, bf16[2,8,16,3,2,256]{5,4,3,2,1,0:T(2,128)(2,1)S(1)}, u32[]{:S(2)}, u32[]{:S(2)}) collective-permute-start(bf16[2,8,16,3,2,256]{5,4,3,2,1,0:T(2,128)(2,1)} %bitcast.10), channel_id=1, source_target_pairs={{1,0},{0,1},{3,2},{2,3},{5,4},{4,5},{7,6},{6,7},{9,8},{8,9},{11,10... | collective-permute-start | bytes 2359304 | tf_op jit(solution)/shard_map/ppermute | solution.py:14
  1.8 10.1 %collective-permute-start.1 = (bf16[2,19,3,2,256]{4,3,2,1,0:T(2,128)(2,1)S(1)}, bf16[2,19,3,2,256]{4,3,2,1,0:T(2,128)(2,1)S(1)}, u32[]{:S(2)}, u32[]{:S(2)}) collective-permute-start(bf16[2,19,3,2,256]{4,3,2,1,0:T(2,128)(2,1)S(1)} %get-tuple-element.52), channel_id=1, source_target_pairs={{12,0},{0,4},{4,8},{8,12},{13,1},{1,5},{5,9},{9,13},{14,2},{2,6},{... | collective-permute-start | bytes 350216 | tf_op jit(solution)/shard_map/ppermute | solution.py:14
  4.4 7.4 %collective-permute-start = (bf16[2,16,3,2,256]{4,3,2,1,0:T(2,128)(2,1)S(1)}, bf16[2,16,3,2,256]{4,3,2,1,0:T(2,128)(2,1)S(1)}, u32[]{:S(2)}, u32[]{:S(2)}) collective-permute-start(bf16[2,16,3,2,256]{4,3,2,1,0:T(2,128)(2,1)S(1)} %get-tuple-element.51), channel_id=1, source_target_pairs={{4,0},{8,4},{12,8},{0,12},{5,1},{9,5},{13,9},{1,13},{6,2},{10,6},{... | collective-permute-start | bytes 294920 | tf_op jit(solution)/shard_map/ppermute | solution.py:14
  7.3 6.8 %collective-permute-start.4 = (bf16[8,32,256]{2,1,0:T(8,128)(2,1)S(1)}, bf16[8,32,256]{2,1,0:T(8,128)(2,1)S(1)}, u32[]{:S(2)}, u32[]{:S(2)}) collective-permute-start(bf16[8,32,256]{2,1,0:T(8,128)(2,1)S(1)} %get-tuple-element.62), channel_id=1, source_target_pairs={{2,0},{0,2},{3,1},{1,3},{6,4},{4,6},{7,5},{5,7},{10,8},{8,10},{11,... | collective-permute-start | bytes 393224 | tf_op jit(solution)/shard_map/ppermute | solution.py:14
  12.9 6.8 %collective-permute-start.3 = (bf16[2,2,2,64,256]{4,3,2,1,0:T(8,128)(2,1)S(1)}, bf16[2,2,2,64,256]{4,3,2,1,0:T(8,128)(2,1)S(1)}, u32[]{:S(2)}, u32[]{:S(2)}) collective-permute-start(bf16[2,2,2,64,256]{4,3,2,1,0:T(8,128)(2,1)S(1)} %get-tuple-element.60), channel_id=1, source_target_pairs={{0,4},{1,3},{2,6},{3,1},{4,0},{5,7},{6,2},{7,5},{8,12},{9,11},{10,... | collective-permute-start | bytes 786440 | tf_op jit(solution)/shard_map/ppermute | solution.py:412
  14.1 1.4 %collective-permute-start.5 = (bf16[8,24,256]{2,1,0:T(8,128)(2,1)S(1)}, bf16[8,24,256]{2,1,0:T(8,128)(2,1)S(1)}, u32[]{:S(2)}, u32[]{:S(2)}) collective-permute-start(bf16[8,24,256]{2,1,0:T(8,128)(2,1)S(1)} %slice.3), channel_id=1, source_target_pairs={{1,0},{0,1},{3,2},{2,3},{5,4},{4,5},{7,6},{6,7},{9,8},{8,9},{11,10... | collective-permute-start | bytes 294920 | tf_op jit(solution)/shard_map/ppermute | solution.py:14
  17.6 5.7 %collective-permute-start.7 = (bf16[2,2,64,256]{3,2,1,0:T(8,128)(2,1)S(1)}, bf16[2,2,64,256]{3,2,1,0:T(8,128)(2,1)S(1)}, u32[]{:S(2)}, u32[]{:S(2)}) collective-permute-start(bf16[2,2,64,256]{3,2,1,0:T(8,128)(2,1)S(1)} %get-tuple-element.71), channel_id=1, source_target_pairs={{0,4},{1,3},{2,6},{3,1},{4,0},{5,7},{6,2},{7,5},{8,12},{9,11},{10,... | collective-permute-start | bytes 393224 | tf_op jit(solution)/shard_map/ppermute | solution.py:412
  18.5 10.9 %collective-permute-start.6 = (bf16[2,2,64,256]{3,2,1,0:T(8,128)(2,1)S(1)}, bf16[2,2,64,256]{3,2,1,0:T(8,128)(2,1)S(1)}, u32[]{:S(2)}, u32[]{:S(2)}) collective-permute-start(bf16[2,2,64,256]{3,2,1,0:T(8,128)(2,1)S(1)} %get-tuple-element.69), channel_id=1, source_target_pairs={{0,4},{1,3},{2,6},{3,1},{4,0},{5,7},{6,2},{7,5},{8,12},{9,11},{10,... | collective-permute-start | bytes 393224 | tf_op jit(solution)/shard_map/ppermute | solution.py:412
  19.7 5.2 %collective-permute-start.9 = (bf16[2,1,64,256]{3,2,1,0:T(8,128)(2,1)S(1)}, bf16[2,1,64,256]{3,2,1,0:T(8,128)(2,1)S(1)}, u32[]{:S(2)}, u32[]{:S(2)}) collective-permute-start(bf16[2,1,64,256]{3,2,1,0:T(8,128)(2,1)S(1)} %get-tuple-element.78), channel_id=1, source_target_pairs={{0,2},{1,5},{2,0},{3,7},{4,6},{5,1},{6,4},{7,3},{8,10},{9,13},{10,... | collective-permute-start | bytes 196616 | tf_op jit(solution)/shard_map/ppermute | solution.py:412
  23.3 4.3 %collective-permute-start.8 = (bf16[2,1,64,256]{3,2,1,0:T(8,128)(2,1)S(1)}, bf16[2,1,64,256]{3,2,1,0:T(8,128)(2,1)S(1)}, u32[]{:S(2)}, u32[]{:S(2)}) collective-permute-start(bf16[2,1,64,256]{3,2,1,0:T(8,128)(2,1)S(1)} %get-tuple-element.77), channel_id=1, source_target_pairs={{0,2},{1,5},{2,0},{3,7},{4,6},{5,1},{6,4},{7,3},{8,10},{9,13},{10,... | collective-permute-start | bytes 196616 | tf_op jit(solution)/shard_map/ppermute | solution.py:412
  24.9 6.8 %collective-permute-start.12 = (bf16[2,1,64,256]{3,2,1,0:T(8,128)(2,1)S(1)}, bf16[2,1,64,256]{3,2,1,0:T(8,128)(2,1)S(1)}, u32[]{:S(2)}, u32[]{:S(2)}) collective-permute-start(bf16[2,1,64,256]{3,2,1,0:T(8,128)(2,1)S(1)} %shard_map.48), channel_id=1, source_target_pairs={{0,8},{1,9},{2,10},{3,11},{4,12},{5,13},{6,14},{7,15},{8,0},{9,1},... | collective-permute-start | bytes 196616 | tf_op jit(solution)/shard_map/ppermute | solution.py:412
  27.7 5.9 %collective-permute-start.11 = (bf16[2,1,64,256]{3,2,1,0:T(8,128)(2,1)S(1)}, bf16[2,1,64,256]{3,2,1,0:T(8,128)(2,1)S(1)}, u32[]{:S(2)}, u32[]{:S(2)}) collective-permute-start(bf16[2,1,64,256]{3,2,1,0:T(8,128)(2,1)S(1)} %shard_map.49), channel_id=1, source_target_pairs={{0,8},{1,9},{2,10},{3,11},{4,12},{5,13},{6,14},{7,15},{8,0},{9,1},... | collective-permute-start | bytes 196616 | tf_op jit(solution)/shard_map/ppermute | solution.py:412
  29.6 5.0 %collective-permute-start.10 = (bf16[4,1,64,256]{3,2,1,0:T(8,128)(2,1)S(1)}, bf16[4,1,64,256]{3,2,1,0:T(8,128)(2,1)S(1)}, u32[]{:S(2)}, u32[]{:S(2)}) collective-permute-start(bf16[4,1,64,256]{3,2,1,0:T(8,128)(2,1)S(1)} %get-tuple-element.82), channel_id=1, source_target_pairs={{0,2},{1,5},{2,0},{3,7},{4,6},{5,1},{6,4},{7,3},{8,10},{9,13},{10,... | collective-permute-start | bytes 393224 | tf_op jit(solution)/shard_map/ppermute | solution.py:412

commit v6 on v5

--- a/solution.py
+++ b/solution.py
@@ -543,7 +543,7 @@
         [field, fields, near, far, ahead_y, back_y],
         [pltpu.VMEM((groups,) + field_shape.shape, bf16)],
     )
-    begun_second = call(begin_second_kernel, total_shape, project_flops, [lefts, right])
+    begun_second = call(begin_second_kernel, total_shape, 8 * project_flops, [lefts, right])
     sent_shape = shape(parts, pieces, rows, width)
     kept_second, own_second, sent_second, sent_own = call(
         second_kernel, (kept_shape, kept_shape, sent_shape, sent_shape), project_flops,

time: 35.5 us -> 33.6 us (0.946)
  waiting for transfers between devices: 9.02 us -> 7.62 us
  starting transfers between devices: 18.4 us -> 17.9 us
    ppermute x5, waiting for transfers between devices: 2.59 us -> 1.42 us  [shifted(): return lax.ppermute(block, axis, route)]
    ppermute x8, starting transfers between devices: 11.5 us -> 11 us  [exchange(): return lax.ppermute(block, axes, route)]
  transfers between devices with their start and end apart: 13 -> 13, of which waited for: 7 -> 9; matrix products, arithmetic and copies ran while one was open for 0% -> 0% of each run, Pallas kernels for 20% -> 21%
where the time goes in v6:
time: 33.6 us; the launch traced here: 33.4 us
  starting transfers between devices  17.9 us (53%)
  Pallas kernels  7.77 us (23%)
  waiting for transfers between devices  7.62 us (23%)
    ppermute x8, starting transfers between devices, exchange(): return lax.ppermute(block, axes, route)  11 us
    pallas_call x17, Pallas kernels, call(): pl.pallas_call(body, out_shape=out_shape, in_specs=[pl.BlockSpec(memory_s...  7.77 us
    ppermute x5, starting transfers between devices, shifted(): return lax.ppermute(block, axis, route)  6.9 us
    ppermute x8, waiting for transfers between devices, exchange(): return lax.ppermute(block, axes, route)  6.2 us
    ppermute x5, waiting for transfers between devices, shifted(): return lax.ppermute(block, axis, route)  1.42 us
  transfers between devices with their start and end apart: 13, of which 9 were waited for; matrix products, arithmetic and copies ran while one was open for 0% of the time, Pallas kernels for 21%

profile of v6, /device:TPU:0, one launch (start us, length us, event | category | flops | bytes accessed | tf_op | source)
XLA Modules:
  0.0 33.4 jit_solution(4063430525827003747)
XLA Ops:
  0.0 0.5 %collective-permute-start.2 = (bf16[2,8,16,3,2,256]{5,4,3,2,1,0:T(2,128)(2,1)}, bf16[2,8,16,3,2,256]{5,4,3,2,1,0:T(2,128)(2,1)S(1)}, u32[]{:S(2)}, u32[]{:S(2)}) collective-permute-start(bf16[2,8,16,3,2,256]{5,4,3,2,1,0:T(2,128)(2,1)} %bitcast.10), channel_id=1, source_target_pairs={{1,0},{0,1},{3,2},{2,3},{5,4},{4,5},{7,6},{6,7},{9,8},{8,9},{11,10... | collective-permute-start | bytes 2359304 | tf_op jit(solution)/shard_map/ppermute | solution.py:14
  0.5 1.4 %shard_map.37 = (bf16[2,16,3,2,256]{4,3,2,1,0:T(2,128)(2,1)S(1)}, bf16[2,19,3,2,256]{4,3,2,1,0:T(2,128)(2,1)S(1)}, bf16[2,8,16,3,2,256]{5,4,3,2,1,0:T(2,128)(2,1...) custom-call(bf16[2,8,16,3,2,256]{5,4,3,2,1,0:T(2,128)(2,1)} %bitcast, ...), custom_call_target="tpu_custom_call" | custom-call | tf_op jit(solution)/shard_map/pallas_call | solution.py:19
  1.8 2.6 %collective-permute-start.1 = (bf16[2,19,3,2,256]{4,3,2,1,0:T(2,128)(2,1)S(1)}, bf16[2,19,3,2,256]{4,3,2,1,0:T(2,128)(2,1)S(1)}, u32[]{:S(2)}, u32[]{:S(2)}) collective-permute-start(bf16[2,19,3,2,256]{4,3,2,1,0:T(2,128)(2,1)S(1)} %get-tuple-element.52), channel_id=1, source_target_pairs={{12,0},{0,4},{4,8},{8,12},{13,1},{1,5},{5,9},{9,13},{14,2},{2,6},{... | collective-permute-start | bytes 350216 | tf_op jit(solution)/shard_map/ppermute | solution.py:14
  4.4 2.1 %collective-permute-start = (bf16[2,16,3,2,256]{4,3,2,1,0:T(2,128)(2,1)S(1)}, bf16[2,16,3,2,256]{4,3,2,1,0:T(2,128)(2,1)S(1)}, u32[]{:S(2)}, u32[]{:S(2)}) collective-permute-start(bf16[2,16,3,2,256]{4,3,2,1,0:T(2,128)(2,1)S(1)} %get-tuple-element.51), channel_id=1, source_target_pairs={{4,0},{8,4},{12,8},{0,12},{5,1},{9,5},{13,9},{1,13},{6,2},{10,6},{... | collective-permute-start | bytes 294920 | tf_op jit(solution)/shard_map/ppermute | solution.py:14
  6.5 0.8 %shard_map.38 = (bf16[8,192,256]{2,1,0:T(8,128)(2,1)S(1)}, bf16[8,32,256]{2,1,0:T(8,128)(2,1)S(1)}, f32[8,8,256]{2,1,0:T(8,128)S(1)}, f32[8,8,256]{2,1,0:T(8,128...) custom-call(bf16[2,8,16,3,2,256]{5,4,3,2,1,0:T(2,128)(2,1)S(1)} %get-tuple-element.46.raw_ref, ...), custom_call_target="tpu_custom_call" | custom-call | tf_op jit(solution)/shard_map/pallas_call | solution.py:19
  7.3 1.7 %collective-permute-start.4 = (bf16[8,32,256]{2,1,0:T(8,128)(2,1)S(1)}, bf16[8,32,256]{2,1,0:T(8,128)(2,1)S(1)}, u32[]{:S(2)}, u32[]{:S(2)}) collective-permute-start(bf16[8,32,256]{2,1,0:T(8,128)(2,1)S(1)} %get-tuple-element.62), channel_id=1, source_target_pairs={{2,0},{0,2},{3,1},{1,3},{6,4},{4,6},{7,5},{5,7},{10,8},{8,10},{11,... | collective-permute-start | bytes 393224 | tf_op jit(solution)/shard_map/ppermute | solution.py:14
  8.9 0.5 %shard_map.39 = (bf16[1152,512]{1,0:T(8,128)(2,1)S(1)}, bf16[256,1536]{1,0:T(8,128)(2,1)S(1)}) custom-call(bf16[8,192,256]{2,1,0:T(8,128)(2,1)S(1)} %get-tuple-element.50.refs_0_, f32[8,8,256]{2,1,0:T(8,128)S(1)} %get-tuple-element.53.refs_1_.refs_3_, f32[8,8,256]{2,1,0:T(8,128)S(1)} %get-tuple-element.54.refs_2_.refs_4_), custom_call_target="tpu_custom_call" | custom-call | flops 150994944 | tf_op jit(solution)/shard_map/pallas_call | solution.py:19
  9.4 0.0 collective-permute-done.2.raw_ref
  9.4 0.3 shard_map.40
  9.7 0.8 %shard_map.41.refs_8_ = f32[2,256,512]{2,1,0:T(8,128)S(1)} custom-call(bf16[256,1536]{1,0:T(8,128)(2,1)S(1)} %get-tuple-element.56.own_ref.refs_6_, bf16[1,256,1536]{2,1,0:T(8,128)(2,1)S(1)} %bitcast.6, bf16[1152,512]{1,0:T(8,128)(2,1)S(1)} %get-tuple-element.58.right_ref), custom_call_target="tpu_custom_call" | custom-call | flops 402653184 | tf_op jit(solution)/shard_map/pallas_call | solution.py:19
  10.6 1.3 %collective-permute-done.refs_1_ = bf16[2,16,3,2,256]{4,3,2,1,0:T(2,128)(2,1)S(1)} collective-permute-done((bf16[2,16,3,2,256]{4,3,2,1,0:T(2,128)(2,1)S(1)}, bf16[2,16,3,2,256]{4,3,2,1,0:T(2,128)(2,1)S(1)}, u32[]{:S(2)}, u32[]{:S(2)}) %collective-permute-start) | collective-permute-done | bytes 98336 | tf_op jit(solution)/shard_map/ppermute | solution.py:14
  11.9 0.0 collective-permute-done.1.refs_2_
  11.9 1.0 %shard_map.42 = (f32[2,2,64,256]{3,2,1,0:T(8,128)S(1)}, f32[2,2,64,256]{3,2,1,0:T(8,128)S(1)}, bf16[2,2,2,64,256]{4,3,2,1,0:T(8,128)(2,1)S(1)}, bf16[384,512]{1,0:T(8,128)(2,1)S(1)}) custom-call(bf16[8,192,256]{2,1,0:T(8,128)(2,1)S(1)} %get-tuple-element.50.refs_0_, bf16[2,16,3,2,256]{4,3,2,1,0:T(2,128)(2,1)S(1)} %collective-permute-done.refs_1_, ...), custom_call_target="tpu_custom_call" | custom-call | flops 402653184 | tf_op jit(solution)/shard_map/pallas_call | solution.py:19
  12.9 0.0 collective-permute-done.4.refs_2_
  12.9 0.1 collective-permute-start.5
  13.0 1.2 %collective-permute-start.3 = (bf16[2,2,2,64,256]{4,3,2,1,0:T(8,128)(2,1)S(1)}, bf16[2,2,2,64,256]{4,3,2,1,0:T(8,128)(2,1)S(1)}, u32[]{:S(2)}, u32[]{:S(2)}) collective-permute-start(bf16[2,2,2,64,256]{4,3,2,1,0:T(8,128)(2,1)S(1)} %get-tuple-element.60), channel_id=1, source_target_pairs={{0,4},{1,3},{2,6},{3,1},{4,0},{5,7},{6,2},{7,5},{8,12},{9,11},{10,... | collective-permute-start | bytes 786440 | tf_op jit(solution)/shard_map/ppermute | solution.py:412
  14.2 0.1 collective-permute-done.5
  14.3 0.7 %shard_map.43.lefts_ref = bf16[2,256,1536]{2,1,0:T(8,128)(2,1)S(1)} custom-call(bf16[8,192,256]{2,1,0:T(8,128)(2,1)S(1)} %get-tuple-element.50.refs_0_, bf16[1,8,192,256]{3,2,1,0:T(8,128)(2,1)S(1)} %bitcast.8, bf16[8,32,256]{2,1,0:T(8,128)(2,1)S(1)} %collective-permute-done.4.refs_2_, bf16[1,8,24,256]{3,2,1,0:T(8,128)(2,1)S(1)} %bitcast.9, ...), custom_call_target="tpu_custom_call" | custom-call | flops 150994944 | tf_op jit(solution)/shard_map/pallas_call | solution.py:19
  15.0 0.8 %shard_map.44.begun_ref = f32[2,256,512]{2,1,0:T(8,128)S(1)} custom-call(bf16[2,256,1536]{2,1,0:T(8,128)(2,1)S(1)} %shard_map.43.lefts_ref, bf16[1152,512]{1,0:T(8,128)(2,1)S(1)} %get-tuple-element.58.right_ref), custom_call_target="tpu_custom_call" | custom-call | flops 3221225472 | tf_op jit(solution)/shard_map/pallas_call | solution.py:19
  15.8 0.6 %shard_map.45 = (f32[2,2,64,256]{3,2,1,0:T(8,128)S(1)}, f32[2,2,64,256]{3,2,1,0:T(8,128)S(1)}, bf16[2,2,64,256]{3,2,1,0:T(8,128)(2,1)S(1)}, bf16[2,2,64,256]{3,2,1,0:T(8,128)(2,1)S(1)}) custom-call(bf16[2,256,1536]{2,1,0:T(8,128)(2,1)S(1)} %shard_map.43.lefts_ref, bf16[384,512]{1,0:T(8,128)(2,1)S(1)} %get-tuple-element.67.right_ref, ...), custom_call_target="tpu_custom_call" | custom-call | flops 402653184 | tf_op jit(solution)/shard_map/pallas_call | solution.py:19
  16.4 1.2 %collective-permute-start.7 = (bf16[2,2,64,256]{3,2,1,0:T(8,128)(2,1)S(1)}, bf16[2,2,64,256]{3,2,1,0:T(8,128)(2,1)S(1)}, u32[]{:S(2)}, u32[]{:S(2)}) collective-permute-start(bf16[2,2,64,256]{3,2,1,0:T(8,128)(2,1)S(1)} %get-tuple-element.71), channel_id=1, source_target_pairs={{0,4},{1,3},{2,6},{3,1},{4,0},{5,7},{6,2},{7,5},{8,12},{9,11},{10,... | collective-permute-start | bytes 393224 | tf_op jit(solution)/shard_map/ppermute | solution.py:412
  17.6 0.9 %collective-permute-start.6 = (bf16[2,2,64,256]{3,2,1,0:T(8,128)(2,1)S(1)}, bf16[2,2,64,256]{3,2,1,0:T(8,128)(2,1)S(1)}, u32[]{:S(2)}, u32[]{:S(2)}) collective-permute-start(bf16[2,2,64,256]{3,2,1,0:T(8,128)(2,1)S(1)} %get-tuple-element.69), channel_id=1, source_target_pairs={{0,4},{1,3},{2,6},{3,1},{4,0},{5,7},{6,2},{7,5},{8,12},{9,11},{10,... | collective-permute-start | bytes 393224 | tf_op jit(solution)/shard_map/ppermute | solution.py:412
  18.5 0.9 %collective-permute-done.3.refs_1_ = bf16[2,2,2,64,256]{4,3,2,1,0:T(8,128)(2,1)S(1)} collective-permute-done((bf16[2,2,2,64,256]{4,3,2,1,0:T(8,128)(2,1)S(1)}, bf16[2,2,2,64,256]{4,3,2,1,0:T(8,128)(2,1)S(1)}, u32[]{:S(2)}, u32[]{:S(2)}) %collective-permute-start.3) | collective-permute-done | bytes 262176 | tf_op jit(solution)/shard_map/ppermute | solution.py:412
  19.5 1.6 %collective-permute-start.9 = (bf16[2,1,64,256]{3,2,1,0:T(8,128)(2,1)S(1)}, bf16[2,1,64,256]{3,2,1,0:T(8,128)(2,1)S(1)}, u32[]{:S(2)}, u32[]{:S(2)}) collective-permute-start(bf16[2,1,64,256]{3,2,1,0:T(8,128)(2,1)S(1)} %get-tuple-element.78), channel_id=1, source_target_pairs={{0,2},{1,5},{2,0},{3,7},{4,6},{5,1},{6,4},{7,3},{8,10},{9,13},{10,... | collective-permute-start | bytes 196616 | tf_op jit(solution)/shard_map/ppermute | solution.py:412
  21.1 0.4 %collective-permute-done.7.refs_1_ = bf16[2,2,64,256]{3,2,1,0:T(8,128)(2,1)S(1)} collective-permute-done((bf16[2,2,64,256]{3,2,1,0:T(8,128)(2,1)S(1)}, bf16[2,2,64,256]{3,2,1,0:T(8,128)(2,1)S(1)}, u32[]{:S(2)}, u32[]{:S(2)}) %collective-permute-start.7) | collective-permute-done | bytes 131104 | tf_op jit(solution)/shard_map/ppermute | solution.py:412
  21.5 1.6 %collective-permute-start.8 = (bf16[2,1,64,256]{3,2,1,0:T(8,128)(2,1)S(1)}, bf16[2,1,64,256]{3,2,1,0:T(8,128)(2,1)S(1)}, u32[]{:S(2)}, u32[]{:S(2)}) collective-permute-start(bf16[2,1,64,256]{3,2,1,0:T(8,128)(2,1)S(1)} %get-tuple-element.77), channel_id=1, source_target_pairs={{0,2},{1,5},{2,0},{3,7},{4,6},{5,1},{6,4},{7,3},{8,10},{9,13},{10,... | collective-permute-start | bytes 196616 | tf_op jit(solution)/shard_map/ppermute | solution.py:412
  23.1 0.8 %collective-permute-done.9.came_ref = bf16[2,1,64,256]{3,2,1,0:T(8,128)(2,1)S(1)} collective-permute-done((bf16[2,1,64,256]{3,2,1,0:T(8,128)(2,1)S(1)}, bf16[2,1,64,256]{3,2,1,0:T(8,128)(2,1)S(1)}, u32[]{:S(2)}, u32[]{:S(2)}) %collective-permute-start.9) | collective-permute-done | bytes 65568 | tf_op jit(solution)/shard_map/ppermute | solution.py:412
  23.9 1.3 %collective-permute-start.12 = (bf16[2,1,64,256]{3,2,1,0:T(8,128)(2,1)S(1)}, bf16[2,1,64,256]{3,2,1,0:T(8,128)(2,1)S(1)}, u32[]{:S(2)}, u32[]{:S(2)}) collective-permute-start(bf16[2,1,64,256]{3,2,1,0:T(8,128)(2,1)S(1)} %shard_map.48), channel_id=1, source_target_pairs={{0,8},{1,9},{2,10},{3,11},{4,12},{5,13},{6,14},{7,15},{8,0},{9,1},... | collective-permute-start | bytes 196616 | tf_op jit(solution)/shard_map/ppermute | solution.py:412
  25.2 0.6 %collective-permute-done.8.came_ref = bf16[2,1,64,256]{3,2,1,0:T(8,128)(2,1)S(1)} collective-permute-done((bf16[2,1,64,256]{3,2,1,0:T(8,128)(2,1)S(1)}, bf16[2,1,64,256]{3,2,1,0:T(8,128)(2,1)S(1)}, u32[]{:S(2)}, u32[]{:S(2)}) %collective-permute-start.8) | collective-permute-done | bytes 65568 | tf_op jit(solution)/shard_map/ppermute | solution.py:412
  25.9 1.7 %collective-permute-start.11 = (bf16[2,1,64,256]{3,2,1,0:T(8,128)(2,1)S(1)}, bf16[2,1,64,256]{3,2,1,0:T(8,128)(2,1)S(1)}, u32[]{:S(2)}, u32[]{:S(2)}) collective-permute-start(bf16[2,1,64,256]{3,2,1,0:T(8,128)(2,1)S(1)} %shard_map.49), channel_id=1, source_target_pairs={{0,8},{1,9},{2,10},{3,11},{4,12},{5,13},{6,14},{7,15},{8,0},{9,1},... | collective-permute-start | bytes 196616 | tf_op jit(solution)/shard_map/ppermute | solution.py:412
  27.6 0.0 collective-permute-done.6.refs_3_
  27.6 0.1 shard_map.50
  27.7 1.5 %collective-permute-start.10 = (bf16[4,1,64,256]{3,2,1,0:T(8,128)(2,1)S(1)}, bf16[4,1,64,256]{3,2,1,0:T(8,128)(2,1)S(1)}, u32[]{:S(2)}, u32[]{:S(2)}) collective-permute-start(bf16[4,1,64,256]{3,2,1,0:T(8,128)(2,1)S(1)} %get-tuple-element.82), channel_id=1, source_target_pairs={{0,2},{1,5},{2,0},{3,7},{4,6},{5,1},{6,4},{7,3},{8,10},{9,13},{10,... | collective-permute-start | bytes 393224 | tf_op jit(solution)/shard_map/ppermute | solution.py:412
  29.2 2.0 %collective-permute-done.12.refs_1_ = bf16[2,1,64,256]{3,2,1,0:T(8,128)(2,1)S(1)} collective-permute-done((bf16[2,1,64,256]{3,2,1,0:T(8,128)(2,1)S(1)}, bf16[2,1,64,256]{3,2,1,0:T(8,128)(2,1)S(1)}, u32[]{:S(2)}, u32[]{:S(2)}) %collective-permute-start.12) | collective-permute-done | bytes 65568 | tf_op jit(solution)/shard_map/ppermute | solution.py:412
  31.2 1.3 %collective-permute-done.11.refs_1_ = bf16[2,1,64,256]{3,2,1,0:T(8,128)(2,1)S(1)} collective-permute-done((bf16[2,1,64,256]{3,2,1,0:T(8,128)(2,1)S(1)}, bf16[2,1,64,256]{3,2,1,0:T(8,128)(2,1)S(1)}, u32[]{:S(2)}, u32[]{:S(2)}) %collective-permute-start.11) | collective-permute-done | bytes 65568 | tf_op jit(solution)/shard_map/ppermute | solution.py:412
  32.5 0.2 collective-permute-done.10.came_ref
  32.7 0.7 %shard_map.53 = f32[2,2,64,256]{3,2,1,0:T(8,128)} custom-call(bf16[4,1,64,256]{3,2,1,0:T(8,128)(2,1)S(1)} %collective-permute-done.10.came_ref, f32[2,1,64,256]{3,2,1,0:T(8,128)S(1)} %shard_map.51.refs_0_, f32[2,1,64,256]{3,2,1,0:T(8,128)S(1)} %shard_map.52.refs_1_), custom_call_target="tpu_custom_call" | custom-call | tf_op jit(solution)/shard_map/pallas_call | solution.py:19
  (7 shorter events, 0.1 us)
Async XLA Ops:
  0.0 9.4 %collective-permute-start.2 = (bf16[2,8,16,3,2,256]{5,4,3,2,1,0:T(2,128)(2,1)}, bf16[2,8,16,3,2,256]{5,4,3,2,1,0:T(2,128)(2,1)S(1)}, u32[]{:S(2)}, u32[]{:S(2)}) collective-permute-start(bf16[2,8,16,3,2,256]{5,4,3,2,1,0:T(2,128)(2,1)} %bitcast.10), channel_id=1, source_target_pairs={{1,0},{0,1},{3,2},{2,3},{5,4},{4,5},{7,6},{6,7},{9,8},{8,9},{11,10... | collective-permute-start | bytes 2359304 | tf_op jit(solution)/shard_map/ppermute | solution.py:14
  1.8 10.1 %collective-permute-start.1 = (bf16[2,19,3,2,256]{4,3,2,1,0:T(2,128)(2,1)S(1)}, bf16[2,19,3,2,256]{4,3,2,1,0:T(2,128)(2,1)S(1)}, u32[]{:S(2)}, u32[]{:S(2)}) collective-permute-start(bf16[2,19,3,2,256]{4,3,2,1,0:T(2,128)(2,1)S(1)} %get-tuple-element.52), channel_id=1, source_target_pairs={{12,0},{0,4},{4,8},{8,12},{13,1},{1,5},{5,9},{9,13},{14,2},{2,6},{... | collective-permute-start | bytes 350216 | tf_op jit(solution)/shard_map/ppermute | solution.py:14
  4.4 7.4 %collective-permute-start = (bf16[2,16,3,2,256]{4,3,2,1,0:T(2,128)(2,1)S(1)}, bf16[2,16,3,2,256]{4,3,2,1,0:T(2,128)(2,1)S(1)}, u32[]{:S(2)}, u32[]{:S(2)}) collective-permute-start(bf16[2,16,3,2,256]{4,3,2,1,0:T(2,128)(2,1)S(1)} %get-tuple-element.51), channel_id=1, source_target_pairs={{4,0},{8,4},{12,8},{0,12},{5,1},{9,5},{13,9},{1,13},{6,2},{10,6},{... | collective-permute-start | bytes 294920 | tf_op jit(solution)/shard_map/ppermute | solution.py:14
  7.3 5.6 %collective-permute-start.4 = (bf16[8,32,256]{2,1,0:T(8,128)(2,1)S(1)}, bf16[8,32,256]{2,1,0:T(8,128)(2,1)S(1)}, u32[]{:S(2)}, u32[]{:S(2)}) collective-permute-start(bf16[8,32,256]{2,1,0:T(8,128)(2,1)S(1)} %get-tuple-element.62), channel_id=1, source_target_pairs={{2,0},{0,2},{3,1},{1,3},{6,4},{4,6},{7,5},{5,7},{10,8},{8,10},{11,... | collective-permute-start | bytes 393224 | tf_op jit(solution)/shard_map/ppermute | solution.py:14
  12.9 1.4 %collective-permute-start.5 = (bf16[8,24,256]{2,1,0:T(8,128)(2,1)S(1)}, bf16[8,24,256]{2,1,0:T(8,128)(2,1)S(1)}, u32[]{:S(2)}, u32[]{:S(2)}) collective-permute-start(bf16[8,24,256]{2,1,0:T(8,128)(2,1)S(1)} %slice.3), channel_id=1, source_target_pairs={{1,0},{0,1},{3,2},{2,3},{5,4},{4,5},{7,6},{6,7},{9,8},{8,9},{11,10... | collective-permute-start | bytes 294920 | tf_op jit(solution)/shard_map/ppermute | solution.py:14
  13.0 6.4 %collective-permute-start.3 = (bf16[2,2,2,64,256]{4,3,2,1,0:T(8,128)(2,1)S(1)}, bf16[2,2,2,64,256]{4,3,2,1,0:T(8,128)(2,1)S(1)}, u32[]{:S(2)}, u32[]{:S(2)}) collective-permute-start(bf16[2,2,2,64,256]{4,3,2,1,0:T(8,128)(2,1)S(1)} %get-tuple-element.60), channel_id=1, source_target_pairs={{0,4},{1,3},{2,6},{3,1},{4,0},{5,7},{6,2},{7,5},{8,12},{9,11},{10,... | collective-permute-start | bytes 786440 | tf_op jit(solution)/shard_map/ppermute | solution.py:412
  16.4 5.0 %collective-permute-start.7 = (bf16[2,2,64,256]{3,2,1,0:T(8,128)(2,1)S(1)}, bf16[2,2,64,256]{3,2,1,0:T(8,128)(2,1)S(1)}, u32[]{:S(2)}, u32[]{:S(2)}) collective-permute-start(bf16[2,2,64,256]{3,2,1,0:T(8,128)(2,1)S(1)} %get-tuple-element.71), channel_id=1, source_target_pairs={{0,4},{1,3},{2,6},{3,1},{4,0},{5,7},{6,2},{7,5},{8,12},{9,11},{10,... | collective-permute-start | bytes 393224 | tf_op jit(solution)/shard_map/ppermute | solution.py:412
  17.6 10.0 %collective-permute-start.6 = (bf16[2,2,64,256]{3,2,1,0:T(8,128)(2,1)S(1)}, bf16[2,2,64,256]{3,2,1,0:T(8,128)(2,1)S(1)}, u32[]{:S(2)}, u32[]{:S(2)}) collective-permute-start(bf16[2,2,64,256]{3,2,1,0:T(8,128)(2,1)S(1)} %get-tuple-element.69), channel_id=1, source_target_pairs={{0,4},{1,3},{2,6},{3,1},{4,0},{5,7},{6,2},{7,5},{8,12},{9,11},{10,... | collective-permute-start | bytes 393224 | tf_op jit(solution)/shard_map/ppermute | solution.py:412
  19.5 4.3 %collective-permute-start.9 = (bf16[2,1,64,256]{3,2,1,0:T(8,128)(2,1)S(1)}, bf16[2,1,64,256]{3,2,1,0:T(8,128)(2,1)S(1)}, u32[]{:S(2)}, u32[]{:S(2)}) collective-permute-start(bf16[2,1,64,256]{3,2,1,0:T(8,128)(2,1)S(1)} %get-tuple-element.78), channel_id=1, source_target_pairs={{0,2},{1,5},{2,0},{3,7},{4,6},{5,1},{6,4},{7,3},{8,10},{9,13},{10,... | collective-permute-start | bytes 196616 | tf_op jit(solution)/shard_map/ppermute | solution.py:412
  21.5 4.3 %collective-permute-start.8 = (bf16[2,1,64,256]{3,2,1,0:T(8,128)(2,1)S(1)}, bf16[2,1,64,256]{3,2,1,0:T(8,128)(2,1)S(1)}, u32[]{:S(2)}, u32[]{:S(2)}) collective-permute-start(bf16[2,1,64,256]{3,2,1,0:T(8,128)(2,1)S(1)} %get-tuple-element.77), channel_id=1, source_target_pairs={{0,2},{1,5},{2,0},{3,7},{4,6},{5,1},{6,4},{7,3},{8,10},{9,13},{10,... | collective-permute-start | bytes 196616 | tf_op jit(solution)/shard_map/ppermute | solution.py:412
  23.9 7.4 %collective-permute-start.12 = (bf16[2,1,64,256]{3,2,1,0:T(8,128)(2,1)S(1)}, bf16[2,1,64,256]{3,2,1,0:T(8,128)(2,1)S(1)}, u32[]{:S(2)}, u32[]{:S(2)}) collective-permute-start(bf16[2,1,64,256]{3,2,1,0:T(8,128)(2,1)S(1)} %shard_map.48), channel_id=1, source_target_pairs={{0,8},{1,9},{2,10},{3,11},{4,12},{5,13},{6,14},{7,15},{8,0},{9,1},... | collective-permute-start | bytes 196616 | tf_op jit(solution)/shard_map/ppermute | solution.py:412
  25.9 6.7 %collective-permute-start.11 = (bf16[2,1,64,256]{3,2,1,0:T(8,128)(2,1)S(1)}, bf16[2,1,64,256]{3,2,1,0:T(8,128)(2,1)S(1)}, u32[]{:S(2)}, u32[]{:S(2)}) collective-permute-start(bf16[2,1,64,256]{3,2,1,0:T(8,128)(2,1)S(1)} %shard_map.49), channel_id=1, source_target_pairs={{0,8},{1,9},{2,10},{3,11},{4,12},{5,13},{6,14},{7,15},{8,0},{9,1},... | collective-permute-start | bytes 196616 | tf_op jit(solution)/shard_map/ppermute | solution.py:412
  27.7 5.0 %collective-permute-start.10 = (bf16[4,1,64,256]{3,2,1,0:T(8,128)(2,1)S(1)}, bf16[4,1,64,256]{3,2,1,0:T(8,128)(2,1)S(1)}, u32[]{:S(2)}, u32[]{:S(2)}) collective-permute-start(bf16[4,1,64,256]{3,2,1,0:T(8,128)(2,1)S(1)} %get-tuple-element.82), channel_id=1, source_target_pairs={{0,2},{1,5},{2,0},{3,7},{4,6},{5,1},{6,4},{7,3},{8,10},{9,13},{10,... | collective-permute-start | bytes 393224 | tf_op jit(solution)/shard_map/ppermute | solution.py:412

commit v7 on v6

--- a/solution.py
+++ b/solution.py
@@ -234,7 +234,9 @@
     right_ref[start + half : start + depth, width:] = -real
 
 
-def inner_kernel(sites, rows_ref, ahead_ref, back_ref, right_ref, turned_ref):
+def inner_kernel(
+    sites, rows_ref, ahead_ref, back_ref, right_ref, turned_ref, matrix_ref, ahead_part_ref, back_part_ref
+):
     planes, depth, width = rows_ref.shape
     same = same_site(sites, depth)
     for x in range(1, planes - 1):
@@ -243,6 +245,11 @@
         moved = move_plane(same, depth // sites, ahead_ref[x], back_ref[x - 1], above, below)
         set_right(right_ref, place_of(x, planes), moved)
     turned_ref[...] = rows_ref[...].reshape(planes * depth, width).T
+    x, count = planes - 1, depth // sites
+    matrix_ref[...] = site_matrix([(ahead_ref[x, :, :depth], same)], count)
+    ahead_part_ref[...] = dot(site_matrix([(ahead_ref[0, :, :depth], same)], count), rows_ref[place_of(1, planes)])
+    below = rows_ref[place_of(x - 1, planes)]
+    back_part_ref[...] = dot(site_matrix([(back_ref[x - 1, :, :depth], same)], count), below)
 
 
 def begin_first_kernel(own_ref, others_ref, right_ref, total_ref):
@@ -327,13 +334,12 @@
 
 
 def first_kernel(
-    sites, rows_ref, high_ref, low_ref, ahead_ref, back_ref, past_maps_ref, own_ref, others_ref, begun_ref,
+    sites, planes, high_ref, low_ref, matrix_ref, ahead_part_ref, back_part_ref, past_maps_ref, own_ref, others_ref, begun_ref,
     *refs,
 ):
     *refs, right_ref, total_ref = refs
-    planes, depth, _ = rows_ref.shape
+    depth = matrix_ref.shape[0]
     same = same_site(sites, depth)
-    count = depth // sites
     _, ys, colours, zs, _ = high_ref.shape
     links = low_ref[:, ys:, :, :, :ys].reshape(-1, ys)
     lanes = past_maps_ref.shape[1] // 2
@@ -344,13 +350,11 @@
     choose = past_maps_ref[start : start + 16, :count].astype(jnp.bfloat16)
     past = dot(choose, (dot(links, spread) * match).astype(jnp.bfloat16))
     past = jnp.where(past_maps_ref[start + 16 : start + 17, :lanes] > 0.5, past[:8], past[8:])
-    count = depth // sites
-    above = rows_ref[place_of(1, planes)]
-    set_right(right_ref, 0, move_plane(same, count, ahead_ref[0], past, above, plane_rows(low_ref, ys)))
-    x = planes - 1
-    below = rows_ref[place_of(x - 1, planes)]
-    moved = move_plane(same, count, ahead_ref[x], back_ref[x - 1], plane_rows(high_ref, ys), below)
-    set_right(right_ref, 1, moved)
+    past = site_matrix([(past[:, :depth], same)], depth // sites)
+    moved = ahead_part_ref[...] + dot(past, plane_rows(low_ref, ys))
+    set_right(right_ref, 0, moved.astype(jnp.bfloat16))
+    moved = dot(matrix_ref[...], plane_rows(high_ref, ys)) + back_part_ref[...]
+    set_right(right_ref, 1, moved.astype(jnp.bfloat16))
     inner = (planes - 2) * depth
     lefts = [own_ref[:, inner:]] + [others_ref[k, :, inner:] for k in range(others_ref.shape[0])]
     terms = [dot(left, right_ref[...]) for left in lefts]
@@ -358,36 +362,41 @@
     project(terms, begun_ref, (keep_other, keep_own), (send_ref.at[0], send_ref.at[1]), total_ref)
 
 
-def move_y_kernel(
-    sites, zs, rows_ref, others_ref, near_ref, far_ref, ahead_ref, back_ref, turned_ref, field_ref
-):
-    planes, depth, width = rows_ref.shape
-    groups = others_ref.shape[0] + 1
+def begin_y_kernel(sites, zs, rows_ref, others_ref, ahead_ref, back_ref, part_ref):
+    planes, depth, _ = rows_ref.shape
+    site, lane = iotas((sites, depth))
+    to_next = jnp.where(lane % sites == site + zs, -1.0, 0.0)
+    to_last = jnp.where(lane % sites == site - zs, -1.0, 0.0)
+    for x in range(planes):
+        ahead, back = ahead_ref[x, :, :depth], back_ref[x, :, :depth]
+        matrix = site_matrix([(ahead, to_next), (back, to_last)], depth // sites)
+        place = place_of(x, planes)
+        part_ref[0, place] = dot(matrix, rows_ref[place])
+        for k in range(others_ref.shape[0]):
+            part_ref[k + 1, place] = dot(matrix, others_ref[k, place])
+
+
+def move_y_kernel(sites, zs, part_ref, near_ref, far_ref, ahead_ref, turned_ref, field_ref):
+    groups, planes, depth, width = part_ref.shape
     row_size = depth // sites * zs
-    reach = depth + near_ref.shape[1]
-    head = back_ref.shape[2] - 128
-    site, lane = iotas((sites, reach))
-    inner = lane < depth
+    tail = 128
+    head = ahead_ref.shape[2] - tail
+    site, lane = iotas((sites, tail))
+    lane = lane + head
     upper = (lane >= depth) & (lane < depth + row_size)
     lower = (lane >= depth + row_size) & (lane < depth + 2 * row_size)
-    lane_z = lane % zs
-    to_next = (inner & (lane % sites == site + zs)) | (upper & (site == sites - zs + lane_z))
-    to_last = (inner & (lane % sites == site - zs)) | (lower & (site == lane_z))
-    to_next = jnp.where(to_next, -1.0, 0.0)
-    to_last = jnp.where(to_last, -1.0, 0.0)
-    _, lane = iotas((8, 128))
-    spare = jnp.zeros((near_ref.shape[1] - far_ref.shape[2], width), far_ref.dtype)
+    to_next = jnp.where(upper & (site == sites - zs + lane % zs), -1.0, 0.0)
+    to_last = jnp.where(lower & (site == lane % zs), -1.0, 0.0)
+    above = jnp.zeros((depth - head, width), jnp.bfloat16)
+    below = jnp.zeros((tail - 2 * row_size - (depth - head), width), jnp.bfloat16)
     for x in range(planes):
-        past = near_ref[x, 2 * row_size : 2 * row_size + 8, :128].astype(jnp.float32)
-        mixed = jnp.where(lane >= depth + row_size - head, past, back_ref[x, :, head:])
-        back = jnp.concatenate([back_ref[x, :, :head], mixed], axis=1)[:, :reach]
-        matrix = site_matrix([(ahead_ref[x, :, :reach], to_next), (back, to_last)], depth // sites)
+        past = near_ref[x, 2 * row_size : 2 * row_size + 8, :tail].astype(jnp.float32)
+        matrix = site_matrix([(ahead_ref[x, :, head:], to_next), (past, to_last)], depth // sites)
         place = place_of(x, planes)
-        column = jnp.concatenate([rows_ref[place], near_ref[x]], axis=0)
-        field_ref[0, place] = dot(matrix, column).astype(jnp.bfloat16)
-        for k in range(groups - 1):
-            column = jnp.concatenate([others_ref[k, place], far_ref[k, x], spare], axis=0)
-            field_ref[k + 1, place] = dot(matrix, column).astype(jnp.bfloat16)
+        for k in range(groups):
+            edge = near_ref[x, : 2 * row_size] if k == 0 else far_ref[k - 1, x]
+            moved = part_ref[k, place] + dot(matrix, jnp.concatenate([above, edge, below], axis=0))
+            field_ref[k, place] = moved.astype(jnp.bfloat16)
     for k in range(groups):
         turned_ref[k] = field_ref[k].reshape(planes * depth, width).T
 
@@ -516,23 +525,36 @@
         inner_kernel(sites, *refs)
 
     def first(*refs):
-        first_kernel(sites, *refs)
+        first_kernel(sites, planes, *refs)
+
+    def begin_y(*refs):
+        begin_y_kernel(sites, zs, *refs)
 
     def move_y(*refs):
         move_y_kernel(sites, zs, *refs)
 
-    right, own = call(
-        inner, (shape(inner_depth, parts * width), turned_shape), 2 * step_flops, [field, ahead_x, back_x]
+    right, own, matrix, ahead_part, back_part = call(
+        inner,
+        (
+            shape(inner_depth, parts * width), turned_shape, shape(depth, depth),
+            shape(depth, width, dtype=f32), shape(depth, width, dtype=f32),
+        ),
+        2 * step_flops,
+        [field, ahead_x, back_x],
     )
     turned = [call(turn_kernel, (field_shape, turned_shape), step_flops // 4, [r]) for r in raw_others]
     fields = jnp.stack([t[0] for t in turned])
     others = jnp.stack([t[1] for t in turned])
     begun_first = call(begin_first_kernel, total_shape, project_flops, [own, others, right])
+    part_y = call(
+        begin_y, shape(groups, planes, depth, width, dtype=f32), 2 * step_flops, [field, fields, ahead_y, back_y]
+    )
+    part_y, begun_first = lax.optimization_barrier((part_y, begun_first))
     kept_first, own_first, sent_first, right_edge = call(
         first,
         (kept_shape, kept_shape, shape(2, parts, pieces, rows, width), shape(2 * depth, parts * width)),
         project_flops,
-        [field, high, low, ahead_x, back_x, past_maps, own, others, begun_first],
+        [high, low, matrix, ahead_part, back_part, past_maps, own, others, begun_first],
         [total],
     )
     near, right_edge = lax.optimization_barrier((near, right_edge))
@@ -540,7 +562,7 @@
     far = jnp.stack([shifted(near_rows, "ma", -step) for step in range(1, groups)])
     lefts = call(
         move_y, shape(groups, width, planes * depth), 2 * step_flops,
-        [field, fields, near, far, ahead_y, back_y],
+        [part_y, near, far, ahead_y],
         [pltpu.VMEM((groups,) + field_shape.shape, bf16)],
     )
     begun_second = call(begin_second_kernel, total_shape, 8 * project_flops, [lefts, right])

time: 33.6 us -> 33.5 us (level)
  Pallas kernels: 7.77 us -> 8.28 us
  waiting for transfers between devices: 7.62 us -> 7.17 us
    ppermute x5, waiting for transfers between devices: 1.42 us -> 0.91 us  [shifted(): return lax.ppermute(block, axis, route)]
    pallas_call x17 -> x18, Pallas kernels: 7.77 us -> 8.28 us  [call(): pl.pallas_call(body, out_shape=out_shape, in_specs=[pl.BlockSpec(memory_s...]
  transfers between devices with their start and end apart: 13 -> 13, of which waited for: 9 -> 10; matrix products, arithmetic and copies ran while one was open for 0% -> 0% of each run, Pallas kernels for 21% -> 23%
where the time goes in v7:
time: 33.5 us; the launch traced here: 33.3 us
  starting transfers between devices  17.7 us (53%)
  Pallas kernels  8.28 us (25%)
  waiting for transfers between devices  7.17 us (21%)
    ppermute x8, starting transfers between devices, exchange(): return lax.ppermute(block, axes, route)  10.8 us
    pallas_call x18, Pallas kernels, call(): pl.pallas_call(body, out_shape=out_shape, in_specs=[pl.BlockSpec(memory_s...  8.28 us
    ppermute x5, starting transfers between devices, shifted(): return lax.ppermute(block, axis, route)  6.9 us
    ppermute x8, waiting for transfers between devices, exchange(): return lax.ppermute(block, axes, route)  6.26 us
    ppermute x5, waiting for transfers between devices, shifted(): return lax.ppermute(block, axis, route)  0.91 us
  transfers between devices with their start and end apart: 13, of which 10 were waited for; matrix products, arithmetic and copies ran while one was open for 0% of the time, Pallas kernels for 23%

profile of v7, /device:TPU:0, one launch (start us, length us, event | category | flops | bytes accessed | tf_op | source)
XLA Modules:
  0.0 33.3 jit_solution(10102009775170459292)
XLA Ops:
  0.0 0.5 %collective-permute-start.2 = (bf16[2,8,16,3,2,256]{5,4,3,2,1,0:T(2,128)(2,1)}, bf16[2,8,16,3,2,256]{5,4,3,2,1,0:T(2,128)(2,1)S(1)}, u32[]{:S(2)}, u32[]{:S(2)}) collective-permute-start(bf16[2,8,16,3,2,256]{5,4,3,2,1,0:T(2,128)(2,1)} %bitcast.10), channel_id=1, source_target_pairs={{1,0},{0,1},{3,2},{2,3},{5,4},{4,5},{7,6},{6,7},{9,8},{8,9},{11,10... | collective-permute-start | bytes 2359304 | tf_op jit(solution)/shard_map/ppermute | solution.py:14
  0.5 1.4 %shard_map.37 = (bf16[2,16,3,2,256]{4,3,2,1,0:T(2,128)(2,1)S(1)}, bf16[2,19,3,2,256]{4,3,2,1,0:T(2,128)(2,1)S(1)}, bf16[2,8,16,3,2,256]{5,4,3,2,1,0:T(2,128)(2,1...) custom-call(bf16[2,8,16,3,2,256]{5,4,3,2,1,0:T(2,128)(2,1)} %bitcast, ...), custom_call_target="tpu_custom_call" | custom-call | tf_op jit(solution)/shard_map/pallas_call | solution.py:19
  1.8 2.6 %collective-permute-start.1 = (bf16[2,19,3,2,256]{4,3,2,1,0:T(2,128)(2,1)S(1)}, bf16[2,19,3,2,256]{4,3,2,1,0:T(2,128)(2,1)S(1)}, u32[]{:S(2)}, u32[]{:S(2)}) collective-permute-start(bf16[2,19,3,2,256]{4,3,2,1,0:T(2,128)(2,1)S(1)} %get-tuple-element.52), channel_id=1, source_target_pairs={{12,0},{0,4},{4,8},{8,12},{13,1},{1,5},{5,9},{9,13},{14,2},{2,6},{... | collective-permute-start | bytes 350216 | tf_op jit(solution)/shard_map/ppermute | solution.py:14
  4.4 2.1 %collective-permute-start = (bf16[2,16,3,2,256]{4,3,2,1,0:T(2,128)(2,1)S(1)}, bf16[2,16,3,2,256]{4,3,2,1,0:T(2,128)(2,1)S(1)}, u32[]{:S(2)}, u32[]{:S(2)}) collective-permute-start(bf16[2,16,3,2,256]{4,3,2,1,0:T(2,128)(2,1)S(1)} %get-tuple-element.51), channel_id=1, source_target_pairs={{4,0},{8,4},{12,8},{0,12},{5,1},{9,5},{13,9},{1,13},{6,2},{10,6},{... | collective-permute-start | bytes 294920 | tf_op jit(solution)/shard_map/ppermute | solution.py:14
  6.5 0.7 %shard_map.38 = (bf16[8,192,256]{2,1,0:T(8,128)(2,1)S(1)}, bf16[8,32,256]{2,1,0:T(8,128)(2,1)S(1)}, f32[8,8,256]{2,1,0:T(8,128)S(1)}, f32[8,8,256]{2,1,0:T(8,128...) custom-call(bf16[2,8,16,3,2,256]{5,4,3,2,1,0:T(2,128)(2,1)S(1)} %get-tuple-element.53.raw_ref, ...), custom_call_target="tpu_custom_call" | custom-call | tf_op jit(solution)/shard_map/pallas_call | solution.py:19
  7.3 1.7 %collective-permute-start.4 = (bf16[8,32,256]{2,1,0:T(8,128)(2,1)S(1)}, bf16[8,32,256]{2,1,0:T(8,128)(2,1)S(1)}, u32[]{:S(2)}, u32[]{:S(2)}) collective-permute-start(bf16[8,32,256]{2,1,0:T(8,128)(2,1)S(1)} %get-tuple-element.74), channel_id=1, source_target_pairs={{2,0},{0,2},{3,1},{1,3},{6,4},{4,6},{7,5},{5,7},{10,8},{8,10},{11,... | collective-permute-start | bytes 393224 | tf_op jit(solution)/shard_map/ppermute | solution.py:14
  8.9 0.5 %shard_map.39 = (bf16[1152,512]{1,0:T(8,128)(2,1)S(1)}, bf16[256,1536]{1,0:T(8,128)(2,1)S(1)}, bf16[192,192]{1,0:T(8,128)(2,1)S(1)}, f32[192,256]{1,0:T(8,128)S(1)}, f32[192,256]{1,0:T(8,128)S(1)}) custom-call(bf16[8,192,256]{2,1,0:T(8,128)(2,1)S(1)} %get-tuple-element.57.refs_0_, f32[8,8,256]{2,1,0:T(8,128)S(1)} %get-tuple-element.58.refs_1_, ...), custom_call_target="tpu_custom_call" | custom-call | flops 150994944 | tf_op jit(solution)/shard_map/pallas_call | solution.py:19
  9.5 0.0 collective-permute-done.2.raw_ref
  9.5 0.3 shard_map.40
  9.8 0.6 %shard_map.41.refs_0_ = f32[2,8,192,256]{3,2,1,0:T(8,128)S(1)} custom-call(bf16[8,192,256]{2,1,0:T(8,128)(2,1)S(1)} %get-tuple-element.57.refs_0_, bf16[1,8,192,256]{3,2,1,0:T(8,128)(2,1)S(1)} %bitcast.8, f32[8,8,256]{2,1,0:T(8,128)S(1)} %get-tuple-element.67.refs_2_.refs_3_, f32[8,8,256]{2,1,0:T(8,128)S(1)} %get-tuple-element.68.refs_3_), custom_call_target="tpu_custom_call" | custom-call | flops 150994944 | tf_op jit(solution)/shard_map/pallas_call | solution.py:19
  10.4 0.8 %shard_map.42.refs_8_ = f32[2,256,512]{2,1,0:T(8,128)S(1)} custom-call(bf16[256,1536]{1,0:T(8,128)(2,1)S(1)} %get-tuple-element.64.own_ref.refs_6_, bf16[1,256,1536]{2,1,0:T(8,128)(2,1)S(1)} %bitcast.6, bf16[1152,512]{1,0:T(8,128)(2,1)S(1)} %get-tuple-element.69.right_ref), custom_call_target="tpu_custom_call" | custom-call | flops 402653184 | tf_op jit(solution)/shard_map/pallas_call | solution.py:19
  11.2 0.7 %collective-permute-done.refs_0_ = bf16[2,16,3,2,256]{4,3,2,1,0:T(2,128)(2,1)S(1)} collective-permute-done((bf16[2,16,3,2,256]{4,3,2,1,0:T(2,128)(2,1)S(1)}, bf16[2,16,3,2,256]{4,3,2,1,0:T(2,128)(2,1)S(1)}, u32[]{:S(2)}, u32[]{:S(2)}) %collective-permute-start) | collective-permute-done | bytes 98336 | tf_op jit(solution)/shard_map/ppermute | solution.py:14
  11.9 0.0 collective-permute-done.1.refs_1_
  11.9 1.0 %shard_map.43 = (f32[2,2,64,256]{3,2,1,0:T(8,128)S(1)}, f32[2,2,64,256]{3,2,1,0:T(8,128)S(1)}, bf16[2,2,2,64,256]{4,3,2,1,0:T(8,128)(2,1)S(1)}, bf16[384,512]{1,0:T(8,128)(2,1)S(1)}) custom-call(bf16[2,16,3,2,256]{4,3,2,1,0:T(2,128)(2,1)S(1)} %collective-permute-done.refs_0_, bf16[2,19,3,2,256]{4,3,2,1,0:T(2,128)(2,1)S(1)} %collective-permute-done.1.refs_1_, ...), custom_call_target="tpu_custom_call" | custom-call | flops 402653184 | tf_op jit(solution)/shard_map/pallas_call | solution.py:19
  12.9 0.1 collective-permute-done.4.refs_1_
  12.9 0.1 collective-permute-start.5
  13.0 1.1 %collective-permute-start.3 = (bf16[2,2,2,64,256]{4,3,2,1,0:T(8,128)(2,1)S(1)}, bf16[2,2,2,64,256]{4,3,2,1,0:T(8,128)(2,1)S(1)}, u32[]{:S(2)}, u32[]{:S(2)}) collective-permute-start(bf16[2,2,2,64,256]{4,3,2,1,0:T(8,128)(2,1)S(1)} %get-tuple-element.72), channel_id=1, source_target_pairs={{0,4},{1,3},{2,6},{3,1},{4,0},{5,7},{6,2},{7,5},{8,12},{9,11},{10,... | collective-permute-start | bytes 786440 | tf_op jit(solution)/shard_map/ppermute | solution.py:421
  14.2 0.2 collective-permute-done.5
  14.3 0.6 %shard_map.44.lefts_ref = bf16[2,256,1536]{2,1,0:T(8,128)(2,1)S(1)} custom-call(f32[2,8,192,256]{3,2,1,0:T(8,128)S(1)} %shard_map.41.refs_0_, bf16[8,32,256]{2,1,0:T(8,128)(2,1)S(1)} %collective-permute-done.4.refs_1_, bf16[1,8,24,256]{3,2,1,0:T(8,128)(2,1)S(1)} %bitcast.9, f32[8,8,256]{2,1,0:T(8,128)S(1)} %get-tuple-element.67.refs_2_.refs_3_), custom_call_target="tpu_custom_call" | custom-call | flops 150994944 | tf_op jit(solution)/shard_map/pallas_call | solution.py:19
  15.0 0.8 %shard_map.45.begun_ref = f32[2,256,512]{2,1,0:T(8,128)S(1)} custom-call(bf16[2,256,1536]{2,1,0:T(8,128)(2,1)S(1)} %shard_map.44.lefts_ref, bf16[1152,512]{1,0:T(8,128)(2,1)S(1)} %get-tuple-element.69.right_ref), custom_call_target="tpu_custom_call" | custom-call | flops 3221225472 | tf_op jit(solution)/shard_map/pallas_call | solution.py:19
  15.8 0.6 %shard_map.46 = (f32[2,2,64,256]{3,2,1,0:T(8,128)S(1)}, f32[2,2,64,256]{3,2,1,0:T(8,128)S(1)}, bf16[2,2,64,256]{3,2,1,0:T(8,128)(2,1)S(1)}, bf16[2,2,64,256]{3,2,1,0:T(8,128)(2,1)S(1)}) custom-call(bf16[2,256,1536]{2,1,0:T(8,128)(2,1)S(1)} %shard_map.44.lefts_ref, bf16[384,512]{1,0:T(8,128)(2,1)S(1)} %get-tuple-element.77.right_ref, ...), custom_call_target="tpu_custom_call" | custom-call | flops 402653184 | tf_op jit(solution)/shard_map/pallas_call | solution.py:19
  16.4 1.1 %collective-permute-start.7 = (bf16[2,2,64,256]{3,2,1,0:T(8,128)(2,1)S(1)}, bf16[2,2,64,256]{3,2,1,0:T(8,128)(2,1)S(1)}, u32[]{:S(2)}, u32[]{:S(2)}) collective-permute-start(bf16[2,2,64,256]{3,2,1,0:T(8,128)(2,1)S(1)} %get-tuple-element.81), channel_id=1, source_target_pairs={{0,4},{1,3},{2,6},{3,1},{4,0},{5,7},{6,2},{7,5},{8,12},{9,11},{10,... | collective-permute-start | bytes 393224 | tf_op jit(solution)/shard_map/ppermute | solution.py:421
  17.5 1.0 %collective-permute-start.6 = (bf16[2,2,64,256]{3,2,1,0:T(8,128)(2,1)S(1)}, bf16[2,2,64,256]{3,2,1,0:T(8,128)(2,1)S(1)}, u32[]{:S(2)}, u32[]{:S(2)}) collective-permute-start(bf16[2,2,64,256]{3,2,1,0:T(8,128)(2,1)S(1)} %get-tuple-element.79), channel_id=1, source_target_pairs={{0,4},{1,3},{2,6},{3,1},{4,0},{5,7},{6,2},{7,5},{8,12},{9,11},{10,... | collective-permute-start | bytes 393224 | tf_op jit(solution)/shard_map/ppermute | solution.py:421
  18.5 1.0 %collective-permute-done.3.refs_1_ = bf16[2,2,2,64,256]{4,3,2,1,0:T(8,128)(2,1)S(1)} collective-permute-done((bf16[2,2,2,64,256]{4,3,2,1,0:T(8,128)(2,1)S(1)}, bf16[2,2,2,64,256]{4,3,2,1,0:T(8,128)(2,1)S(1)}, u32[]{:S(2)}, u32[]{:S(2)}) %collective-permute-start.3) | collective-permute-done | bytes 262176 | tf_op jit(solution)/shard_map/ppermute | solution.py:421
  19.5 1.6 %collective-permute-start.9 = (bf16[2,1,64,256]{3,2,1,0:T(8,128)(2,1)S(1)}, bf16[2,1,64,256]{3,2,1,0:T(8,128)(2,1)S(1)}, u32[]{:S(2)}, u32[]{:S(2)}) collective-permute-start(bf16[2,1,64,256]{3,2,1,0:T(8,128)(2,1)S(1)} %get-tuple-element.88), channel_id=1, source_target_pairs={{0,2},{1,5},{2,0},{3,7},{4,6},{5,1},{6,4},{7,3},{8,10},{9,13},{10,... | collective-permute-start | bytes 196616 | tf_op jit(solution)/shard_map/ppermute | solution.py:421
  21.1 0.4 %collective-permute-done.7.refs_1_ = bf16[2,2,64,256]{3,2,1,0:T(8,128)(2,1)S(1)} collective-permute-done((bf16[2,2,64,256]{3,2,1,0:T(8,128)(2,1)S(1)}, bf16[2,2,64,256]{3,2,1,0:T(8,128)(2,1)S(1)}, u32[]{:S(2)}, u32[]{:S(2)}) %collective-permute-start.7) | collective-permute-done | bytes 131104 | tf_op jit(solution)/shard_map/ppermute | solution.py:421
  21.5 1.6 %collective-permute-start.8 = (bf16[2,1,64,256]{3,2,1,0:T(8,128)(2,1)S(1)}, bf16[2,1,64,256]{3,2,1,0:T(8,128)(2,1)S(1)}, u32[]{:S(2)}, u32[]{:S(2)}) collective-permute-start(bf16[2,1,64,256]{3,2,1,0:T(8,128)(2,1)S(1)} %get-tuple-element.87), channel_id=1, source_target_pairs={{0,2},{1,5},{2,0},{3,7},{4,6},{5,1},{6,4},{7,3},{8,10},{9,13},{10,... | collective-permute-start | bytes 196616 | tf_op jit(solution)/shard_map/ppermute | solution.py:421
  23.0 0.8 %collective-permute-done.9.came_ref = bf16[2,1,64,256]{3,2,1,0:T(8,128)(2,1)S(1)} collective-permute-done((bf16[2,1,64,256]{3,2,1,0:T(8,128)(2,1)S(1)}, bf16[2,1,64,256]{3,2,1,0:T(8,128)(2,1)S(1)}, u32[]{:S(2)}, u32[]{:S(2)}) %collective-permute-start.9) | collective-permute-done | bytes 65568 | tf_op jit(solution)/shard_map/ppermute | solution.py:421
  23.8 1.3 %collective-permute-start.12 = (bf16[2,1,64,256]{3,2,1,0:T(8,128)(2,1)S(1)}, bf16[2,1,64,256]{3,2,1,0:T(8,128)(2,1)S(1)}, u32[]{:S(2)}, u32[]{:S(2)}) collective-permute-start(bf16[2,1,64,256]{3,2,1,0:T(8,128)(2,1)S(1)} %shard_map.49), channel_id=1, source_target_pairs={{0,8},{1,9},{2,10},{3,11},{4,12},{5,13},{6,14},{7,15},{8,0},{9,1},... | collective-permute-start | bytes 196616 | tf_op jit(solution)/shard_map/ppermute | solution.py:421
  25.1 0.7 %collective-permute-done.8.came_ref = bf16[2,1,64,256]{3,2,1,0:T(8,128)(2,1)S(1)} collective-permute-done((bf16[2,1,64,256]{3,2,1,0:T(8,128)(2,1)S(1)}, bf16[2,1,64,256]{3,2,1,0:T(8,128)(2,1)S(1)}, u32[]{:S(2)}, u32[]{:S(2)}) %collective-permute-start.8) | collective-permute-done | bytes 65568 | tf_op jit(solution)/shard_map/ppermute | solution.py:421
  25.8 1.7 %collective-permute-start.11 = (bf16[2,1,64,256]{3,2,1,0:T(8,128)(2,1)S(1)}, bf16[2,1,64,256]{3,2,1,0:T(8,128)(2,1)S(1)}, u32[]{:S(2)}, u32[]{:S(2)}) collective-permute-start(bf16[2,1,64,256]{3,2,1,0:T(8,128)(2,1)S(1)} %shard_map.50), channel_id=1, source_target_pairs={{0,8},{1,9},{2,10},{3,11},{4,12},{5,13},{6,14},{7,15},{8,0},{9,1},... | collective-permute-start | bytes 196616 | tf_op jit(solution)/shard_map/ppermute | solution.py:421
  27.5 0.0 collective-permute-done.6.refs_3_
  27.5 0.1 shard_map.51
  27.6 1.5 %collective-permute-start.10 = (bf16[4,1,64,256]{3,2,1,0:T(8,128)(2,1)S(1)}, bf16[4,1,64,256]{3,2,1,0:T(8,128)(2,1)S(1)}, u32[]{:S(2)}, u32[]{:S(2)}) collective-permute-start(bf16[4,1,64,256]{3,2,1,0:T(8,128)(2,1)S(1)} %get-tuple-element.92), channel_id=1, source_target_pairs={{0,2},{1,5},{2,0},{3,7},{4,6},{5,1},{6,4},{7,3},{8,10},{9,13},{10,... | collective-permute-start | bytes 393224 | tf_op jit(solution)/shard_map/ppermute | solution.py:421
  29.1 2.2 %collective-permute-done.12.refs_1_ = bf16[2,1,64,256]{3,2,1,0:T(8,128)(2,1)S(1)} collective-permute-done((bf16[2,1,64,256]{3,2,1,0:T(8,128)(2,1)S(1)}, bf16[2,1,64,256]{3,2,1,0:T(8,128)(2,1)S(1)}, u32[]{:S(2)}, u32[]{:S(2)}) %collective-permute-start.12) | collective-permute-done | bytes 65568 | tf_op jit(solution)/shard_map/ppermute | solution.py:421
  31.3 1.2 %collective-permute-done.11.refs_1_ = bf16[2,1,64,256]{3,2,1,0:T(8,128)(2,1)S(1)} collective-permute-done((bf16[2,1,64,256]{3,2,1,0:T(8,128)(2,1)S(1)}, bf16[2,1,64,256]{3,2,1,0:T(8,128)(2,1)S(1)}, u32[]{:S(2)}, u32[]{:S(2)}) %collective-permute-start.11) | collective-permute-done | bytes 65568 | tf_op jit(solution)/shard_map/ppermute | solution.py:421
  32.5 0.1 collective-permute-done.10.came_ref
  32.6 0.7 %shard_map.54 = f32[2,2,64,256]{3,2,1,0:T(8,128)} custom-call(bf16[4,1,64,256]{3,2,1,0:T(8,128)(2,1)S(1)} %collective-permute-done.10.came_ref, f32[2,1,64,256]{3,2,1,0:T(8,128)S(1)} %shard_map.52.refs_0_, f32[2,1,64,256]{3,2,1,0:T(8,128)S(1)} %shard_map.53.refs_1_), custom_call_target="tpu_custom_call" | custom-call | tf_op jit(solution)/shard_map/pallas_call | solution.py:19
  (7 shorter events, 0.1 us)
Async XLA Ops:
  0.0 9.5 %collective-permute-start.2 = (bf16[2,8,16,3,2,256]{5,4,3,2,1,0:T(2,128)(2,1)}, bf16[2,8,16,3,2,256]{5,4,3,2,1,0:T(2,128)(2,1)S(1)}, u32[]{:S(2)}, u32[]{:S(2)}) collective-permute-start(bf16[2,8,16,3,2,256]{5,4,3,2,1,0:T(2,128)(2,1)} %bitcast.10), channel_id=1, source_target_pairs={{1,0},{0,1},{3,2},{2,3},{5,4},{4,5},{7,6},{6,7},{9,8},{8,9},{11,10... | collective-permute-start | bytes 2359304 | tf_op jit(solution)/shard_map/ppermute | solution.py:14
  1.8 10.1 %collective-permute-start.1 = (bf16[2,19,3,2,256]{4,3,2,1,0:T(2,128)(2,1)S(1)}, bf16[2,19,3,2,256]{4,3,2,1,0:T(2,128)(2,1)S(1)}, u32[]{:S(2)}, u32[]{:S(2)}) collective-permute-start(bf16[2,19,3,2,256]{4,3,2,1,0:T(2,128)(2,1)S(1)} %get-tuple-element.52), channel_id=1, source_target_pairs={{12,0},{0,4},{4,8},{8,12},{13,1},{1,5},{5,9},{9,13},{14,2},{2,6},{... | collective-permute-start | bytes 350216 | tf_op jit(solution)/shard_map/ppermute | solution.py:14
  4.4 7.4 %collective-permute-start = (bf16[2,16,3,2,256]{4,3,2,1,0:T(2,128)(2,1)S(1)}, bf16[2,16,3,2,256]{4,3,2,1,0:T(2,128)(2,1)S(1)}, u32[]{:S(2)}, u32[]{:S(2)}) collective-permute-start(bf16[2,16,3,2,256]{4,3,2,1,0:T(2,128)(2,1)S(1)} %get-tuple-element.51), channel_id=1, source_target_pairs={{4,0},{8,4},{12,8},{0,12},{5,1},{9,5},{13,9},{1,13},{6,2},{10,6},{... | collective-permute-start | bytes 294920 | tf_op jit(solution)/shard_map/ppermute | solution.py:14
  7.3 5.6 %collective-permute-start.4 = (bf16[8,32,256]{2,1,0:T(8,128)(2,1)S(1)}, bf16[8,32,256]{2,1,0:T(8,128)(2,1)S(1)}, u32[]{:S(2)}, u32[]{:S(2)}) collective-permute-start(bf16[8,32,256]{2,1,0:T(8,128)(2,1)S(1)} %get-tuple-element.74), channel_id=1, source_target_pairs={{2,0},{0,2},{3,1},{1,3},{6,4},{4,6},{7,5},{5,7},{10,8},{8,10},{11,... | collective-permute-start | bytes 393224 | tf_op jit(solution)/shard_map/ppermute | solution.py:14
  12.9 1.4 %collective-permute-start.5 = (bf16[8,24,256]{2,1,0:T(8,128)(2,1)S(1)}, bf16[8,24,256]{2,1,0:T(8,128)(2,1)S(1)}, u32[]{:S(2)}, u32[]{:S(2)}) collective-permute-start(bf16[8,24,256]{2,1,0:T(8,128)(2,1)S(1)} %slice.3), channel_id=1, source_target_pairs={{1,0},{0,1},{3,2},{2,3},{5,4},{4,5},{7,6},{6,7},{9,8},{8,9},{11,10... | collective-permute-start | bytes 294920 | tf_op jit(solution)/shard_map/ppermute | solution.py:14
  13.0 6.4 %collective-permute-start.3 = (bf16[2,2,2,64,256]{4,3,2,1,0:T(8,128)(2,1)S(1)}, bf16[2,2,2,64,256]{4,3,2,1,0:T(8,128)(2,1)S(1)}, u32[]{:S(2)}, u32[]{:S(2)}) collective-permute-start(bf16[2,2,2,64,256]{4,3,2,1,0:T(8,128)(2,1)S(1)} %get-tuple-element.72), channel_id=1, source_target_pairs={{0,4},{1,3},{2,6},{3,1},{4,0},{5,7},{6,2},{7,5},{8,12},{9,11},{10,... | collective-permute-start | bytes 786440 | tf_op jit(solution)/shard_map/ppermute | solution.py:421
  16.4 5.0 %collective-permute-start.7 = (bf16[2,2,64,256]{3,2,1,0:T(8,128)(2,1)S(1)}, bf16[2,2,64,256]{3,2,1,0:T(8,128)(2,1)S(1)}, u32[]{:S(2)}, u32[]{:S(2)}) collective-permute-start(bf16[2,2,64,256]{3,2,1,0:T(8,128)(2,1)S(1)} %get-tuple-element.81), channel_id=1, source_target_pairs={{0,4},{1,3},{2,6},{3,1},{4,0},{5,7},{6,2},{7,5},{8,12},{9,11},{10,... | collective-permute-start | bytes 393224 | tf_op jit(solution)/shard_map/ppermute | solution.py:421
  17.5 9.9 %collective-permute-start.6 = (bf16[2,2,64,256]{3,2,1,0:T(8,128)(2,1)S(1)}, bf16[2,2,64,256]{3,2,1,0:T(8,128)(2,1)S(1)}, u32[]{:S(2)}, u32[]{:S(2)}) collective-permute-start(bf16[2,2,64,256]{3,2,1,0:T(8,128)(2,1)S(1)} %get-tuple-element.79), channel_id=1, source_target_pairs={{0,4},{1,3},{2,6},{3,1},{4,0},{5,7},{6,2},{7,5},{8,12},{9,11},{10,... | collective-permute-start | bytes 393224 | tf_op jit(solution)/shard_map/ppermute | solution.py:421
  19.5 4.3 %collective-permute-start.9 = (bf16[2,1,64,256]{3,2,1,0:T(8,128)(2,1)S(1)}, bf16[2,1,64,256]{3,2,1,0:T(8,128)(2,1)S(1)}, u32[]{:S(2)}, u32[]{:S(2)}) collective-permute-start(bf16[2,1,64,256]{3,2,1,0:T(8,128)(2,1)S(1)} %get-tuple-element.88), channel_id=1, source_target_pairs={{0,2},{1,5},{2,0},{3,7},{4,6},{5,1},{6,4},{7,3},{8,10},{9,13},{10,... | collective-permute-start | bytes 196616 | tf_op jit(solution)/shard_map/ppermute | solution.py:421
  21.5 4.3 %collective-permute-start.8 = (bf16[2,1,64,256]{3,2,1,0:T(8,128)(2,1)S(1)}, bf16[2,1,64,256]{3,2,1,0:T(8,128)(2,1)S(1)}, u32[]{:S(2)}, u32[]{:S(2)}) collective-permute-start(bf16[2,1,64,256]{3,2,1,0:T(8,128)(2,1)S(1)} %get-tuple-element.87), channel_id=1, source_target_pairs={{0,2},{1,5},{2,0},{3,7},{4,6},{5,1},{6,4},{7,3},{8,10},{9,13},{10,... | collective-permute-start | bytes 196616 | tf_op jit(solution)/shard_map/ppermute | solution.py:421
  23.8 7.4 %collective-permute-start.12 = (bf16[2,1,64,256]{3,2,1,0:T(8,128)(2,1)S(1)}, bf16[2,1,64,256]{3,2,1,0:T(8,128)(2,1)S(1)}, u32[]{:S(2)}, u32[]{:S(2)}) collective-permute-start(bf16[2,1,64,256]{3,2,1,0:T(8,128)(2,1)S(1)} %shard_map.49), channel_id=1, source_target_pairs={{0,8},{1,9},{2,10},{3,11},{4,12},{5,13},{6,14},{7,15},{8,0},{9,1},... | collective-permute-start | bytes 196616 | tf_op jit(solution)/shard_map/ppermute | solution.py:421
  25.8 6.7 %collective-permute-start.11 = (bf16[2,1,64,256]{3,2,1,0:T(8,128)(2,1)S(1)}, bf16[2,1,64,256]{3,2,1,0:T(8,128)(2,1)S(1)}, u32[]{:S(2)}, u32[]{:S(2)}) collective-permute-start(bf16[2,1,64,256]{3,2,1,0:T(8,128)(2,1)S(1)} %shard_map.50), channel_id=1, source_target_pairs={{0,8},{1,9},{2,10},{3,11},{4,12},{5,13},{6,14},{7,15},{8,0},{9,1},... | collective-permute-start | bytes 196616 | tf_op jit(solution)/shard_map/ppermute | solution.py:421
  27.6 5.0 %collective-permute-start.10 = (bf16[4,1,64,256]{3,2,1,0:T(8,128)(2,1)S(1)}, bf16[4,1,64,256]{3,2,1,0:T(8,128)(2,1)S(1)}, u32[]{:S(2)}, u32[]{:S(2)}) collective-permute-start(bf16[4,1,64,256]{3,2,1,0:T(8,128)(2,1)S(1)} %get-tuple-element.92), channel_id=1, source_target_pairs={{0,2},{1,5},{2,0},{3,7},{4,6},{5,1},{6,4},{7,3},{8,10},{9,13},{10,... | collective-permute-start | bytes 393224 | tf_op jit(solution)/shard_map/ppermute | solution.py:421

commit v8 on v7

--- a/solution.py
+++ b/solution.py
@@ -289,48 +289,37 @@
 
 
 def project(terms, begun_ref, keep_refs, send_refs, total_ref):
+    groups, blocks, rows, _ = total_ref.shape
+    parts, count, _, width = keep_refs[0].shape
     for k, term in enumerate(terms):
-        total_ref[k] = begun_ref[k] + term
-    groups, own_modes, _ = total_ref.shape
+        total_ref[k] = (begun_ref[k] + term).reshape(blocks, rows, parts * width)
     my_modes = lax.axis_index("ma")
     odd_core = my_bit("ma", 0)
     top = my_bit("gx", bits("gx")[-1])
     across_x, across_y = lax.axis_size("gx"), lax.axis_size("gy")
-    parts, count, rows, width = keep_refs[0].shape
     plan = steps()
     mine = my_side(plan[0])
 
-    def piece(gx, gy):
-        start = (gx * across_y + gy) * rows
-        group = lax.rem(start // own_modes + groups - my_modes, groups)
-        begin = start % own_modes
-        return total_ref[group, begin : begin + rows]
+    def at(side, index):
+        owners = []
+        for core in range(2):
+            place = {"gx": 0, "gy": 0}
+            for k, step in enumerate(plan):
+                axis, bit = step[core]
+                digit = side if k == 0 else index >> (len(plan) - 1 - k) & 1
+                place[axis] += digit * (1 << bit)
+            owners.append(place["gx"] * across_y + place["gy"])
+        return jnp.where(odd_core == 0, owners[0], owners[1])
 
     for kind in range(2):
         half = lax.bitwise_xor(top, 1 - kind)
-
-        def chosen(gx, gy):
-            return jnp.where(half == 0, piece(gx, gy), piece(gx + across_x // 2, gy))
-
-        def at(index):
-            places = []
-            for core in range(2):
-                place = {"gx": 0, "gy": 0}
-                for k, step in enumerate(plan):
-                    axis, bit = step[core]
-                    place[axis] |= (index >> (len(plan) - 1 - k) & 1) << bit
-                places.append((place["gx"], place["gy"]))
-            if places[0] == places[1]:
-                return chosen(*places[0])
-            return jnp.where(odd_core == 0, chosen(*places[0]), chosen(*places[1]))
-
         for index in range(count):
-            low, high = at(index), at(index + count)
-            keep = jnp.where(mine == 0, low, high)
-            send = jnp.where(mine == 0, high, low).astype(jnp.bfloat16)
-            for p in range(parts):
-                keep_refs[kind][p, index] = keep[:, p * width : (p + 1) * width]
-                send_refs[kind][p, index] = send[:, p * width : (p + 1) * width]
+            for ref, side in ((keep_refs[kind], mine), (send_refs[kind], 1 - mine)):
+                owner = half * (across_x // 2 * across_y) + at(side, index)
+                group = lax.rem(lax.div(owner, blocks) + groups - my_modes, groups)
+                block = total_ref[group, lax.rem(owner, blocks)].astype(ref.dtype)
+                for p in range(parts):
+                    ref[p, index] = block[:, p * width : (p + 1) * width]
 
 
 def first_kernel(
@@ -483,7 +472,7 @@
     turned_shape = shape(width, planes * depth)
     total_shape = shape(groups, width, parts * width, dtype=f32)
     link_shape = shape(planes, 8, lanes, dtype=f32)
-    total = pltpu.VMEM(total_shape.shape, f32)
+    total = pltpu.VMEM((groups, width // rows, rows, parts * width), f32)
     step_flops = 2 * planes * depth * depth * width
     project_flops = 2 * groups * width * planes * depth * parts * width
 

time: 33.5 us -> 33.4 us (level)
  transfers between devices with their start and end apart: 13 -> 13, of which waited for: 10 -> 9; matrix products, arithmetic and copies ran while one was open for 0% -> 0% of each run, Pallas kernels for 23% -> 22%
where the time goes in v8:
time: 33.4 us; the launch traced here: 33.3 us
  starting transfers between devices  17.5 us (52%)
  Pallas kernels  8.13 us (24%)
  waiting for transfers between devices  7.48 us (22%)
    ppermute x8, starting transfers between devices, exchange(): return lax.ppermute(block, axes, route)  10.6 us
    pallas_call x18, Pallas kernels, call(): pl.pallas_call(body, out_shape=out_shape, in_specs=[pl.BlockSpec(memory_s...  8.13 us
    ppermute x5, starting transfers between devices, shifted(): return lax.ppermute(block, axis, route)  6.9 us
    ppermute x8, waiting for transfers between devices, exchange(): return lax.ppermute(block, axes, route)  6.43 us
    ppermute x5, waiting for transfers between devices, shifted(): return lax.ppermute(block, axis, route)  1.05 us
  transfers between devices with their start and end apart: 13, of which 9 were waited for; matrix products, arithmetic and copies ran while one was open for 0% of the time, Pallas kernels for 22%

profile of v8, /device:TPU:0, one launch (start us, length us, event | category | flops | bytes accessed | tf_op | source)
XLA Modules:
  0.0 33.3 jit_solution(17961225904636006099)
XLA Ops:
  0.0 0.5 %collective-permute-start.2 = (bf16[2,8,16,3,2,256]{5,4,3,2,1,0:T(2,128)(2,1)}, bf16[2,8,16,3,2,256]{5,4,3,2,1,0:T(2,128)(2,1)S(1)}, u32[]{:S(2)}, u32[]{:S(2)}) collective-permute-start(bf16[2,8,16,3,2,256]{5,4,3,2,1,0:T(2,128)(2,1)} %bitcast.10), channel_id=1, source_target_pairs={{1,0},{0,1},{3,2},{2,3},{5,4},{4,5},{7,6},{6,7},{9,8},{8,9},{11,10... | collective-permute-start | bytes 2359304 | tf_op jit(solution)/shard_map/ppermute | solution.py:14
  0.5 1.4 %shard_map.37 = (bf16[2,16,3,2,256]{4,3,2,1,0:T(2,128)(2,1)S(1)}, bf16[2,19,3,2,256]{4,3,2,1,0:T(2,128)(2,1)S(1)}, bf16[2,8,16,3,2,256]{5,4,3,2,1,0:T(2,128)(2,1...) custom-call(bf16[2,8,16,3,2,256]{5,4,3,2,1,0:T(2,128)(2,1)} %bitcast, ...), custom_call_target="tpu_custom_call" | custom-call | tf_op jit(solution)/shard_map/pallas_call | solution.py:19
  1.8 2.6 %collective-permute-start.1 = (bf16[2,19,3,2,256]{4,3,2,1,0:T(2,128)(2,1)S(1)}, bf16[2,19,3,2,256]{4,3,2,1,0:T(2,128)(2,1)S(1)}, u32[]{:S(2)}, u32[]{:S(2)}) collective-permute-start(bf16[2,19,3,2,256]{4,3,2,1,0:T(2,128)(2,1)S(1)} %get-tuple-element.52), channel_id=1, source_target_pairs={{12,0},{0,4},{4,8},{8,12},{13,1},{1,5},{5,9},{9,13},{14,2},{2,6},{... | collective-permute-start | bytes 350216 | tf_op jit(solution)/shard_map/ppermute | solution.py:14
  4.4 2.1 %collective-permute-start = (bf16[2,16,3,2,256]{4,3,2,1,0:T(2,128)(2,1)S(1)}, bf16[2,16,3,2,256]{4,3,2,1,0:T(2,128)(2,1)S(1)}, u32[]{:S(2)}, u32[]{:S(2)}) collective-permute-start(bf16[2,16,3,2,256]{4,3,2,1,0:T(2,128)(2,1)S(1)} %get-tuple-element.51), channel_id=1, source_target_pairs={{4,0},{8,4},{12,8},{0,12},{5,1},{9,5},{13,9},{1,13},{6,2},{10,6},{... | collective-permute-start | bytes 294920 | tf_op jit(solution)/shard_map/ppermute | solution.py:14
  6.5 0.7 %shard_map.38 = (bf16[8,192,256]{2,1,0:T(8,128)(2,1)S(1)}, bf16[8,32,256]{2,1,0:T(8,128)(2,1)S(1)}, f32[8,8,256]{2,1,0:T(8,128)S(1)}, f32[8,8,256]{2,1,0:T(8,128...) custom-call(bf16[2,8,16,3,2,256]{5,4,3,2,1,0:T(2,128)(2,1)S(1)} %get-tuple-element.53.raw_ref, ...), custom_call_target="tpu_custom_call" | custom-call | tf_op jit(solution)/shard_map/pallas_call | solution.py:19
  7.3 1.7 %collective-permute-start.4 = (bf16[8,32,256]{2,1,0:T(8,128)(2,1)S(1)}, bf16[8,32,256]{2,1,0:T(8,128)(2,1)S(1)}, u32[]{:S(2)}, u32[]{:S(2)}) collective-permute-start(bf16[8,32,256]{2,1,0:T(8,128)(2,1)S(1)} %get-tuple-element.74), channel_id=1, source_target_pairs={{2,0},{0,2},{3,1},{1,3},{6,4},{4,6},{7,5},{5,7},{10,8},{8,10},{11,... | collective-permute-start | bytes 393224 | tf_op jit(solution)/shard_map/ppermute | solution.py:14
  8.9 0.5 %shard_map.39 = (bf16[1152,512]{1,0:T(8,128)(2,1)S(1)}, bf16[256,1536]{1,0:T(8,128)(2,1)S(1)}, bf16[192,192]{1,0:T(8,128)(2,1)S(1)}, f32[192,256]{1,0:T(8,128)S(1)}, f32[192,256]{1,0:T(8,128)S(1)}) custom-call(bf16[8,192,256]{2,1,0:T(8,128)(2,1)S(1)} %get-tuple-element.57.refs_0_, f32[8,8,256]{2,1,0:T(8,128)S(1)} %get-tuple-element.58.refs_1_, ...), custom_call_target="tpu_custom_call" | custom-call | flops 150994944 | tf_op jit(solution)/shard_map/pallas_call | solution.py:19
  9.5 0.0 collective-permute-done.2.raw_ref
  9.5 0.3 shard_map.40
  9.8 0.6 %shard_map.41.refs_0_ = f32[2,8,192,256]{3,2,1,0:T(8,128)S(1)} custom-call(bf16[8,192,256]{2,1,0:T(8,128)(2,1)S(1)} %get-tuple-element.57.refs_0_, bf16[1,8,192,256]{3,2,1,0:T(8,128)(2,1)S(1)} %bitcast.8, f32[8,8,256]{2,1,0:T(8,128)S(1)} %get-tuple-element.67.refs_2_.refs_3_, f32[8,8,256]{2,1,0:T(8,128)S(1)} %get-tuple-element.68.refs_3_), custom_call_target="tpu_custom_call" | custom-call | flops 150994944 | tf_op jit(solution)/shard_map/pallas_call | solution.py:19
  10.4 0.8 %shard_map.42.refs_8_ = f32[2,256,512]{2,1,0:T(8,128)S(1)} custom-call(bf16[256,1536]{1,0:T(8,128)(2,1)S(1)} %get-tuple-element.64.own_ref.refs_6_, bf16[1,256,1536]{2,1,0:T(8,128)(2,1)S(1)} %bitcast.6, bf16[1152,512]{1,0:T(8,128)(2,1)S(1)} %get-tuple-element.69.right_ref), custom_call_target="tpu_custom_call" | custom-call | flops 402653184 | tf_op jit(solution)/shard_map/pallas_call | solution.py:19
  11.2 0.7 %collective-permute-done.refs_0_ = bf16[2,16,3,2,256]{4,3,2,1,0:T(2,128)(2,1)S(1)} collective-permute-done((bf16[2,16,3,2,256]{4,3,2,1,0:T(2,128)(2,1)S(1)}, bf16[2,16,3,2,256]{4,3,2,1,0:T(2,128)(2,1)S(1)}, u32[]{:S(2)}, u32[]{:S(2)}) %collective-permute-start) | collective-permute-done | bytes 98336 | tf_op jit(solution)/shard_map/ppermute | solution.py:14
  11.9 0.0 collective-permute-done.1.refs_1_
  11.9 0.9 %shard_map.43 = (f32[2,2,64,256]{3,2,1,0:T(8,128)S(1)}, f32[2,2,64,256]{3,2,1,0:T(8,128)S(1)}, bf16[2,2,2,64,256]{4,3,2,1,0:T(8,128)(2,1)S(1)}, bf16[384,512]{1,0:T(8,128)(2,1)S(1)}) custom-call(bf16[2,16,3,2,256]{4,3,2,1,0:T(2,128)(2,1)S(1)} %collective-permute-done.refs_0_, bf16[2,19,3,2,256]{4,3,2,1,0:T(2,128)(2,1)S(1)} %collective-permute-done.1.refs_1_, ...), custom_call_target="tpu_custom_call" | custom-call | flops 402653184 | tf_op jit(solution)/shard_map/pallas_call | solution.py:19
  12.8 0.1 collective-permute-done.4.refs_1_
  12.9 0.1 collective-permute-start.5
  13.0 1.1 %collective-permute-start.3 = (bf16[2,2,2,64,256]{4,3,2,1,0:T(8,128)(2,1)S(1)}, bf16[2,2,2,64,256]{4,3,2,1,0:T(8,128)(2,1)S(1)}, u32[]{:S(2)}, u32[]{:S(2)}) collective-permute-start(bf16[2,2,2,64,256]{4,3,2,1,0:T(8,128)(2,1)S(1)} %get-tuple-element.72), channel_id=1, source_target_pairs={{0,4},{1,3},{2,6},{3,1},{4,0},{5,7},{6,2},{7,5},{8,12},{9,11},{10,... | collective-permute-start | bytes 786440 | tf_op jit(solution)/shard_map/ppermute | solution.py:410
  14.1 0.2 collective-permute-done.5
  14.3 0.6 %shard_map.44.lefts_ref = bf16[2,256,1536]{2,1,0:T(8,128)(2,1)S(1)} custom-call(f32[2,8,192,256]{3,2,1,0:T(8,128)S(1)} %shard_map.41.refs_0_, bf16[8,32,256]{2,1,0:T(8,128)(2,1)S(1)} %collective-permute-done.4.refs_1_, bf16[1,8,24,256]{3,2,1,0:T(8,128)(2,1)S(1)} %bitcast.9, f32[8,8,256]{2,1,0:T(8,128)S(1)} %get-tuple-element.67.refs_2_.refs_3_), custom_call_target="tpu_custom_call" | custom-call | flops 150994944 | tf_op jit(solution)/shard_map/pallas_call | solution.py:19
  15.0 0.8 %shard_map.45.begun_ref = f32[2,256,512]{2,1,0:T(8,128)S(1)} custom-call(bf16[2,256,1536]{2,1,0:T(8,128)(2,1)S(1)} %shard_map.44.lefts_ref, bf16[1152,512]{1,0:T(8,128)(2,1)S(1)} %get-tuple-element.69.right_ref), custom_call_target="tpu_custom_call" | custom-call | flops 3221225472 | tf_op jit(solution)/shard_map/pallas_call | solution.py:19
  15.8 0.5 %shard_map.46 = (f32[2,2,64,256]{3,2,1,0:T(8,128)S(1)}, f32[2,2,64,256]{3,2,1,0:T(8,128)S(1)}, bf16[2,2,64,256]{3,2,1,0:T(8,128)(2,1)S(1)}, bf16[2,2,64,256]{3,2,1,0:T(8,128)(2,1)S(1)}) custom-call(bf16[2,256,1536]{2,1,0:T(8,128)(2,1)S(1)} %shard_map.44.lefts_ref, bf16[384,512]{1,0:T(8,128)(2,1)S(1)} %get-tuple-element.77.right_ref, ...), custom_call_target="tpu_custom_call" | custom-call | flops 402653184 | tf_op jit(solution)/shard_map/pallas_call | solution.py:19
  16.3 1.1 %collective-permute-start.7 = (bf16[2,2,64,256]{3,2,1,0:T(8,128)(2,1)S(1)}, bf16[2,2,64,256]{3,2,1,0:T(8,128)(2,1)S(1)}, u32[]{:S(2)}, u32[]{:S(2)}) collective-permute-start(bf16[2,2,64,256]{3,2,1,0:T(8,128)(2,1)S(1)} %get-tuple-element.81), channel_id=1, source_target_pairs={{0,4},{1,3},{2,6},{3,1},{4,0},{5,7},{6,2},{7,5},{8,12},{9,11},{10,... | collective-permute-start | bytes 393224 | tf_op jit(solution)/shard_map/ppermute | solution.py:410
  17.4 1.0 %collective-permute-start.6 = (bf16[2,2,64,256]{3,2,1,0:T(8,128)(2,1)S(1)}, bf16[2,2,64,256]{3,2,1,0:T(8,128)(2,1)S(1)}, u32[]{:S(2)}, u32[]{:S(2)}) collective-permute-start(bf16[2,2,64,256]{3,2,1,0:T(8,128)(2,1)S(1)} %get-tuple-element.79), channel_id=1, source_target_pairs={{0,4},{1,3},{2,6},{3,1},{4,0},{5,7},{6,2},{7,5},{8,12},{9,11},{10,... | collective-permute-start | bytes 393224 | tf_op jit(solution)/shard_map/ppermute | solution.py:410
  18.4 1.1 %collective-permute-done.3.refs_1_ = bf16[2,2,2,64,256]{4,3,2,1,0:T(8,128)(2,1)S(1)} collective-permute-done((bf16[2,2,2,64,256]{4,3,2,1,0:T(8,128)(2,1)S(1)}, bf16[2,2,2,64,256]{4,3,2,1,0:T(8,128)(2,1)S(1)}, u32[]{:S(2)}, u32[]{:S(2)}) %collective-permute-start.3) | collective-permute-done | bytes 262176 | tf_op jit(solution)/shard_map/ppermute | solution.py:410
  19.5 1.6 %collective-permute-start.9 = (bf16[2,1,64,256]{3,2,1,0:T(8,128)(2,1)S(1)}, bf16[2,1,64,256]{3,2,1,0:T(8,128)(2,1)S(1)}, u32[]{:S(2)}, u32[]{:S(2)}) collective-permute-start(bf16[2,1,64,256]{3,2,1,0:T(8,128)(2,1)S(1)} %get-tuple-element.88), channel_id=1, source_target_pairs={{0,2},{1,5},{2,0},{3,7},{4,6},{5,1},{6,4},{7,3},{8,10},{9,13},{10,... | collective-permute-start | bytes 196616 | tf_op jit(solution)/shard_map/ppermute | solution.py:410
  21.1 0.3 collective-permute-done.7.refs_1_
  21.4 1.6 %collective-permute-start.8 = (bf16[2,1,64,256]{3,2,1,0:T(8,128)(2,1)S(1)}, bf16[2,1,64,256]{3,2,1,0:T(8,128)(2,1)S(1)}, u32[]{:S(2)}, u32[]{:S(2)}) collective-permute-start(bf16[2,1,64,256]{3,2,1,0:T(8,128)(2,1)S(1)} %get-tuple-element.87), channel_id=1, source_target_pairs={{0,2},{1,5},{2,0},{3,7},{4,6},{5,1},{6,4},{7,3},{8,10},{9,13},{10,... | collective-permute-start | bytes 196616 | tf_op jit(solution)/shard_map/ppermute | solution.py:410
  22.9 0.9 %collective-permute-done.9.came_ref = bf16[2,1,64,256]{3,2,1,0:T(8,128)(2,1)S(1)} collective-permute-done((bf16[2,1,64,256]{3,2,1,0:T(8,128)(2,1)S(1)}, bf16[2,1,64,256]{3,2,1,0:T(8,128)(2,1)S(1)}, u32[]{:S(2)}, u32[]{:S(2)}) %collective-permute-start.9) | collective-permute-done | bytes 65568 | tf_op jit(solution)/shard_map/ppermute | solution.py:410
  23.8 1.2 %collective-permute-start.12 = (bf16[2,1,64,256]{3,2,1,0:T(8,128)(2,1)S(1)}, bf16[2,1,64,256]{3,2,1,0:T(8,128)(2,1)S(1)}, u32[]{:S(2)}, u32[]{:S(2)}) collective-permute-start(bf16[2,1,64,256]{3,2,1,0:T(8,128)(2,1)S(1)} %shard_map.49), channel_id=1, source_target_pairs={{0,8},{1,9},{2,10},{3,11},{4,12},{5,13},{6,14},{7,15},{8,0},{9,1},... | collective-permute-start | bytes 196616 | tf_op jit(solution)/shard_map/ppermute | solution.py:410
  25.1 0.6 %collective-permute-done.8.came_ref = bf16[2,1,64,256]{3,2,1,0:T(8,128)(2,1)S(1)} collective-permute-done((bf16[2,1,64,256]{3,2,1,0:T(8,128)(2,1)S(1)}, bf16[2,1,64,256]{3,2,1,0:T(8,128)(2,1)S(1)}, u32[]{:S(2)}, u32[]{:S(2)}) %collective-permute-start.8) | collective-permute-done | bytes 65568 | tf_op jit(solution)/shard_map/ppermute | solution.py:410
  25.7 1.6 %collective-permute-start.11 = (bf16[2,1,64,256]{3,2,1,0:T(8,128)(2,1)S(1)}, bf16[2,1,64,256]{3,2,1,0:T(8,128)(2,1)S(1)}, u32[]{:S(2)}, u32[]{:S(2)}) collective-permute-start(bf16[2,1,64,256]{3,2,1,0:T(8,128)(2,1)S(1)} %shard_map.50), channel_id=1, source_target_pairs={{0,8},{1,9},{2,10},{3,11},{4,12},{5,13},{6,14},{7,15},{8,0},{9,1},... | collective-permute-start | bytes 196616 | tf_op jit(solution)/shard_map/ppermute | solution.py:410
  27.3 0.0 collective-permute-done.6.refs_3_
  27.3 0.1 shard_map.51
  27.4 1.6 %collective-permute-start.10 = (bf16[4,1,64,256]{3,2,1,0:T(8,128)(2,1)S(1)}, bf16[4,1,64,256]{3,2,1,0:T(8,128)(2,1)S(1)}, u32[]{:S(2)}, u32[]{:S(2)}) collective-permute-start(bf16[4,1,64,256]{3,2,1,0:T(8,128)(2,1)S(1)} %get-tuple-element.92), channel_id=1, source_target_pairs={{0,2},{1,5},{2,0},{3,7},{4,6},{5,1},{6,4},{7,3},{8,10},{9,13},{10,... | collective-permute-start | bytes 393224 | tf_op jit(solution)/shard_map/ppermute | solution.py:410
  28.9 2.5 %collective-permute-done.12.refs_1_ = bf16[2,1,64,256]{3,2,1,0:T(8,128)(2,1)S(1)} collective-permute-done((bf16[2,1,64,256]{3,2,1,0:T(8,128)(2,1)S(1)}, bf16[2,1,64,256]{3,2,1,0:T(8,128)(2,1)S(1)}, u32[]{:S(2)}, u32[]{:S(2)}) %collective-permute-start.12) | collective-permute-done | bytes 65568 | tf_op jit(solution)/shard_map/ppermute | solution.py:410
  31.5 1.0 %collective-permute-done.11.refs_1_ = bf16[2,1,64,256]{3,2,1,0:T(8,128)(2,1)S(1)} collective-permute-done((bf16[2,1,64,256]{3,2,1,0:T(8,128)(2,1)S(1)}, bf16[2,1,64,256]{3,2,1,0:T(8,128)(2,1)S(1)}, u32[]{:S(2)}, u32[]{:S(2)}) %collective-permute-start.11) | collective-permute-done | bytes 65568 | tf_op jit(solution)/shard_map/ppermute | solution.py:410
  32.5 0.0 collective-permute-done.10.came_ref
  32.5 0.7 %shard_map.54 = f32[2,2,64,256]{3,2,1,0:T(8,128)} custom-call(bf16[4,1,64,256]{3,2,1,0:T(8,128)(2,1)S(1)} %collective-permute-done.10.came_ref, f32[2,1,64,256]{3,2,1,0:T(8,128)S(1)} %shard_map.52.refs_0_, f32[2,1,64,256]{3,2,1,0:T(8,128)S(1)} %shard_map.53.refs_1_), custom_call_target="tpu_custom_call" | custom-call | tf_op jit(solution)/shard_map/pallas_call | solution.py:19
  (7 shorter events, 0.1 us)
Async XLA Ops:
  0.0 9.5 %collective-permute-start.2 = (bf16[2,8,16,3,2,256]{5,4,3,2,1,0:T(2,128)(2,1)}, bf16[2,8,16,3,2,256]{5,4,3,2,1,0:T(2,128)(2,1)S(1)}, u32[]{:S(2)}, u32[]{:S(2)}) collective-permute-start(bf16[2,8,16,3,2,256]{5,4,3,2,1,0:T(2,128)(2,1)} %bitcast.10), channel_id=1, source_target_pairs={{1,0},{0,1},{3,2},{2,3},{5,4},{4,5},{7,6},{6,7},{9,8},{8,9},{11,10... | collective-permute-start | bytes 2359304 | tf_op jit(solution)/shard_map/ppermute | solution.py:14
  1.8 10.1 %collective-permute-start.1 = (bf16[2,19,3,2,256]{4,3,2,1,0:T(2,128)(2,1)S(1)}, bf16[2,19,3,2,256]{4,3,2,1,0:T(2,128)(2,1)S(1)}, u32[]{:S(2)}, u32[]{:S(2)}) collective-permute-start(bf16[2,19,3,2,256]{4,3,2,1,0:T(2,128)(2,1)S(1)} %get-tuple-element.52), channel_id=1, source_target_pairs={{12,0},{0,4},{4,8},{8,12},{13,1},{1,5},{5,9},{9,13},{14,2},{2,6},{... | collective-permute-start | bytes 350216 | tf_op jit(solution)/shard_map/ppermute | solution.py:14
  4.4 7.4 %collective-permute-start = (bf16[2,16,3,2,256]{4,3,2,1,0:T(2,128)(2,1)S(1)}, bf16[2,16,3,2,256]{4,3,2,1,0:T(2,128)(2,1)S(1)}, u32[]{:S(2)}, u32[]{:S(2)}) collective-permute-start(bf16[2,16,3,2,256]{4,3,2,1,0:T(2,128)(2,1)S(1)} %get-tuple-element.51), channel_id=1, source_target_pairs={{4,0},{8,4},{12,8},{0,12},{5,1},{9,5},{13,9},{1,13},{6,2},{10,6},{... | collective-permute-start | bytes 294920 | tf_op jit(solution)/shard_map/ppermute | solution.py:14
  7.3 5.6 %collective-permute-start.4 = (bf16[8,32,256]{2,1,0:T(8,128)(2,1)S(1)}, bf16[8,32,256]{2,1,0:T(8,128)(2,1)S(1)}, u32[]{:S(2)}, u32[]{:S(2)}) collective-permute-start(bf16[8,32,256]{2,1,0:T(8,128)(2,1)S(1)} %get-tuple-element.74), channel_id=1, source_target_pairs={{2,0},{0,2},{3,1},{1,3},{6,4},{4,6},{7,5},{5,7},{10,8},{8,10},{11,... | collective-permute-start | bytes 393224 | tf_op jit(solution)/shard_map/ppermute | solution.py:14
  12.9 1.4 %collective-permute-start.5 = (bf16[8,24,256]{2,1,0:T(8,128)(2,1)S(1)}, bf16[8,24,256]{2,1,0:T(8,128)(2,1)S(1)}, u32[]{:S(2)}, u32[]{:S(2)}) collective-permute-start(bf16[8,24,256]{2,1,0:T(8,128)(2,1)S(1)} %slice.3), channel_id=1, source_target_pairs={{1,0},{0,1},{3,2},{2,3},{5,4},{4,5},{7,6},{6,7},{9,8},{8,9},{11,10... | collective-permute-start | bytes 294920 | tf_op jit(solution)/shard_map/ppermute | solution.py:14
  13.0 6.4 %collective-permute-start.3 = (bf16[2,2,2,64,256]{4,3,2,1,0:T(8,128)(2,1)S(1)}, bf16[2,2,2,64,256]{4,3,2,1,0:T(8,128)(2,1)S(1)}, u32[]{:S(2)}, u32[]{:S(2)}) collective-permute-start(bf16[2,2,2,64,256]{4,3,2,1,0:T(8,128)(2,1)S(1)} %get-tuple-element.72), channel_id=1, source_target_pairs={{0,4},{1,3},{2,6},{3,1},{4,0},{5,7},{6,2},{7,5},{8,12},{9,11},{10,... | collective-permute-start | bytes 786440 | tf_op jit(solution)/shard_map/ppermute | solution.py:410
  16.3 5.0 %collective-permute-start.7 = (bf16[2,2,64,256]{3,2,1,0:T(8,128)(2,1)S(1)}, bf16[2,2,64,256]{3,2,1,0:T(8,128)(2,1)S(1)}, u32[]{:S(2)}, u32[]{:S(2)}) collective-permute-start(bf16[2,2,64,256]{3,2,1,0:T(8,128)(2,1)S(1)} %get-tuple-element.81), channel_id=1, source_target_pairs={{0,4},{1,3},{2,6},{3,1},{4,0},{5,7},{6,2},{7,5},{8,12},{9,11},{10,... | collective-permute-start | bytes 393224 | tf_op jit(solution)/shard_map/ppermute | solution.py:410
  17.4 9.9 %collective-permute-start.6 = (bf16[2,2,64,256]{3,2,1,0:T(8,128)(2,1)S(1)}, bf16[2,2,64,256]{3,2,1,0:T(8,128)(2,1)S(1)}, u32[]{:S(2)}, u32[]{:S(2)}) collective-permute-start(bf16[2,2,64,256]{3,2,1,0:T(8,128)(2,1)S(1)} %get-tuple-element.79), channel_id=1, source_target_pairs={{0,4},{1,3},{2,6},{3,1},{4,0},{5,7},{6,2},{7,5},{8,12},{9,11},{10,... | collective-permute-start | bytes 393224 | tf_op jit(solution)/shard_map/ppermute | solution.py:410
  19.5 4.3 %collective-permute-start.9 = (bf16[2,1,64,256]{3,2,1,0:T(8,128)(2,1)S(1)}, bf16[2,1,64,256]{3,2,1,0:T(8,128)(2,1)S(1)}, u32[]{:S(2)}, u32[]{:S(2)}) collective-permute-start(bf16[2,1,64,256]{3,2,1,0:T(8,128)(2,1)S(1)} %get-tuple-element.88), channel_id=1, source_target_pairs={{0,2},{1,5},{2,0},{3,7},{4,6},{5,1},{6,4},{7,3},{8,10},{9,13},{10,... | collective-permute-start | bytes 196616 | tf_op jit(solution)/shard_map/ppermute | solution.py:410
  21.4 4.3 %collective-permute-start.8 = (bf16[2,1,64,256]{3,2,1,0:T(8,128)(2,1)S(1)}, bf16[2,1,64,256]{3,2,1,0:T(8,128)(2,1)S(1)}, u32[]{:S(2)}, u32[]{:S(2)}) collective-permute-start(bf16[2,1,64,256]{3,2,1,0:T(8,128)(2,1)S(1)} %get-tuple-element.87), channel_id=1, source_target_pairs={{0,2},{1,5},{2,0},{3,7},{4,6},{5,1},{6,4},{7,3},{8,10},{9,13},{10,... | collective-permute-start | bytes 196616 | tf_op jit(solution)/shard_map/ppermute | solution.py:410
  23.8 7.6 %collective-permute-start.12 = (bf16[2,1,64,256]{3,2,1,0:T(8,128)(2,1)S(1)}, bf16[2,1,64,256]{3,2,1,0:T(8,128)(2,1)S(1)}, u32[]{:S(2)}, u32[]{:S(2)}) collective-permute-start(bf16[2,1,64,256]{3,2,1,0:T(8,128)(2,1)S(1)} %shard_map.49), channel_id=1, source_target_pairs={{0,8},{1,9},{2,10},{3,11},{4,12},{5,13},{6,14},{7,15},{8,0},{9,1},... | collective-permute-start | bytes 196616 | tf_op jit(solution)/shard_map/ppermute | solution.py:410
  25.7 6.8 %collective-permute-start.11 = (bf16[2,1,64,256]{3,2,1,0:T(8,128)(2,1)S(1)}, bf16[2,1,64,256]{3,2,1,0:T(8,128)(2,1)S(1)}, u32[]{:S(2)}, u32[]{:S(2)}) collective-permute-start(bf16[2,1,64,256]{3,2,1,0:T(8,128)(2,1)S(1)} %shard_map.50), channel_id=1, source_target_pairs={{0,8},{1,9},{2,10},{3,11},{4,12},{5,13},{6,14},{7,15},{8,0},{9,1},... | collective-permute-start | bytes 196616 | tf_op jit(solution)/shard_map/ppermute | solution.py:410
  27.4 5.1 %collective-permute-start.10 = (bf16[4,1,64,256]{3,2,1,0:T(8,128)(2,1)S(1)}, bf16[4,1,64,256]{3,2,1,0:T(8,128)(2,1)S(1)}, u32[]{:S(2)}, u32[]{:S(2)}) collective-permute-start(bf16[4,1,64,256]{3,2,1,0:T(8,128)(2,1)S(1)} %get-tuple-element.92), channel_id=1, source_target_pairs={{0,2},{1,5},{2,0},{3,7},{4,6},{5,1},{6,4},{7,3},{8,10},{9,13},{10,... | collective-permute-start | bytes 393224 | tf_op jit(solution)/shard_map/ppermute | solution.py:410

commit v9 on v8

--- a/solution.py
+++ b/solution.py
@@ -260,13 +260,6 @@
         total_ref[k + 1] = dot(others_ref[k, :, :inner], right)
 
 
-def begin_second_kernel(lefts_ref, right_ref, total_ref):
-    inner = right_ref.shape[0]
-    right = right_ref[...]
-    for k in range(lefts_ref.shape[0]):
-        total_ref[k] = dot(lefts_ref[k, :, :inner], right)
-
-
 def bits(axis):
     return range(lax.axis_size(axis).bit_length() - 1)
 
@@ -288,15 +281,17 @@
     return jnp.where(my_bit("ma", 0) == 0, even, odd)
 
 
-def project(terms, begun_ref, keep_refs, send_refs, total_ref):
-    groups, blocks, rows, _ = total_ref.shape
-    parts, count, _, width = keep_refs[0].shape
-    for k, term in enumerate(terms):
-        total_ref[k] = (begun_ref[k] + term).reshape(blocks, rows, parts * width)
-    my_modes = lax.axis_index("ma")
+def half_of(kind):
+    half = lax.bitwise_xor(my_bit("gx", bits("gx")[-1]), 1 - kind)
+    return lax.bitwise_xor(half, lax.axis_index("ma"))
+
+
+def share(total, keep_ref, send_ref, total_ref):
+    blocks, rows, double = total_ref.shape
+    parts, count, _, width = keep_ref.shape
+    total_ref[...] = total.reshape(blocks, rows, double)
     odd_core = my_bit("ma", 0)
-    top = my_bit("gx", bits("gx")[-1])
-    across_x, across_y = lax.axis_size("gx"), lax.axis_size("gy")
+    across_y = lax.axis_size("gy")
     plan = steps()
     mine = my_side(plan[0])
 
@@ -311,22 +306,25 @@
             owners.append(place["gx"] * across_y + place["gy"])
         return jnp.where(odd_core == 0, owners[0], owners[1])
 
-    for kind in range(2):
-        half = lax.bitwise_xor(top, 1 - kind)
-        for index in range(count):
-            for ref, side in ((keep_refs[kind], mine), (send_refs[kind], 1 - mine)):
-                owner = half * (across_x // 2 * across_y) + at(side, index)
-                group = lax.rem(lax.div(owner, blocks) + groups - my_modes, groups)
-                block = total_ref[group, lax.rem(owner, blocks)].astype(ref.dtype)
-                for p in range(parts):
-                    ref[p, index] = block[:, p * width : (p + 1) * width]
+    for index in range(count):
+        for ref, side in ((keep_ref, mine), (send_ref, 1 - mine)):
+            block = total_ref[at(side, index)].astype(ref.dtype)
+            for p in range(parts):
+                ref[p, index] = block[:, p * width : (p + 1) * width]
+
+
+def first_share(kind, own_ref, others_ref, begun_ref, right, keep_ref, send_ref, total_ref):
+    half = half_of(kind)
+    inner = own_ref.shape[1] - right.shape[0]
+    left = jnp.where(half == 0, own_ref[:, inner:], others_ref[0, :, inner:])
+    share(begun_ref[half] + dot(left, right), keep_ref, send_ref, total_ref)
 
 
 def first_kernel(
-    sites, planes, high_ref, low_ref, matrix_ref, ahead_part_ref, back_part_ref, past_maps_ref, own_ref, others_ref, begun_ref,
+    sites, high_ref, low_ref, matrix_ref, ahead_part_ref, back_part_ref, past_maps_ref, own_ref, others_ref, begun_ref,
     *refs,
 ):
-    *refs, right_ref, total_ref = refs
+    keep_ref, send_ref, right_ref, total_ref = refs
     depth = matrix_ref.shape[0]
     same = same_site(sites, depth)
     _, ys, colours, zs, _ = high_ref.shape
@@ -344,11 +342,11 @@
     set_right(right_ref, 0, moved.astype(jnp.bfloat16))
     moved = dot(matrix_ref[...], plane_rows(high_ref, ys)) + back_part_ref[...]
     set_right(right_ref, 1, moved.astype(jnp.bfloat16))
-    inner = (planes - 2) * depth
-    lefts = [own_ref[:, inner:]] + [others_ref[k, :, inner:] for k in range(others_ref.shape[0])]
-    terms = [dot(left, right_ref[...]) for left in lefts]
-    keep_other, keep_own, send_ref = refs
-    project(terms, begun_ref, (keep_other, keep_own), (send_ref.at[0], send_ref.at[1]), total_ref)
+    first_share(0, own_ref, others_ref, begun_ref, right_ref[...], keep_ref, send_ref, total_ref)
+
+
+def first_own_kernel(own_ref, others_ref, begun_ref, right_ref, keep_ref, send_ref, total_ref):
+    first_share(1, own_ref, others_ref, begun_ref, right_ref[...], keep_ref, send_ref, total_ref)
 
 
 def begin_y_kernel(sites, zs, rows_ref, others_ref, ahead_ref, back_ref, part_ref):
@@ -390,12 +388,21 @@
         turned_ref[k] = field_ref[k].reshape(planes * depth, width).T
 
 
-def second_kernel(lefts_ref, right_ref, begun_ref, *refs):
-    *refs, total_ref = refs
-    inner = lefts_ref.shape[2] - right_ref.shape[0]
-    lefts = [lefts_ref[k, :, inner:] for k in range(lefts_ref.shape[0])]
-    terms = [dot(left, right_ref[...]) for left in lefts]
-    project(terms, begun_ref, refs[:2], refs[2:], total_ref)
+def second_share(kind, lefts_ref, right_ref, edge_ref, keep_ref, send_ref, total_ref):
+    half = half_of(kind)
+    inner = right_ref.shape[0]
+    total = dot(lefts_ref[half, :, :inner], right_ref[...]) + dot(lefts_ref[half, :, inner:], edge_ref[...])
+    share(total, keep_ref, send_ref, total_ref)
+
+
+def second_kernel(lefts_ref, right_ref, edge_ref, keep_ref, send_ref, total_ref):
+    second_share(0, lefts_ref, right_ref, edge_ref, keep_ref, send_ref, total_ref)
+
+
+def second_own_kernel(lefts_ref, right_ref, edge_ref, first_ref, keep_ref, send_ref, total_ref):
+    parts = first_ref.shape[0]
+    send_ref[:parts] = first_ref[...]
+    second_share(1, lefts_ref, right_ref, edge_ref, keep_ref, send_ref.at[parts:], total_ref)
 
 
 def exchange(block, step):
@@ -472,7 +479,7 @@
     turned_shape = shape(width, planes * depth)
     total_shape = shape(groups, width, parts * width, dtype=f32)
     link_shape = shape(planes, 8, lanes, dtype=f32)
-    total = pltpu.VMEM((groups, width // rows, rows, parts * width), f32)
+    total = pltpu.VMEM((width // rows, rows, parts * width), f32)
     step_flops = 2 * planes * depth * depth * width
     project_flops = 2 * groups * width * planes * depth * parts * width
 
@@ -509,12 +516,13 @@
     top = ("gx", bits("gx")[-1])
     pieces = across_x * across_y // 4
     kept_shape = shape(parts, pieces, rows, width, dtype=f32)
+    sent_shape = shape(parts, pieces, rows, width)
 
     def inner(*refs):
         inner_kernel(sites, *refs)
 
     def first(*refs):
-        first_kernel(sites, planes, *refs)
+        first_kernel(sites, *refs)
 
     def begin_y(*refs):
         begin_y_kernel(sites, zs, *refs)
@@ -539,13 +547,14 @@
         begin_y, shape(groups, planes, depth, width, dtype=f32), 2 * step_flops, [field, fields, ahead_y, back_y]
     )
     part_y, begun_first = lax.optimization_barrier((part_y, begun_first))
-    kept_first, own_first, sent_first, right_edge = call(
+    kept_first, sent_first, right_edge = call(
         first,
-        (kept_shape, kept_shape, shape(2, parts, pieces, rows, width), shape(2 * depth, parts * width)),
+        (kept_shape, sent_shape, shape(2 * depth, parts * width)),
         project_flops,
         [high, low, matrix, ahead_part, back_part, past_maps, own, others, begun_first],
         [total],
     )
+    came_first = exchange(sent_first, plan[0])
     near, right_edge = lax.optimization_barrier((near, right_edge))
     near_rows = near[:, : 2 * row_size]
     far = jnp.stack([shifted(near_rows, "ma", -step) for step in range(1, groups)])
@@ -554,30 +563,39 @@
         [part_y, near, far, ahead_y],
         [pltpu.VMEM((groups,) + field_shape.shape, bf16)],
     )
-    begun_second = call(begin_second_kernel, total_shape, 8 * project_flops, [lefts, right])
-    sent_shape = shape(parts, pieces, rows, width)
-    kept_second, own_second, sent_second, sent_own = call(
-        second_kernel, (kept_shape, kept_shape, sent_shape, sent_shape), project_flops,
-        [lefts, right_edge, begun_second], [total],
-    )
-    came_first = exchange(sent_first, plan[0])
-    crossing = [(kept_first, came_first, 0), (kept_second, exchange(sent_second, plan[0]), None)]
-    staying = [(own_first, came_first, 1), (own_second, exchange(sent_own, plan[0]), None)]
+    kept_second, sent_second = call(
+        second_kernel, (kept_shape, sent_shape), 8 * project_flops, [lefts, right, right_edge], [total]
+    )
+    came_second = exchange(sent_second, plan[0])
+    crossing = [(kept_first, came_first), (kept_second, came_second)]
     after = kept_second
+    staying = None
     for step in plan[1:]:
-        for d, (kept, came, which) in enumerate(crossing):
+        for d, (kept, came) in enumerate(crossing):
             came, after = lax.optimization_barrier((came, after))
-            kept, came = halve([(kept, came, which)], step)
-            crossing[d], after = (kept, came, None), kept
+            crossing[d] = halve([(kept, came, None)], step)
+            after = crossing[d][0]
+            if staying is None:
+                own_first, sent_own = call(
+                    first_own_kernel, (kept_shape, sent_shape), 0, [own, others, begun_first, right_edge], [total]
+                )
+                right_edge, after = lax.optimization_barrier((right_edge, after))
+                own_second, sent_own = call(
+                    second_own_kernel, (kept_shape, shape(2 * parts, pieces, rows, width)), 0,
+                    [lefts, right, right_edge, sent_own], [total],
+                )
+                came_own = exchange(sent_own, plan[0])
+                staying = [(own_first, came_own, slice(0, parts)), (own_second, came_own, slice(parts, 2 * parts))]
     crossed = []
-    for kept, came, _ in crossing:
+    for kept, came in crossing:
         came, after = lax.optimization_barrier((came, after))
-        after = call(sum_kernel, pltpu.VMEM(kept.shape, bf16), 0, [kept, came])
+        after = call(sum_kernel, pltpu.VMEM(kept.shape, bf16), 8 * project_flops, [kept, came])
         crossed.append(exchange(after, (top, top)))
     for step in plan[1:]:
-        kept, came, which = staying[-1]
+        kept, came, which = staying[0]
         came, after = lax.optimization_barrier((came, after))
-        kept, came = halve(staying[:-1] + [(kept, came, which)], step)
+        sums = [(kept, came, which)] + [(k, came, w) for k, _, w in staying[1:]]
+        kept, came = halve(sums, step)
         staying, after = [(kept, came, None)], kept
     kept, came, _ = staying[0]
     totals = []

time: 33.4 us -> 35.4 us (1.060)
  waiting for transfers between devices: 7.48 us -> 11 us
  starting transfers between devices: 17.5 us -> 15.7 us
    ppermute x8, waiting for transfers between devices: 6.43 us -> 9.67 us  [exchange(): return lax.ppermute(block, axes, route)]
    ppermute x8, starting transfers between devices: 10.6 us -> 8.84 us  [exchange(): return lax.ppermute(block, axes, route)]
    pallas_call x18 -> x19, Pallas kernels: 8.13 us -> 8.39 us  [call(): pl.pallas_call(body, out_shape=out_shape, in_specs=[pl.BlockSpec(memory_s...]
where the time goes in v9:
time: 35.4 us; the launch traced here: 35.2 us
  starting transfers between devices  15.7 us (44%)
  waiting for transfers between devices  11 us (31%)
  Pallas kernels  8.39 us (24%)
    ppermute x8, waiting for transfers between devices, exchange(): return lax.ppermute(block, axes, route)  9.67 us
    ppermute x8, starting transfers between devices, exchange(): return lax.ppermute(block, axes, route)  8.84 us
    pallas_call x19, Pallas kernels, call(): pl.pallas_call(body, out_shape=out_shape, in_specs=[pl.BlockSpec(memory_s...  8.39 us
    ppermute x5, starting transfers between devices, shifted(): return lax.ppermute(block, axis, route)  6.9 us
    ppermute x5, waiting for transfers between devices, shifted(): return lax.ppermute(block, axis, route)  1.3 us
  transfers between devices with their start and end apart: 13, of which 9 were waited for; matrix products, arithmetic and copies ran while one was open for 0% of the time, Pallas kernels for 22%

profile of v9, /device:TPU:0, one launch (start us, length us, event | category | flops | bytes accessed | tf_op | source)
XLA Modules:
  0.0 35.2 jit_solution(4193352024020587894)
XLA Ops:
  0.0 0.5 %collective-permute-start = (bf16[2,8,16,3,2,256]{5,4,3,2,1,0:T(2,128)(2,1)}, bf16[2,8,16,3,2,256]{5,4,3,2,1,0:T(2,128)(2,1)S(1)}, u32[]{:S(2)}, u32[]{:S(2)}) collective-permute-start(bf16[2,8,16,3,2,256]{5,4,3,2,1,0:T(2,128)(2,1)} %bitcast.11), channel_id=1, source_target_pairs={{1,0},{0,1},{3,2},{2,3},{5,4},{4,5},{7,6},{6,7},{9,8},{8,9},{11,10... | collective-permute-start | bytes 2359304 | tf_op jit(solution)/shard_map/ppermute | solution.py:14
  0.5 1.4 %shard_map.37 = (bf16[2,16,3,2,256]{4,3,2,1,0:T(2,128)(2,1)S(1)}, bf16[2,19,3,2,256]{4,3,2,1,0:T(2,128)(2,1)S(1)}, bf16[2,8,16,3,2,256]{5,4,3,2,1,0:T(2,128)(2,1...) custom-call(bf16[2,8,16,3,2,256]{5,4,3,2,1,0:T(2,128)(2,1)} %bitcast, ...), custom_call_target="tpu_custom_call" | custom-call | tf_op jit(solution)/shard_map/pallas_call | solution.py:19
  1.8 2.6 %collective-permute-start.3 = (bf16[2,19,3,2,256]{4,3,2,1,0:T(2,128)(2,1)S(1)}, bf16[2,19,3,2,256]{4,3,2,1,0:T(2,128)(2,1)S(1)}, u32[]{:S(2)}, u32[]{:S(2)}) collective-permute-start(bf16[2,19,3,2,256]{4,3,2,1,0:T(2,128)(2,1)S(1)} %get-tuple-element.68), channel_id=1, source_target_pairs={{12,0},{0,4},{4,8},{8,12},{13,1},{1,5},{5,9},{9,13},{14,2},{2,6},{... | collective-permute-start | bytes 350216 | tf_op jit(solution)/shard_map/ppermute | solution.py:14
  4.4 2.1 %collective-permute-start.2 = (bf16[2,16,3,2,256]{4,3,2,1,0:T(2,128)(2,1)S(1)}, bf16[2,16,3,2,256]{4,3,2,1,0:T(2,128)(2,1)S(1)}, u32[]{:S(2)}, u32[]{:S(2)}) collective-permute-start(bf16[2,16,3,2,256]{4,3,2,1,0:T(2,128)(2,1)S(1)} %get-tuple-element.67), channel_id=1, source_target_pairs={{4,0},{8,4},{12,8},{0,12},{5,1},{9,5},{13,9},{1,13},{6,2},{10,6},{... | collective-permute-start | bytes 294920 | tf_op jit(solution)/shard_map/ppermute | solution.py:14
  6.5 0.7 %shard_map.38 = (bf16[8,192,256]{2,1,0:T(8,128)(2,1)S(1)}, bf16[8,32,256]{2,1,0:T(8,128)(2,1)S(1)}, f32[8,8,256]{2,1,0:T(8,128)S(1)}, f32[8,8,256]{2,1,0:T(8,128...) custom-call(bf16[2,8,16,3,2,256]{5,4,3,2,1,0:T(2,128)(2,1)S(1)} %get-tuple-element.52.raw_ref, ...), custom_call_target="tpu_custom_call" | custom-call | tf_op jit(solution)/shard_map/pallas_call | solution.py:19
  7.3 1.7 %collective-permute-start.1 = (bf16[8,32,256]{2,1,0:T(8,128)(2,1)S(1)}, bf16[8,32,256]{2,1,0:T(8,128)(2,1)S(1)}, u32[]{:S(2)}, u32[]{:S(2)}) collective-permute-start(bf16[8,32,256]{2,1,0:T(8,128)(2,1)S(1)} %get-tuple-element.66), channel_id=1, source_target_pairs={{2,0},{0,2},{3,1},{1,3},{6,4},{4,6},{7,5},{5,7},{10,8},{8,10},{11,... | collective-permute-start | bytes 393224 | tf_op jit(solution)/shard_map/ppermute | solution.py:14
  8.9 0.5 %shard_map.39 = (bf16[1152,512]{1,0:T(8,128)(2,1)S(1)}, bf16[256,1536]{1,0:T(8,128)(2,1)S(1)}, bf16[192,192]{1,0:T(8,128)(2,1)S(1)}, f32[192,256]{1,0:T(8,128)S(1)}, f32[192,256]{1,0:T(8,128)S(1)}) custom-call(bf16[8,192,256]{2,1,0:T(8,128)(2,1)S(1)} %get-tuple-element.56.refs_0_, f32[8,8,256]{2,1,0:T(8,128)S(1)} %get-tuple-element.57.refs_1_, ...), custom_call_target="tpu_custom_call" | custom-call | flops 150994944 | tf_op jit(solution)/shard_map/pallas_call | solution.py:19
  9.5 0.0 collective-permute-done.raw_ref
  9.5 0.3 shard_map.40
  9.8 0.6 %shard_map.41.refs_0_ = f32[2,8,192,256]{3,2,1,0:T(8,128)S(1)} custom-call(bf16[8,192,256]{2,1,0:T(8,128)(2,1)S(1)} %get-tuple-element.56.refs_0_, bf16[1,8,192,256]{3,2,1,0:T(8,128)(2,1)S(1)} %bitcast.9, f32[8,8,256]{2,1,0:T(8,128)S(1)} %get-tuple-element.62.refs_2_.refs_3_, f32[8,8,256]{2,1,0:T(8,128)S(1)} %get-tuple-element.63.refs_3_), custom_call_target="tpu_custom_call" | custom-call | flops 150994944 | tf_op jit(solution)/shard_map/pallas_call | solution.py:19
  10.4 0.8 %shard_map.42.refs_8_.begun_ref = f32[2,256,512]{2,1,0:T(8,128)S(1)} custom-call(bf16[256,1536]{1,0:T(8,128)(2,1)S(1)} %get-tuple-element.59.own_ref.refs_6_, bf16[1,256,1536]{2,1,0:T(8,128)(2,1)S(1)} %bitcast.6, bf16[1152,512]{1,0:T(8,128)(2,1)S(1)} %get-tuple-element.64.right_ref), custom_call_target="tpu_custom_call" | custom-call | flops 402653184 | tf_op jit(solution)/shard_map/pallas_call | solution.py:19
  11.2 0.7 %collective-permute-done.2.refs_0_ = bf16[2,16,3,2,256]{4,3,2,1,0:T(2,128)(2,1)S(1)} collective-permute-done((bf16[2,16,3,2,256]{4,3,2,1,0:T(2,128)(2,1)S(1)}, bf16[2,16,3,2,256]{4,3,2,1,0:T(2,128)(2,1)S(1)}, u32[]{:S(2)}, u32[]{:S(2)}) %collective-permute-start.2) | collective-permute-done | bytes 98336 | tf_op jit(solution)/shard_map/ppermute | solution.py:14
  11.9 0.0 collective-permute-done.3.refs_1_
  11.9 0.8 %shard_map.43 = (f32[2,2,64,256]{3,2,1,0:T(8,128)S(1)}, bf16[2,2,64,256]{3,2,1,0:T(8,128)(2,1)S(1)}, bf16[384,512]{1,0:T(8,128)(2,1)S(1)}) custom-call(bf16[2,16,3,2,256]{4,3,2,1,0:T(2,128)(2,1)S(1)} %collective-permute-done.2.refs_0_, bf16[2,19,3,2,256]{4,3,2,1,0:T(2,128)(2,1)S(1)} %collective-permute-done.3.refs_1_, ...), custom_call_target="tpu_custom_call" | custom-call | flops 402653184 | tf_op jit(solution)/shard_map/pallas_call | solution.py:19
  12.7 0.3 collective-permute-done.1.refs_1_
  12.9 0.1 collective-permute-start.4
  13.0 0.9 %collective-permute-start.5 = (bf16[2,2,64,256]{3,2,1,0:T(8,128)(2,1)S(1)}, bf16[2,2,64,256]{3,2,1,0:T(8,128)(2,1)S(1)}, u32[]{:S(2)}, u32[]{:S(2)}) collective-permute-start(bf16[2,2,64,256]{3,2,1,0:T(8,128)(2,1)S(1)} %get-tuple-element.79), channel_id=1, source_target_pairs={{0,4},{1,3},{2,6},{3,1},{4,0},{5,7},{6,2},{7,5},{8,12},{9,11},{10,... | collective-permute-start | bytes 393224 | tf_op jit(solution)/shard_map/ppermute | solution.py:417
  14.0 0.3 collective-permute-done.4
  14.3 0.6 %shard_map.45.lefts_ref = bf16[2,256,1536]{2,1,0:T(8,128)(2,1)S(1)} custom-call(f32[2,8,192,256]{3,2,1,0:T(8,128)S(1)} %shard_map.41.refs_0_, bf16[8,32,256]{2,1,0:T(8,128)(2,1)S(1)} %collective-permute-done.1.refs_1_, bf16[1,8,24,256]{3,2,1,0:T(8,128)(2,1)S(1)} %bitcast.10, f32[8,8,256]{2,1,0:T(8,128)S(1)} %get-tuple-element.62.refs_2_.refs_3_), custom_call_target="tpu_custom_call" | custom-call | flops 150994944 | tf_op jit(solution)/shard_map/pallas_call | solution.py:19
  15.0 0.7 %shard_map.46 = (f32[2,2,64,256]{3,2,1,0:T(8,128)S(1)}, bf16[2,2,64,256]{3,2,1,0:T(8,128)(2,1)S(1)}) custom-call(bf16[2,256,1536]{2,1,0:T(8,128)(2,1)S(1)} %shard_map.45.lefts_ref, bf16[1152,512]{1,0:T(8,128)(2,1)S(1)} %get-tuple-element.64.right_ref, bf16[384,512]{1,0:T(8,128)(2,1)S(1)} %get-tuple-element.83.right_ref.edge_ref), custom_call_target="tpu_custom_call" | custom-call | flops 3221225472 | tf_op jit(solution)/shard_map/pallas_call | solution.py:19
  15.6 0.9 %collective-permute-start.7 = (bf16[2,2,64,256]{3,2,1,0:T(8,128)(2,1)S(1)}, bf16[2,2,64,256]{3,2,1,0:T(8,128)(2,1)S(1)}, u32[]{:S(2)}, u32[]{:S(2)}) collective-permute-start(bf16[2,2,64,256]{3,2,1,0:T(8,128)(2,1)S(1)} %get-tuple-element.86), channel_id=1, source_target_pairs={{0,4},{1,3},{2,6},{3,1},{4,0},{5,7},{6,2},{7,5},{8,12},{9,11},{10,... | collective-permute-start | bytes 393224 | tf_op jit(solution)/shard_map/ppermute | solution.py:417
  16.6 1.5 %collective-permute-done.5.refs_1_ = bf16[2,2,64,256]{3,2,1,0:T(8,128)(2,1)S(1)} collective-permute-done((bf16[2,2,64,256]{3,2,1,0:T(8,128)(2,1)S(1)}, bf16[2,2,64,256]{3,2,1,0:T(8,128)(2,1)S(1)}, u32[]{:S(2)}, u32[]{:S(2)}) %collective-permute-start.5) | collective-permute-done | bytes 131104 | tf_op jit(solution)/shard_map/ppermute | solution.py:417
  18.1 1.6 %collective-permute-start.9 = (bf16[2,1,64,256]{3,2,1,0:T(8,128)(2,1)S(1)}, bf16[2,1,64,256]{3,2,1,0:T(8,128)(2,1)S(1)}, u32[]{:S(2)}, u32[]{:S(2)}) collective-permute-start(bf16[2,1,64,256]{3,2,1,0:T(8,128)(2,1)S(1)} %get-tuple-element.89), channel_id=1, source_target_pairs={{0,2},{1,5},{2,0},{3,7},{4,6},{5,1},{6,4},{7,3},{8,10},{9,13},{10,... | collective-permute-start | bytes 196616 | tf_op jit(solution)/shard_map/ppermute | solution.py:417
  19.6 0.4 %shard_map.44 = (f32[2,2,64,256]{3,2,1,0:T(8,128)S(1)}, bf16[2,2,64,256]{3,2,1,0:T(8,128)(2,1)S(1)}) custom-call(bf16[256,1536]{1,0:T(8,128)(2,1)S(1)} %get-tuple-element.59.own_ref.refs_6_, bf16[1,256,1536]{2,1,0:T(8,128)(2,1)S(1)} %bitcast.8, f32[2,256,512]{2,1,0:T(8,128)S(1)} %shard_map.42.refs_8_.begun_ref, ...), custom_call_target="tpu_custom_call" | custom-call | tf_op jit(solution)/shard_map/pallas_call | solution.py:19
  20.0 0.7 %shard_map.48 = (f32[2,2,64,256]{3,2,1,0:T(8,128)S(1)}, bf16[4,2,64,256]{3,2,1,0:T(8,128)(2,1)S(1)}) custom-call(bf16[2,256,1536]{2,1,0:T(8,128)(2,1)S(1)} %shard_map.45.lefts_ref, bf16[1152,512]{1,0:T(8,128)(2,1)S(1)} %get-tuple-element.64.right_ref, bf16[384,512]{1,0:T(8,128)(2,1)S(1)} %get-tuple-element.83.right_ref.edge_ref, ...), custom_call_target="tpu_custom_call" | custom-call | tf_op jit(solution)/shard_map/pallas_call | solution.py:19
  20.7 0.9 %collective-permute-start.6 = (bf16[4,2,64,256]{3,2,1,0:T(8,128)(2,1)S(1)}, bf16[4,2,64,256]{3,2,1,0:T(8,128)(2,1)S(1)}, u32[]{:S(2)}, u32[]{:S(2)}) collective-permute-start(bf16[4,2,64,256]{3,2,1,0:T(8,128)(2,1)S(1)} %get-tuple-element.85), channel_id=1, source_target_pairs={{0,4},{1,3},{2,6},{3,1},{4,0},{5,7},{6,2},{7,5},{8,12},{9,11},{10,... | collective-permute-start | bytes 786440 | tf_op jit(solution)/shard_map/ppermute | solution.py:417
  21.6 0.0 collective-permute-done.7.refs_1_
  21.7 0.9 %collective-permute-start.8 = (bf16[2,1,64,256]{3,2,1,0:T(8,128)(2,1)S(1)}, bf16[2,1,64,256]{3,2,1,0:T(8,128)(2,1)S(1)}, u32[]{:S(2)}, u32[]{:S(2)}) collective-permute-start(bf16[2,1,64,256]{3,2,1,0:T(8,128)(2,1)S(1)} %get-tuple-element.88), channel_id=1, source_target_pairs={{0,2},{1,5},{2,0},{3,7},{4,6},{5,1},{6,4},{7,3},{8,10},{9,13},{10,... | collective-permute-start | bytes 196616 | tf_op jit(solution)/shard_map/ppermute | solution.py:417
  22.6 0.2 collective-permute-done.9.came_ref
  22.8 1.7 %collective-permute-start.12 = (bf16[2,1,64,256]{3,2,1,0:T(8,128)(2,1)S(1)}, bf16[2,1,64,256]{3,2,1,0:T(8,128)(2,1)S(1)}, u32[]{:S(2)}, u32[]{:S(2)}) collective-permute-start(bf16[2,1,64,256]{3,2,1,0:T(8,128)(2,1)S(1)} %shard_map.50), channel_id=1, source_target_pairs={{0,8},{1,9},{2,10},{3,11},{4,12},{5,13},{6,14},{7,15},{8,0},{9,1},... | collective-permute-start | bytes 196616 | tf_op jit(solution)/shard_map/ppermute | solution.py:417
  24.5 1.6 %collective-permute-done.8.came_ref = bf16[2,1,64,256]{3,2,1,0:T(8,128)(2,1)S(1)} collective-permute-done((bf16[2,1,64,256]{3,2,1,0:T(8,128)(2,1)S(1)}, bf16[2,1,64,256]{3,2,1,0:T(8,128)(2,1)S(1)}, u32[]{:S(2)}, u32[]{:S(2)}) %collective-permute-start.8) | collective-permute-done | bytes 65568 | tf_op jit(solution)/shard_map/ppermute | solution.py:417
  26.0 1.8 %collective-permute-start.11 = (bf16[2,1,64,256]{3,2,1,0:T(8,128)(2,1)S(1)}, bf16[2,1,64,256]{3,2,1,0:T(8,128)(2,1)S(1)}, u32[]{:S(2)}, u32[]{:S(2)}) collective-permute-start(bf16[2,1,64,256]{3,2,1,0:T(8,128)(2,1)S(1)} %shard_map.51), channel_id=1, source_target_pairs={{0,8},{1,9},{2,10},{3,11},{4,12},{5,13},{6,14},{7,15},{8,0},{9,1},... | collective-permute-start | bytes 196616 | tf_op jit(solution)/shard_map/ppermute | solution.py:417
  27.8 1.6 %collective-permute-done.6.refs_1_.refs_3_ = bf16[4,2,64,256]{3,2,1,0:T(8,128)(2,1)S(1)} collective-permute-done((bf16[4,2,64,256]{3,2,1,0:T(8,128)(2,1)S(1)}, bf16[4,2,64,256]{3,2,1,0:T(8,128)(2,1)S(1)}, u32[]{:S(2)}, u32[]{:S(2)}) %collective-permute-start.6) | collective-permute-done | bytes 262176 | tf_op jit(solution)/shard_map/ppermute | solution.py:417
  29.4 0.1 shard_map.52
  29.5 0.1 collective-permute-start.10
  29.6 0.0 collective-permute-done.12.refs_1_
  29.6 1.7 %collective-permute-done.11.refs_1_ = bf16[2,1,64,256]{3,2,1,0:T(8,128)(2,1)S(1)} collective-permute-done((bf16[2,1,64,256]{3,2,1,0:T(8,128)(2,1)S(1)}, bf16[2,1,64,256]{3,2,1,0:T(8,128)(2,1)S(1)}, u32[]{:S(2)}, u32[]{:S(2)}) %collective-permute-start.11) | collective-permute-done | bytes 65568 | tf_op jit(solution)/shard_map/ppermute | solution.py:417
  31.4 3.2 %collective-permute-done.10.came_ref = bf16[4,1,64,256]{3,2,1,0:T(8,128)(2,1)S(1)} collective-permute-done((bf16[4,1,64,256]{3,2,1,0:T(8,128)(2,1)S(1)}, bf16[4,1,64,256]{3,2,1,0:T(8,128)(2,1)S(1)}, u32[]{:S(2)}, u32[]{:S(2)}) %collective-permute-start.10) | collective-permute-done | bytes 131104 | tf_op jit(solution)/shard_map/ppermute | solution.py:417
  34.5 0.7 %shard_map.55 = f32[2,2,64,256]{3,2,1,0:T(8,128)} custom-call(bf16[4,1,64,256]{3,2,1,0:T(8,128)(2,1)S(1)} %collective-permute-done.10.came_ref, f32[2,1,64,256]{3,2,1,0:T(8,128)S(1)} %shard_map.53.refs_0_, f32[2,1,64,256]{3,2,1,0:T(8,128)S(1)} %shard_map.54.refs_1_), custom_call_target="tpu_custom_call" | custom-call | tf_op jit(solution)/shard_map/pallas_call | solution.py:19
  (7 shorter events, 0.1 us)
Async XLA Ops:
  0.0 9.5 %collective-permute-start = (bf16[2,8,16,3,2,256]{5,4,3,2,1,0:T(2,128)(2,1)}, bf16[2,8,16,3,2,256]{5,4,3,2,1,0:T(2,128)(2,1)S(1)}, u32[]{:S(2)}, u32[]{:S(2)}) collective-permute-start(bf16[2,8,16,3,2,256]{5,4,3,2,1,0:T(2,128)(2,1)} %bitcast.11), channel_id=1, source_target_pairs={{1,0},{0,1},{3,2},{2,3},{5,4},{4,5},{7,6},{6,7},{9,8},{8,9},{11,10... | collective-permute-start | bytes 2359304 | tf_op jit(solution)/shard_map/ppermute | solution.py:14
  1.8 10.1 %collective-permute-start.3 = (bf16[2,19,3,2,256]{4,3,2,1,0:T(2,128)(2,1)S(1)}, bf16[2,19,3,2,256]{4,3,2,1,0:T(2,128)(2,1)S(1)}, u32[]{:S(2)}, u32[]{:S(2)}) collective-permute-start(bf16[2,19,3,2,256]{4,3,2,1,0:T(2,128)(2,1)S(1)} %get-tuple-element.68), channel_id=1, source_target_pairs={{12,0},{0,4},{4,8},{8,12},{13,1},{1,5},{5,9},{9,13},{14,2},{2,6},{... | collective-permute-start | bytes 350216 | tf_op jit(solution)/shard_map/ppermute | solution.py:14
  4.4 7.4 %collective-permute-start.2 = (bf16[2,16,3,2,256]{4,3,2,1,0:T(2,128)(2,1)S(1)}, bf16[2,16,3,2,256]{4,3,2,1,0:T(2,128)(2,1)S(1)}, u32[]{:S(2)}, u32[]{:S(2)}) collective-permute-start(bf16[2,16,3,2,256]{4,3,2,1,0:T(2,128)(2,1)S(1)} %get-tuple-element.67), channel_id=1, source_target_pairs={{4,0},{8,4},{12,8},{0,12},{5,1},{9,5},{13,9},{1,13},{6,2},{10,6},{... | collective-permute-start | bytes 294920 | tf_op jit(solution)/shard_map/ppermute | solution.py:14
  7.3 5.6 %collective-permute-start.1 = (bf16[8,32,256]{2,1,0:T(8,128)(2,1)S(1)}, bf16[8,32,256]{2,1,0:T(8,128)(2,1)S(1)}, u32[]{:S(2)}, u32[]{:S(2)}) collective-permute-start(bf16[8,32,256]{2,1,0:T(8,128)(2,1)S(1)} %get-tuple-element.66), channel_id=1, source_target_pairs={{2,0},{0,2},{3,1},{1,3},{6,4},{4,6},{7,5},{5,7},{10,8},{8,10},{11,... | collective-permute-start | bytes 393224 | tf_op jit(solution)/shard_map/ppermute | solution.py:14
  12.9 1.4 %collective-permute-start.4 = (bf16[8,24,256]{2,1,0:T(8,128)(2,1)S(1)}, bf16[8,24,256]{2,1,0:T(8,128)(2,1)S(1)}, u32[]{:S(2)}, u32[]{:S(2)}) collective-permute-start(bf16[8,24,256]{2,1,0:T(8,128)(2,1)S(1)} %slice.3), channel_id=1, source_target_pairs={{1,0},{0,1},{3,2},{2,3},{5,4},{4,5},{7,6},{6,7},{9,8},{8,9},{11,10... | collective-permute-start | bytes 294920 | tf_op jit(solution)/shard_map/ppermute | solution.py:14
  13.0 5.0 %collective-permute-start.5 = (bf16[2,2,64,256]{3,2,1,0:T(8,128)(2,1)S(1)}, bf16[2,2,64,256]{3,2,1,0:T(8,128)(2,1)S(1)}, u32[]{:S(2)}, u32[]{:S(2)}) collective-permute-start(bf16[2,2,64,256]{3,2,1,0:T(8,128)(2,1)S(1)} %get-tuple-element.79), channel_id=1, source_target_pairs={{0,4},{1,3},{2,6},{3,1},{4,0},{5,7},{6,2},{7,5},{8,12},{9,11},{10,... | collective-permute-start | bytes 393224 | tf_op jit(solution)/shard_map/ppermute | solution.py:417
  15.6 6.0 %collective-permute-start.7 = (bf16[2,2,64,256]{3,2,1,0:T(8,128)(2,1)S(1)}, bf16[2,2,64,256]{3,2,1,0:T(8,128)(2,1)S(1)}, u32[]{:S(2)}, u32[]{:S(2)}) collective-permute-start(bf16[2,2,64,256]{3,2,1,0:T(8,128)(2,1)S(1)} %get-tuple-element.86), channel_id=1, source_target_pairs={{0,4},{1,3},{2,6},{3,1},{4,0},{5,7},{6,2},{7,5},{8,12},{9,11},{10,... | collective-permute-start | bytes 393224 | tf_op jit(solution)/shard_map/ppermute | solution.py:417
  18.1 4.7 %collective-permute-start.9 = (bf16[2,1,64,256]{3,2,1,0:T(8,128)(2,1)S(1)}, bf16[2,1,64,256]{3,2,1,0:T(8,128)(2,1)S(1)}, u32[]{:S(2)}, u32[]{:S(2)}) collective-permute-start(bf16[2,1,64,256]{3,2,1,0:T(8,128)(2,1)S(1)} %get-tuple-element.89), channel_id=1, source_target_pairs={{0,2},{1,5},{2,0},{3,7},{4,6},{5,1},{6,4},{7,3},{8,10},{9,13},{10,... | collective-permute-start | bytes 196616 | tf_op jit(solution)/shard_map/ppermute | solution.py:417
  20.7 8.7 %collective-permute-start.6 = (bf16[4,2,64,256]{3,2,1,0:T(8,128)(2,1)S(1)}, bf16[4,2,64,256]{3,2,1,0:T(8,128)(2,1)S(1)}, u32[]{:S(2)}, u32[]{:S(2)}) collective-permute-start(bf16[4,2,64,256]{3,2,1,0:T(8,128)(2,1)S(1)} %get-tuple-element.85), channel_id=1, source_target_pairs={{0,4},{1,3},{2,6},{3,1},{4,0},{5,7},{6,2},{7,5},{8,12},{9,11},{10,... | collective-permute-start | bytes 786440 | tf_op jit(solution)/shard_map/ppermute | solution.py:417
  21.7 4.3 %collective-permute-start.8 = (bf16[2,1,64,256]{3,2,1,0:T(8,128)(2,1)S(1)}, bf16[2,1,64,256]{3,2,1,0:T(8,128)(2,1)S(1)}, u32[]{:S(2)}, u32[]{:S(2)}) collective-permute-start(bf16[2,1,64,256]{3,2,1,0:T(8,128)(2,1)S(1)} %get-tuple-element.88), channel_id=1, source_target_pairs={{0,2},{1,5},{2,0},{3,7},{4,6},{5,1},{6,4},{7,3},{8,10},{9,13},{10,... | collective-permute-start | bytes 196616 | tf_op jit(solution)/shard_map/ppermute | solution.py:417
  22.8 6.8 %collective-permute-start.12 = (bf16[2,1,64,256]{3,2,1,0:T(8,128)(2,1)S(1)}, bf16[2,1,64,256]{3,2,1,0:T(8,128)(2,1)S(1)}, u32[]{:S(2)}, u32[]{:S(2)}) collective-permute-start(bf16[2,1,64,256]{3,2,1,0:T(8,128)(2,1)S(1)} %shard_map.50), channel_id=1, source_target_pairs={{0,8},{1,9},{2,10},{3,11},{4,12},{5,13},{6,14},{7,15},{8,0},{9,1},... | collective-permute-start | bytes 196616 | tf_op jit(solution)/shard_map/ppermute | solution.py:417
  26.0 5.3 %collective-permute-start.11 = (bf16[2,1,64,256]{3,2,1,0:T(8,128)(2,1)S(1)}, bf16[2,1,64,256]{3,2,1,0:T(8,128)(2,1)S(1)}, u32[]{:S(2)}, u32[]{:S(2)}) collective-permute-start(bf16[2,1,64,256]{3,2,1,0:T(8,128)(2,1)S(1)} %shard_map.51), channel_id=1, source_target_pairs={{0,8},{1,9},{2,10},{3,11},{4,12},{5,13},{6,14},{7,15},{8,0},{9,1},... | collective-permute-start | bytes 196616 | tf_op jit(solution)/shard_map/ppermute | solution.py:417
  29.5 5.0 %collective-permute-start.10 = (bf16[4,1,64,256]{3,2,1,0:T(8,128)(2,1)S(1)}, bf16[4,1,64,256]{3,2,1,0:T(8,128)(2,1)S(1)}, u32[]{:S(2)}, u32[]{:S(2)}) collective-permute-start(bf16[4,1,64,256]{3,2,1,0:T(8,128)(2,1)S(1)} %get-tuple-element.94), channel_id=1, source_target_pairs={{0,2},{1,5},{2,0},{3,7},{4,6},{5,1},{6,4},{7,3},{8,10},{9,13},{10,... | collective-permute-start | bytes 393224 | tf_op jit(solution)/shard_map/ppermute | solution.py:417

commit v10 on v9

--- a/solution.py
+++ b/solution.py
@@ -567,29 +567,27 @@
         second_kernel, (kept_shape, sent_shape), 8 * project_flops, [lefts, right, right_edge], [total]
     )
     came_second = exchange(sent_second, plan[0])
+    right_edge, kept_second = lax.optimization_barrier((right_edge, kept_second))
+    own_first, sent_own = call(
+        first_own_kernel, (kept_shape, sent_shape), 0, [own, others, begun_first, right_edge], [total]
+    )
+    own_second, sent_own = call(
+        second_own_kernel, (kept_shape, shape(2 * parts, pieces, rows, width)), 0,
+        [lefts, right, right_edge, sent_own], [total],
+    )
+    came_own = exchange(sent_own, plan[0])
+    staying = [(own_first, came_own, slice(0, parts)), (own_second, came_own, slice(parts, 2 * parts))]
     crossing = [(kept_first, came_first), (kept_second, came_second)]
-    after = kept_second
-    staying = None
+    after = own_second
     for step in plan[1:]:
         for d, (kept, came) in enumerate(crossing):
             came, after = lax.optimization_barrier((came, after))
-            crossing[d] = halve([(kept, came, None)], step)
+            crossing[d] = halve([(kept, came, None)], step, 4 * project_flops if d else 0)
             after = crossing[d][0]
-            if staying is None:
-                own_first, sent_own = call(
-                    first_own_kernel, (kept_shape, sent_shape), 0, [own, others, begun_first, right_edge], [total]
-                )
-                right_edge, after = lax.optimization_barrier((right_edge, after))
-                own_second, sent_own = call(
-                    second_own_kernel, (kept_shape, shape(2 * parts, pieces, rows, width)), 0,
-                    [lefts, right, right_edge, sent_own], [total],
-                )
-                came_own = exchange(sent_own, plan[0])
-                staying = [(own_first, came_own, slice(0, parts)), (own_second, came_own, slice(parts, 2 * parts))]
     crossed = []
     for kept, came in crossing:
         came, after = lax.optimization_barrier((came, after))
-        after = call(sum_kernel, pltpu.VMEM(kept.shape, bf16), 8 * project_flops, [kept, came])
+        after = call(sum_kernel, pltpu.VMEM(kept.shape, bf16), 0, [kept, came])
         crossed.append(exchange(after, (top, top)))
     for step in plan[1:]:
         kept, came, which = staying[0]

time: 35.4 us -> 33.2 us (0.938)
  waiting for transfers between devices: 11 us -> 7.22 us
  starting transfers between devices: 15.7 us -> 17.3 us
    ppermute x8, waiting for transfers between devices: 9.67 us -> 5.91 us  [exchange(): return lax.ppermute(block, axes, route)]
    ppermute x8, starting transfers between devices: 8.84 us -> 10.4 us  [exchange(): return lax.ppermute(block, axes, route)]
  transfers between devices with their start and end apart: 13 -> 13, of which waited for: 9 -> 7; matrix products, arithmetic and copies ran while one was open for 0% -> 0% of each run, Pallas kernels for 22% -> 23%
where the time goes in v10:
time: 33.2 us; the launch traced here: 33.1 us
  starting transfers between devices  17.3 us (52%)
  Pallas kernels  8.39 us (25%)
  waiting for transfers between devices  7.22 us (22%)
    ppermute x8, starting transfers between devices, exchange(): return lax.ppermute(block, axes, route)  10.4 us
    pallas_call x19, Pallas kernels, call(): pl.pallas_call(body, out_shape=out_shape, in_specs=[pl.BlockSpec(memory_s...  8.39 us
    ppermute x5, starting transfers between devices, shifted(): return lax.ppermute(block, axis, route)  6.9 us
    ppermute x8, waiting for transfers between devices, exchange(): return lax.ppermute(block, axes, route)  5.91 us
    ppermute x5, waiting for transfers between devices, shifted(): return lax.ppermute(block, axis, route)  1.3 us
  transfers between devices with their start and end apart: 13, of which 7 were waited for; matrix products, arithmetic and copies ran while one was open for 0% of the time, Pallas kernels for 23%

profile of v10, /device:TPU:0, one launch (start us, length us, event | category | flops | bytes accessed | tf_op | source)
XLA Modules:
  0.0 33.1 jit_solution(7718775974456312074)
XLA Ops:
  0.0 0.5 %collective-permute-start = (bf16[2,8,16,3,2,256]{5,4,3,2,1,0:T(2,128)(2,1)}, bf16[2,8,16,3,2,256]{5,4,3,2,1,0:T(2,128)(2,1)S(1)}, u32[]{:S(2)}, u32[]{:S(2)}) collective-permute-start(bf16[2,8,16,3,2,256]{5,4,3,2,1,0:T(2,128)(2,1)} %bitcast.11), channel_id=1, source_target_pairs={{1,0},{0,1},{3,2},{2,3},{5,4},{4,5},{7,6},{6,7},{9,8},{8,9},{11,10... | collective-permute-start | bytes 2359304 | tf_op jit(solution)/shard_map/ppermute | solution.py:14
  0.5 1.4 %shard_map.37 = (bf16[2,16,3,2,256]{4,3,2,1,0:T(2,128)(2,1)S(1)}, bf16[2,19,3,2,256]{4,3,2,1,0:T(2,128)(2,1)S(1)}, bf16[2,8,16,3,2,256]{5,4,3,2,1,0:T(2,128)(2,1...) custom-call(bf16[2,8,16,3,2,256]{5,4,3,2,1,0:T(2,128)(2,1)} %bitcast, ...), custom_call_target="tpu_custom_call" | custom-call | tf_op jit(solution)/shard_map/pallas_call | solution.py:19
  1.8 2.6 %collective-permute-start.3 = (bf16[2,19,3,2,256]{4,3,2,1,0:T(2,128)(2,1)S(1)}, bf16[2,19,3,2,256]{4,3,2,1,0:T(2,128)(2,1)S(1)}, u32[]{:S(2)}, u32[]{:S(2)}) collective-permute-start(bf16[2,19,3,2,256]{4,3,2,1,0:T(2,128)(2,1)S(1)} %get-tuple-element.70), channel_id=1, source_target_pairs={{12,0},{0,4},{4,8},{8,12},{13,1},{1,5},{5,9},{9,13},{14,2},{2,6},{... | collective-permute-start | bytes 350216 | tf_op jit(solution)/shard_map/ppermute | solution.py:14
  4.4 2.1 %collective-permute-start.2 = (bf16[2,16,3,2,256]{4,3,2,1,0:T(2,128)(2,1)S(1)}, bf16[2,16,3,2,256]{4,3,2,1,0:T(2,128)(2,1)S(1)}, u32[]{:S(2)}, u32[]{:S(2)}) collective-permute-start(bf16[2,16,3,2,256]{4,3,2,1,0:T(2,128)(2,1)S(1)} %get-tuple-element.69), channel_id=1, source_target_pairs={{4,0},{8,4},{12,8},{0,12},{5,1},{9,5},{13,9},{1,13},{6,2},{10,6},{... | collective-permute-start | bytes 294920 | tf_op jit(solution)/shard_map/ppermute | solution.py:14
  6.5 0.7 %shard_map.38 = (bf16[8,192,256]{2,1,0:T(8,128)(2,1)S(1)}, bf16[8,32,256]{2,1,0:T(8,128)(2,1)S(1)}, f32[8,8,256]{2,1,0:T(8,128)S(1)}, f32[8,8,256]{2,1,0:T(8,128...) custom-call(bf16[2,8,16,3,2,256]{5,4,3,2,1,0:T(2,128)(2,1)S(1)} %get-tuple-element.54.raw_ref, ...), custom_call_target="tpu_custom_call" | custom-call | tf_op jit(solution)/shard_map/pallas_call | solution.py:19
  7.3 1.7 %collective-permute-start.1 = (bf16[8,32,256]{2,1,0:T(8,128)(2,1)S(1)}, bf16[8,32,256]{2,1,0:T(8,128)(2,1)S(1)}, u32[]{:S(2)}, u32[]{:S(2)}) collective-permute-start(bf16[8,32,256]{2,1,0:T(8,128)(2,1)S(1)} %get-tuple-element.68), channel_id=1, source_target_pairs={{2,0},{0,2},{3,1},{1,3},{6,4},{4,6},{7,5},{5,7},{10,8},{8,10},{11,... | collective-permute-start | bytes 393224 | tf_op jit(solution)/shard_map/ppermute | solution.py:14
  8.9 0.5 %shard_map.39 = (bf16[1152,512]{1,0:T(8,128)(2,1)S(1)}, bf16[256,1536]{1,0:T(8,128)(2,1)S(1)}, bf16[192,192]{1,0:T(8,128)(2,1)S(1)}, f32[192,256]{1,0:T(8,128)S(1)}, f32[192,256]{1,0:T(8,128)S(1)}) custom-call(bf16[8,192,256]{2,1,0:T(8,128)(2,1)S(1)} %get-tuple-element.58.refs_0_, f32[8,8,256]{2,1,0:T(8,128)S(1)} %get-tuple-element.59.refs_1_, ...), custom_call_target="tpu_custom_call" | custom-call | flops 150994944 | tf_op jit(solution)/shard_map/pallas_call | solution.py:19
  9.5 0.0 collective-permute-done.raw_ref
  9.5 0.3 shard_map.40
  9.8 0.6 %shard_map.41.refs_0_ = f32[2,8,192,256]{3,2,1,0:T(8,128)S(1)} custom-call(bf16[8,192,256]{2,1,0:T(8,128)(2,1)S(1)} %get-tuple-element.58.refs_0_, bf16[1,8,192,256]{3,2,1,0:T(8,128)(2,1)S(1)} %bitcast.9, f32[8,8,256]{2,1,0:T(8,128)S(1)} %get-tuple-element.64.refs_2_.refs_3_, f32[8,8,256]{2,1,0:T(8,128)S(1)} %get-tuple-element.65.refs_3_), custom_call_target="tpu_custom_call" | custom-call | flops 150994944 | tf_op jit(solution)/shard_map/pallas_call | solution.py:19
  10.4 0.8 %shard_map.42.refs_8_.begun_ref = f32[2,256,512]{2,1,0:T(8,128)S(1)} custom-call(bf16[256,1536]{1,0:T(8,128)(2,1)S(1)} %get-tuple-element.61.own_ref.refs_6_, bf16[1,256,1536]{2,1,0:T(8,128)(2,1)S(1)} %bitcast.6, bf16[1152,512]{1,0:T(8,128)(2,1)S(1)} %get-tuple-element.66.right_ref), custom_call_target="tpu_custom_call" | custom-call | flops 402653184 | tf_op jit(solution)/shard_map/pallas_call | solution.py:19
  11.2 0.7 %collective-permute-done.2.refs_0_ = bf16[2,16,3,2,256]{4,3,2,1,0:T(2,128)(2,1)S(1)} collective-permute-done((bf16[2,16,3,2,256]{4,3,2,1,0:T(2,128)(2,1)S(1)}, bf16[2,16,3,2,256]{4,3,2,1,0:T(2,128)(2,1)S(1)}, u32[]{:S(2)}, u32[]{:S(2)}) %collective-permute-start.2) | collective-permute-done | bytes 98336 | tf_op jit(solution)/shard_map/ppermute | solution.py:14
  11.9 0.0 collective-permute-done.3.refs_1_
  11.9 0.8 %shard_map.43 = (f32[2,2,64,256]{3,2,1,0:T(8,128)S(1)}, bf16[2,2,64,256]{3,2,1,0:T(8,128)(2,1)S(1)}, bf16[384,512]{1,0:T(8,128)(2,1)S(1)}) custom-call(bf16[2,16,3,2,256]{4,3,2,1,0:T(2,128)(2,1)S(1)} %collective-permute-done.2.refs_0_, bf16[2,19,3,2,256]{4,3,2,1,0:T(2,128)(2,1)S(1)} %collective-permute-done.3.refs_1_, ...), custom_call_target="tpu_custom_call" | custom-call | flops 402653184 | tf_op jit(solution)/shard_map/pallas_call | solution.py:19
  12.7 0.3 collective-permute-done.1.refs_1_
  12.9 0.1 collective-permute-start.4
  13.0 0.9 %collective-permute-start.7 = (bf16[2,2,64,256]{3,2,1,0:T(8,128)(2,1)S(1)}, bf16[2,2,64,256]{3,2,1,0:T(8,128)(2,1)S(1)}, u32[]{:S(2)}, u32[]{:S(2)}) collective-permute-start(bf16[2,2,64,256]{3,2,1,0:T(8,128)(2,1)S(1)} %get-tuple-element.87), channel_id=1, source_target_pairs={{0,4},{1,3},{2,6},{3,1},{4,0},{5,7},{6,2},{7,5},{8,12},{9,11},{10,... | collective-permute-start | bytes 393224 | tf_op jit(solution)/shard_map/ppermute | solution.py:417
  14.0 0.3 %collective-permute-done.4 = bf16[8,24,256]{2,1,0:T(8,128)(2,1)S(1)} collective-permute-done((bf16[8,24,256]{2,1,0:T(8,128)(2,1)S(1)}, bf16[8,24,256]{2,1,0:T(8,128)(2,1)S(1)}, u32[]{:S(2)}, u32[]{:S(2)}) %collective-permute-start.4) | collective-permute-done | bytes 98336 | tf_op jit(solution)/shard_map/ppermute | solution.py:14
  14.3 0.6 %shard_map.44.lefts_ref = bf16[2,256,1536]{2,1,0:T(8,128)(2,1)S(1)} custom-call(f32[2,8,192,256]{3,2,1,0:T(8,128)S(1)} %shard_map.41.refs_0_, bf16[8,32,256]{2,1,0:T(8,128)(2,1)S(1)} %collective-permute-done.1.refs_1_, bf16[1,8,24,256]{3,2,1,0:T(8,128)(2,1)S(1)} %bitcast.10, f32[8,8,256]{2,1,0:T(8,128)S(1)} %get-tuple-element.64.refs_2_.refs_3_), custom_call_target="tpu_custom_call" | custom-call | flops 150994944 | tf_op jit(solution)/shard_map/pallas_call | solution.py:19
  15.0 0.7 %shard_map.45 = (f32[2,2,64,256]{3,2,1,0:T(8,128)S(1)}, bf16[2,2,64,256]{3,2,1,0:T(8,128)(2,1)S(1)}) custom-call(bf16[2,256,1536]{2,1,0:T(8,128)(2,1)S(1)} %shard_map.44.lefts_ref, bf16[1152,512]{1,0:T(8,128)(2,1)S(1)} %get-tuple-element.66.right_ref, bf16[384,512]{1,0:T(8,128)(2,1)S(1)} %get-tuple-element.80.edge_ref.right_ref), custom_call_target="tpu_custom_call" | custom-call | flops 3221225472 | tf_op jit(solution)/shard_map/pallas_call | solution.py:19
  15.6 0.9 %collective-permute-start.6 = (bf16[2,2,64,256]{3,2,1,0:T(8,128)(2,1)S(1)}, bf16[2,2,64,256]{3,2,1,0:T(8,128)(2,1)S(1)}, u32[]{:S(2)}, u32[]{:S(2)}) collective-permute-start(bf16[2,2,64,256]{3,2,1,0:T(8,128)(2,1)S(1)} %get-tuple-element.85), channel_id=1, source_target_pairs={{0,4},{1,3},{2,6},{3,1},{4,0},{5,7},{6,2},{7,5},{8,12},{9,11},{10,... | collective-permute-start | bytes 393224 | tf_op jit(solution)/shard_map/ppermute | solution.py:417
  16.6 0.4 %shard_map.46 = (f32[2,2,64,256]{3,2,1,0:T(8,128)S(1)}, bf16[2,2,64,256]{3,2,1,0:T(8,128)(2,1)S(1)}) custom-call(bf16[256,1536]{1,0:T(8,128)(2,1)S(1)} %get-tuple-element.61.own_ref.refs_6_, bf16[1,256,1536]{2,1,0:T(8,128)(2,1)S(1)} %bitcast.8, f32[2,256,512]{2,1,0:T(8,128)S(1)} %shard_map.42.refs_8_.begun_ref, ...), custom_call_target="tpu_custom_call" | custom-call | tf_op jit(solution)/shard_map/pallas_call | solution.py:19
  17.0 0.7 %shard_map.47 = (f32[2,2,64,256]{3,2,1,0:T(8,128)S(1)}, bf16[4,2,64,256]{3,2,1,0:T(8,128)(2,1)S(1)}) custom-call(bf16[2,256,1536]{2,1,0:T(8,128)(2,1)S(1)} %shard_map.44.lefts_ref, bf16[1152,512]{1,0:T(8,128)(2,1)S(1)} %get-tuple-element.66.right_ref, bf16[384,512]{1,0:T(8,128)(2,1)S(1)} %get-tuple-element.80.edge_ref.right_ref, ...), custom_call_target="tpu_custom_call" | custom-call | tf_op jit(solution)/shard_map/pallas_call | solution.py:19
  17.6 1.2 %collective-permute-start.5 = (bf16[4,2,64,256]{3,2,1,0:T(8,128)(2,1)S(1)}, bf16[4,2,64,256]{3,2,1,0:T(8,128)(2,1)S(1)}, u32[]{:S(2)}, u32[]{:S(2)}) collective-permute-start(bf16[4,2,64,256]{3,2,1,0:T(8,128)(2,1)S(1)} %get-tuple-element.83), channel_id=1, source_target_pairs={{0,4},{1,3},{2,6},{3,1},{4,0},{5,7},{6,2},{7,5},{8,12},{9,11},{10,... | collective-permute-start | bytes 786440 | tf_op jit(solution)/shard_map/ppermute | solution.py:417
  18.9 0.0 collective-permute-done.7.refs_1_
  18.9 1.6 %collective-permute-start.9 = (bf16[2,1,64,256]{3,2,1,0:T(8,128)(2,1)S(1)}, bf16[2,1,64,256]{3,2,1,0:T(8,128)(2,1)S(1)}, u32[]{:S(2)}, u32[]{:S(2)}) collective-permute-start(bf16[2,1,64,256]{3,2,1,0:T(8,128)(2,1)S(1)} %get-tuple-element.94), channel_id=1, source_target_pairs={{0,2},{1,5},{2,0},{3,7},{4,6},{5,1},{6,4},{7,3},{8,10},{9,13},{10,... | collective-permute-start | bytes 196616 | tf_op jit(solution)/shard_map/ppermute | solution.py:417
  20.5 0.2 collective-permute-done.6.refs_1_
  20.7 1.6 %collective-permute-start.8 = (bf16[2,1,64,256]{3,2,1,0:T(8,128)(2,1)S(1)}, bf16[2,1,64,256]{3,2,1,0:T(8,128)(2,1)S(1)}, u32[]{:S(2)}, u32[]{:S(2)}) collective-permute-start(bf16[2,1,64,256]{3,2,1,0:T(8,128)(2,1)S(1)} %get-tuple-element.93), channel_id=1, source_target_pairs={{0,2},{1,5},{2,0},{3,7},{4,6},{5,1},{6,4},{7,3},{8,10},{9,13},{10,... | collective-permute-start | bytes 196616 | tf_op jit(solution)/shard_map/ppermute | solution.py:417
  22.3 1.7 %collective-permute-done.9.came_ref = bf16[2,1,64,256]{3,2,1,0:T(8,128)(2,1)S(1)} collective-permute-done((bf16[2,1,64,256]{3,2,1,0:T(8,128)(2,1)S(1)}, bf16[2,1,64,256]{3,2,1,0:T(8,128)(2,1)S(1)}, u32[]{:S(2)}, u32[]{:S(2)}) %collective-permute-start.9) | collective-permute-done | bytes 65568 | tf_op jit(solution)/shard_map/ppermute | solution.py:417
  24.0 1.4 %collective-permute-start.12 = (bf16[2,1,64,256]{3,2,1,0:T(8,128)(2,1)S(1)}, bf16[2,1,64,256]{3,2,1,0:T(8,128)(2,1)S(1)}, u32[]{:S(2)}, u32[]{:S(2)}) collective-permute-start(bf16[2,1,64,256]{3,2,1,0:T(8,128)(2,1)S(1)} %shard_map.50), channel_id=1, source_target_pairs={{0,8},{1,9},{2,10},{3,11},{4,12},{5,13},{6,14},{7,15},{8,0},{9,1},... | collective-permute-start | bytes 196616 | tf_op jit(solution)/shard_map/ppermute | solution.py:417
  25.4 0.0 collective-permute-done.8.came_ref
  25.5 1.6 %collective-permute-start.11 = (bf16[2,1,64,256]{3,2,1,0:T(8,128)(2,1)S(1)}, bf16[2,1,64,256]{3,2,1,0:T(8,128)(2,1)S(1)}, u32[]{:S(2)}, u32[]{:S(2)}) collective-permute-start(bf16[2,1,64,256]{3,2,1,0:T(8,128)(2,1)S(1)} %shard_map.51), channel_id=1, source_target_pairs={{0,8},{1,9},{2,10},{3,11},{4,12},{5,13},{6,14},{7,15},{8,0},{9,1},... | collective-permute-start | bytes 196616 | tf_op jit(solution)/shard_map/ppermute | solution.py:417
  27.1 0.0 collective-permute-done.5.refs_1_.refs_3_
  27.1 0.1 shard_map.52
  27.2 1.2 %collective-permute-start.10 = (bf16[4,1,64,256]{3,2,1,0:T(8,128)(2,1)S(1)}, bf16[4,1,64,256]{3,2,1,0:T(8,128)(2,1)S(1)}, u32[]{:S(2)}, u32[]{:S(2)}) collective-permute-start(bf16[4,1,64,256]{3,2,1,0:T(8,128)(2,1)S(1)} %get-tuple-element.98), channel_id=1, source_target_pairs={{0,2},{1,5},{2,0},{3,7},{4,6},{5,1},{6,4},{7,3},{8,10},{9,13},{10,... | collective-permute-start | bytes 393224 | tf_op jit(solution)/shard_map/ppermute | solution.py:417
  28.3 2.7 %collective-permute-done.12.refs_1_ = bf16[2,1,64,256]{3,2,1,0:T(8,128)(2,1)S(1)} collective-permute-done((bf16[2,1,64,256]{3,2,1,0:T(8,128)(2,1)S(1)}, bf16[2,1,64,256]{3,2,1,0:T(8,128)(2,1)S(1)}, u32[]{:S(2)}, u32[]{:S(2)}) %collective-permute-start.12) | collective-permute-done | bytes 65568 | tf_op jit(solution)/shard_map/ppermute | solution.py:417
  31.1 1.2 %collective-permute-done.11.refs_1_ = bf16[2,1,64,256]{3,2,1,0:T(8,128)(2,1)S(1)} collective-permute-done((bf16[2,1,64,256]{3,2,1,0:T(8,128)(2,1)S(1)}, bf16[2,1,64,256]{3,2,1,0:T(8,128)(2,1)S(1)}, u32[]{:S(2)}, u32[]{:S(2)}) %collective-permute-start.11) | collective-permute-done | bytes 65568 | tf_op jit(solution)/shard_map/ppermute | solution.py:417
  32.3 0.0 collective-permute-done.10.came_ref
  32.4 0.7 %shard_map.55 = f32[2,2,64,256]{3,2,1,0:T(8,128)} custom-call(bf16[4,1,64,256]{3,2,1,0:T(8,128)(2,1)S(1)} %collective-permute-done.10.came_ref, f32[2,1,64,256]{3,2,1,0:T(8,128)S(1)} %shard_map.53.refs_0_, f32[2,1,64,256]{3,2,1,0:T(8,128)S(1)} %shard_map.54.refs_1_), custom_call_target="tpu_custom_call" | custom-call | tf_op jit(solution)/shard_map/pallas_call | solution.py:19
  (7 shorter events, 0.1 us)
Async XLA Ops:
  0.0 9.5 %collective-permute-start = (bf16[2,8,16,3,2,256]{5,4,3,2,1,0:T(2,128)(2,1)}, bf16[2,8,16,3,2,256]{5,4,3,2,1,0:T(2,128)(2,1)S(1)}, u32[]{:S(2)}, u32[]{:S(2)}) collective-permute-start(bf16[2,8,16,3,2,256]{5,4,3,2,1,0:T(2,128)(2,1)} %bitcast.11), channel_id=1, source_target_pairs={{1,0},{0,1},{3,2},{2,3},{5,4},{4,5},{7,6},{6,7},{9,8},{8,9},{11,10... | collective-permute-start | bytes 2359304 | tf_op jit(solution)/shard_map/ppermute | solution.py:14
  1.8 10.1 %collective-permute-start.3 = (bf16[2,19,3,2,256]{4,3,2,1,0:T(2,128)(2,1)S(1)}, bf16[2,19,3,2,256]{4,3,2,1,0:T(2,128)(2,1)S(1)}, u32[]{:S(2)}, u32[]{:S(2)}) collective-permute-start(bf16[2,19,3,2,256]{4,3,2,1,0:T(2,128)(2,1)S(1)} %get-tuple-element.70), channel_id=1, source_target_pairs={{12,0},{0,4},{4,8},{8,12},{13,1},{1,5},{5,9},{9,13},{14,2},{2,6},{... | collective-permute-start | bytes 350216 | tf_op jit(solution)/shard_map/ppermute | solution.py:14
  4.4 7.4 %collective-permute-start.2 = (bf16[2,16,3,2,256]{4,3,2,1,0:T(2,128)(2,1)S(1)}, bf16[2,16,3,2,256]{4,3,2,1,0:T(2,128)(2,1)S(1)}, u32[]{:S(2)}, u32[]{:S(2)}) collective-permute-start(bf16[2,16,3,2,256]{4,3,2,1,0:T(2,128)(2,1)S(1)} %get-tuple-element.69), channel_id=1, source_target_pairs={{4,0},{8,4},{12,8},{0,12},{5,1},{9,5},{13,9},{1,13},{6,2},{10,6},{... | collective-permute-start | bytes 294920 | tf_op jit(solution)/shard_map/ppermute | solution.py:14
  7.3 5.6 %collective-permute-start.1 = (bf16[8,32,256]{2,1,0:T(8,128)(2,1)S(1)}, bf16[8,32,256]{2,1,0:T(8,128)(2,1)S(1)}, u32[]{:S(2)}, u32[]{:S(2)}) collective-permute-start(bf16[8,32,256]{2,1,0:T(8,128)(2,1)S(1)} %get-tuple-element.68), channel_id=1, source_target_pairs={{2,0},{0,2},{3,1},{1,3},{6,4},{4,6},{7,5},{5,7},{10,8},{8,10},{11,... | collective-permute-start | bytes 393224 | tf_op jit(solution)/shard_map/ppermute | solution.py:14
  12.9 1.4 %collective-permute-start.4 = (bf16[8,24,256]{2,1,0:T(8,128)(2,1)S(1)}, bf16[8,24,256]{2,1,0:T(8,128)(2,1)S(1)}, u32[]{:S(2)}, u32[]{:S(2)}) collective-permute-start(bf16[8,24,256]{2,1,0:T(8,128)(2,1)S(1)} %slice.3), channel_id=1, source_target_pairs={{1,0},{0,1},{3,2},{2,3},{5,4},{4,5},{7,6},{6,7},{9,8},{8,9},{11,10... | collective-permute-start | bytes 294920 | tf_op jit(solution)/shard_map/ppermute | solution.py:14
  13.0 5.9 %collective-permute-start.7 = (bf16[2,2,64,256]{3,2,1,0:T(8,128)(2,1)S(1)}, bf16[2,2,64,256]{3,2,1,0:T(8,128)(2,1)S(1)}, u32[]{:S(2)}, u32[]{:S(2)}) collective-permute-start(bf16[2,2,64,256]{3,2,1,0:T(8,128)(2,1)S(1)} %get-tuple-element.87), channel_id=1, source_target_pairs={{0,4},{1,3},{2,6},{3,1},{4,0},{5,7},{6,2},{7,5},{8,12},{9,11},{10,... | collective-permute-start | bytes 393224 | tf_op jit(solution)/shard_map/ppermute | solution.py:417
  15.6 5.0 %collective-permute-start.6 = (bf16[2,2,64,256]{3,2,1,0:T(8,128)(2,1)S(1)}, bf16[2,2,64,256]{3,2,1,0:T(8,128)(2,1)S(1)}, u32[]{:S(2)}, u32[]{:S(2)}) collective-permute-start(bf16[2,2,64,256]{3,2,1,0:T(8,128)(2,1)S(1)} %get-tuple-element.85), channel_id=1, source_target_pairs={{0,4},{1,3},{2,6},{3,1},{4,0},{5,7},{6,2},{7,5},{8,12},{9,11},{10,... | collective-permute-start | bytes 393224 | tf_op jit(solution)/shard_map/ppermute | solution.py:417
  17.6 9.5 %collective-permute-start.5 = (bf16[4,2,64,256]{3,2,1,0:T(8,128)(2,1)S(1)}, bf16[4,2,64,256]{3,2,1,0:T(8,128)(2,1)S(1)}, u32[]{:S(2)}, u32[]{:S(2)}) collective-permute-start(bf16[4,2,64,256]{3,2,1,0:T(8,128)(2,1)S(1)} %get-tuple-element.83), channel_id=1, source_target_pairs={{0,4},{1,3},{2,6},{3,1},{4,0},{5,7},{6,2},{7,5},{8,12},{9,11},{10,... | collective-permute-start | bytes 786440 | tf_op jit(solution)/shard_map/ppermute | solution.py:417
  18.9 5.1 %collective-permute-start.9 = (bf16[2,1,64,256]{3,2,1,0:T(8,128)(2,1)S(1)}, bf16[2,1,64,256]{3,2,1,0:T(8,128)(2,1)S(1)}, u32[]{:S(2)}, u32[]{:S(2)}) collective-permute-start(bf16[2,1,64,256]{3,2,1,0:T(8,128)(2,1)S(1)} %get-tuple-element.94), channel_id=1, source_target_pairs={{0,2},{1,5},{2,0},{3,7},{4,6},{5,1},{6,4},{7,3},{8,10},{9,13},{10,... | collective-permute-start | bytes 196616 | tf_op jit(solution)/shard_map/ppermute | solution.py:417
  20.7 4.7 %collective-permute-start.8 = (bf16[2,1,64,256]{3,2,1,0:T(8,128)(2,1)S(1)}, bf16[2,1,64,256]{3,2,1,0:T(8,128)(2,1)S(1)}, u32[]{:S(2)}, u32[]{:S(2)}) collective-permute-start(bf16[2,1,64,256]{3,2,1,0:T(8,128)(2,1)S(1)} %get-tuple-element.93), channel_id=1, source_target_pairs={{0,2},{1,5},{2,0},{3,7},{4,6},{5,1},{6,4},{7,3},{8,10},{9,13},{10,... | collective-permute-start | bytes 196616 | tf_op jit(solution)/shard_map/ppermute | solution.py:417
  24.0 7.1 %collective-permute-start.12 = (bf16[2,1,64,256]{3,2,1,0:T(8,128)(2,1)S(1)}, bf16[2,1,64,256]{3,2,1,0:T(8,128)(2,1)S(1)}, u32[]{:S(2)}, u32[]{:S(2)}) collective-permute-start(bf16[2,1,64,256]{3,2,1,0:T(8,128)(2,1)S(1)} %shard_map.50), channel_id=1, source_target_pairs={{0,8},{1,9},{2,10},{3,11},{4,12},{5,13},{6,14},{7,15},{8,0},{9,1},... | collective-permute-start | bytes 196616 | tf_op jit(solution)/shard_map/ppermute | solution.py:417
  25.5 6.9 %collective-permute-start.11 = (bf16[2,1,64,256]{3,2,1,0:T(8,128)(2,1)S(1)}, bf16[2,1,64,256]{3,2,1,0:T(8,128)(2,1)S(1)}, u32[]{:S(2)}, u32[]{:S(2)}) collective-permute-start(bf16[2,1,64,256]{3,2,1,0:T(8,128)(2,1)S(1)} %shard_map.51), channel_id=1, source_target_pairs={{0,8},{1,9},{2,10},{3,11},{4,12},{5,13},{6,14},{7,15},{8,0},{9,1},... | collective-permute-start | bytes 196616 | tf_op jit(solution)/shard_map/ppermute | solution.py:417
  27.2 5.2 %collective-permute-start.10 = (bf16[4,1,64,256]{3,2,1,0:T(8,128)(2,1)S(1)}, bf16[4,1,64,256]{3,2,1,0:T(8,128)(2,1)S(1)}, u32[]{:S(2)}, u32[]{:S(2)}) collective-permute-start(bf16[4,1,64,256]{3,2,1,0:T(8,128)(2,1)S(1)} %get-tuple-element.98), channel_id=1, source_target_pairs={{0,2},{1,5},{2,0},{3,7},{4,6},{5,1},{6,4},{7,3},{8,10},{9,13},{10,... | collective-permute-start | bytes 393224 | tf_op jit(solution)/shard_map/ppermute | solution.py:417

commit v11 on v10

--- a/solution.py
+++ b/solution.py
@@ -363,8 +363,9 @@
             part_ref[k + 1, place] = dot(matrix, others_ref[k, place])
 
 
-def move_y_kernel(sites, zs, part_ref, near_ref, far_ref, ahead_ref, turned_ref, field_ref):
-    groups, planes, depth, width = part_ref.shape
+def move_y(kind, sites, zs, part_ref, near_ref, far_ref, ahead_ref, turned_ref, field_ref):
+    _, planes, depth, width = part_ref.shape
+    half = half_of(kind)
     row_size = depth // sites * zs
     tail = 128
     head = ahead_ref.shape[2] - tail
@@ -380,29 +381,22 @@
         past = near_ref[x, 2 * row_size : 2 * row_size + 8, :tail].astype(jnp.float32)
         matrix = site_matrix([(ahead_ref[x, :, head:], to_next), (past, to_last)], depth // sites)
         place = place_of(x, planes)
-        for k in range(groups):
-            edge = near_ref[x, : 2 * row_size] if k == 0 else far_ref[k - 1, x]
-            moved = part_ref[k, place] + dot(matrix, jnp.concatenate([above, edge, below], axis=0))
-            field_ref[k, place] = moved.astype(jnp.bfloat16)
-    for k in range(groups):
-        turned_ref[k] = field_ref[k].reshape(planes * depth, width).T
-
-
-def second_share(kind, lefts_ref, right_ref, edge_ref, keep_ref, send_ref, total_ref):
-    half = half_of(kind)
+        edge = jnp.where(half == 0, near_ref[x, : 2 * row_size], far_ref[0, x])
+        moved = part_ref[half, place] + dot(matrix, jnp.concatenate([above, edge, below], axis=0))
+        field_ref[place] = moved.astype(jnp.bfloat16)
+    turned_ref[...] = field_ref[...].reshape(planes * depth, width).T
+
+
+def second_share(left_ref, right_ref, edge_ref, keep_ref, send_ref, total_ref):
     inner = right_ref.shape[0]
-    total = dot(lefts_ref[half, :, :inner], right_ref[...]) + dot(lefts_ref[half, :, inner:], edge_ref[...])
+    total = dot(left_ref[:, :inner], right_ref[...]) + dot(left_ref[:, inner:], edge_ref[...])
     share(total, keep_ref, send_ref, total_ref)
 
 
-def second_kernel(lefts_ref, right_ref, edge_ref, keep_ref, send_ref, total_ref):
-    second_share(0, lefts_ref, right_ref, edge_ref, keep_ref, send_ref, total_ref)
-
-
-def second_own_kernel(lefts_ref, right_ref, edge_ref, first_ref, keep_ref, send_ref, total_ref):
+def second_own_kernel(left_ref, right_ref, edge_ref, first_ref, keep_ref, send_ref, total_ref):
     parts = first_ref.shape[0]
     send_ref[:parts] = first_ref[...]
-    second_share(1, lefts_ref, right_ref, edge_ref, keep_ref, send_ref.at[parts:], total_ref)
+    second_share(left_ref, right_ref, edge_ref, keep_ref, send_ref.at[parts:], total_ref)
 
 
 def exchange(block, step):
@@ -527,8 +521,11 @@
     def begin_y(*refs):
         begin_y_kernel(sites, zs, *refs)
 
-    def move_y(*refs):
-        move_y_kernel(sites, zs, *refs)
+    def move_cross(*refs):
+        move_y(0, sites, zs, *refs)
+
+    def move_own(*refs):
+        move_y(1, sites, zs, *refs)
 
     right, own, matrix, ahead_part, back_part = call(
         inner,
@@ -558,22 +555,21 @@
     near, right_edge = lax.optimization_barrier((near, right_edge))
     near_rows = near[:, : 2 * row_size]
     far = jnp.stack([shifted(near_rows, "ma", -step) for step in range(1, groups)])
-    lefts = call(
-        move_y, shape(groups, width, planes * depth), 2 * step_flops,
-        [part_y, near, far, ahead_y],
-        [pltpu.VMEM((groups,) + field_shape.shape, bf16)],
-    )
+    move_operands = [part_y, near, far, ahead_y]
+    move_scratch = [pltpu.VMEM(field_shape.shape, bf16)]
+    left = call(move_cross, turned_shape, step_flops, move_operands, move_scratch)
     kept_second, sent_second = call(
-        second_kernel, (kept_shape, sent_shape), 8 * project_flops, [lefts, right, right_edge], [total]
+        second_share, (kept_shape, sent_shape), 8 * project_flops, [left, right, right_edge], [total]
     )
     came_second = exchange(sent_second, plan[0])
-    right_edge, kept_second = lax.optimization_barrier((right_edge, kept_second))
+    right_edge, part_y, kept_second = lax.optimization_barrier((right_edge, part_y, kept_second))
+    left = call(move_own, turned_shape, 0, [part_y] + move_operands[1:], move_scratch)
     own_first, sent_own = call(
         first_own_kernel, (kept_shape, sent_shape), 0, [own, others, begun_first, right_edge], [total]
     )
     own_second, sent_own = call(
         second_own_kernel, (kept_shape, shape(2 * parts, pieces, rows, width)), 0,
-        [lefts, right, right_edge, sent_own], [total],
+        [left, right, right_edge, sent_own], [total],
     )
     came_own = exchange(sent_own, plan[0])
     staying = [(own_first, came_own, slice(0, parts)), (own_second, came_own, slice(parts, 2 * parts))]

time: 33.2 us -> 33.3 us (level)
    pallas_call x19 -> x20, Pallas kernels: 8.39 us -> 8.64 us  [call(): pl.pallas_call(body, out_shape=out_shape, in_specs=[pl.BlockSpec(memory_s...]
  transfers between devices with their start and end apart: 13 -> 13, of which waited for: 7 -> 7; matrix products, arithmetic and copies ran while one was open for 0% -> 0% of each run, Pallas kernels for 23% -> 24%
where the time goes in v11:
time: 33.3 us; the launch traced here: 33.2 us
  starting transfers between devices  17.1 us (51%)
  Pallas kernels  8.64 us (26%)
  waiting for transfers between devices  7.3 us (22%)
    ppermute x8, starting transfers between devices, exchange(): return lax.ppermute(block, axes, route)  10.2 us
    pallas_call x20, Pallas kernels, call(): pl.pallas_call(body, out_shape=out_shape, in_specs=[pl.BlockSpec(memory_s...  8.64 us
    ppermute x5, starting transfers between devices, shifted(): return lax.ppermute(block, axis, route)  6.9 us
    ppermute x8, waiting for transfers between devices, exchange(): return lax.ppermute(block, axes, route)  6.02 us
    ppermute x5, waiting for transfers between devices, shifted(): return lax.ppermute(block, axis, route)  1.29 us
  transfers between devices with their start and end apart: 13, of which 7 were waited for; matrix products, arithmetic and copies ran while one was open for 0% of the time, Pallas kernels for 24%

profile of v11, /device:TPU:0, one launch (start us, length us, event | category | flops | bytes accessed | tf_op | source)
XLA Modules:
  0.0 33.2 jit_solution(7031757555121318072)
XLA Ops:
  0.0 0.5 %collective-permute-start = (bf16[2,8,16,3,2,256]{5,4,3,2,1,0:T(2,128)(2,1)}, bf16[2,8,16,3,2,256]{5,4,3,2,1,0:T(2,128)(2,1)S(1)}, u32[]{:S(2)}, u32[]{:S(2)}) collective-permute-start(bf16[2,8,16,3,2,256]{5,4,3,2,1,0:T(2,128)(2,1)} %bitcast.12), channel_id=1, source_target_pairs={{1,0},{0,1},{3,2},{2,3},{5,4},{4,5},{7,6},{6,7},{9,8},{8,9},{11,10... | collective-permute-start | bytes 2359304 | tf_op jit(solution)/shard_map/ppermute | solution.py:14
  0.5 1.4 %shard_map.37 = (bf16[2,16,3,2,256]{4,3,2,1,0:T(2,128)(2,1)S(1)}, bf16[2,19,3,2,256]{4,3,2,1,0:T(2,128)(2,1)S(1)}, bf16[2,8,16,3,2,256]{5,4,3,2,1,0:T(2,128)(2,1...) custom-call(bf16[2,8,16,3,2,256]{5,4,3,2,1,0:T(2,128)(2,1)} %bitcast, ...), custom_call_target="tpu_custom_call" | custom-call | tf_op jit(solution)/shard_map/pallas_call | solution.py:19
  1.8 2.6 %collective-permute-start.3 = (bf16[2,19,3,2,256]{4,3,2,1,0:T(2,128)(2,1)S(1)}, bf16[2,19,3,2,256]{4,3,2,1,0:T(2,128)(2,1)S(1)}, u32[]{:S(2)}, u32[]{:S(2)}) collective-permute-start(bf16[2,19,3,2,256]{4,3,2,1,0:T(2,128)(2,1)S(1)} %get-tuple-element.71), channel_id=1, source_target_pairs={{12,0},{0,4},{4,8},{8,12},{13,1},{1,5},{5,9},{9,13},{14,2},{2,6},{... | collective-permute-start | bytes 350216 | tf_op jit(solution)/shard_map/ppermute | solution.py:14
  4.4 2.1 %collective-permute-start.2 = (bf16[2,16,3,2,256]{4,3,2,1,0:T(2,128)(2,1)S(1)}, bf16[2,16,3,2,256]{4,3,2,1,0:T(2,128)(2,1)S(1)}, u32[]{:S(2)}, u32[]{:S(2)}) collective-permute-start(bf16[2,16,3,2,256]{4,3,2,1,0:T(2,128)(2,1)S(1)} %get-tuple-element.70), channel_id=1, source_target_pairs={{4,0},{8,4},{12,8},{0,12},{5,1},{9,5},{13,9},{1,13},{6,2},{10,6},{... | collective-permute-start | bytes 294920 | tf_op jit(solution)/shard_map/ppermute | solution.py:14
  6.5 0.7 %shard_map.38 = (bf16[8,192,256]{2,1,0:T(8,128)(2,1)S(1)}, bf16[8,32,256]{2,1,0:T(8,128)(2,1)S(1)}, f32[8,8,256]{2,1,0:T(8,128)S(1)}, f32[8,8,256]{2,1,0:T(8,128...) custom-call(bf16[2,8,16,3,2,256]{5,4,3,2,1,0:T(2,128)(2,1)S(1)} %get-tuple-element.55.raw_ref, ...), custom_call_target="tpu_custom_call" | custom-call | tf_op jit(solution)/shard_map/pallas_call | solution.py:19
  7.3 1.7 %collective-permute-start.1 = (bf16[8,32,256]{2,1,0:T(8,128)(2,1)S(1)}, bf16[8,32,256]{2,1,0:T(8,128)(2,1)S(1)}, u32[]{:S(2)}, u32[]{:S(2)}) collective-permute-start(bf16[8,32,256]{2,1,0:T(8,128)(2,1)S(1)} %get-tuple-element.69), channel_id=1, source_target_pairs={{2,0},{0,2},{3,1},{1,3},{6,4},{4,6},{7,5},{5,7},{10,8},{8,10},{11,... | collective-permute-start | bytes 393224 | tf_op jit(solution)/shard_map/ppermute | solution.py:14
  8.9 0.5 %shard_map.39 = (bf16[1152,512]{1,0:T(8,128)(2,1)S(1)}, bf16[256,1536]{1,0:T(8,128)(2,1)S(1)}, bf16[192,192]{1,0:T(8,128)(2,1)S(1)}, f32[192,256]{1,0:T(8,128)S(1)}, f32[192,256]{1,0:T(8,128)S(1)}) custom-call(bf16[8,192,256]{2,1,0:T(8,128)(2,1)S(1)} %get-tuple-element.59.refs_0_, f32[8,8,256]{2,1,0:T(8,128)S(1)} %get-tuple-element.60.refs_1_, ...), custom_call_target="tpu_custom_call" | custom-call | flops 150994944 | tf_op jit(solution)/shard_map/pallas_call | solution.py:19
  9.5 0.0 collective-permute-done.raw_ref
  9.5 0.3 shard_map.40
  9.8 0.6 %shard_map.41.refs_0_ = f32[2,8,192,256]{3,2,1,0:T(8,128)S(1)} custom-call(bf16[8,192,256]{2,1,0:T(8,128)(2,1)S(1)} %get-tuple-element.59.refs_0_, bf16[1,8,192,256]{3,2,1,0:T(8,128)(2,1)S(1)} %bitcast.9, f32[8,8,256]{2,1,0:T(8,128)S(1)} %get-tuple-element.65.refs_2_.refs_3_, f32[8,8,256]{2,1,0:T(8,128)S(1)} %get-tuple-element.66.refs_3_), custom_call_target="tpu_custom_call" | custom-call | flops 150994944 | tf_op jit(solution)/shard_map/pallas_call | solution.py:19
  10.4 0.8 %shard_map.42.refs_8_.begun_ref = f32[2,256,512]{2,1,0:T(8,128)S(1)} custom-call(bf16[256,1536]{1,0:T(8,128)(2,1)S(1)} %get-tuple-element.62.own_ref.refs_6_, bf16[1,256,1536]{2,1,0:T(8,128)(2,1)S(1)} %bitcast.6, bf16[1152,512]{1,0:T(8,128)(2,1)S(1)} %get-tuple-element.67.right_ref), custom_call_target="tpu_custom_call" | custom-call | flops 402653184 | tf_op jit(solution)/shard_map/pallas_call | solution.py:19
  11.2 0.7 %collective-permute-done.2.refs_0_ = bf16[2,16,3,2,256]{4,3,2,1,0:T(2,128)(2,1)S(1)} collective-permute-done((bf16[2,16,3,2,256]{4,3,2,1,0:T(2,128)(2,1)S(1)}, bf16[2,16,3,2,256]{4,3,2,1,0:T(2,128)(2,1)S(1)}, u32[]{:S(2)}, u32[]{:S(2)}) %collective-permute-start.2) | collective-permute-done | bytes 98336 | tf_op jit(solution)/shard_map/ppermute | solution.py:14
  11.9 0.0 collective-permute-done.3.refs_1_
  11.9 0.8 %shard_map.43 = (f32[2,2,64,256]{3,2,1,0:T(8,128)S(1)}, bf16[2,2,64,256]{3,2,1,0:T(8,128)(2,1)S(1)}, bf16[384,512]{1,0:T(8,128)(2,1)S(1)}) custom-call(bf16[2,16,3,2,256]{4,3,2,1,0:T(2,128)(2,1)S(1)} %collective-permute-done.2.refs_0_, bf16[2,19,3,2,256]{4,3,2,1,0:T(2,128)(2,1)S(1)} %collective-permute-done.3.refs_1_, ...), custom_call_target="tpu_custom_call" | custom-call | flops 402653184 | tf_op jit(solution)/shard_map/pallas_call | solution.py:19
  12.7 0.3 collective-permute-done.1.refs_1_
  12.9 0.1 collective-permute-start.4
  13.0 0.9 %collective-permute-start.7 = (bf16[2,2,64,256]{3,2,1,0:T(8,128)(2,1)S(1)}, bf16[2,2,64,256]{3,2,1,0:T(8,128)(2,1)S(1)}, u32[]{:S(2)}, u32[]{:S(2)}) collective-permute-start(bf16[2,2,64,256]{3,2,1,0:T(8,128)(2,1)S(1)} %get-tuple-element.89), channel_id=1, source_target_pairs={{0,4},{1,3},{2,6},{3,1},{4,0},{5,7},{6,2},{7,5},{8,12},{9,11},{10,... | collective-permute-start | bytes 393224 | tf_op jit(solution)/shard_map/ppermute | solution.py:411
  14.0 0.3 %collective-permute-done.4 = bf16[8,24,256]{2,1,0:T(8,128)(2,1)S(1)} collective-permute-done((bf16[8,24,256]{2,1,0:T(8,128)(2,1)S(1)}, bf16[8,24,256]{2,1,0:T(8,128)(2,1)S(1)}, u32[]{:S(2)}, u32[]{:S(2)}) %collective-permute-start.4) | collective-permute-done | bytes 98336 | tf_op jit(solution)/shard_map/ppermute | solution.py:14
  14.3 0.4 %shard_map.44.left_ref = bf16[256,1536]{1,0:T(8,128)(2,1)S(1)} custom-call(f32[2,8,192,256]{3,2,1,0:T(8,128)S(1)} %shard_map.41.refs_0_, bf16[8,32,256]{2,1,0:T(8,128)(2,1)S(1)} %collective-permute-done.1.refs_1_, bf16[1,8,24,256]{3,2,1,0:T(8,128)(2,1)S(1)} %bitcast.10, f32[8,8,256]{2,1,0:T(8,128)S(1)} %get-tuple-element.65.refs_2_.refs_3_), custom_call_target="tpu_custom_call" | custom-call | flops 75497472 | tf_op jit(solution)/shard_map/pallas_call | solution.py:19
  14.7 0.7 %shard_map.45 = (f32[2,2,64,256]{3,2,1,0:T(8,128)S(1)}, bf16[2,2,64,256]{3,2,1,0:T(8,128)(2,1)S(1)}) custom-call(bf16[256,1536]{1,0:T(8,128)(2,1)S(1)} %shard_map.44.left_ref, bf16[1152,512]{1,0:T(8,128)(2,1)S(1)} %get-tuple-element.67.right_ref, bf16[384,512]{1,0:T(8,128)(2,1)S(1)} %get-tuple-element.81.edge_ref.right_ref), custom_call_target="tpu_custom_call" | custom-call | flops 3221225472 | tf_op jit(solution)/shard_map/pallas_call | solution.py:19
  15.4 0.9 %collective-permute-start.6 = (bf16[2,2,64,256]{3,2,1,0:T(8,128)(2,1)S(1)}, bf16[2,2,64,256]{3,2,1,0:T(8,128)(2,1)S(1)}, u32[]{:S(2)}, u32[]{:S(2)}) collective-permute-start(bf16[2,2,64,256]{3,2,1,0:T(8,128)(2,1)S(1)} %get-tuple-element.87), channel_id=1, source_target_pairs={{0,4},{1,3},{2,6},{3,1},{4,0},{5,7},{6,2},{7,5},{8,12},{9,11},{10,... | collective-permute-start | bytes 393224 | tf_op jit(solution)/shard_map/ppermute | solution.py:411
  16.4 0.4 %shard_map.46 = (f32[2,2,64,256]{3,2,1,0:T(8,128)S(1)}, bf16[2,2,64,256]{3,2,1,0:T(8,128)(2,1)S(1)}) custom-call(bf16[256,1536]{1,0:T(8,128)(2,1)S(1)} %get-tuple-element.62.own_ref.refs_6_, bf16[1,256,1536]{2,1,0:T(8,128)(2,1)S(1)} %bitcast.8, f32[2,256,512]{2,1,0:T(8,128)S(1)} %shard_map.42.refs_8_.begun_ref, ...), custom_call_target="tpu_custom_call" | custom-call | tf_op jit(solution)/shard_map/pallas_call | solution.py:19
  16.7 0.4 %shard_map.47.left_ref = bf16[256,1536]{1,0:T(8,128)(2,1)S(1)} custom-call(f32[2,8,192,256]{3,2,1,0:T(8,128)S(1)} %shard_map.41.refs_0_, bf16[8,32,256]{2,1,0:T(8,128)(2,1)S(1)} %collective-permute-done.1.refs_1_, bf16[1,8,24,256]{3,2,1,0:T(8,128)(2,1)S(1)} %bitcast.11, f32[8,8,256]{2,1,0:T(8,128)S(1)} %get-tuple-element.65.refs_2_.refs_3_), custom_call_target="tpu_custom_call" | custom-call | tf_op jit(solution)/shard_map/pallas_call | solution.py:19
  17.2 0.7 %shard_map.48 = (f32[2,2,64,256]{3,2,1,0:T(8,128)S(1)}, bf16[4,2,64,256]{3,2,1,0:T(8,128)(2,1)S(1)}) custom-call(bf16[256,1536]{1,0:T(8,128)(2,1)S(1)} %shard_map.47.left_ref, bf16[1152,512]{1,0:T(8,128)(2,1)S(1)} %get-tuple-element.67.right_ref, bf16[384,512]{1,0:T(8,128)(2,1)S(1)} %get-tuple-element.81.edge_ref.right_ref, ...), custom_call_target="tpu_custom_call" | custom-call | tf_op jit(solution)/shard_map/pallas_call | solution.py:19
  17.9 1.2 %collective-permute-start.5 = (bf16[4,2,64,256]{3,2,1,0:T(8,128)(2,1)S(1)}, bf16[4,2,64,256]{3,2,1,0:T(8,128)(2,1)S(1)}, u32[]{:S(2)}, u32[]{:S(2)}) collective-permute-start(bf16[4,2,64,256]{3,2,1,0:T(8,128)(2,1)S(1)} %get-tuple-element.85), channel_id=1, source_target_pairs={{0,4},{1,3},{2,6},{3,1},{4,0},{5,7},{6,2},{7,5},{8,12},{9,11},{10,... | collective-permute-start | bytes 786440 | tf_op jit(solution)/shard_map/ppermute | solution.py:411
  19.1 0.0 collective-permute-done.7.refs_1_
  19.1 1.6 %collective-permute-start.9 = (bf16[2,1,64,256]{3,2,1,0:T(8,128)(2,1)S(1)}, bf16[2,1,64,256]{3,2,1,0:T(8,128)(2,1)S(1)}, u32[]{:S(2)}, u32[]{:S(2)}) collective-permute-start(bf16[2,1,64,256]{3,2,1,0:T(8,128)(2,1)S(1)} %get-tuple-element.96), channel_id=1, source_target_pairs={{0,2},{1,5},{2,0},{3,7},{4,6},{5,1},{6,4},{7,3},{8,10},{9,13},{10,... | collective-permute-start | bytes 196616 | tf_op jit(solution)/shard_map/ppermute | solution.py:411
  20.7 0.0 collective-permute-done.6.refs_1_
  20.7 1.3 %collective-permute-start.8 = (bf16[2,1,64,256]{3,2,1,0:T(8,128)(2,1)S(1)}, bf16[2,1,64,256]{3,2,1,0:T(8,128)(2,1)S(1)}, u32[]{:S(2)}, u32[]{:S(2)}) collective-permute-start(bf16[2,1,64,256]{3,2,1,0:T(8,128)(2,1)S(1)} %get-tuple-element.95), channel_id=1, source_target_pairs={{0,2},{1,5},{2,0},{3,7},{4,6},{5,1},{6,4},{7,3},{8,10},{9,13},{10,... | collective-permute-start | bytes 196616 | tf_op jit(solution)/shard_map/ppermute | solution.py:411
  22.1 2.2 %collective-permute-done.9.came_ref = bf16[2,1,64,256]{3,2,1,0:T(8,128)(2,1)S(1)} collective-permute-done((bf16[2,1,64,256]{3,2,1,0:T(8,128)(2,1)S(1)}, bf16[2,1,64,256]{3,2,1,0:T(8,128)(2,1)S(1)}, u32[]{:S(2)}, u32[]{:S(2)}) %collective-permute-start.9) | collective-permute-done | bytes 65568 | tf_op jit(solution)/shard_map/ppermute | solution.py:411
  24.3 1.4 %collective-permute-start.12 = (bf16[2,1,64,256]{3,2,1,0:T(8,128)(2,1)S(1)}, bf16[2,1,64,256]{3,2,1,0:T(8,128)(2,1)S(1)}, u32[]{:S(2)}, u32[]{:S(2)}) collective-permute-start(bf16[2,1,64,256]{3,2,1,0:T(8,128)(2,1)S(1)} %shard_map.51), channel_id=1, source_target_pairs={{0,8},{1,9},{2,10},{3,11},{4,12},{5,13},{6,14},{7,15},{8,0},{9,1},... | collective-permute-start | bytes 196616 | tf_op jit(solution)/shard_map/ppermute | solution.py:411
  25.6 0.0 collective-permute-done.8.came_ref
  25.7 1.7 %collective-permute-start.11 = (bf16[2,1,64,256]{3,2,1,0:T(8,128)(2,1)S(1)}, bf16[2,1,64,256]{3,2,1,0:T(8,128)(2,1)S(1)}, u32[]{:S(2)}, u32[]{:S(2)}) collective-permute-start(bf16[2,1,64,256]{3,2,1,0:T(8,128)(2,1)S(1)} %shard_map.52), channel_id=1, source_target_pairs={{0,8},{1,9},{2,10},{3,11},{4,12},{5,13},{6,14},{7,15},{8,0},{9,1},... | collective-permute-start | bytes 196616 | tf_op jit(solution)/shard_map/ppermute | solution.py:411
  27.3 0.0 collective-permute-done.5.refs_1_.refs_3_
  27.3 0.1 shard_map.53
  27.4 1.2 %collective-permute-start.10 = (bf16[4,1,64,256]{3,2,1,0:T(8,128)(2,1)S(1)}, bf16[4,1,64,256]{3,2,1,0:T(8,128)(2,1)S(1)}, u32[]{:S(2)}, u32[]{:S(2)}) collective-permute-start(bf16[4,1,64,256]{3,2,1,0:T(8,128)(2,1)S(1)} %get-tuple-element.100), channel_id=1, source_target_pairs={{0,2},{1,5},{2,0},{3,7},{4,6},{5,1},{6,4},{7,3},{8,10},{9,13},{10,... | collective-permute-start | bytes 393224 | tf_op jit(solution)/shard_map/ppermute | solution.py:411
  28.6 2.4 %collective-permute-done.12.refs_1_ = bf16[2,1,64,256]{3,2,1,0:T(8,128)(2,1)S(1)} collective-permute-done((bf16[2,1,64,256]{3,2,1,0:T(8,128)(2,1)S(1)}, bf16[2,1,64,256]{3,2,1,0:T(8,128)(2,1)S(1)}, u32[]{:S(2)}, u32[]{:S(2)}) %collective-permute-start.12) | collective-permute-done | bytes 65568 | tf_op jit(solution)/shard_map/ppermute | solution.py:411
  31.0 1.4 %collective-permute-done.11.refs_1_ = bf16[2,1,64,256]{3,2,1,0:T(8,128)(2,1)S(1)} collective-permute-done((bf16[2,1,64,256]{3,2,1,0:T(8,128)(2,1)S(1)}, bf16[2,1,64,256]{3,2,1,0:T(8,128)(2,1)S(1)}, u32[]{:S(2)}, u32[]{:S(2)}) %collective-permute-start.11) | collective-permute-done | bytes 65568 | tf_op jit(solution)/shard_map/ppermute | solution.py:411
  32.4 0.1 collective-permute-done.10.came_ref
  32.4 0.7 %shard_map.56 = f32[2,2,64,256]{3,2,1,0:T(8,128)} custom-call(bf16[4,1,64,256]{3,2,1,0:T(8,128)(2,1)S(1)} %collective-permute-done.10.came_ref, f32[2,1,64,256]{3,2,1,0:T(8,128)S(1)} %shard_map.54.refs_0_, f32[2,1,64,256]{3,2,1,0:T(8,128)S(1)} %shard_map.55.refs_1_), custom_call_target="tpu_custom_call" | custom-call | tf_op jit(solution)/shard_map/pallas_call | solution.py:19
  (7 shorter events, 0.1 us)
Async XLA Ops:
  0.0 9.5 %collective-permute-start = (bf16[2,8,16,3,2,256]{5,4,3,2,1,0:T(2,128)(2,1)}, bf16[2,8,16,3,2,256]{5,4,3,2,1,0:T(2,128)(2,1)S(1)}, u32[]{:S(2)}, u32[]{:S(2)}) collective-permute-start(bf16[2,8,16,3,2,256]{5,4,3,2,1,0:T(2,128)(2,1)} %bitcast.12), channel_id=1, source_target_pairs={{1,0},{0,1},{3,2},{2,3},{5,4},{4,5},{7,6},{6,7},{9,8},{8,9},{11,10... | collective-permute-start | bytes 2359304 | tf_op jit(solution)/shard_map/ppermute | solution.py:14
  1.8 10.1 %collective-permute-start.3 = (bf16[2,19,3,2,256]{4,3,2,1,0:T(2,128)(2,1)S(1)}, bf16[2,19,3,2,256]{4,3,2,1,0:T(2,128)(2,1)S(1)}, u32[]{:S(2)}, u32[]{:S(2)}) collective-permute-start(bf16[2,19,3,2,256]{4,3,2,1,0:T(2,128)(2,1)S(1)} %get-tuple-element.71), channel_id=1, source_target_pairs={{12,0},{0,4},{4,8},{8,12},{13,1},{1,5},{5,9},{9,13},{14,2},{2,6},{... | collective-permute-start | bytes 350216 | tf_op jit(solution)/shard_map/ppermute | solution.py:14
  4.4 7.4 %collective-permute-start.2 = (bf16[2,16,3,2,256]{4,3,2,1,0:T(2,128)(2,1)S(1)}, bf16[2,16,3,2,256]{4,3,2,1,0:T(2,128)(2,1)S(1)}, u32[]{:S(2)}, u32[]{:S(2)}) collective-permute-start(bf16[2,16,3,2,256]{4,3,2,1,0:T(2,128)(2,1)S(1)} %get-tuple-element.70), channel_id=1, source_target_pairs={{4,0},{8,4},{12,8},{0,12},{5,1},{9,5},{13,9},{1,13},{6,2},{10,6},{... | collective-permute-start | bytes 294920 | tf_op jit(solution)/shard_map/ppermute | solution.py:14
  7.3 5.6 %collective-permute-start.1 = (bf16[8,32,256]{2,1,0:T(8,128)(2,1)S(1)}, bf16[8,32,256]{2,1,0:T(8,128)(2,1)S(1)}, u32[]{:S(2)}, u32[]{:S(2)}) collective-permute-start(bf16[8,32,256]{2,1,0:T(8,128)(2,1)S(1)} %get-tuple-element.69), channel_id=1, source_target_pairs={{2,0},{0,2},{3,1},{1,3},{6,4},{4,6},{7,5},{5,7},{10,8},{8,10},{11,... | collective-permute-start | bytes 393224 | tf_op jit(solution)/shard_map/ppermute | solution.py:14
  12.9 1.4 %collective-permute-start.4 = (bf16[8,24,256]{2,1,0:T(8,128)(2,1)S(1)}, bf16[8,24,256]{2,1,0:T(8,128)(2,1)S(1)}, u32[]{:S(2)}, u32[]{:S(2)}) collective-permute-start(bf16[8,24,256]{2,1,0:T(8,128)(2,1)S(1)} %slice.3), channel_id=1, source_target_pairs={{1,0},{0,1},{3,2},{2,3},{5,4},{4,5},{7,6},{6,7},{9,8},{8,9},{11,10... | collective-permute-start | bytes 294920 | tf_op jit(solution)/shard_map/ppermute | solution.py:14
  13.0 6.1 %collective-permute-start.7 = (bf16[2,2,64,256]{3,2,1,0:T(8,128)(2,1)S(1)}, bf16[2,2,64,256]{3,2,1,0:T(8,128)(2,1)S(1)}, u32[]{:S(2)}, u32[]{:S(2)}) collective-permute-start(bf16[2,2,64,256]{3,2,1,0:T(8,128)(2,1)S(1)} %get-tuple-element.89), channel_id=1, source_target_pairs={{0,4},{1,3},{2,6},{3,1},{4,0},{5,7},{6,2},{7,5},{8,12},{9,11},{10,... | collective-permute-start | bytes 393224 | tf_op jit(solution)/shard_map/ppermute | solution.py:411
  15.4 5.3 %collective-permute-start.6 = (bf16[2,2,64,256]{3,2,1,0:T(8,128)(2,1)S(1)}, bf16[2,2,64,256]{3,2,1,0:T(8,128)(2,1)S(1)}, u32[]{:S(2)}, u32[]{:S(2)}) collective-permute-start(bf16[2,2,64,256]{3,2,1,0:T(8,128)(2,1)S(1)} %get-tuple-element.87), channel_id=1, source_target_pairs={{0,4},{1,3},{2,6},{3,1},{4,0},{5,7},{6,2},{7,5},{8,12},{9,11},{10,... | collective-permute-start | bytes 393224 | tf_op jit(solution)/shard_map/ppermute | solution.py:411
  17.9 9.5 %collective-permute-start.5 = (bf16[4,2,64,256]{3,2,1,0:T(8,128)(2,1)S(1)}, bf16[4,2,64,256]{3,2,1,0:T(8,128)(2,1)S(1)}, u32[]{:S(2)}, u32[]{:S(2)}) collective-permute-start(bf16[4,2,64,256]{3,2,1,0:T(8,128)(2,1)S(1)} %get-tuple-element.85), channel_id=1, source_target_pairs={{0,4},{1,3},{2,6},{3,1},{4,0},{5,7},{6,2},{7,5},{8,12},{9,11},{10,... | collective-permute-start | bytes 786440 | tf_op jit(solution)/shard_map/ppermute | solution.py:411
  19.1 5.1 %collective-permute-start.9 = (bf16[2,1,64,256]{3,2,1,0:T(8,128)(2,1)S(1)}, bf16[2,1,64,256]{3,2,1,0:T(8,128)(2,1)S(1)}, u32[]{:S(2)}, u32[]{:S(2)}) collective-permute-start(bf16[2,1,64,256]{3,2,1,0:T(8,128)(2,1)S(1)} %get-tuple-element.96), channel_id=1, source_target_pairs={{0,2},{1,5},{2,0},{3,7},{4,6},{5,1},{6,4},{7,3},{8,10},{9,13},{10,... | collective-permute-start | bytes 196616 | tf_op jit(solution)/shard_map/ppermute | solution.py:411
  20.7 4.9 %collective-permute-start.8 = (bf16[2,1,64,256]{3,2,1,0:T(8,128)(2,1)S(1)}, bf16[2,1,64,256]{3,2,1,0:T(8,128)(2,1)S(1)}, u32[]{:S(2)}, u32[]{:S(2)}) collective-permute-start(bf16[2,1,64,256]{3,2,1,0:T(8,128)(2,1)S(1)} %get-tuple-element.95), channel_id=1, source_target_pairs={{0,2},{1,5},{2,0},{3,7},{4,6},{5,1},{6,4},{7,3},{8,10},{9,13},{10,... | collective-permute-start | bytes 196616 | tf_op jit(solution)/shard_map/ppermute | solution.py:411
  24.3 6.7 %collective-permute-start.12 = (bf16[2,1,64,256]{3,2,1,0:T(8,128)(2,1)S(1)}, bf16[2,1,64,256]{3,2,1,0:T(8,128)(2,1)S(1)}, u32[]{:S(2)}, u32[]{:S(2)}) collective-permute-start(bf16[2,1,64,256]{3,2,1,0:T(8,128)(2,1)S(1)} %shard_map.51), channel_id=1, source_target_pairs={{0,8},{1,9},{2,10},{3,11},{4,12},{5,13},{6,14},{7,15},{8,0},{9,1},... | collective-permute-start | bytes 196616 | tf_op jit(solution)/shard_map/ppermute | solution.py:411
  25.7 6.7 %collective-permute-start.11 = (bf16[2,1,64,256]{3,2,1,0:T(8,128)(2,1)S(1)}, bf16[2,1,64,256]{3,2,1,0:T(8,128)(2,1)S(1)}, u32[]{:S(2)}, u32[]{:S(2)}) collective-permute-start(bf16[2,1,64,256]{3,2,1,0:T(8,128)(2,1)S(1)} %shard_map.52), channel_id=1, source_target_pairs={{0,8},{1,9},{2,10},{3,11},{4,12},{5,13},{6,14},{7,15},{8,0},{9,1},... | collective-permute-start | bytes 196616 | tf_op jit(solution)/shard_map/ppermute | solution.py:411
  27.4 5.0 %collective-permute-start.10 = (bf16[4,1,64,256]{3,2,1,0:T(8,128)(2,1)S(1)}, bf16[4,1,64,256]{3,2,1,0:T(8,128)(2,1)S(1)}, u32[]{:S(2)}, u32[]{:S(2)}) collective-permute-start(bf16[4,1,64,256]{3,2,1,0:T(8,128)(2,1)S(1)} %get-tuple-element.100), channel_id=1, source_target_pairs={{0,2},{1,5},{2,0},{3,7},{4,6},{5,1},{6,4},{7,3},{8,10},{9,13},{10,... | collective-permute-start | bytes 393224 | tf_op jit(solution)/shard_map/ppermute | solution.py:411

commit v12 on v11

--- a/solution.py
+++ b/solution.py
@@ -571,19 +571,24 @@
         second_own_kernel, (kept_shape, shape(2 * parts, pieces, rows, width)), 0,
         [left, right, right_edge, sent_own], [total],
     )
-    came_own = exchange(sent_own, plan[0])
-    staying = [(own_first, came_own, slice(0, parts)), (own_second, came_own, slice(parts, 2 * parts))]
     crossing = [(kept_first, came_first), (kept_second, came_second)]
     after = own_second
+    staying = None
     for step in plan[1:]:
         for d, (kept, came) in enumerate(crossing):
             came, after = lax.optimization_barrier((came, after))
-            crossing[d] = halve([(kept, came, None)], step, 4 * project_flops if d else 0)
+            crossing[d] = halve([(kept, came, None)], step)
             after = crossing[d][0]
+            if staying is None:
+                sent_own, after = lax.optimization_barrier((sent_own, after))
+                came_own = exchange(sent_own, plan[0])
+                staying = [
+                    (own_first, came_own, slice(0, parts)), (own_second, came_own, slice(parts, 2 * parts))
+                ]
     crossed = []
     for kept, came in crossing:
         came, after = lax.optimization_barrier((came, after))
-        after = call(sum_kernel, pltpu.VMEM(kept.shape, bf16), 0, [kept, came])
+        after = call(sum_kernel, pltpu.VMEM(kept.shape, bf16), 8 * project_flops, [kept, came])
         crossed.append(exchange(after, (top, top)))
     for step in plan[1:]:
         kept, came, which = staying[0]

time: 33.3 us -> 33.5 us (level)
  transfers between devices with their start and end apart: 13 -> 13, of which waited for: 7 -> 9; matrix products, arithmetic and copies ran while one was open for 0% -> 0% of each run, Pallas kernels for 24% -> 24%
where the time goes in v12:
time: 33.5 us; the launch traced here: 33.3 us
  starting transfers between devices  17 us (51%)
  Pallas kernels  8.63 us (26%)
  waiting for transfers between devices  7.5 us (22%)
    ppermute x8, starting transfers between devices, exchange(): return lax.ppermute(block, axes, route)  10.1 us
    pallas_call x20, Pallas kernels, call(): pl.pallas_call(body, out_shape=out_shape, in_specs=[pl.BlockSpec(memory_s...  8.63 us
    ppermute x5, starting transfers between devices, shifted(): return lax.ppermute(block, axis, route)  6.9 us
    ppermute x8, waiting for transfers between devices, exchange(): return lax.ppermute(block, axes, route)  6.21 us
    ppermute x5, waiting for transfers between devices, shifted(): return lax.ppermute(block, axis, route)  1.29 us
  transfers between devices with their start and end apart: 13, of which 9 were waited for; matrix products, arithmetic and copies ran while one was open for 0% of the time, Pallas kernels for 24%

profile of v12, /device:TPU:0, one launch (start us, length us, event | category | flops | bytes accessed | tf_op | source)
XLA Modules:
  0.0 33.3 jit_solution(19152913353449544)
XLA Ops:
  0.0 0.5 %collective-permute-start = (bf16[2,8,16,3,2,256]{5,4,3,2,1,0:T(2,128)(2,1)}, bf16[2,8,16,3,2,256]{5,4,3,2,1,0:T(2,128)(2,1)S(1)}, u32[]{:S(2)}, u32[]{:S(2)}) collective-permute-start(bf16[2,8,16,3,2,256]{5,4,3,2,1,0:T(2,128)(2,1)} %bitcast.12), channel_id=1, source_target_pairs={{1,0},{0,1},{3,2},{2,3},{5,4},{4,5},{7,6},{6,7},{9,8},{8,9},{11,10... | collective-permute-start | bytes 2359304 | tf_op jit(solution)/shard_map/ppermute | solution.py:14
  0.5 1.4 %shard_map.37 = (bf16[2,16,3,2,256]{4,3,2,1,0:T(2,128)(2,1)S(1)}, bf16[2,19,3,2,256]{4,3,2,1,0:T(2,128)(2,1)S(1)}, bf16[2,8,16,3,2,256]{5,4,3,2,1,0:T(2,128)(2,1...) custom-call(bf16[2,8,16,3,2,256]{5,4,3,2,1,0:T(2,128)(2,1)} %bitcast, ...), custom_call_target="tpu_custom_call" | custom-call | tf_op jit(solution)/shard_map/pallas_call | solution.py:19
  1.8 2.6 %collective-permute-start.3 = (bf16[2,19,3,2,256]{4,3,2,1,0:T(2,128)(2,1)S(1)}, bf16[2,19,3,2,256]{4,3,2,1,0:T(2,128)(2,1)S(1)}, u32[]{:S(2)}, u32[]{:S(2)}) collective-permute-start(bf16[2,19,3,2,256]{4,3,2,1,0:T(2,128)(2,1)S(1)} %get-tuple-element.71), channel_id=1, source_target_pairs={{12,0},{0,4},{4,8},{8,12},{13,1},{1,5},{5,9},{9,13},{14,2},{2,6},{... | collective-permute-start | bytes 350216 | tf_op jit(solution)/shard_map/ppermute | solution.py:14
  4.4 2.1 %collective-permute-start.2 = (bf16[2,16,3,2,256]{4,3,2,1,0:T(2,128)(2,1)S(1)}, bf16[2,16,3,2,256]{4,3,2,1,0:T(2,128)(2,1)S(1)}, u32[]{:S(2)}, u32[]{:S(2)}) collective-permute-start(bf16[2,16,3,2,256]{4,3,2,1,0:T(2,128)(2,1)S(1)} %get-tuple-element.70), channel_id=1, source_target_pairs={{4,0},{8,4},{12,8},{0,12},{5,1},{9,5},{13,9},{1,13},{6,2},{10,6},{... | collective-permute-start | bytes 294920 | tf_op jit(solution)/shard_map/ppermute | solution.py:14
  6.5 0.7 %shard_map.38 = (bf16[8,192,256]{2,1,0:T(8,128)(2,1)S(1)}, bf16[8,32,256]{2,1,0:T(8,128)(2,1)S(1)}, f32[8,8,256]{2,1,0:T(8,128)S(1)}, f32[8,8,256]{2,1,0:T(8,128...) custom-call(bf16[2,8,16,3,2,256]{5,4,3,2,1,0:T(2,128)(2,1)S(1)} %get-tuple-element.55.raw_ref, ...), custom_call_target="tpu_custom_call" | custom-call | tf_op jit(solution)/shard_map/pallas_call | solution.py:19
  7.3 1.7 %collective-permute-start.1 = (bf16[8,32,256]{2,1,0:T(8,128)(2,1)S(1)}, bf16[8,32,256]{2,1,0:T(8,128)(2,1)S(1)}, u32[]{:S(2)}, u32[]{:S(2)}) collective-permute-start(bf16[8,32,256]{2,1,0:T(8,128)(2,1)S(1)} %get-tuple-element.69), channel_id=1, source_target_pairs={{2,0},{0,2},{3,1},{1,3},{6,4},{4,6},{7,5},{5,7},{10,8},{8,10},{11,... | collective-permute-start | bytes 393224 | tf_op jit(solution)/shard_map/ppermute | solution.py:14
  8.9 0.5 %shard_map.39 = (bf16[1152,512]{1,0:T(8,128)(2,1)S(1)}, bf16[256,1536]{1,0:T(8,128)(2,1)S(1)}, bf16[192,192]{1,0:T(8,128)(2,1)S(1)}, f32[192,256]{1,0:T(8,128)S(1)}, f32[192,256]{1,0:T(8,128)S(1)}) custom-call(bf16[8,192,256]{2,1,0:T(8,128)(2,1)S(1)} %get-tuple-element.59.refs_0_, f32[8,8,256]{2,1,0:T(8,128)S(1)} %get-tuple-element.60.refs_1_, ...), custom_call_target="tpu_custom_call" | custom-call | flops 150994944 | tf_op jit(solution)/shard_map/pallas_call | solution.py:19
  9.5 0.0 collective-permute-done.raw_ref
  9.5 0.3 shard_map.40
  9.8 0.6 %shard_map.41.refs_0_ = f32[2,8,192,256]{3,2,1,0:T(8,128)S(1)} custom-call(bf16[8,192,256]{2,1,0:T(8,128)(2,1)S(1)} %get-tuple-element.59.refs_0_, bf16[1,8,192,256]{3,2,1,0:T(8,128)(2,1)S(1)} %bitcast.9, f32[8,8,256]{2,1,0:T(8,128)S(1)} %get-tuple-element.65.refs_2_.refs_3_, f32[8,8,256]{2,1,0:T(8,128)S(1)} %get-tuple-element.66.refs_3_), custom_call_target="tpu_custom_call" | custom-call | flops 150994944 | tf_op jit(solution)/shard_map/pallas_call | solution.py:19
  10.4 0.8 %shard_map.42.refs_8_.begun_ref = f32[2,256,512]{2,1,0:T(8,128)S(1)} custom-call(bf16[256,1536]{1,0:T(8,128)(2,1)S(1)} %get-tuple-element.62.own_ref.refs_6_, bf16[1,256,1536]{2,1,0:T(8,128)(2,1)S(1)} %bitcast.6, bf16[1152,512]{1,0:T(8,128)(2,1)S(1)} %get-tuple-element.67.right_ref), custom_call_target="tpu_custom_call" | custom-call | flops 402653184 | tf_op jit(solution)/shard_map/pallas_call | solution.py:19
  11.2 0.7 %collective-permute-done.2.refs_0_ = bf16[2,16,3,2,256]{4,3,2,1,0:T(2,128)(2,1)S(1)} collective-permute-done((bf16[2,16,3,2,256]{4,3,2,1,0:T(2,128)(2,1)S(1)}, bf16[2,16,3,2,256]{4,3,2,1,0:T(2,128)(2,1)S(1)}, u32[]{:S(2)}, u32[]{:S(2)}) %collective-permute-start.2) | collective-permute-done | bytes 98336 | tf_op jit(solution)/shard_map/ppermute | solution.py:14
  11.9 0.0 collective-permute-done.3.refs_1_
  11.9 0.8 %shard_map.43 = (f32[2,2,64,256]{3,2,1,0:T(8,128)S(1)}, bf16[2,2,64,256]{3,2,1,0:T(8,128)(2,1)S(1)}, bf16[384,512]{1,0:T(8,128)(2,1)S(1)}) custom-call(bf16[2,16,3,2,256]{4,3,2,1,0:T(2,128)(2,1)S(1)} %collective-permute-done.2.refs_0_, bf16[2,19,3,2,256]{4,3,2,1,0:T(2,128)(2,1)S(1)} %collective-permute-done.3.refs_1_, ...), custom_call_target="tpu_custom_call" | custom-call | flops 402653184 | tf_op jit(solution)/shard_map/pallas_call | solution.py:19
  12.7 0.3 collective-permute-done.1.refs_1_
  12.9 0.1 collective-permute-start.4
  13.0 0.9 %collective-permute-start.5 = (bf16[2,2,64,256]{3,2,1,0:T(8,128)(2,1)S(1)}, bf16[2,2,64,256]{3,2,1,0:T(8,128)(2,1)S(1)}, u32[]{:S(2)}, u32[]{:S(2)}) collective-permute-start(bf16[2,2,64,256]{3,2,1,0:T(8,128)(2,1)S(1)} %get-tuple-element.87), channel_id=1, source_target_pairs={{0,4},{1,3},{2,6},{3,1},{4,0},{5,7},{6,2},{7,5},{8,12},{9,11},{10,... | collective-permute-start | bytes 393224 | tf_op jit(solution)/shard_map/ppermute | solution.py:411
  14.0 0.3 %collective-permute-done.4 = bf16[8,24,256]{2,1,0:T(8,128)(2,1)S(1)} collective-permute-done((bf16[8,24,256]{2,1,0:T(8,128)(2,1)S(1)}, bf16[8,24,256]{2,1,0:T(8,128)(2,1)S(1)}, u32[]{:S(2)}, u32[]{:S(2)}) %collective-permute-start.4) | collective-permute-done | bytes 98336 | tf_op jit(solution)/shard_map/ppermute | solution.py:14
  14.3 0.4 %shard_map.44.left_ref = bf16[256,1536]{1,0:T(8,128)(2,1)S(1)} custom-call(f32[2,8,192,256]{3,2,1,0:T(8,128)S(1)} %shard_map.41.refs_0_, bf16[8,32,256]{2,1,0:T(8,128)(2,1)S(1)} %collective-permute-done.1.refs_1_, bf16[1,8,24,256]{3,2,1,0:T(8,128)(2,1)S(1)} %bitcast.10, f32[8,8,256]{2,1,0:T(8,128)S(1)} %get-tuple-element.65.refs_2_.refs_3_), custom_call_target="tpu_custom_call" | custom-call | flops 75497472 | tf_op jit(solution)/shard_map/pallas_call | solution.py:19
  14.7 0.7 %shard_map.45 = (f32[2,2,64,256]{3,2,1,0:T(8,128)S(1)}, bf16[2,2,64,256]{3,2,1,0:T(8,128)(2,1)S(1)}) custom-call(bf16[256,1536]{1,0:T(8,128)(2,1)S(1)} %shard_map.44.left_ref, bf16[1152,512]{1,0:T(8,128)(2,1)S(1)} %get-tuple-element.67.right_ref, bf16[384,512]{1,0:T(8,128)(2,1)S(1)} %get-tuple-element.81.edge_ref.right_ref), custom_call_target="tpu_custom_call" | custom-call | flops 3221225472 | tf_op jit(solution)/shard_map/pallas_call | solution.py:19
  15.4 0.9 %collective-permute-start.7 = (bf16[2,2,64,256]{3,2,1,0:T(8,128)(2,1)S(1)}, bf16[2,2,64,256]{3,2,1,0:T(8,128)(2,1)S(1)}, u32[]{:S(2)}, u32[]{:S(2)}) collective-permute-start(bf16[2,2,64,256]{3,2,1,0:T(8,128)(2,1)S(1)} %get-tuple-element.93), channel_id=1, source_target_pairs={{0,4},{1,3},{2,6},{3,1},{4,0},{5,7},{6,2},{7,5},{8,12},{9,11},{10,... | collective-permute-start | bytes 393224 | tf_op jit(solution)/shard_map/ppermute | solution.py:411
  16.4 0.4 %shard_map.46 = (f32[2,2,64,256]{3,2,1,0:T(8,128)S(1)}, bf16[2,2,64,256]{3,2,1,0:T(8,128)(2,1)S(1)}) custom-call(bf16[256,1536]{1,0:T(8,128)(2,1)S(1)} %get-tuple-element.62.own_ref.refs_6_, bf16[1,256,1536]{2,1,0:T(8,128)(2,1)S(1)} %bitcast.8, f32[2,256,512]{2,1,0:T(8,128)S(1)} %shard_map.42.refs_8_.begun_ref, ...), custom_call_target="tpu_custom_call" | custom-call | tf_op jit(solution)/shard_map/pallas_call | solution.py:19
  16.7 0.4 %shard_map.47.left_ref = bf16[256,1536]{1,0:T(8,128)(2,1)S(1)} custom-call(f32[2,8,192,256]{3,2,1,0:T(8,128)S(1)} %shard_map.41.refs_0_, bf16[8,32,256]{2,1,0:T(8,128)(2,1)S(1)} %collective-permute-done.1.refs_1_, bf16[1,8,24,256]{3,2,1,0:T(8,128)(2,1)S(1)} %bitcast.11, f32[8,8,256]{2,1,0:T(8,128)S(1)} %get-tuple-element.65.refs_2_.refs_3_), custom_call_target="tpu_custom_call" | custom-call | tf_op jit(solution)/shard_map/pallas_call | solution.py:19
  17.2 0.7 %shard_map.48 = (f32[2,2,64,256]{3,2,1,0:T(8,128)S(1)}, bf16[4,2,64,256]{3,2,1,0:T(8,128)(2,1)S(1)}) custom-call(bf16[256,1536]{1,0:T(8,128)(2,1)S(1)} %shard_map.47.left_ref, bf16[1152,512]{1,0:T(8,128)(2,1)S(1)} %get-tuple-element.67.right_ref, bf16[384,512]{1,0:T(8,128)(2,1)S(1)} %get-tuple-element.81.edge_ref.right_ref, ...), custom_call_target="tpu_custom_call" | custom-call | tf_op jit(solution)/shard_map/pallas_call | solution.py:19
  17.9 0.2 collective-permute-done.5.refs_1_
  18.1 1.6 %collective-permute-start.9 = (bf16[2,1,64,256]{3,2,1,0:T(8,128)(2,1)S(1)}, bf16[2,1,64,256]{3,2,1,0:T(8,128)(2,1)S(1)}, u32[]{:S(2)}, u32[]{:S(2)}) collective-permute-start(bf16[2,1,64,256]{3,2,1,0:T(8,128)(2,1)S(1)} %get-tuple-element.96), channel_id=1, source_target_pairs={{0,2},{1,5},{2,0},{3,7},{4,6},{5,1},{6,4},{7,3},{8,10},{9,13},{10,... | collective-permute-start | bytes 196616 | tf_op jit(solution)/shard_map/ppermute | solution.py:411
  19.6 1.0 %collective-permute-start.6 = (bf16[4,2,64,256]{3,2,1,0:T(8,128)(2,1)S(1)}, bf16[4,2,64,256]{3,2,1,0:T(8,128)(2,1)S(1)}, u32[]{:S(2)}, u32[]{:S(2)}) collective-permute-start(bf16[4,2,64,256]{3,2,1,0:T(8,128)(2,1)S(1)} %get-tuple-element.91), channel_id=1, source_target_pairs={{0,4},{1,3},{2,6},{3,1},{4,0},{5,7},{6,2},{7,5},{8,12},{9,11},{10,... | collective-permute-start | bytes 786440 | tf_op jit(solution)/shard_map/ppermute | solution.py:411
  20.7 0.0 collective-permute-done.7.refs_1_
  20.7 1.4 %collective-permute-start.8 = (bf16[2,1,64,256]{3,2,1,0:T(8,128)(2,1)S(1)}, bf16[2,1,64,256]{3,2,1,0:T(8,128)(2,1)S(1)}, u32[]{:S(2)}, u32[]{:S(2)}) collective-permute-start(bf16[2,1,64,256]{3,2,1,0:T(8,128)(2,1)S(1)} %get-tuple-element.95), channel_id=1, source_target_pairs={{0,2},{1,5},{2,0},{3,7},{4,6},{5,1},{6,4},{7,3},{8,10},{9,13},{10,... | collective-permute-start | bytes 196616 | tf_op jit(solution)/shard_map/ppermute | solution.py:411
  22.1 1.0 %collective-permute-done.9.came_ref = bf16[2,1,64,256]{3,2,1,0:T(8,128)(2,1)S(1)} collective-permute-done((bf16[2,1,64,256]{3,2,1,0:T(8,128)(2,1)S(1)}, bf16[2,1,64,256]{3,2,1,0:T(8,128)(2,1)S(1)}, u32[]{:S(2)}, u32[]{:S(2)}) %collective-permute-start.9) | collective-permute-done | bytes 65568 | tf_op jit(solution)/shard_map/ppermute | solution.py:411
  23.1 1.6 %collective-permute-start.12 = (bf16[2,1,64,256]{3,2,1,0:T(8,128)(2,1)S(1)}, bf16[2,1,64,256]{3,2,1,0:T(8,128)(2,1)S(1)}, u32[]{:S(2)}, u32[]{:S(2)}) collective-permute-start(bf16[2,1,64,256]{3,2,1,0:T(8,128)(2,1)S(1)} %shard_map.51), channel_id=1, source_target_pairs={{0,8},{1,9},{2,10},{3,11},{4,12},{5,13},{6,14},{7,15},{8,0},{9,1},... | collective-permute-start | bytes 196616 | tf_op jit(solution)/shard_map/ppermute | solution.py:411
  24.7 1.1 %collective-permute-done.8.came_ref = bf16[2,1,64,256]{3,2,1,0:T(8,128)(2,1)S(1)} collective-permute-done((bf16[2,1,64,256]{3,2,1,0:T(8,128)(2,1)S(1)}, bf16[2,1,64,256]{3,2,1,0:T(8,128)(2,1)S(1)}, u32[]{:S(2)}, u32[]{:S(2)}) %collective-permute-start.8) | collective-permute-done | bytes 65568 | tf_op jit(solution)/shard_map/ppermute | solution.py:411
  25.8 1.7 %collective-permute-start.11 = (bf16[2,1,64,256]{3,2,1,0:T(8,128)(2,1)S(1)}, bf16[2,1,64,256]{3,2,1,0:T(8,128)(2,1)S(1)}, u32[]{:S(2)}, u32[]{:S(2)}) collective-permute-start(bf16[2,1,64,256]{3,2,1,0:T(8,128)(2,1)S(1)} %shard_map.52), channel_id=1, source_target_pairs={{0,8},{1,9},{2,10},{3,11},{4,12},{5,13},{6,14},{7,15},{8,0},{9,1},... | collective-permute-start | bytes 196616 | tf_op jit(solution)/shard_map/ppermute | solution.py:411
  27.5 0.0 collective-permute-done.6.refs_1_.refs_3_
  27.5 0.1 shard_map.53
  27.6 1.1 %collective-permute-start.10 = (bf16[4,1,64,256]{3,2,1,0:T(8,128)(2,1)S(1)}, bf16[4,1,64,256]{3,2,1,0:T(8,128)(2,1)S(1)}, u32[]{:S(2)}, u32[]{:S(2)}) collective-permute-start(bf16[4,1,64,256]{3,2,1,0:T(8,128)(2,1)S(1)} %get-tuple-element.100), channel_id=1, source_target_pairs={{0,2},{1,5},{2,0},{3,7},{4,6},{5,1},{6,4},{7,3},{8,10},{9,13},{10,... | collective-permute-start | bytes 393224 | tf_op jit(solution)/shard_map/ppermute | solution.py:411
  28.6 1.7 %collective-permute-done.12.refs_1_ = bf16[2,1,64,256]{3,2,1,0:T(8,128)(2,1)S(1)} collective-permute-done((bf16[2,1,64,256]{3,2,1,0:T(8,128)(2,1)S(1)}, bf16[2,1,64,256]{3,2,1,0:T(8,128)(2,1)S(1)}, u32[]{:S(2)}, u32[]{:S(2)}) %collective-permute-start.12) | collective-permute-done | bytes 65568 | tf_op jit(solution)/shard_map/ppermute | solution.py:411
  30.4 1.0 %collective-permute-done.11.refs_1_ = bf16[2,1,64,256]{3,2,1,0:T(8,128)(2,1)S(1)} collective-permute-done((bf16[2,1,64,256]{3,2,1,0:T(8,128)(2,1)S(1)}, bf16[2,1,64,256]{3,2,1,0:T(8,128)(2,1)S(1)}, u32[]{:S(2)}, u32[]{:S(2)}) %collective-permute-start.11) | collective-permute-done | bytes 65568 | tf_op jit(solution)/shard_map/ppermute | solution.py:411
  31.3 1.2 %collective-permute-done.10.came_ref = bf16[4,1,64,256]{3,2,1,0:T(8,128)(2,1)S(1)} collective-permute-done((bf16[4,1,64,256]{3,2,1,0:T(8,128)(2,1)S(1)}, bf16[4,1,64,256]{3,2,1,0:T(8,128)(2,1)S(1)}, u32[]{:S(2)}, u32[]{:S(2)}) %collective-permute-start.10) | collective-permute-done | bytes 131104 | tf_op jit(solution)/shard_map/ppermute | solution.py:411
  32.6 0.7 %shard_map.56 = f32[2,2,64,256]{3,2,1,0:T(8,128)} custom-call(bf16[4,1,64,256]{3,2,1,0:T(8,128)(2,1)S(1)} %collective-permute-done.10.came_ref, f32[2,1,64,256]{3,2,1,0:T(8,128)S(1)} %shard_map.54.refs_0_, f32[2,1,64,256]{3,2,1,0:T(8,128)S(1)} %shard_map.55.refs_1_), custom_call_target="tpu_custom_call" | custom-call | tf_op jit(solution)/shard_map/pallas_call | solution.py:19
  (7 shorter events, 0.1 us)
Async XLA Ops:
  0.0 9.5 %collective-permute-start = (bf16[2,8,16,3,2,256]{5,4,3,2,1,0:T(2,128)(2,1)}, bf16[2,8,16,3,2,256]{5,4,3,2,1,0:T(2,128)(2,1)S(1)}, u32[]{:S(2)}, u32[]{:S(2)}) collective-permute-start(bf16[2,8,16,3,2,256]{5,4,3,2,1,0:T(2,128)(2,1)} %bitcast.12), channel_id=1, source_target_pairs={{1,0},{0,1},{3,2},{2,3},{5,4},{4,5},{7,6},{6,7},{9,8},{8,9},{11,10... | collective-permute-start | bytes 2359304 | tf_op jit(solution)/shard_map/ppermute | solution.py:14
  1.8 10.1 %collective-permute-start.3 = (bf16[2,19,3,2,256]{4,3,2,1,0:T(2,128)(2,1)S(1)}, bf16[2,19,3,2,256]{4,3,2,1,0:T(2,128)(2,1)S(1)}, u32[]{:S(2)}, u32[]{:S(2)}) collective-permute-start(bf16[2,19,3,2,256]{4,3,2,1,0:T(2,128)(2,1)S(1)} %get-tuple-element.71), channel_id=1, source_target_pairs={{12,0},{0,4},{4,8},{8,12},{13,1},{1,5},{5,9},{9,13},{14,2},{2,6},{... | collective-permute-start | bytes 350216 | tf_op jit(solution)/shard_map/ppermute | solution.py:14
  4.4 7.4 %collective-permute-start.2 = (bf16[2,16,3,2,256]{4,3,2,1,0:T(2,128)(2,1)S(1)}, bf16[2,16,3,2,256]{4,3,2,1,0:T(2,128)(2,1)S(1)}, u32[]{:S(2)}, u32[]{:S(2)}) collective-permute-start(bf16[2,16,3,2,256]{4,3,2,1,0:T(2,128)(2,1)S(1)} %get-tuple-element.70), channel_id=1, source_target_pairs={{4,0},{8,4},{12,8},{0,12},{5,1},{9,5},{13,9},{1,13},{6,2},{10,6},{... | collective-permute-start | bytes 294920 | tf_op jit(solution)/shard_map/ppermute | solution.py:14
  7.3 5.6 %collective-permute-start.1 = (bf16[8,32,256]{2,1,0:T(8,128)(2,1)S(1)}, bf16[8,32,256]{2,1,0:T(8,128)(2,1)S(1)}, u32[]{:S(2)}, u32[]{:S(2)}) collective-permute-start(bf16[8,32,256]{2,1,0:T(8,128)(2,1)S(1)} %get-tuple-element.69), channel_id=1, source_target_pairs={{2,0},{0,2},{3,1},{1,3},{6,4},{4,6},{7,5},{5,7},{10,8},{8,10},{11,... | collective-permute-start | bytes 393224 | tf_op jit(solution)/shard_map/ppermute | solution.py:14
  12.9 1.4 %collective-permute-start.4 = (bf16[8,24,256]{2,1,0:T(8,128)(2,1)S(1)}, bf16[8,24,256]{2,1,0:T(8,128)(2,1)S(1)}, u32[]{:S(2)}, u32[]{:S(2)}) collective-permute-start(bf16[8,24,256]{2,1,0:T(8,128)(2,1)S(1)} %slice.3), channel_id=1, source_target_pairs={{1,0},{0,1},{3,2},{2,3},{5,4},{4,5},{7,6},{6,7},{9,8},{8,9},{11,10... | collective-permute-start | bytes 294920 | tf_op jit(solution)/shard_map/ppermute | solution.py:14
  13.0 5.0 %collective-permute-start.5 = (bf16[2,2,64,256]{3,2,1,0:T(8,128)(2,1)S(1)}, bf16[2,2,64,256]{3,2,1,0:T(8,128)(2,1)S(1)}, u32[]{:S(2)}, u32[]{:S(2)}) collective-permute-start(bf16[2,2,64,256]{3,2,1,0:T(8,128)(2,1)S(1)} %get-tuple-element.87), channel_id=1, source_target_pairs={{0,4},{1,3},{2,6},{3,1},{4,0},{5,7},{6,2},{7,5},{8,12},{9,11},{10,... | collective-permute-start | bytes 393224 | tf_op jit(solution)/shard_map/ppermute | solution.py:411
  15.4 5.2 %collective-permute-start.7 = (bf16[2,2,64,256]{3,2,1,0:T(8,128)(2,1)S(1)}, bf16[2,2,64,256]{3,2,1,0:T(8,128)(2,1)S(1)}, u32[]{:S(2)}, u32[]{:S(2)}) collective-permute-start(bf16[2,2,64,256]{3,2,1,0:T(8,128)(2,1)S(1)} %get-tuple-element.93), channel_id=1, source_target_pairs={{0,4},{1,3},{2,6},{3,1},{4,0},{5,7},{6,2},{7,5},{8,12},{9,11},{10,... | collective-permute-start | bytes 393224 | tf_op jit(solution)/shard_map/ppermute | solution.py:411
  18.1 5.0 %collective-permute-start.9 = (bf16[2,1,64,256]{3,2,1,0:T(8,128)(2,1)S(1)}, bf16[2,1,64,256]{3,2,1,0:T(8,128)(2,1)S(1)}, u32[]{:S(2)}, u32[]{:S(2)}) collective-permute-start(bf16[2,1,64,256]{3,2,1,0:T(8,128)(2,1)S(1)} %get-tuple-element.96), channel_id=1, source_target_pairs={{0,2},{1,5},{2,0},{3,7},{4,6},{5,1},{6,4},{7,3},{8,10},{9,13},{10,... | collective-permute-start | bytes 196616 | tf_op jit(solution)/shard_map/ppermute | solution.py:411
  19.6 7.8 %collective-permute-start.6 = (bf16[4,2,64,256]{3,2,1,0:T(8,128)(2,1)S(1)}, bf16[4,2,64,256]{3,2,1,0:T(8,128)(2,1)S(1)}, u32[]{:S(2)}, u32[]{:S(2)}) collective-permute-start(bf16[4,2,64,256]{3,2,1,0:T(8,128)(2,1)S(1)} %get-tuple-element.91), channel_id=1, source_target_pairs={{0,4},{1,3},{2,6},{3,1},{4,0},{5,7},{6,2},{7,5},{8,12},{9,11},{10,... | collective-permute-start | bytes 786440 | tf_op jit(solution)/shard_map/ppermute | solution.py:411
  20.7 5.1 %collective-permute-start.8 = (bf16[2,1,64,256]{3,2,1,0:T(8,128)(2,1)S(1)}, bf16[2,1,64,256]{3,2,1,0:T(8,128)(2,1)S(1)}, u32[]{:S(2)}, u32[]{:S(2)}) collective-permute-start(bf16[2,1,64,256]{3,2,1,0:T(8,128)(2,1)S(1)} %get-tuple-element.95), channel_id=1, source_target_pairs={{0,2},{1,5},{2,0},{3,7},{4,6},{5,1},{6,4},{7,3},{8,10},{9,13},{10,... | collective-permute-start | bytes 196616 | tf_op jit(solution)/shard_map/ppermute | solution.py:411
  23.1 7.2 %collective-permute-start.12 = (bf16[2,1,64,256]{3,2,1,0:T(8,128)(2,1)S(1)}, bf16[2,1,64,256]{3,2,1,0:T(8,128)(2,1)S(1)}, u32[]{:S(2)}, u32[]{:S(2)}) collective-permute-start(bf16[2,1,64,256]{3,2,1,0:T(8,128)(2,1)S(1)} %shard_map.51), channel_id=1, source_target_pairs={{0,8},{1,9},{2,10},{3,11},{4,12},{5,13},{6,14},{7,15},{8,0},{9,1},... | collective-permute-start | bytes 196616 | tf_op jit(solution)/shard_map/ppermute | solution.py:411
  25.8 5.5 %collective-permute-start.11 = (bf16[2,1,64,256]{3,2,1,0:T(8,128)(2,1)S(1)}, bf16[2,1,64,256]{3,2,1,0:T(8,128)(2,1)S(1)}, u32[]{:S(2)}, u32[]{:S(2)}) collective-permute-start(bf16[2,1,64,256]{3,2,1,0:T(8,128)(2,1)S(1)} %shard_map.52), channel_id=1, source_target_pairs={{0,8},{1,9},{2,10},{3,11},{4,12},{5,13},{6,14},{7,15},{8,0},{9,1},... | collective-permute-start | bytes 196616 | tf_op jit(solution)/shard_map/ppermute | solution.py:411
  27.6 5.0 %collective-permute-start.10 = (bf16[4,1,64,256]{3,2,1,0:T(8,128)(2,1)S(1)}, bf16[4,1,64,256]{3,2,1,0:T(8,128)(2,1)S(1)}, u32[]{:S(2)}, u32[]{:S(2)}) collective-permute-start(bf16[4,1,64,256]{3,2,1,0:T(8,128)(2,1)S(1)} %get-tuple-element.100), channel_id=1, source_target_pairs={{0,2},{1,5},{2,0},{3,7},{4,6},{5,1},{6,4},{7,3},{8,10},{9,13},{10,... | collective-permute-start | bytes 393224 | tf_op jit(solution)/shard_map/ppermute | solution.py:411

commit v13 on v10

--- a/solution.py
+++ b/solution.py
@@ -140,11 +140,11 @@
 
 def edges_kernel(
     raw_hbm, links_x_hbm, links_y_hbm,
-    first_ref, last_ref, raw_ref, links_x_ref, links_y_ref, maps_ref, past_maps_ref, arrived,
+    first_ref, last_ref, links_x_ref, links_y_ref, maps_ref, past_maps_ref, arrived,
 ):
     parts, planes, ys, colours, zs, _ = raw_hbm.shape
-    sources = (raw_hbm.at[:, planes - 1], raw_hbm.at[:, 0], links_x_hbm, links_y_hbm, raw_hbm)
-    targets = (last_ref.at[:, :ys], first_ref, links_x_ref, links_y_ref, raw_ref)
+    sources = (raw_hbm.at[:, planes - 1], raw_hbm.at[:, 0], links_x_hbm, links_y_hbm)
+    targets = (last_ref.at[:, :ys], first_ref, links_x_ref, links_y_ref)
     copies = [
         pltpu.make_async_copy(source, target, arrived.at[i])
         for i, (source, target) in enumerate(zip(sources, targets))
@@ -172,9 +172,11 @@
 
 
 def prepare_kernel(
-    raw_ref, links_x_ref, links_y_ref, maps_ref,
-    rows_ref, ends_ref, ahead_x_ref, back_x_ref, ahead_y_ref, back_y_ref,
+    raw_hbm, links_x_ref, links_y_ref, maps_ref,
+    rows_ref, ends_ref, ahead_x_ref, back_x_ref, ahead_y_ref, back_y_ref, raw_ref, arrived,
 ):
+    copy = pltpu.make_async_copy(raw_hbm, raw_ref, arrived)
+    copy.start()
     planes, depth, width = rows_ref.shape
     zs = raw_ref.shape[4]
     ys = raw_ref.shape[2]
@@ -195,6 +197,7 @@
     ends = (lane == wanted).astype(jnp.bfloat16)
     filler = jnp.zeros((8, width - 128), jnp.float32)
     spare = ends_ref.shape[1] - 2 * row_size - 8
+    copy.wait()
     for x in range(planes):
         plane = plane_rows(raw_ref.at[:, x], ys)
         rows_ref[place_of(x, planes)] = plane
@@ -490,13 +493,13 @@
         edges_kernel,
         (
             shape(parts, ys, colours, zs, width), shape(parts, ys + colours, colours, zs, width),
-            *(shape(*a.shape) for a in inputs),
+            *(shape(*a.shape) for a in inputs[1:]),
             shape(map_rows(parts, colours, planes, ys, zs)[-1], 2 * lanes, dtype=f32),
             shape(map_rows(parts, colours, 1, ys, zs)[-1], 2 * lanes, dtype=f32),
         ),
         0,
         inputs,
-        [pltpu.SemaphoreType.DMA((5,))],
+        [pltpu.SemaphoreType.DMA((4,))],
         [pltpu.HBM] * len(inputs),
     )
     low = shifted(last_plane, "gx", 1)
@@ -505,7 +508,9 @@
         prepare_kernel,
         (field_shape, shape(planes, edge, width), link_shape, link_shape, link_shape, link_shape),
         0,
-        inputs,
+        [raw] + inputs,
+        [pltpu.VMEM(raw.shape, bf16), pltpu.SemaphoreType.DMA],
+        [pltpu.HBM] + [pltpu.VMEM] * len(inputs),
     )
     near = shifted(ends, "gy", 1)
     if across_y != 2:

time: 33.2 us -> 33.7 us (1.015)
  waiting for transfers between devices: 7.22 us -> 7.92 us
  starting transfers between devices: 17.3 us -> 16.6 us
  Pallas kernels: 8.39 us -> 8.86 us
    ppermute x5, waiting for transfers between devices: 1.3 us -> 2.13 us  [shifted(): return lax.ppermute(block, axis, route)]
    ppermute x8, starting transfers between devices: 10.4 us -> 9.62 us  [exchange(): return lax.ppermute(block, axes, route)]
    pallas_call x19, Pallas kernels: 8.39 us -> 8.86 us  [call(): pl.pallas_call(body, out_shape=out_shape, in_specs=[pl.BlockSpec(memory_s...]
  transfers between devices with their start and end apart: 13 -> 13, of which waited for: 7 -> 6; matrix products, arithmetic and copies ran while one was open for 0% -> 0% of each run, Pallas kernels for 23% -> 24%
where the time goes in v13:
time: 33.7 us; the launch traced here: 33.5 us
  starting transfers between devices  16.6 us (49%)
  Pallas kernels  8.86 us (26%)
  waiting for transfers between devices  7.92 us (24%)
    ppermute x8, starting transfers between devices, exchange(): return lax.ppermute(block, axes, route)  9.62 us
    pallas_call x19, Pallas kernels, call(): pl.pallas_call(body, out_shape=out_shape, in_specs=[pl.BlockSpec(memory_s...  8.86 us
    ppermute x5, starting transfers between devices, shifted(): return lax.ppermute(block, axis, route)  6.95 us
    ppermute x8, waiting for transfers between devices, exchange(): return lax.ppermute(block, axes, route)  5.79 us
    ppermute x5, waiting for transfers between devices, shifted(): return lax.ppermute(block, axis, route)  2.13 us
  transfers between devices with their start and end apart: 13, of which 6 were waited for; matrix products, arithmetic and copies ran while one was open for 0% of the time, Pallas kernels for 24%

profile of v13, /device:TPU:0, one launch (start us, length us, event | category | flops | bytes accessed | tf_op | source)
XLA Modules:
  0.0 33.5 jit_solution(15457532255048007940)
XLA Ops:
  0.0 0.5 %collective-permute-start = (bf16[2,8,16,3,2,256]{5,4,3,2,1,0:T(2,128)(2,1)}, bf16[2,8,16,3,2,256]{5,4,3,2,1,0:T(2,128)(2,1)S(1)}, u32[]{:S(2)}, u32[]{:S(2)}) collective-permute-start(bf16[2,8,16,3,2,256]{5,4,3,2,1,0:T(2,128)(2,1)} %bitcast.11), channel_id=1, source_target_pairs={{1,0},{0,1},{3,2},{2,3},{5,4},{4,5},{7,6},{6,7},{9,8},{8,9},{11,10... | collective-permute-start | bytes 2359304 | tf_op jit(solution)/shard_map/ppermute | solution.py:14
  0.5 1.1 %shard_map.37 = (bf16[2,16,3,2,256]{4,3,2,1,0:T(2,128)(2,1)S(1)}, bf16[2,19,3,2,256]{4,3,2,1,0:T(2,128)(2,1)S(1)}, bf16[2,3,3,8,2,16]{5,4,3,2,1,0:T(2,128)(2,1)S...) custom-call(bf16[2,8,16,3,2,256]{5,4,3,2,1,0:T(2,128)(2,1)} %bitcast.12, ...), custom_call_target="tpu_custom_call" | custom-call | tf_op jit(solution)/shard_map/pallas_call | solution.py:19
  1.5 2.6 %collective-permute-start.3 = (bf16[2,19,3,2,256]{4,3,2,1,0:T(2,128)(2,1)S(1)}, bf16[2,19,3,2,256]{4,3,2,1,0:T(2,128)(2,1)S(1)}, u32[]{:S(2)}, u32[]{:S(2)}) collective-permute-start(bf16[2,19,3,2,256]{4,3,2,1,0:T(2,128)(2,1)S(1)} %get-tuple-element.68), channel_id=1, source_target_pairs={{12,0},{0,4},{4,8},{8,12},{13,1},{1,5},{5,9},{9,13},{14,2},{2,6},{... | collective-permute-start | bytes 350216 | tf_op jit(solution)/shard_map/ppermute | solution.py:14
  4.1 2.1 %collective-permute-start.2 = (bf16[2,16,3,2,256]{4,3,2,1,0:T(2,128)(2,1)S(1)}, bf16[2,16,3,2,256]{4,3,2,1,0:T(2,128)(2,1)S(1)}, u32[]{:S(2)}, u32[]{:S(2)}) collective-permute-start(bf16[2,16,3,2,256]{4,3,2,1,0:T(2,128)(2,1)S(1)} %get-tuple-element.67), channel_id=1, source_target_pairs={{4,0},{8,4},{12,8},{0,12},{5,1},{9,5},{13,9},{1,13},{6,2},{10,6},{... | collective-permute-start | bytes 294920 | tf_op jit(solution)/shard_map/ppermute | solution.py:14
  6.2 1.5 %shard_map.38 = (bf16[8,192,256]{2,1,0:T(8,128)(2,1)S(1)}, bf16[8,32,256]{2,1,0:T(8,128)(2,1)S(1)}, f32[8,8,256]{2,1,0:T(8,128)S(1)}, f32[8,8,256]{2,1,0:T(8,128...) custom-call(bf16[2,8,16,3,2,256]{5,4,3,2,1,0:T(2,128)(2,1)} %bitcast.13, ...), custom_call_target="tpu_custom_call" | custom-call | tf_op jit(solution)/shard_map/pallas_call | solution.py:19
  7.8 1.7 %collective-permute-start.1 = (bf16[8,32,256]{2,1,0:T(8,128)(2,1)S(1)}, bf16[8,32,256]{2,1,0:T(8,128)(2,1)S(1)}, u32[]{:S(2)}, u32[]{:S(2)}) collective-permute-start(bf16[8,32,256]{2,1,0:T(8,128)(2,1)S(1)} %get-tuple-element.66), channel_id=1, source_target_pairs={{2,0},{0,2},{3,1},{1,3},{6,4},{4,6},{7,5},{5,7},{10,8},{8,10},{11,... | collective-permute-start | bytes 393224 | tf_op jit(solution)/shard_map/ppermute | solution.py:14
  9.5 0.5 %shard_map.39 = (bf16[1152,512]{1,0:T(8,128)(2,1)S(1)}, bf16[256,1536]{1,0:T(8,128)(2,1)S(1)}, bf16[192,192]{1,0:T(8,128)(2,1)S(1)}, f32[192,256]{1,0:T(8,128)S(1)}, f32[192,256]{1,0:T(8,128)S(1)}) custom-call(bf16[8,192,256]{2,1,0:T(8,128)(2,1)S(1)} %get-tuple-element.56.refs_0_, f32[8,8,256]{2,1,0:T(8,128)S(1)} %get-tuple-element.57.refs_1_, ...), custom_call_target="tpu_custom_call" | custom-call | flops 150994944 | tf_op jit(solution)/shard_map/pallas_call | solution.py:19
  10.0 0.0 collective-permute-done.raw_ref
  10.0 0.3 shard_map.40
  10.3 0.6 %shard_map.41.refs_0_ = f32[2,8,192,256]{3,2,1,0:T(8,128)S(1)} custom-call(bf16[8,192,256]{2,1,0:T(8,128)(2,1)S(1)} %get-tuple-element.56.refs_0_, bf16[1,8,192,256]{3,2,1,0:T(8,128)(2,1)S(1)} %bitcast.9, f32[8,8,256]{2,1,0:T(8,128)S(1)} %get-tuple-element.62.refs_2_.refs_3_, f32[8,8,256]{2,1,0:T(8,128)S(1)} %get-tuple-element.63.refs_3_), custom_call_target="tpu_custom_call" | custom-call | flops 150994944 | tf_op jit(solution)/shard_map/pallas_call | solution.py:19
  10.9 0.8 %shard_map.42.refs_8_.begun_ref = f32[2,256,512]{2,1,0:T(8,128)S(1)} custom-call(bf16[256,1536]{1,0:T(8,128)(2,1)S(1)} %get-tuple-element.59.own_ref.refs_6_, bf16[1,256,1536]{2,1,0:T(8,128)(2,1)S(1)} %bitcast.6, bf16[1152,512]{1,0:T(8,128)(2,1)S(1)} %get-tuple-element.64.right_ref), custom_call_target="tpu_custom_call" | custom-call | flops 402653184 | tf_op jit(solution)/shard_map/pallas_call | solution.py:19
  11.7 0.0 collective-permute-done.2.refs_0_
  11.7 0.0 collective-permute-done.3.refs_1_
  11.8 0.8 %shard_map.43 = (f32[2,2,64,256]{3,2,1,0:T(8,128)S(1)}, bf16[2,2,64,256]{3,2,1,0:T(8,128)(2,1)S(1)}, bf16[384,512]{1,0:T(8,128)(2,1)S(1)}) custom-call(bf16[2,16,3,2,256]{4,3,2,1,0:T(2,128)(2,1)S(1)} %collective-permute-done.2.refs_0_, bf16[2,19,3,2,256]{4,3,2,1,0:T(2,128)(2,1)S(1)} %collective-permute-done.3.refs_1_, ...), custom_call_target="tpu_custom_call" | custom-call | flops 402653184 | tf_op jit(solution)/shard_map/pallas_call | solution.py:19
  12.5 0.9 %collective-permute-done.1.refs_1_ = bf16[8,32,256]{2,1,0:T(8,128)(2,1)S(1)} collective-permute-done((bf16[8,32,256]{2,1,0:T(8,128)(2,1)S(1)}, bf16[8,32,256]{2,1,0:T(8,128)(2,1)S(1)}, u32[]{:S(2)}, u32[]{:S(2)}) %collective-permute-start.1) | collective-permute-done | bytes 131104 | tf_op jit(solution)/shard_map/ppermute | solution.py:14
  13.5 0.1 collective-permute-start.4
  13.5 0.1 collective-permute-start.7
  13.6 1.2 %collective-permute-done.4 = bf16[8,24,256]{2,1,0:T(8,128)(2,1)S(1)} collective-permute-done((bf16[8,24,256]{2,1,0:T(8,128)(2,1)S(1)}, bf16[8,24,256]{2,1,0:T(8,128)(2,1)S(1)}, u32[]{:S(2)}, u32[]{:S(2)}) %collective-permute-start.4) | collective-permute-done | bytes 98336 | tf_op jit(solution)/shard_map/ppermute | solution.py:14
  14.8 0.6 %shard_map.44.lefts_ref = bf16[2,256,1536]{2,1,0:T(8,128)(2,1)S(1)} custom-call(f32[2,8,192,256]{3,2,1,0:T(8,128)S(1)} %shard_map.41.refs_0_, bf16[8,32,256]{2,1,0:T(8,128)(2,1)S(1)} %collective-permute-done.1.refs_1_, bf16[1,8,24,256]{3,2,1,0:T(8,128)(2,1)S(1)} %bitcast.10, f32[8,8,256]{2,1,0:T(8,128)S(1)} %get-tuple-element.62.refs_2_.refs_3_), custom_call_target="tpu_custom_call" | custom-call | flops 150994944 | tf_op jit(solution)/shard_map/pallas_call | solution.py:19
  15.5 0.7 %shard_map.45 = (f32[2,2,64,256]{3,2,1,0:T(8,128)S(1)}, bf16[2,2,64,256]{3,2,1,0:T(8,128)(2,1)S(1)}) custom-call(bf16[2,256,1536]{2,1,0:T(8,128)(2,1)S(1)} %shard_map.44.lefts_ref, bf16[1152,512]{1,0:T(8,128)(2,1)S(1)} %get-tuple-element.64.right_ref, bf16[384,512]{1,0:T(8,128)(2,1)S(1)} %get-tuple-element.78.edge_ref.right_ref), custom_call_target="tpu_custom_call" | custom-call | flops 3221225472 | tf_op jit(solution)/shard_map/pallas_call | solution.py:19
  16.2 0.9 %collective-permute-start.6 = (bf16[2,2,64,256]{3,2,1,0:T(8,128)(2,1)S(1)}, bf16[2,2,64,256]{3,2,1,0:T(8,128)(2,1)S(1)}, u32[]{:S(2)}, u32[]{:S(2)}) collective-permute-start(bf16[2,2,64,256]{3,2,1,0:T(8,128)(2,1)S(1)} %get-tuple-element.83), channel_id=1, source_target_pairs={{0,4},{1,3},{2,6},{3,1},{4,0},{5,7},{6,2},{7,5},{8,12},{9,11},{10,... | collective-permute-start | bytes 393224 | tf_op jit(solution)/shard_map/ppermute | solution.py:420
  17.1 0.4 %shard_map.46 = (f32[2,2,64,256]{3,2,1,0:T(8,128)S(1)}, bf16[2,2,64,256]{3,2,1,0:T(8,128)(2,1)S(1)}) custom-call(bf16[256,1536]{1,0:T(8,128)(2,1)S(1)} %get-tuple-element.59.own_ref.refs_6_, bf16[1,256,1536]{2,1,0:T(8,128)(2,1)S(1)} %bitcast.8, f32[2,256,512]{2,1,0:T(8,128)S(1)} %shard_map.42.refs_8_.begun_ref, ...), custom_call_target="tpu_custom_call" | custom-call | tf_op jit(solution)/shard_map/pallas_call | solution.py:19
  17.4 0.7 %shard_map.47 = (f32[2,2,64,256]{3,2,1,0:T(8,128)S(1)}, bf16[4,2,64,256]{3,2,1,0:T(8,128)(2,1)S(1)}) custom-call(bf16[2,256,1536]{2,1,0:T(8,128)(2,1)S(1)} %shard_map.44.lefts_ref, bf16[1152,512]{1,0:T(8,128)(2,1)S(1)} %get-tuple-element.64.right_ref, bf16[384,512]{1,0:T(8,128)(2,1)S(1)} %get-tuple-element.78.edge_ref.right_ref, ...), custom_call_target="tpu_custom_call" | custom-call | tf_op jit(solution)/shard_map/pallas_call | solution.py:19
  18.1 1.3 %collective-permute-start.5 = (bf16[4,2,64,256]{3,2,1,0:T(8,128)(2,1)S(1)}, bf16[4,2,64,256]{3,2,1,0:T(8,128)(2,1)S(1)}, u32[]{:S(2)}, u32[]{:S(2)}) collective-permute-start(bf16[4,2,64,256]{3,2,1,0:T(8,128)(2,1)S(1)} %get-tuple-element.81), channel_id=1, source_target_pairs={{0,4},{1,3},{2,6},{3,1},{4,0},{5,7},{6,2},{7,5},{8,12},{9,11},{10,... | collective-permute-start | bytes 786440 | tf_op jit(solution)/shard_map/ppermute | solution.py:420
  19.4 0.0 collective-permute-done.7.refs_1_
  19.4 1.6 %collective-permute-start.9 = (bf16[2,1,64,256]{3,2,1,0:T(8,128)(2,1)S(1)}, bf16[2,1,64,256]{3,2,1,0:T(8,128)(2,1)S(1)}, u32[]{:S(2)}, u32[]{:S(2)}) collective-permute-start(bf16[2,1,64,256]{3,2,1,0:T(8,128)(2,1)S(1)} %get-tuple-element.92), channel_id=1, source_target_pairs={{0,2},{1,5},{2,0},{3,7},{4,6},{5,1},{6,4},{7,3},{8,10},{9,13},{10,... | collective-permute-start | bytes 196616 | tf_op jit(solution)/shard_map/ppermute | solution.py:420
  21.0 0.2 collective-permute-done.6.refs_1_
  21.3 1.6 %collective-permute-start.8 = (bf16[2,1,64,256]{3,2,1,0:T(8,128)(2,1)S(1)}, bf16[2,1,64,256]{3,2,1,0:T(8,128)(2,1)S(1)}, u32[]{:S(2)}, u32[]{:S(2)}) collective-permute-start(bf16[2,1,64,256]{3,2,1,0:T(8,128)(2,1)S(1)} %get-tuple-element.91), channel_id=1, source_target_pairs={{0,2},{1,5},{2,0},{3,7},{4,6},{5,1},{6,4},{7,3},{8,10},{9,13},{10,... | collective-permute-start | bytes 196616 | tf_op jit(solution)/shard_map/ppermute | solution.py:420
  22.8 1.7 %collective-permute-done.9.came_ref = bf16[2,1,64,256]{3,2,1,0:T(8,128)(2,1)S(1)} collective-permute-done((bf16[2,1,64,256]{3,2,1,0:T(8,128)(2,1)S(1)}, bf16[2,1,64,256]{3,2,1,0:T(8,128)(2,1)S(1)}, u32[]{:S(2)}, u32[]{:S(2)}) %collective-permute-start.9) | collective-permute-done | bytes 65568 | tf_op jit(solution)/shard_map/ppermute | solution.py:420
  24.5 1.0 %collective-permute-start.12 = (bf16[2,1,64,256]{3,2,1,0:T(8,128)(2,1)S(1)}, bf16[2,1,64,256]{3,2,1,0:T(8,128)(2,1)S(1)}, u32[]{:S(2)}, u32[]{:S(2)}) collective-permute-start(bf16[2,1,64,256]{3,2,1,0:T(8,128)(2,1)S(1)} %shard_map.50), channel_id=1, source_target_pairs={{0,8},{1,9},{2,10},{3,11},{4,12},{5,13},{6,14},{7,15},{8,0},{9,1},... | collective-permute-start | bytes 196616 | tf_op jit(solution)/shard_map/ppermute | solution.py:420
  25.6 0.0 collective-permute-done.8.came_ref
  25.6 2.0 %collective-permute-start.11 = (bf16[2,1,64,256]{3,2,1,0:T(8,128)(2,1)S(1)}, bf16[2,1,64,256]{3,2,1,0:T(8,128)(2,1)S(1)}, u32[]{:S(2)}, u32[]{:S(2)}) collective-permute-start(bf16[2,1,64,256]{3,2,1,0:T(8,128)(2,1)S(1)} %shard_map.51), channel_id=1, source_target_pairs={{0,8},{1,9},{2,10},{3,11},{4,12},{5,13},{6,14},{7,15},{8,0},{9,1},... | collective-permute-start | bytes 196616 | tf_op jit(solution)/shard_map/ppermute | solution.py:420
  27.6 0.0 collective-permute-done.5.refs_1_.refs_3_
  27.6 0.1 shard_map.52
  27.7 1.2 %collective-permute-start.10 = (bf16[4,1,64,256]{3,2,1,0:T(8,128)(2,1)S(1)}, bf16[4,1,64,256]{3,2,1,0:T(8,128)(2,1)S(1)}, u32[]{:S(2)}, u32[]{:S(2)}) collective-permute-start(bf16[4,1,64,256]{3,2,1,0:T(8,128)(2,1)S(1)} %get-tuple-element.96), channel_id=1, source_target_pairs={{0,2},{1,5},{2,0},{3,7},{4,6},{5,1},{6,4},{7,3},{8,10},{9,13},{10,... | collective-permute-start | bytes 393224 | tf_op jit(solution)/shard_map/ppermute | solution.py:420
  28.9 3.0 %collective-permute-done.12.refs_1_ = bf16[2,1,64,256]{3,2,1,0:T(8,128)(2,1)S(1)} collective-permute-done((bf16[2,1,64,256]{3,2,1,0:T(8,128)(2,1)S(1)}, bf16[2,1,64,256]{3,2,1,0:T(8,128)(2,1)S(1)}, u32[]{:S(2)}, u32[]{:S(2)}) %collective-permute-start.12) | collective-permute-done | bytes 65568 | tf_op jit(solution)/shard_map/ppermute | solution.py:420
  31.9 0.9 %collective-permute-done.11.refs_1_ = bf16[2,1,64,256]{3,2,1,0:T(8,128)(2,1)S(1)} collective-permute-done((bf16[2,1,64,256]{3,2,1,0:T(8,128)(2,1)S(1)}, bf16[2,1,64,256]{3,2,1,0:T(8,128)(2,1)S(1)}, u32[]{:S(2)}, u32[]{:S(2)}) %collective-permute-start.11) | collective-permute-done | bytes 65568 | tf_op jit(solution)/shard_map/ppermute | solution.py:420
  32.8 0.0 collective-permute-done.10.came_ref
  32.8 0.7 %shard_map.55 = f32[2,2,64,256]{3,2,1,0:T(8,128)} custom-call(bf16[4,1,64,256]{3,2,1,0:T(8,128)(2,1)S(1)} %collective-permute-done.10.came_ref, f32[2,1,64,256]{3,2,1,0:T(8,128)S(1)} %shard_map.53.refs_0_, f32[2,1,64,256]{3,2,1,0:T(8,128)S(1)} %shard_map.54.refs_1_), custom_call_target="tpu_custom_call" | custom-call | tf_op jit(solution)/shard_map/pallas_call | solution.py:19
  (7 shorter events, 0.1 us)
Async XLA Ops:
  0.0 10.0 %collective-permute-start = (bf16[2,8,16,3,2,256]{5,4,3,2,1,0:T(2,128)(2,1)}, bf16[2,8,16,3,2,256]{5,4,3,2,1,0:T(2,128)(2,1)S(1)}, u32[]{:S(2)}, u32[]{:S(2)}) collective-permute-start(bf16[2,8,16,3,2,256]{5,4,3,2,1,0:T(2,128)(2,1)} %bitcast.11), channel_id=1, source_target_pairs={{1,0},{0,1},{3,2},{2,3},{5,4},{4,5},{7,6},{6,7},{9,8},{8,9},{11,10... | collective-permute-start | bytes 2359304 | tf_op jit(solution)/shard_map/ppermute | solution.py:14
  1.5 10.2 %collective-permute-start.3 = (bf16[2,19,3,2,256]{4,3,2,1,0:T(2,128)(2,1)S(1)}, bf16[2,19,3,2,256]{4,3,2,1,0:T(2,128)(2,1)S(1)}, u32[]{:S(2)}, u32[]{:S(2)}) collective-permute-start(bf16[2,19,3,2,256]{4,3,2,1,0:T(2,128)(2,1)S(1)} %get-tuple-element.68), channel_id=1, source_target_pairs={{12,0},{0,4},{4,8},{8,12},{13,1},{1,5},{5,9},{9,13},{14,2},{2,6},{... | collective-permute-start | bytes 350216 | tf_op jit(solution)/shard_map/ppermute | solution.py:14
  4.1 7.6 %collective-permute-start.2 = (bf16[2,16,3,2,256]{4,3,2,1,0:T(2,128)(2,1)S(1)}, bf16[2,16,3,2,256]{4,3,2,1,0:T(2,128)(2,1)S(1)}, u32[]{:S(2)}, u32[]{:S(2)}) collective-permute-start(bf16[2,16,3,2,256]{4,3,2,1,0:T(2,128)(2,1)S(1)} %get-tuple-element.67), channel_id=1, source_target_pairs={{4,0},{8,4},{12,8},{0,12},{5,1},{9,5},{13,9},{1,13},{6,2},{10,6},{... | collective-permute-start | bytes 294920 | tf_op jit(solution)/shard_map/ppermute | solution.py:14
  7.8 5.7 %collective-permute-start.1 = (bf16[8,32,256]{2,1,0:T(8,128)(2,1)S(1)}, bf16[8,32,256]{2,1,0:T(8,128)(2,1)S(1)}, u32[]{:S(2)}, u32[]{:S(2)}) collective-permute-start(bf16[8,32,256]{2,1,0:T(8,128)(2,1)S(1)} %get-tuple-element.66), channel_id=1, source_target_pairs={{2,0},{0,2},{3,1},{1,3},{6,4},{4,6},{7,5},{5,7},{10,8},{8,10},{11,... | collective-permute-start | bytes 393224 | tf_op jit(solution)/shard_map/ppermute | solution.py:14
  13.5 1.4 %collective-permute-start.4 = (bf16[8,24,256]{2,1,0:T(8,128)(2,1)S(1)}, bf16[8,24,256]{2,1,0:T(8,128)(2,1)S(1)}, u32[]{:S(2)}, u32[]{:S(2)}) collective-permute-start(bf16[8,24,256]{2,1,0:T(8,128)(2,1)S(1)} %slice.3), channel_id=1, source_target_pairs={{1,0},{0,1},{3,2},{2,3},{5,4},{4,5},{7,6},{6,7},{9,8},{8,9},{11,10... | collective-permute-start | bytes 294920 | tf_op jit(solution)/shard_map/ppermute | solution.py:14
  13.5 5.8 %collective-permute-start.7 = (bf16[2,2,64,256]{3,2,1,0:T(8,128)(2,1)S(1)}, bf16[2,2,64,256]{3,2,1,0:T(8,128)(2,1)S(1)}, u32[]{:S(2)}, u32[]{:S(2)}) collective-permute-start(bf16[2,2,64,256]{3,2,1,0:T(8,128)(2,1)S(1)} %get-tuple-element.85), channel_id=1, source_target_pairs={{0,4},{1,3},{2,6},{3,1},{4,0},{5,7},{6,2},{7,5},{8,12},{9,11},{10,... | collective-permute-start | bytes 393224 | tf_op jit(solution)/shard_map/ppermute | solution.py:420
  16.2 5.0 %collective-permute-start.6 = (bf16[2,2,64,256]{3,2,1,0:T(8,128)(2,1)S(1)}, bf16[2,2,64,256]{3,2,1,0:T(8,128)(2,1)S(1)}, u32[]{:S(2)}, u32[]{:S(2)}) collective-permute-start(bf16[2,2,64,256]{3,2,1,0:T(8,128)(2,1)S(1)} %get-tuple-element.83), channel_id=1, source_target_pairs={{0,4},{1,3},{2,6},{3,1},{4,0},{5,7},{6,2},{7,5},{8,12},{9,11},{10,... | collective-permute-start | bytes 393224 | tf_op jit(solution)/shard_map/ppermute | solution.py:420
  18.1 9.5 %collective-permute-start.5 = (bf16[4,2,64,256]{3,2,1,0:T(8,128)(2,1)S(1)}, bf16[4,2,64,256]{3,2,1,0:T(8,128)(2,1)S(1)}, u32[]{:S(2)}, u32[]{:S(2)}) collective-permute-start(bf16[4,2,64,256]{3,2,1,0:T(8,128)(2,1)S(1)} %get-tuple-element.81), channel_id=1, source_target_pairs={{0,4},{1,3},{2,6},{3,1},{4,0},{5,7},{6,2},{7,5},{8,12},{9,11},{10,... | collective-permute-start | bytes 786440 | tf_op jit(solution)/shard_map/ppermute | solution.py:420
  19.4 5.1 %collective-permute-start.9 = (bf16[2,1,64,256]{3,2,1,0:T(8,128)(2,1)S(1)}, bf16[2,1,64,256]{3,2,1,0:T(8,128)(2,1)S(1)}, u32[]{:S(2)}, u32[]{:S(2)}) collective-permute-start(bf16[2,1,64,256]{3,2,1,0:T(8,128)(2,1)S(1)} %get-tuple-element.92), channel_id=1, source_target_pairs={{0,2},{1,5},{2,0},{3,7},{4,6},{5,1},{6,4},{7,3},{8,10},{9,13},{10,... | collective-permute-start | bytes 196616 | tf_op jit(solution)/shard_map/ppermute | solution.py:420
  21.3 4.3 %collective-permute-start.8 = (bf16[2,1,64,256]{3,2,1,0:T(8,128)(2,1)S(1)}, bf16[2,1,64,256]{3,2,1,0:T(8,128)(2,1)S(1)}, u32[]{:S(2)}, u32[]{:S(2)}) collective-permute-start(bf16[2,1,64,256]{3,2,1,0:T(8,128)(2,1)S(1)} %get-tuple-element.91), channel_id=1, source_target_pairs={{0,2},{1,5},{2,0},{3,7},{4,6},{5,1},{6,4},{7,3},{8,10},{9,13},{10,... | collective-permute-start | bytes 196616 | tf_op jit(solution)/shard_map/ppermute | solution.py:420
  24.5 7.3 %collective-permute-start.12 = (bf16[2,1,64,256]{3,2,1,0:T(8,128)(2,1)S(1)}, bf16[2,1,64,256]{3,2,1,0:T(8,128)(2,1)S(1)}, u32[]{:S(2)}, u32[]{:S(2)}) collective-permute-start(bf16[2,1,64,256]{3,2,1,0:T(8,128)(2,1)S(1)} %shard_map.50), channel_id=1, source_target_pairs={{0,8},{1,9},{2,10},{3,11},{4,12},{5,13},{6,14},{7,15},{8,0},{9,1},... | collective-permute-start | bytes 196616 | tf_op jit(solution)/shard_map/ppermute | solution.py:420
  25.6 7.1 %collective-permute-start.11 = (bf16[2,1,64,256]{3,2,1,0:T(8,128)(2,1)S(1)}, bf16[2,1,64,256]{3,2,1,0:T(8,128)(2,1)S(1)}, u32[]{:S(2)}, u32[]{:S(2)}) collective-permute-start(bf16[2,1,64,256]{3,2,1,0:T(8,128)(2,1)S(1)} %shard_map.51), channel_id=1, source_target_pairs={{0,8},{1,9},{2,10},{3,11},{4,12},{5,13},{6,14},{7,15},{8,0},{9,1},... | collective-permute-start | bytes 196616 | tf_op jit(solution)/shard_map/ppermute | solution.py:420
  27.7 5.1 %collective-permute-start.10 = (bf16[4,1,64,256]{3,2,1,0:T(8,128)(2,1)S(1)}, bf16[4,1,64,256]{3,2,1,0:T(8,128)(2,1)S(1)}, u32[]{:S(2)}, u32[]{:S(2)}) collective-permute-start(bf16[4,1,64,256]{3,2,1,0:T(8,128)(2,1)S(1)} %get-tuple-element.96), channel_id=1, source_target_pairs={{0,2},{1,5},{2,0},{3,7},{4,6},{5,1},{6,4},{7,3},{8,10},{9,13},{10,... | collective-permute-start | bytes 393224 | tf_op jit(solution)/shard_map/ppermute | solution.py:420

commit v14 on v10

--- a/solution.py
+++ b/solution.py
@@ -264,9 +264,11 @@
     return range(lax.axis_size(axis).bit_length() - 1)
 
 
-def steps():
+def steps(turns=True):
     one = [("gx", bit) for bit in bits("gx")[:-1]]
     two = [("gy", bit) for bit in bits("gy")]
+    if not turns:
+        return [(step, step) for step in two + one]
     both = min(len(one), len(two))
     pairs = [pair for ends in zip(one, two) for pair in (ends, ends[::-1])]
     return pairs + [(step, step) for step in one[both:] + two[both:]]
@@ -286,13 +288,12 @@
     return lax.bitwise_xor(half, lax.axis_index("ma"))
 
 
-def share(total, keep_ref, send_ref, total_ref):
+def share(plan, total, keep_ref, send_ref, total_ref):
     blocks, rows, double = total_ref.shape
     parts, count, _, width = keep_ref.shape
     total_ref[...] = total.reshape(blocks, rows, double)
     odd_core = my_bit("ma", 0)
     across_y = lax.axis_size("gy")
-    plan = steps()
     mine = my_side(plan[0])
 
     def at(side, index):
@@ -317,7 +318,7 @@
     half = half_of(kind)
     inner = own_ref.shape[1] - right.shape[0]
     left = jnp.where(half == 0, own_ref[:, inner:], others_ref[0, :, inner:])
-    share(begun_ref[half] + dot(left, right), keep_ref, send_ref, total_ref)
+    share(steps(kind == 1), begun_ref[half] + dot(left, right), keep_ref, send_ref, total_ref)
 
 
 def first_kernel(
@@ -392,7 +393,7 @@
     half = half_of(kind)
     inner = right_ref.shape[0]
     total = dot(lefts_ref[half, :, :inner], right_ref[...]) + dot(lefts_ref[half, :, inner:], edge_ref[...])
-    share(total, keep_ref, send_ref, total_ref)
+    share(steps(), total, keep_ref, send_ref, total_ref)
 
 
 def second_kernel(lefts_ref, right_ref, edge_ref, keep_ref, send_ref, total_ref):
@@ -554,7 +555,8 @@
         [high, low, matrix, ahead_part, back_part, past_maps, own, others, begun_first],
         [total],
     )
-    came_first = exchange(sent_first, plan[0])
+    plan_first = steps(False)
+    came_first = exchange(sent_first, plan_first[0])
     near, right_edge = lax.optimization_barrier((near, right_edge))
     near_rows = near[:, : 2 * row_size]
     far = jnp.stack([shifted(near_rows, "ma", -step) for step in range(1, groups)])
@@ -579,10 +581,10 @@
     staying = [(own_first, came_own, slice(0, parts)), (own_second, came_own, slice(parts, 2 * parts))]
     crossing = [(kept_first, came_first), (kept_second, came_second)]
     after = own_second
-    for step in plan[1:]:
+    for turn in zip(plan_first[1:], plan[1:]):
         for d, (kept, came) in enumerate(crossing):
             came, after = lax.optimization_barrier((came, after))
-            crossing[d] = halve([(kept, came, None)], step, 4 * project_flops if d else 0)
+            crossing[d] = halve([(kept, came, None)], turn[d], 4 * project_flops if d else 0)
             after = crossing[d][0]
     crossed = []
     for kept, came in crossing:

time: 33.2 us -> 35.4 us (1.066)
  waiting for transfers between devices: 7.22 us -> 9.49 us
    ppermute x8, waiting for transfers between devices: 5.91 us -> 8.54 us  [exchange(): return lax.ppermute(block, axes, route)]
  transfers between devices with their start and end apart: 13 -> 13, of which waited for: 7 -> 7; matrix products, arithmetic and copies ran while one was open for 0% -> 0% of each run, Pallas kernels for 23% -> 22%
where the time goes in v14:
time: 35.4 us; the launch traced here: 35.3 us
  starting transfers between devices  17.3 us (49%)
  waiting for transfers between devices  9.49 us (27%)
  Pallas kernels  8.39 us (24%)
    ppermute x8, starting transfers between devices, exchange(): return lax.ppermute(block, axes, route)  10.4 us
    ppermute x8, waiting for transfers between devices, exchange(): return lax.ppermute(block, axes, route)  8.54 us
    pallas_call x19, Pallas kernels, call(): pl.pallas_call(body, out_shape=out_shape, in_specs=[pl.BlockSpec(memory_s...  8.39 us
    ppermute x5, starting transfers between devices, shifted(): return lax.ppermute(block, axis, route)  6.9 us
    ppermute x5, waiting for transfers between devices, shifted(): return lax.ppermute(block, axis, route)  0.95 us
  transfers between devices with their start and end apart: 13, of which 7 were waited for; matrix products, arithmetic and copies ran while one was open for 0% of the time, Pallas kernels for 22%

profile of v14, /device:TPU:0, one launch (start us, length us, event | category | flops | bytes accessed | tf_op | source)
XLA Modules:
  0.0 35.3 jit_solution(2297598807158254529)
XLA Ops:
  0.0 0.5 %collective-permute-start = (bf16[2,8,16,3,2,256]{5,4,3,2,1,0:T(2,128)(2,1)}, bf16[2,8,16,3,2,256]{5,4,3,2,1,0:T(2,128)(2,1)S(1)}, u32[]{:S(2)}, u32[]{:S(2)}) collective-permute-start(bf16[2,8,16,3,2,256]{5,4,3,2,1,0:T(2,128)(2,1)} %bitcast.11), channel_id=1, source_target_pairs={{1,0},{0,1},{3,2},{2,3},{5,4},{4,5},{7,6},{6,7},{9,8},{8,9},{11,10... | collective-permute-start | bytes 2359304 | tf_op jit(solution)/shard_map/ppermute | solution.py:14
  0.5 1.4 %shard_map.37 = (bf16[2,16,3,2,256]{4,3,2,1,0:T(2,128)(2,1)S(1)}, bf16[2,19,3,2,256]{4,3,2,1,0:T(2,128)(2,1)S(1)}, bf16[2,8,16,3,2,256]{5,4,3,2,1,0:T(2,128)(2,1...) custom-call(bf16[2,8,16,3,2,256]{5,4,3,2,1,0:T(2,128)(2,1)} %bitcast, ...), custom_call_target="tpu_custom_call" | custom-call | tf_op jit(solution)/shard_map/pallas_call | solution.py:19
  1.8 2.6 %collective-permute-start.3 = (bf16[2,19,3,2,256]{4,3,2,1,0:T(2,128)(2,1)S(1)}, bf16[2,19,3,2,256]{4,3,2,1,0:T(2,128)(2,1)S(1)}, u32[]{:S(2)}, u32[]{:S(2)}) collective-permute-start(bf16[2,19,3,2,256]{4,3,2,1,0:T(2,128)(2,1)S(1)} %get-tuple-element.70), channel_id=1, source_target_pairs={{12,0},{0,4},{4,8},{8,12},{13,1},{1,5},{5,9},{9,13},{14,2},{2,6},{... | collective-permute-start | bytes 350216 | tf_op jit(solution)/shard_map/ppermute | solution.py:14
  4.4 2.1 %collective-permute-start.2 = (bf16[2,16,3,2,256]{4,3,2,1,0:T(2,128)(2,1)S(1)}, bf16[2,16,3,2,256]{4,3,2,1,0:T(2,128)(2,1)S(1)}, u32[]{:S(2)}, u32[]{:S(2)}) collective-permute-start(bf16[2,16,3,2,256]{4,3,2,1,0:T(2,128)(2,1)S(1)} %get-tuple-element.69), channel_id=1, source_target_pairs={{4,0},{8,4},{12,8},{0,12},{5,1},{9,5},{13,9},{1,13},{6,2},{10,6},{... | collective-permute-start | bytes 294920 | tf_op jit(solution)/shard_map/ppermute | solution.py:14
  6.5 0.7 %shard_map.38 = (bf16[8,192,256]{2,1,0:T(8,128)(2,1)S(1)}, bf16[8,32,256]{2,1,0:T(8,128)(2,1)S(1)}, f32[8,8,256]{2,1,0:T(8,128)S(1)}, f32[8,8,256]{2,1,0:T(8,128...) custom-call(bf16[2,8,16,3,2,256]{5,4,3,2,1,0:T(2,128)(2,1)S(1)} %get-tuple-element.54.raw_ref, ...), custom_call_target="tpu_custom_call" | custom-call | tf_op jit(solution)/shard_map/pallas_call | solution.py:19
  7.3 1.7 %collective-permute-start.1 = (bf16[8,32,256]{2,1,0:T(8,128)(2,1)S(1)}, bf16[8,32,256]{2,1,0:T(8,128)(2,1)S(1)}, u32[]{:S(2)}, u32[]{:S(2)}) collective-permute-start(bf16[8,32,256]{2,1,0:T(8,128)(2,1)S(1)} %get-tuple-element.68), channel_id=1, source_target_pairs={{2,0},{0,2},{3,1},{1,3},{6,4},{4,6},{7,5},{5,7},{10,8},{8,10},{11,... | collective-permute-start | bytes 393224 | tf_op jit(solution)/shard_map/ppermute | solution.py:14
  8.9 0.5 %shard_map.39 = (bf16[1152,512]{1,0:T(8,128)(2,1)S(1)}, bf16[256,1536]{1,0:T(8,128)(2,1)S(1)}, bf16[192,192]{1,0:T(8,128)(2,1)S(1)}, f32[192,256]{1,0:T(8,128)S(1)}, f32[192,256]{1,0:T(8,128)S(1)}) custom-call(bf16[8,192,256]{2,1,0:T(8,128)(2,1)S(1)} %get-tuple-element.58.refs_0_, f32[8,8,256]{2,1,0:T(8,128)S(1)} %get-tuple-element.59.refs_1_, ...), custom_call_target="tpu_custom_call" | custom-call | flops 150994944 | tf_op jit(solution)/shard_map/pallas_call | solution.py:19
  9.5 0.0 collective-permute-done.raw_ref
  9.5 0.3 shard_map.40
  9.8 0.6 %shard_map.41.refs_0_ = f32[2,8,192,256]{3,2,1,0:T(8,128)S(1)} custom-call(bf16[8,192,256]{2,1,0:T(8,128)(2,1)S(1)} %get-tuple-element.58.refs_0_, bf16[1,8,192,256]{3,2,1,0:T(8,128)(2,1)S(1)} %bitcast.9, f32[8,8,256]{2,1,0:T(8,128)S(1)} %get-tuple-element.64.refs_2_.refs_3_, f32[8,8,256]{2,1,0:T(8,128)S(1)} %get-tuple-element.65.refs_3_), custom_call_target="tpu_custom_call" | custom-call | flops 150994944 | tf_op jit(solution)/shard_map/pallas_call | solution.py:19
  10.4 0.8 %shard_map.42.refs_8_.begun_ref = f32[2,256,512]{2,1,0:T(8,128)S(1)} custom-call(bf16[256,1536]{1,0:T(8,128)(2,1)S(1)} %get-tuple-element.61.own_ref.refs_6_, bf16[1,256,1536]{2,1,0:T(8,128)(2,1)S(1)} %bitcast.6, bf16[1152,512]{1,0:T(8,128)(2,1)S(1)} %get-tuple-element.66.right_ref), custom_call_target="tpu_custom_call" | custom-call | flops 402653184 | tf_op jit(solution)/shard_map/pallas_call | solution.py:19
  11.2 0.7 %collective-permute-done.2.refs_0_ = bf16[2,16,3,2,256]{4,3,2,1,0:T(2,128)(2,1)S(1)} collective-permute-done((bf16[2,16,3,2,256]{4,3,2,1,0:T(2,128)(2,1)S(1)}, bf16[2,16,3,2,256]{4,3,2,1,0:T(2,128)(2,1)S(1)}, u32[]{:S(2)}, u32[]{:S(2)}) %collective-permute-start.2) | collective-permute-done | bytes 98336 | tf_op jit(solution)/shard_map/ppermute | solution.py:14
  11.9 0.0 collective-permute-done.3.refs_1_
  11.9 0.8 %shard_map.43 = (f32[2,2,64,256]{3,2,1,0:T(8,128)S(1)}, bf16[2,2,64,256]{3,2,1,0:T(8,128)(2,1)S(1)}, bf16[384,512]{1,0:T(8,128)(2,1)S(1)}) custom-call(bf16[2,16,3,2,256]{4,3,2,1,0:T(2,128)(2,1)S(1)} %collective-permute-done.2.refs_0_, bf16[2,19,3,2,256]{4,3,2,1,0:T(2,128)(2,1)S(1)} %collective-permute-done.3.refs_1_, ...), custom_call_target="tpu_custom_call" | custom-call | flops 402653184 | tf_op jit(solution)/shard_map/pallas_call | solution.py:19
  12.7 0.3 collective-permute-done.1.refs_1_
  12.9 0.1 collective-permute-start.4
  13.0 1.6 %collective-permute-start.7 = (bf16[2,2,64,256]{3,2,1,0:T(8,128)(2,1)S(1)}, bf16[2,2,64,256]{3,2,1,0:T(8,128)(2,1)S(1)}, u32[]{:S(2)}, u32[]{:S(2)}) collective-permute-start(bf16[2,2,64,256]{3,2,1,0:T(8,128)(2,1)S(1)} %get-tuple-element.87), channel_id=1, source_target_pairs={{0,2},{1,3},{2,0},{3,1},{4,6},{5,7},{6,4},{7,5},{8,10},{9,11},{10,... | collective-permute-start | bytes 393224 | tf_op jit(solution)/shard_map/ppermute | solution.py:418
  14.6 0.0 collective-permute-done.4
  14.6 0.6 %shard_map.44.lefts_ref = bf16[2,256,1536]{2,1,0:T(8,128)(2,1)S(1)} custom-call(f32[2,8,192,256]{3,2,1,0:T(8,128)S(1)} %shard_map.41.refs_0_, bf16[8,32,256]{2,1,0:T(8,128)(2,1)S(1)} %collective-permute-done.1.refs_1_, bf16[1,8,24,256]{3,2,1,0:T(8,128)(2,1)S(1)} %bitcast.10, f32[8,8,256]{2,1,0:T(8,128)S(1)} %get-tuple-element.64.refs_2_.refs_3_), custom_call_target="tpu_custom_call" | custom-call | flops 150994944 | tf_op jit(solution)/shard_map/pallas_call | solution.py:19
  15.2 0.7 %shard_map.45 = (f32[2,2,64,256]{3,2,1,0:T(8,128)S(1)}, bf16[2,2,64,256]{3,2,1,0:T(8,128)(2,1)S(1)}) custom-call(bf16[2,256,1536]{2,1,0:T(8,128)(2,1)S(1)} %shard_map.44.lefts_ref, bf16[1152,512]{1,0:T(8,128)(2,1)S(1)} %get-tuple-element.66.right_ref, bf16[384,512]{1,0:T(8,128)(2,1)S(1)} %get-tuple-element.80.edge_ref.right_ref), custom_call_target="tpu_custom_call" | custom-call | flops 3221225472 | tf_op jit(solution)/shard_map/pallas_call | solution.py:19
  15.9 1.0 %collective-permute-start.6 = (bf16[2,2,64,256]{3,2,1,0:T(8,128)(2,1)S(1)}, bf16[2,2,64,256]{3,2,1,0:T(8,128)(2,1)S(1)}, u32[]{:S(2)}, u32[]{:S(2)}) collective-permute-start(bf16[2,2,64,256]{3,2,1,0:T(8,128)(2,1)S(1)} %get-tuple-element.85), channel_id=1, source_target_pairs={{0,4},{1,3},{2,6},{3,1},{4,0},{5,7},{6,2},{7,5},{8,12},{9,11},{10,... | collective-permute-start | bytes 393224 | tf_op jit(solution)/shard_map/ppermute | solution.py:418
  16.9 0.4 %shard_map.46 = (f32[2,2,64,256]{3,2,1,0:T(8,128)S(1)}, bf16[2,2,64,256]{3,2,1,0:T(8,128)(2,1)S(1)}) custom-call(bf16[256,1536]{1,0:T(8,128)(2,1)S(1)} %get-tuple-element.61.own_ref.refs_6_, bf16[1,256,1536]{2,1,0:T(8,128)(2,1)S(1)} %bitcast.8, f32[2,256,512]{2,1,0:T(8,128)S(1)} %shard_map.42.refs_8_.begun_ref, ...), custom_call_target="tpu_custom_call" | custom-call | tf_op jit(solution)/shard_map/pallas_call | solution.py:19
  17.2 0.7 %shard_map.47 = (f32[2,2,64,256]{3,2,1,0:T(8,128)S(1)}, bf16[4,2,64,256]{3,2,1,0:T(8,128)(2,1)S(1)}) custom-call(bf16[2,256,1536]{2,1,0:T(8,128)(2,1)S(1)} %shard_map.44.lefts_ref, bf16[1152,512]{1,0:T(8,128)(2,1)S(1)} %get-tuple-element.66.right_ref, bf16[384,512]{1,0:T(8,128)(2,1)S(1)} %get-tuple-element.80.edge_ref.right_ref, ...), custom_call_target="tpu_custom_call" | custom-call | tf_op jit(solution)/shard_map/pallas_call | solution.py:19
  17.9 1.2 %collective-permute-start.5 = (bf16[4,2,64,256]{3,2,1,0:T(8,128)(2,1)S(1)}, bf16[4,2,64,256]{3,2,1,0:T(8,128)(2,1)S(1)}, u32[]{:S(2)}, u32[]{:S(2)}) collective-permute-start(bf16[4,2,64,256]{3,2,1,0:T(8,128)(2,1)S(1)} %get-tuple-element.83), channel_id=1, source_target_pairs={{0,4},{1,3},{2,6},{3,1},{4,0},{5,7},{6,2},{7,5},{8,12},{9,11},{10,... | collective-permute-start | bytes 786440 | tf_op jit(solution)/shard_map/ppermute | solution.py:418
  19.1 0.0 collective-permute-done.7.refs_1_
  19.2 1.0 %collective-permute-start.9 = (bf16[2,1,64,256]{3,2,1,0:T(8,128)(2,1)S(1)}, bf16[2,1,64,256]{3,2,1,0:T(8,128)(2,1)S(1)}, u32[]{:S(2)}, u32[]{:S(2)}) collective-permute-start(bf16[2,1,64,256]{3,2,1,0:T(8,128)(2,1)S(1)} %get-tuple-element.94), channel_id=1, source_target_pairs={{0,4},{1,5},{2,6},{3,7},{4,0},{5,1},{6,2},{7,3},{8,12},{9,13},{10,... | collective-permute-start | bytes 196616 | tf_op jit(solution)/shard_map/ppermute | solution.py:418
  20.1 0.8 %collective-permute-done.6.refs_1_ = bf16[2,2,64,256]{3,2,1,0:T(8,128)(2,1)S(1)} collective-permute-done((bf16[2,2,64,256]{3,2,1,0:T(8,128)(2,1)S(1)}, bf16[2,2,64,256]{3,2,1,0:T(8,128)(2,1)S(1)}, u32[]{:S(2)}, u32[]{:S(2)}) %collective-permute-start.6) | collective-permute-done | bytes 131104 | tf_op jit(solution)/shard_map/ppermute | solution.py:418
  21.0 1.3 %collective-permute-start.8 = (bf16[2,1,64,256]{3,2,1,0:T(8,128)(2,1)S(1)}, bf16[2,1,64,256]{3,2,1,0:T(8,128)(2,1)S(1)}, u32[]{:S(2)}, u32[]{:S(2)}) collective-permute-start(bf16[2,1,64,256]{3,2,1,0:T(8,128)(2,1)S(1)} %get-tuple-element.93), channel_id=1, source_target_pairs={{0,2},{1,5},{2,0},{3,7},{4,6},{5,1},{6,4},{7,3},{8,10},{9,13},{10,... | collective-permute-start | bytes 196616 | tf_op jit(solution)/shard_map/ppermute | solution.py:418
  22.3 4.1 %collective-permute-done.9.came_ref = bf16[2,1,64,256]{3,2,1,0:T(8,128)(2,1)S(1)} collective-permute-done((bf16[2,1,64,256]{3,2,1,0:T(8,128)(2,1)S(1)}, bf16[2,1,64,256]{3,2,1,0:T(8,128)(2,1)S(1)}, u32[]{:S(2)}, u32[]{:S(2)}) %collective-permute-start.9) | collective-permute-done | bytes 65568 | tf_op jit(solution)/shard_map/ppermute | solution.py:418
  26.4 1.5 %collective-permute-start.12 = (bf16[2,1,64,256]{3,2,1,0:T(8,128)(2,1)S(1)}, bf16[2,1,64,256]{3,2,1,0:T(8,128)(2,1)S(1)}, u32[]{:S(2)}, u32[]{:S(2)}) collective-permute-start(bf16[2,1,64,256]{3,2,1,0:T(8,128)(2,1)S(1)} %shard_map.50), channel_id=1, source_target_pairs={{0,8},{1,9},{2,10},{3,11},{4,12},{5,13},{6,14},{7,15},{8,0},{9,1},... | collective-permute-start | bytes 196616 | tf_op jit(solution)/shard_map/ppermute | solution.py:418
  27.9 0.0 collective-permute-done.8.came_ref
  27.9 1.5 %collective-permute-start.11 = (bf16[2,1,64,256]{3,2,1,0:T(8,128)(2,1)S(1)}, bf16[2,1,64,256]{3,2,1,0:T(8,128)(2,1)S(1)}, u32[]{:S(2)}, u32[]{:S(2)}) collective-permute-start(bf16[2,1,64,256]{3,2,1,0:T(8,128)(2,1)S(1)} %shard_map.51), channel_id=1, source_target_pairs={{0,8},{1,9},{2,10},{3,11},{4,12},{5,13},{6,14},{7,15},{8,0},{9,1},... | collective-permute-start | bytes 196616 | tf_op jit(solution)/shard_map/ppermute | solution.py:418
  29.5 0.0 collective-permute-done.5.refs_1_.refs_3_
  29.5 0.1 shard_map.52
  29.5 1.4 %collective-permute-start.10 = (bf16[4,1,64,256]{3,2,1,0:T(8,128)(2,1)S(1)}, bf16[4,1,64,256]{3,2,1,0:T(8,128)(2,1)S(1)}, u32[]{:S(2)}, u32[]{:S(2)}) collective-permute-start(bf16[4,1,64,256]{3,2,1,0:T(8,128)(2,1)S(1)} %get-tuple-element.98), channel_id=1, source_target_pairs={{0,2},{1,5},{2,0},{3,7},{4,6},{5,1},{6,4},{7,3},{8,10},{9,13},{10,... | collective-permute-start | bytes 393224 | tf_op jit(solution)/shard_map/ppermute | solution.py:418
  30.9 0.7 %collective-permute-done.12.refs_1_ = bf16[2,1,64,256]{3,2,1,0:T(8,128)(2,1)S(1)} collective-permute-done((bf16[2,1,64,256]{3,2,1,0:T(8,128)(2,1)S(1)}, bf16[2,1,64,256]{3,2,1,0:T(8,128)(2,1)S(1)}, u32[]{:S(2)}, u32[]{:S(2)}) %collective-permute-start.12) | collective-permute-done | bytes 65568 | tf_op jit(solution)/shard_map/ppermute | solution.py:418
  31.6 2.4 %collective-permute-done.11.refs_1_ = bf16[2,1,64,256]{3,2,1,0:T(8,128)(2,1)S(1)} collective-permute-done((bf16[2,1,64,256]{3,2,1,0:T(8,128)(2,1)S(1)}, bf16[2,1,64,256]{3,2,1,0:T(8,128)(2,1)S(1)}, u32[]{:S(2)}, u32[]{:S(2)}) %collective-permute-start.11) | collective-permute-done | bytes 65568 | tf_op jit(solution)/shard_map/ppermute | solution.py:418
  34.0 0.5 %collective-permute-done.10.came_ref = bf16[4,1,64,256]{3,2,1,0:T(8,128)(2,1)S(1)} collective-permute-done((bf16[4,1,64,256]{3,2,1,0:T(8,128)(2,1)S(1)}, bf16[4,1,64,256]{3,2,1,0:T(8,128)(2,1)S(1)}, u32[]{:S(2)}, u32[]{:S(2)}) %collective-permute-start.10) | collective-permute-done | bytes 131104 | tf_op jit(solution)/shard_map/ppermute | solution.py:418
  34.6 0.7 %shard_map.55 = f32[2,2,64,256]{3,2,1,0:T(8,128)} custom-call(bf16[4,1,64,256]{3,2,1,0:T(8,128)(2,1)S(1)} %collective-permute-done.10.came_ref, f32[2,1,64,256]{3,2,1,0:T(8,128)S(1)} %shard_map.53.refs_0_, f32[2,1,64,256]{3,2,1,0:T(8,128)S(1)} %shard_map.54.refs_1_), custom_call_target="tpu_custom_call" | custom-call | tf_op jit(solution)/shard_map/pallas_call | solution.py:19
  (7 shorter events, 0.1 us)
Async XLA Ops:
  0.0 9.5 %collective-permute-start = (bf16[2,8,16,3,2,256]{5,4,3,2,1,0:T(2,128)(2,1)}, bf16[2,8,16,3,2,256]{5,4,3,2,1,0:T(2,128)(2,1)S(1)}, u32[]{:S(2)}, u32[]{:S(2)}) collective-permute-start(bf16[2,8,16,3,2,256]{5,4,3,2,1,0:T(2,128)(2,1)} %bitcast.11), channel_id=1, source_target_pairs={{1,0},{0,1},{3,2},{2,3},{5,4},{4,5},{7,6},{6,7},{9,8},{8,9},{11,10... | collective-permute-start | bytes 2359304 | tf_op jit(solution)/shard_map/ppermute | solution.py:14
  1.8 10.1 %collective-permute-start.3 = (bf16[2,19,3,2,256]{4,3,2,1,0:T(2,128)(2,1)S(1)}, bf16[2,19,3,2,256]{4,3,2,1,0:T(2,128)(2,1)S(1)}, u32[]{:S(2)}, u32[]{:S(2)}) collective-permute-start(bf16[2,19,3,2,256]{4,3,2,1,0:T(2,128)(2,1)S(1)} %get-tuple-element.70), channel_id=1, source_target_pairs={{12,0},{0,4},{4,8},{8,12},{13,1},{1,5},{5,9},{9,13},{14,2},{2,6},{... | collective-permute-start | bytes 350216 | tf_op jit(solution)/shard_map/ppermute | solution.py:14
  4.4 7.4 %collective-permute-start.2 = (bf16[2,16,3,2,256]{4,3,2,1,0:T(2,128)(2,1)S(1)}, bf16[2,16,3,2,256]{4,3,2,1,0:T(2,128)(2,1)S(1)}, u32[]{:S(2)}, u32[]{:S(2)}) collective-permute-start(bf16[2,16,3,2,256]{4,3,2,1,0:T(2,128)(2,1)S(1)} %get-tuple-element.69), channel_id=1, source_target_pairs={{4,0},{8,4},{12,8},{0,12},{5,1},{9,5},{13,9},{1,13},{6,2},{10,6},{... | collective-permute-start | bytes 294920 | tf_op jit(solution)/shard_map/ppermute | solution.py:14
  7.3 5.6 %collective-permute-start.1 = (bf16[8,32,256]{2,1,0:T(8,128)(2,1)S(1)}, bf16[8,32,256]{2,1,0:T(8,128)(2,1)S(1)}, u32[]{:S(2)}, u32[]{:S(2)}) collective-permute-start(bf16[8,32,256]{2,1,0:T(8,128)(2,1)S(1)} %get-tuple-element.68), channel_id=1, source_target_pairs={{2,0},{0,2},{3,1},{1,3},{6,4},{4,6},{7,5},{5,7},{10,8},{8,10},{11,... | collective-permute-start | bytes 393224 | tf_op jit(solution)/shard_map/ppermute | solution.py:14
  12.9 1.6 %collective-permute-start.4 = (bf16[8,24,256]{2,1,0:T(8,128)(2,1)S(1)}, bf16[8,24,256]{2,1,0:T(8,128)(2,1)S(1)}, u32[]{:S(2)}, u32[]{:S(2)}) collective-permute-start(bf16[8,24,256]{2,1,0:T(8,128)(2,1)S(1)} %slice.3), channel_id=1, source_target_pairs={{1,0},{0,1},{3,2},{2,3},{5,4},{4,5},{7,6},{6,7},{9,8},{8,9},{11,10... | collective-permute-start | bytes 294920 | tf_op jit(solution)/shard_map/ppermute | solution.py:14
  13.0 6.1 %collective-permute-start.7 = (bf16[2,2,64,256]{3,2,1,0:T(8,128)(2,1)S(1)}, bf16[2,2,64,256]{3,2,1,0:T(8,128)(2,1)S(1)}, u32[]{:S(2)}, u32[]{:S(2)}) collective-permute-start(bf16[2,2,64,256]{3,2,1,0:T(8,128)(2,1)S(1)} %get-tuple-element.87), channel_id=1, source_target_pairs={{0,2},{1,3},{2,0},{3,1},{4,6},{5,7},{6,4},{7,5},{8,10},{9,11},{10,... | collective-permute-start | bytes 393224 | tf_op jit(solution)/shard_map/ppermute | solution.py:418
  15.9 5.0 %collective-permute-start.6 = (bf16[2,2,64,256]{3,2,1,0:T(8,128)(2,1)S(1)}, bf16[2,2,64,256]{3,2,1,0:T(8,128)(2,1)S(1)}, u32[]{:S(2)}, u32[]{:S(2)}) collective-permute-start(bf16[2,2,64,256]{3,2,1,0:T(8,128)(2,1)S(1)} %get-tuple-element.85), channel_id=1, source_target_pairs={{0,4},{1,3},{2,6},{3,1},{4,0},{5,7},{6,2},{7,5},{8,12},{9,11},{10,... | collective-permute-start | bytes 393224 | tf_op jit(solution)/shard_map/ppermute | solution.py:418
  17.9 11.5 %collective-permute-start.5 = (bf16[4,2,64,256]{3,2,1,0:T(8,128)(2,1)S(1)}, bf16[4,2,64,256]{3,2,1,0:T(8,128)(2,1)S(1)}, u32[]{:S(2)}, u32[]{:S(2)}) collective-permute-start(bf16[4,2,64,256]{3,2,1,0:T(8,128)(2,1)S(1)} %get-tuple-element.83), channel_id=1, source_target_pairs={{0,4},{1,3},{2,6},{3,1},{4,0},{5,7},{6,2},{7,5},{8,12},{9,11},{10,... | collective-permute-start | bytes 786440 | tf_op jit(solution)/shard_map/ppermute | solution.py:418
  19.2 7.2 %collective-permute-start.9 = (bf16[2,1,64,256]{3,2,1,0:T(8,128)(2,1)S(1)}, bf16[2,1,64,256]{3,2,1,0:T(8,128)(2,1)S(1)}, u32[]{:S(2)}, u32[]{:S(2)}) collective-permute-start(bf16[2,1,64,256]{3,2,1,0:T(8,128)(2,1)S(1)} %get-tuple-element.94), channel_id=1, source_target_pairs={{0,4},{1,5},{2,6},{3,7},{4,0},{5,1},{6,2},{7,3},{8,12},{9,13},{10,... | collective-permute-start | bytes 196616 | tf_op jit(solution)/shard_map/ppermute | solution.py:418
  21.0 6.9 %collective-permute-start.8 = (bf16[2,1,64,256]{3,2,1,0:T(8,128)(2,1)S(1)}, bf16[2,1,64,256]{3,2,1,0:T(8,128)(2,1)S(1)}, u32[]{:S(2)}, u32[]{:S(2)}) collective-permute-start(bf16[2,1,64,256]{3,2,1,0:T(8,128)(2,1)S(1)} %get-tuple-element.93), channel_id=1, source_target_pairs={{0,2},{1,5},{2,0},{3,7},{4,6},{5,1},{6,4},{7,3},{8,10},{9,13},{10,... | collective-permute-start | bytes 196616 | tf_op jit(solution)/shard_map/ppermute | solution.py:418
  26.4 5.2 %collective-permute-start.12 = (bf16[2,1,64,256]{3,2,1,0:T(8,128)(2,1)S(1)}, bf16[2,1,64,256]{3,2,1,0:T(8,128)(2,1)S(1)}, u32[]{:S(2)}, u32[]{:S(2)}) collective-permute-start(bf16[2,1,64,256]{3,2,1,0:T(8,128)(2,1)S(1)} %shard_map.50), channel_id=1, source_target_pairs={{0,8},{1,9},{2,10},{3,11},{4,12},{5,13},{6,14},{7,15},{8,0},{9,1},... | collective-permute-start | bytes 196616 | tf_op jit(solution)/shard_map/ppermute | solution.py:418
  27.9 6.1 %collective-permute-start.11 = (bf16[2,1,64,256]{3,2,1,0:T(8,128)(2,1)S(1)}, bf16[2,1,64,256]{3,2,1,0:T(8,128)(2,1)S(1)}, u32[]{:S(2)}, u32[]{:S(2)}) collective-permute-start(bf16[2,1,64,256]{3,2,1,0:T(8,128)(2,1)S(1)} %shard_map.51), channel_id=1, source_target_pairs={{0,8},{1,9},{2,10},{3,11},{4,12},{5,13},{6,14},{7,15},{8,0},{9,1},... | collective-permute-start | bytes 196616 | tf_op jit(solution)/shard_map/ppermute | solution.py:418
  29.5 5.0 %collective-permute-start.10 = (bf16[4,1,64,256]{3,2,1,0:T(8,128)(2,1)S(1)}, bf16[4,1,64,256]{3,2,1,0:T(8,128)(2,1)S(1)}, u32[]{:S(2)}, u32[]{:S(2)}) collective-permute-start(bf16[4,1,64,256]{3,2,1,0:T(8,128)(2,1)S(1)} %get-tuple-element.98), channel_id=1, source_target_pairs={{0,2},{1,5},{2,0},{3,7},{4,6},{5,1},{6,4},{7,3},{8,10},{9,13},{10,... | collective-permute-start | bytes 393224 | tf_op jit(solution)/shard_map/ppermute | solution.py:418

commit v15 on v10

--- a/solution.py
+++ b/solution.py
@@ -374,16 +374,17 @@
     lower = (lane >= depth + row_size) & (lane < depth + 2 * row_size)
     to_next = jnp.where(upper & (site == sites - zs + lane % zs), -1.0, 0.0)
     to_last = jnp.where(lower & (site == lane % zs), -1.0, 0.0)
-    above = jnp.zeros((depth - head, width), jnp.bfloat16)
-    below = jnp.zeros((tail - 2 * row_size - (depth - head), width), jnp.bfloat16)
+    above = jnp.zeros((depth - head, width), jnp.float32)
+    below = jnp.zeros((tail - 2 * row_size - (depth - head), width), jnp.float32)
     for x in range(planes):
-        past = near_ref[x, 2 * row_size : 2 * row_size + 8, :tail].astype(jnp.float32)
+        near = near_ref[x].astype(jnp.float32)
+        past = near[2 * row_size : 2 * row_size + 8, :tail]
         matrix = site_matrix([(ahead_ref[x, :, head:], to_next), (past, to_last)], depth // sites)
         place = place_of(x, planes)
         for k in range(groups):
-            edge = near_ref[x, : 2 * row_size] if k == 0 else far_ref[k - 1, x]
-            moved = part_ref[k, place] + dot(matrix, jnp.concatenate([above, edge, below], axis=0))
-            field_ref[k, place] = moved.astype(jnp.bfloat16)
+            edge = near[: 2 * row_size] if k == 0 else far_ref[k - 1, x].astype(jnp.float32)
+            column = jnp.concatenate([above, edge, below], axis=0).astype(jnp.bfloat16)
+            field_ref[k, place] = (part_ref[k, place] + dot(matrix, column)).astype(jnp.bfloat16)
     for k in range(groups):
         turned_ref[k] = field_ref[k].reshape(planes * depth, width).T
 

time: 33.2 us -> 33.2 us (level)
  no operation moved by 1% of the time
where the time goes in v15:
time: 33.2 us; the launch traced here: 33.1 us
  starting transfers between devices  17.3 us (52%)
  Pallas kernels  8.39 us (25%)
  waiting for transfers between devices  7.21 us (22%)
    ppermute x8, starting transfers between devices, exchange(): return lax.ppermute(block, axes, route)  10.4 us
    pallas_call x19, Pallas kernels, call(): pl.pallas_call(body, out_shape=out_shape, in_specs=[pl.BlockSpec(memory_s...  8.39 us
    ppermute x5, starting transfers between devices, shifted(): return lax.ppermute(block, axis, route)  6.9 us
    ppermute x8, waiting for transfers between devices, exchange(): return lax.ppermute(block, axes, route)  5.91 us
    ppermute x5, waiting for transfers between devices, shifted(): return lax.ppermute(block, axis, route)  1.3 us
  transfers between devices with their start and end apart: 13, of which 7 were waited for; matrix products, arithmetic and copies ran while one was open for 0% of the time, Pallas kernels for 23%

profile of v15, /device:TPU:0, one launch (start us, length us, event | category | flops | bytes accessed | tf_op | source)
XLA Modules:
  0.0 33.1 jit_solution(16732700386627371138)
XLA Ops:
  0.0 0.5 %collective-permute-start = (bf16[2,8,16,3,2,256]{5,4,3,2,1,0:T(2,128)(2,1)}, bf16[2,8,16,3,2,256]{5,4,3,2,1,0:T(2,128)(2,1)S(1)}, u32[]{:S(2)}, u32[]{:S(2)}) collective-permute-start(bf16[2,8,16,3,2,256]{5,4,3,2,1,0:T(2,128)(2,1)} %bitcast.11), channel_id=1, source_target_pairs={{1,0},{0,1},{3,2},{2,3},{5,4},{4,5},{7,6},{6,7},{9,8},{8,9},{11,10... | collective-permute-start | bytes 2359304 | tf_op jit(solution)/shard_map/ppermute | solution.py:14
  0.5 1.4 %shard_map.37 = (bf16[2,16,3,2,256]{4,3,2,1,0:T(2,128)(2,1)S(1)}, bf16[2,19,3,2,256]{4,3,2,1,0:T(2,128)(2,1)S(1)}, bf16[2,8,16,3,2,256]{5,4,3,2,1,0:T(2,128)(2,1...) custom-call(bf16[2,8,16,3,2,256]{5,4,3,2,1,0:T(2,128)(2,1)} %bitcast, ...), custom_call_target="tpu_custom_call" | custom-call | tf_op jit(solution)/shard_map/pallas_call | solution.py:19
  1.8 2.6 %collective-permute-start.3 = (bf16[2,19,3,2,256]{4,3,2,1,0:T(2,128)(2,1)S(1)}, bf16[2,19,3,2,256]{4,3,2,1,0:T(2,128)(2,1)S(1)}, u32[]{:S(2)}, u32[]{:S(2)}) collective-permute-start(bf16[2,19,3,2,256]{4,3,2,1,0:T(2,128)(2,1)S(1)} %get-tuple-element.70), channel_id=1, source_target_pairs={{12,0},{0,4},{4,8},{8,12},{13,1},{1,5},{5,9},{9,13},{14,2},{2,6},{... | collective-permute-start | bytes 350216 | tf_op jit(solution)/shard_map/ppermute | solution.py:14
  4.4 2.1 %collective-permute-start.2 = (bf16[2,16,3,2,256]{4,3,2,1,0:T(2,128)(2,1)S(1)}, bf16[2,16,3,2,256]{4,3,2,1,0:T(2,128)(2,1)S(1)}, u32[]{:S(2)}, u32[]{:S(2)}) collective-permute-start(bf16[2,16,3,2,256]{4,3,2,1,0:T(2,128)(2,1)S(1)} %get-tuple-element.69), channel_id=1, source_target_pairs={{4,0},{8,4},{12,8},{0,12},{5,1},{9,5},{13,9},{1,13},{6,2},{10,6},{... | collective-permute-start | bytes 294920 | tf_op jit(solution)/shard_map/ppermute | solution.py:14
  6.5 0.7 %shard_map.38 = (bf16[8,192,256]{2,1,0:T(8,128)(2,1)S(1)}, bf16[8,32,256]{2,1,0:T(8,128)(2,1)S(1)}, f32[8,8,256]{2,1,0:T(8,128)S(1)}, f32[8,8,256]{2,1,0:T(8,128...) custom-call(bf16[2,8,16,3,2,256]{5,4,3,2,1,0:T(2,128)(2,1)S(1)} %get-tuple-element.54.raw_ref, ...), custom_call_target="tpu_custom_call" | custom-call | tf_op jit(solution)/shard_map/pallas_call | solution.py:19
  7.3 1.7 %collective-permute-start.1 = (bf16[8,32,256]{2,1,0:T(8,128)(2,1)S(1)}, bf16[8,32,256]{2,1,0:T(8,128)(2,1)S(1)}, u32[]{:S(2)}, u32[]{:S(2)}) collective-permute-start(bf16[8,32,256]{2,1,0:T(8,128)(2,1)S(1)} %get-tuple-element.68), channel_id=1, source_target_pairs={{2,0},{0,2},{3,1},{1,3},{6,4},{4,6},{7,5},{5,7},{10,8},{8,10},{11,... | collective-permute-start | bytes 393224 | tf_op jit(solution)/shard_map/ppermute | solution.py:14
  8.9 0.5 %shard_map.39 = (bf16[1152,512]{1,0:T(8,128)(2,1)S(1)}, bf16[256,1536]{1,0:T(8,128)(2,1)S(1)}, bf16[192,192]{1,0:T(8,128)(2,1)S(1)}, f32[192,256]{1,0:T(8,128)S(1)}, f32[192,256]{1,0:T(8,128)S(1)}) custom-call(bf16[8,192,256]{2,1,0:T(8,128)(2,1)S(1)} %get-tuple-element.58.refs_0_, f32[8,8,256]{2,1,0:T(8,128)S(1)} %get-tuple-element.59.refs_1_, ...), custom_call_target="tpu_custom_call" | custom-call | flops 150994944 | tf_op jit(solution)/shard_map/pallas_call | solution.py:19
  9.5 0.0 collective-permute-done.raw_ref
  9.5 0.3 shard_map.40
  9.8 0.6 %shard_map.41.refs_0_ = f32[2,8,192,256]{3,2,1,0:T(8,128)S(1)} custom-call(bf16[8,192,256]{2,1,0:T(8,128)(2,1)S(1)} %get-tuple-element.58.refs_0_, bf16[1,8,192,256]{3,2,1,0:T(8,128)(2,1)S(1)} %bitcast.9, f32[8,8,256]{2,1,0:T(8,128)S(1)} %get-tuple-element.64.refs_2_.refs_3_, f32[8,8,256]{2,1,0:T(8,128)S(1)} %get-tuple-element.65.refs_3_), custom_call_target="tpu_custom_call" | custom-call | flops 150994944 | tf_op jit(solution)/shard_map/pallas_call | solution.py:19
  10.4 0.8 %shard_map.42.refs_8_.begun_ref = f32[2,256,512]{2,1,0:T(8,128)S(1)} custom-call(bf16[256,1536]{1,0:T(8,128)(2,1)S(1)} %get-tuple-element.61.own_ref.refs_6_, bf16[1,256,1536]{2,1,0:T(8,128)(2,1)S(1)} %bitcast.6, bf16[1152,512]{1,0:T(8,128)(2,1)S(1)} %get-tuple-element.66.right_ref), custom_call_target="tpu_custom_call" | custom-call | flops 402653184 | tf_op jit(solution)/shard_map/pallas_call | solution.py:19
  11.2 0.7 %collective-permute-done.2.refs_0_ = bf16[2,16,3,2,256]{4,3,2,1,0:T(2,128)(2,1)S(1)} collective-permute-done((bf16[2,16,3,2,256]{4,3,2,1,0:T(2,128)(2,1)S(1)}, bf16[2,16,3,2,256]{4,3,2,1,0:T(2,128)(2,1)S(1)}, u32[]{:S(2)}, u32[]{:S(2)}) %collective-permute-start.2) | collective-permute-done | bytes 98336 | tf_op jit(solution)/shard_map/ppermute | solution.py:14
  11.9 0.0 collective-permute-done.3.refs_1_
  11.9 0.8 %shard_map.43 = (f32[2,2,64,256]{3,2,1,0:T(8,128)S(1)}, bf16[2,2,64,256]{3,2,1,0:T(8,128)(2,1)S(1)}, bf16[384,512]{1,0:T(8,128)(2,1)S(1)}) custom-call(bf16[2,16,3,2,256]{4,3,2,1,0:T(2,128)(2,1)S(1)} %collective-permute-done.2.refs_0_, bf16[2,19,3,2,256]{4,3,2,1,0:T(2,128)(2,1)S(1)} %collective-permute-done.3.refs_1_, ...), custom_call_target="tpu_custom_call" | custom-call | flops 402653184 | tf_op jit(solution)/shard_map/pallas_call | solution.py:19
  12.7 0.3 collective-permute-done.1.refs_1_
  12.9 0.1 collective-permute-start.4
  13.0 0.9 %collective-permute-start.7 = (bf16[2,2,64,256]{3,2,1,0:T(8,128)(2,1)S(1)}, bf16[2,2,64,256]{3,2,1,0:T(8,128)(2,1)S(1)}, u32[]{:S(2)}, u32[]{:S(2)}) collective-permute-start(bf16[2,2,64,256]{3,2,1,0:T(8,128)(2,1)S(1)} %get-tuple-element.87), channel_id=1, source_target_pairs={{0,4},{1,3},{2,6},{3,1},{4,0},{5,7},{6,2},{7,5},{8,12},{9,11},{10,... | collective-permute-start | bytes 393224 | tf_op jit(solution)/shard_map/ppermute | solution.py:418
  14.0 0.3 %collective-permute-done.4 = bf16[8,24,256]{2,1,0:T(8,128)(2,1)S(1)} collective-permute-done((bf16[8,24,256]{2,1,0:T(8,128)(2,1)S(1)}, bf16[8,24,256]{2,1,0:T(8,128)(2,1)S(1)}, u32[]{:S(2)}, u32[]{:S(2)}) %collective-permute-start.4) | collective-permute-done | bytes 98336 | tf_op jit(solution)/shard_map/ppermute | solution.py:14
  14.3 0.6 %shard_map.44.lefts_ref = bf16[2,256,1536]{2,1,0:T(8,128)(2,1)S(1)} custom-call(f32[2,8,192,256]{3,2,1,0:T(8,128)S(1)} %shard_map.41.refs_0_, bf16[8,32,256]{2,1,0:T(8,128)(2,1)S(1)} %collective-permute-done.1.refs_1_, bf16[1,8,24,256]{3,2,1,0:T(8,128)(2,1)S(1)} %bitcast.10, f32[8,8,256]{2,1,0:T(8,128)S(1)} %get-tuple-element.64.refs_2_.refs_3_), custom_call_target="tpu_custom_call" | custom-call | flops 150994944 | tf_op jit(solution)/shard_map/pallas_call | solution.py:19
  15.0 0.7 %shard_map.45 = (f32[2,2,64,256]{3,2,1,0:T(8,128)S(1)}, bf16[2,2,64,256]{3,2,1,0:T(8,128)(2,1)S(1)}) custom-call(bf16[2,256,1536]{2,1,0:T(8,128)(2,1)S(1)} %shard_map.44.lefts_ref, bf16[1152,512]{1,0:T(8,128)(2,1)S(1)} %get-tuple-element.66.right_ref, bf16[384,512]{1,0:T(8,128)(2,1)S(1)} %get-tuple-element.80.edge_ref.right_ref), custom_call_target="tpu_custom_call" | custom-call | flops 3221225472 | tf_op jit(solution)/shard_map/pallas_call | solution.py:19
  15.6 0.9 %collective-permute-start.6 = (bf16[2,2,64,256]{3,2,1,0:T(8,128)(2,1)S(1)}, bf16[2,2,64,256]{3,2,1,0:T(8,128)(2,1)S(1)}, u32[]{:S(2)}, u32[]{:S(2)}) collective-permute-start(bf16[2,2,64,256]{3,2,1,0:T(8,128)(2,1)S(1)} %get-tuple-element.85), channel_id=1, source_target_pairs={{0,4},{1,3},{2,6},{3,1},{4,0},{5,7},{6,2},{7,5},{8,12},{9,11},{10,... | collective-permute-start | bytes 393224 | tf_op jit(solution)/shard_map/ppermute | solution.py:418
  16.6 0.4 %shard_map.46 = (f32[2,2,64,256]{3,2,1,0:T(8,128)S(1)}, bf16[2,2,64,256]{3,2,1,0:T(8,128)(2,1)S(1)}) custom-call(bf16[256,1536]{1,0:T(8,128)(2,1)S(1)} %get-tuple-element.61.own_ref.refs_6_, bf16[1,256,1536]{2,1,0:T(8,128)(2,1)S(1)} %bitcast.8, f32[2,256,512]{2,1,0:T(8,128)S(1)} %shard_map.42.refs_8_.begun_ref, ...), custom_call_target="tpu_custom_call" | custom-call | tf_op jit(solution)/shard_map/pallas_call | solution.py:19
  17.0 0.7 %shard_map.47 = (f32[2,2,64,256]{3,2,1,0:T(8,128)S(1)}, bf16[4,2,64,256]{3,2,1,0:T(8,128)(2,1)S(1)}) custom-call(bf16[2,256,1536]{2,1,0:T(8,128)(2,1)S(1)} %shard_map.44.lefts_ref, bf16[1152,512]{1,0:T(8,128)(2,1)S(1)} %get-tuple-element.66.right_ref, bf16[384,512]{1,0:T(8,128)(2,1)S(1)} %get-tuple-element.80.edge_ref.right_ref, ...), custom_call_target="tpu_custom_call" | custom-call | tf_op jit(solution)/shard_map/pallas_call | solution.py:19
  17.6 1.2 %collective-permute-start.5 = (bf16[4,2,64,256]{3,2,1,0:T(8,128)(2,1)S(1)}, bf16[4,2,64,256]{3,2,1,0:T(8,128)(2,1)S(1)}, u32[]{:S(2)}, u32[]{:S(2)}) collective-permute-start(bf16[4,2,64,256]{3,2,1,0:T(8,128)(2,1)S(1)} %get-tuple-element.83), channel_id=1, source_target_pairs={{0,4},{1,3},{2,6},{3,1},{4,0},{5,7},{6,2},{7,5},{8,12},{9,11},{10,... | collective-permute-start | bytes 786440 | tf_op jit(solution)/shard_map/ppermute | solution.py:418
  18.9 0.0 collective-permute-done.7.refs_1_
  18.9 1.6 %collective-permute-start.9 = (bf16[2,1,64,256]{3,2,1,0:T(8,128)(2,1)S(1)}, bf16[2,1,64,256]{3,2,1,0:T(8,128)(2,1)S(1)}, u32[]{:S(2)}, u32[]{:S(2)}) collective-permute-start(bf16[2,1,64,256]{3,2,1,0:T(8,128)(2,1)S(1)} %get-tuple-element.94), channel_id=1, source_target_pairs={{0,2},{1,5},{2,0},{3,7},{4,6},{5,1},{6,4},{7,3},{8,10},{9,13},{10,... | collective-permute-start | bytes 196616 | tf_op jit(solution)/shard_map/ppermute | solution.py:418
  20.5 0.2 collective-permute-done.6.refs_1_
  20.7 1.6 %collective-permute-start.8 = (bf16[2,1,64,256]{3,2,1,0:T(8,128)(2,1)S(1)}, bf16[2,1,64,256]{3,2,1,0:T(8,128)(2,1)S(1)}, u32[]{:S(2)}, u32[]{:S(2)}) collective-permute-start(bf16[2,1,64,256]{3,2,1,0:T(8,128)(2,1)S(1)} %get-tuple-element.93), channel_id=1, source_target_pairs={{0,2},{1,5},{2,0},{3,7},{4,6},{5,1},{6,4},{7,3},{8,10},{9,13},{10,... | collective-permute-start | bytes 196616 | tf_op jit(solution)/shard_map/ppermute | solution.py:418
  22.3 1.7 %collective-permute-done.9.came_ref = bf16[2,1,64,256]{3,2,1,0:T(8,128)(2,1)S(1)} collective-permute-done((bf16[2,1,64,256]{3,2,1,0:T(8,128)(2,1)S(1)}, bf16[2,1,64,256]{3,2,1,0:T(8,128)(2,1)S(1)}, u32[]{:S(2)}, u32[]{:S(2)}) %collective-permute-start.9) | collective-permute-done | bytes 65568 | tf_op jit(solution)/shard_map/ppermute | solution.py:418
  24.0 1.4 %collective-permute-start.12 = (bf16[2,1,64,256]{3,2,1,0:T(8,128)(2,1)S(1)}, bf16[2,1,64,256]{3,2,1,0:T(8,128)(2,1)S(1)}, u32[]{:S(2)}, u32[]{:S(2)}) collective-permute-start(bf16[2,1,64,256]{3,2,1,0:T(8,128)(2,1)S(1)} %shard_map.50), channel_id=1, source_target_pairs={{0,8},{1,9},{2,10},{3,11},{4,12},{5,13},{6,14},{7,15},{8,0},{9,1},... | collective-permute-start | bytes 196616 | tf_op jit(solution)/shard_map/ppermute | solution.py:418
  25.4 0.0 collective-permute-done.8.came_ref
  25.4 1.7 %collective-permute-start.11 = (bf16[2,1,64,256]{3,2,1,0:T(8,128)(2,1)S(1)}, bf16[2,1,64,256]{3,2,1,0:T(8,128)(2,1)S(1)}, u32[]{:S(2)}, u32[]{:S(2)}) collective-permute-start(bf16[2,1,64,256]{3,2,1,0:T(8,128)(2,1)S(1)} %shard_map.51), channel_id=1, source_target_pairs={{0,8},{1,9},{2,10},{3,11},{4,12},{5,13},{6,14},{7,15},{8,0},{9,1},... | collective-permute-start | bytes 196616 | tf_op jit(solution)/shard_map/ppermute | solution.py:418
  27.1 0.0 collective-permute-done.5.refs_1_.refs_3_
  27.1 0.1 shard_map.52
  27.2 1.2 %collective-permute-start.10 = (bf16[4,1,64,256]{3,2,1,0:T(8,128)(2,1)S(1)}, bf16[4,1,64,256]{3,2,1,0:T(8,128)(2,1)S(1)}, u32[]{:S(2)}, u32[]{:S(2)}) collective-permute-start(bf16[4,1,64,256]{3,2,1,0:T(8,128)(2,1)S(1)} %get-tuple-element.98), channel_id=1, source_target_pairs={{0,2},{1,5},{2,0},{3,7},{4,6},{5,1},{6,4},{7,3},{8,10},{9,13},{10,... | collective-permute-start | bytes 393224 | tf_op jit(solution)/shard_map/ppermute | solution.py:418
  28.3 2.7 %collective-permute-done.12.refs_1_ = bf16[2,1,64,256]{3,2,1,0:T(8,128)(2,1)S(1)} collective-permute-done((bf16[2,1,64,256]{3,2,1,0:T(8,128)(2,1)S(1)}, bf16[2,1,64,256]{3,2,1,0:T(8,128)(2,1)S(1)}, u32[]{:S(2)}, u32[]{:S(2)}) %collective-permute-start.12) | collective-permute-done | bytes 65568 | tf_op jit(solution)/shard_map/ppermute | solution.py:418
  31.1 1.2 %collective-permute-done.11.refs_1_ = bf16[2,1,64,256]{3,2,1,0:T(8,128)(2,1)S(1)} collective-permute-done((bf16[2,1,64,256]{3,2,1,0:T(8,128)(2,1)S(1)}, bf16[2,1,64,256]{3,2,1,0:T(8,128)(2,1)S(1)}, u32[]{:S(2)}, u32[]{:S(2)}) %collective-permute-start.11) | collective-permute-done | bytes 65568 | tf_op jit(solution)/shard_map/ppermute | solution.py:418
  32.3 0.0 collective-permute-done.10.came_ref
  32.3 0.7 %shard_map.55 = f32[2,2,64,256]{3,2,1,0:T(8,128)} custom-call(bf16[4,1,64,256]{3,2,1,0:T(8,128)(2,1)S(1)} %collective-permute-done.10.came_ref, f32[2,1,64,256]{3,2,1,0:T(8,128)S(1)} %shard_map.53.refs_0_, f32[2,1,64,256]{3,2,1,0:T(8,128)S(1)} %shard_map.54.refs_1_), custom_call_target="tpu_custom_call" | custom-call | tf_op jit(solution)/shard_map/pallas_call | solution.py:19
  (7 shorter events, 0.1 us)
Async XLA Ops:
  0.0 9.5 %collective-permute-start = (bf16[2,8,16,3,2,256]{5,4,3,2,1,0:T(2,128)(2,1)}, bf16[2,8,16,3,2,256]{5,4,3,2,1,0:T(2,128)(2,1)S(1)}, u32[]{:S(2)}, u32[]{:S(2)}) collective-permute-start(bf16[2,8,16,3,2,256]{5,4,3,2,1,0:T(2,128)(2,1)} %bitcast.11), channel_id=1, source_target_pairs={{1,0},{0,1},{3,2},{2,3},{5,4},{4,5},{7,6},{6,7},{9,8},{8,9},{11,10... | collective-permute-start | bytes 2359304 | tf_op jit(solution)/shard_map/ppermute | solution.py:14
  1.8 10.1 %collective-permute-start.3 = (bf16[2,19,3,2,256]{4,3,2,1,0:T(2,128)(2,1)S(1)}, bf16[2,19,3,2,256]{4,3,2,1,0:T(2,128)(2,1)S(1)}, u32[]{:S(2)}, u32[]{:S(2)}) collective-permute-start(bf16[2,19,3,2,256]{4,3,2,1,0:T(2,128)(2,1)S(1)} %get-tuple-element.70), channel_id=1, source_target_pairs={{12,0},{0,4},{4,8},{8,12},{13,1},{1,5},{5,9},{9,13},{14,2},{2,6},{... | collective-permute-start | bytes 350216 | tf_op jit(solution)/shard_map/ppermute | solution.py:14
  4.4 7.4 %collective-permute-start.2 = (bf16[2,16,3,2,256]{4,3,2,1,0:T(2,128)(2,1)S(1)}, bf16[2,16,3,2,256]{4,3,2,1,0:T(2,128)(2,1)S(1)}, u32[]{:S(2)}, u32[]{:S(2)}) collective-permute-start(bf16[2,16,3,2,256]{4,3,2,1,0:T(2,128)(2,1)S(1)} %get-tuple-element.69), channel_id=1, source_target_pairs={{4,0},{8,4},{12,8},{0,12},{5,1},{9,5},{13,9},{1,13},{6,2},{10,6},{... | collective-permute-start | bytes 294920 | tf_op jit(solution)/shard_map/ppermute | solution.py:14
  7.3 5.6 %collective-permute-start.1 = (bf16[8,32,256]{2,1,0:T(8,128)(2,1)S(1)}, bf16[8,32,256]{2,1,0:T(8,128)(2,1)S(1)}, u32[]{:S(2)}, u32[]{:S(2)}) collective-permute-start(bf16[8,32,256]{2,1,0:T(8,128)(2,1)S(1)} %get-tuple-element.68), channel_id=1, source_target_pairs={{2,0},{0,2},{3,1},{1,3},{6,4},{4,6},{7,5},{5,7},{10,8},{8,10},{11,... | collective-permute-start | bytes 393224 | tf_op jit(solution)/shard_map/ppermute | solution.py:14
  12.9 1.4 %collective-permute-start.4 = (bf16[8,24,256]{2,1,0:T(8,128)(2,1)S(1)}, bf16[8,24,256]{2,1,0:T(8,128)(2,1)S(1)}, u32[]{:S(2)}, u32[]{:S(2)}) collective-permute-start(bf16[8,24,256]{2,1,0:T(8,128)(2,1)S(1)} %slice.3), channel_id=1, source_target_pairs={{1,0},{0,1},{3,2},{2,3},{5,4},{4,5},{7,6},{6,7},{9,8},{8,9},{11,10... | collective-permute-start | bytes 294920 | tf_op jit(solution)/shard_map/ppermute | solution.py:14
  13.0 5.9 %collective-permute-start.7 = (bf16[2,2,64,256]{3,2,1,0:T(8,128)(2,1)S(1)}, bf16[2,2,64,256]{3,2,1,0:T(8,128)(2,1)S(1)}, u32[]{:S(2)}, u32[]{:S(2)}) collective-permute-start(bf16[2,2,64,256]{3,2,1,0:T(8,128)(2,1)S(1)} %get-tuple-element.87), channel_id=1, source_target_pairs={{0,4},{1,3},{2,6},{3,1},{4,0},{5,7},{6,2},{7,5},{8,12},{9,11},{10,... | collective-permute-start | bytes 393224 | tf_op jit(solution)/shard_map/ppermute | solution.py:418
  15.6 5.0 %collective-permute-start.6 = (bf16[2,2,64,256]{3,2,1,0:T(8,128)(2,1)S(1)}, bf16[2,2,64,256]{3,2,1,0:T(8,128)(2,1)S(1)}, u32[]{:S(2)}, u32[]{:S(2)}) collective-permute-start(bf16[2,2,64,256]{3,2,1,0:T(8,128)(2,1)S(1)} %get-tuple-element.85), channel_id=1, source_target_pairs={{0,4},{1,3},{2,6},{3,1},{4,0},{5,7},{6,2},{7,5},{8,12},{9,11},{10,... | collective-permute-start | bytes 393224 | tf_op jit(solution)/shard_map/ppermute | solution.py:418
  17.6 9.5 %collective-permute-start.5 = (bf16[4,2,64,256]{3,2,1,0:T(8,128)(2,1)S(1)}, bf16[4,2,64,256]{3,2,1,0:T(8,128)(2,1)S(1)}, u32[]{:S(2)}, u32[]{:S(2)}) collective-permute-start(bf16[4,2,64,256]{3,2,1,0:T(8,128)(2,1)S(1)} %get-tuple-element.83), channel_id=1, source_target_pairs={{0,4},{1,3},{2,6},{3,1},{4,0},{5,7},{6,2},{7,5},{8,12},{9,11},{10,... | collective-permute-start | bytes 786440 | tf_op jit(solution)/shard_map/ppermute | solution.py:418
  18.9 5.1 %collective-permute-start.9 = (bf16[2,1,64,256]{3,2,1,0:T(8,128)(2,1)S(1)}, bf16[2,1,64,256]{3,2,1,0:T(8,128)(2,1)S(1)}, u32[]{:S(2)}, u32[]{:S(2)}) collective-permute-start(bf16[2,1,64,256]{3,2,1,0:T(8,128)(2,1)S(1)} %get-tuple-element.94), channel_id=1, source_target_pairs={{0,2},{1,5},{2,0},{3,7},{4,6},{5,1},{6,4},{7,3},{8,10},{9,13},{10,... | collective-permute-start | bytes 196616 | tf_op jit(solution)/shard_map/ppermute | solution.py:418
  20.7 4.7 %collective-permute-start.8 = (bf16[2,1,64,256]{3,2,1,0:T(8,128)(2,1)S(1)}, bf16[2,1,64,256]{3,2,1,0:T(8,128)(2,1)S(1)}, u32[]{:S(2)}, u32[]{:S(2)}) collective-permute-start(bf16[2,1,64,256]{3,2,1,0:T(8,128)(2,1)S(1)} %get-tuple-element.93), channel_id=1, source_target_pairs={{0,2},{1,5},{2,0},{3,7},{4,6},{5,1},{6,4},{7,3},{8,10},{9,13},{10,... | collective-permute-start | bytes 196616 | tf_op jit(solution)/shard_map/ppermute | solution.py:418
  24.0 7.0 %collective-permute-start.12 = (bf16[2,1,64,256]{3,2,1,0:T(8,128)(2,1)S(1)}, bf16[2,1,64,256]{3,2,1,0:T(8,128)(2,1)S(1)}, u32[]{:S(2)}, u32[]{:S(2)}) collective-permute-start(bf16[2,1,64,256]{3,2,1,0:T(8,128)(2,1)S(1)} %shard_map.50), channel_id=1, source_target_pairs={{0,8},{1,9},{2,10},{3,11},{4,12},{5,13},{6,14},{7,15},{8,0},{9,1},... | collective-permute-start | bytes 196616 | tf_op jit(solution)/shard_map/ppermute | solution.py:418
  25.4 6.9 %collective-permute-start.11 = (bf16[2,1,64,256]{3,2,1,0:T(8,128)(2,1)S(1)}, bf16[2,1,64,256]{3,2,1,0:T(8,128)(2,1)S(1)}, u32[]{:S(2)}, u32[]{:S(2)}) collective-permute-start(bf16[2,1,64,256]{3,2,1,0:T(8,128)(2,1)S(1)} %shard_map.51), channel_id=1, source_target_pairs={{0,8},{1,9},{2,10},{3,11},{4,12},{5,13},{6,14},{7,15},{8,0},{9,1},... | collective-permute-start | bytes 196616 | tf_op jit(solution)/shard_map/ppermute | solution.py:418
  27.2 5.2 %collective-permute-start.10 = (bf16[4,1,64,256]{3,2,1,0:T(8,128)(2,1)S(1)}, bf16[4,1,64,256]{3,2,1,0:T(8,128)(2,1)S(1)}, u32[]{:S(2)}, u32[]{:S(2)}) collective-permute-start(bf16[4,1,64,256]{3,2,1,0:T(8,128)(2,1)S(1)} %get-tuple-element.98), channel_id=1, source_target_pairs={{0,2},{1,5},{2,0},{3,7},{4,6},{5,1},{6,4},{7,3},{8,10},{9,13},{10,... | collective-permute-start | bytes 393224 | tf_op jit(solution)/shard_map/ppermute | solution.py:418

commit v16 on v15

--- a/solution.py
+++ b/solution.py
@@ -268,7 +268,7 @@
     one = [("gx", bit) for bit in bits("gx")[:-1]]
     two = [("gy", bit) for bit in bits("gy")]
     both = min(len(one), len(two))
-    pairs = [pair for ends in zip(one, two) for pair in (ends, ends[::-1])]
+    pairs = [pair for ends in zip(two, one) for pair in (ends, ends[::-1])]
     return pairs + [(step, step) for step in one[both:] + two[both:]]
 
 

time: 33.2 us -> 33.6 us (1.012)
  waiting for transfers between devices: 7.21 us -> 8.09 us
  starting transfers between devices: 17.3 us -> 16.8 us
    ppermute x8, waiting for transfers between devices: 5.91 us -> 7.14 us  [exchange(): return lax.ppermute(block, axes, route)]
    ppermute x8, starting transfers between devices: 10.4 us -> 9.95 us  [exchange(): return lax.ppermute(block, axes, route)]
    ppermute x5, waiting for transfers between devices: 1.3 us -> 0.96 us  [shifted(): return lax.ppermute(block, axis, route)]
where the time goes in v16:
time: 33.6 us; the launch traced here: 33.5 us
  starting transfers between devices  16.8 us (50%)
  Pallas kernels  8.39 us (25%)
  waiting for transfers between devices  8.09 us (24%)
    ppermute x8, starting transfers between devices, exchange(): return lax.ppermute(block, axes, route)  9.95 us
    pallas_call x19, Pallas kernels, call(): pl.pallas_call(body, out_shape=out_shape, in_specs=[pl.BlockSpec(memory_s...  8.39 us
    ppermute x8, waiting for transfers between devices, exchange(): return lax.ppermute(block, axes, route)  7.14 us
    ppermute x5, starting transfers between devices, shifted(): return lax.ppermute(block, axis, route)  6.9 us
    ppermute x5, waiting for transfers between devices, shifted(): return lax.ppermute(block, axis, route)  0.96 us
  transfers between devices with their start and end apart: 13, of which 7 were waited for; matrix products, arithmetic and copies ran while one was open for 0% of the time, Pallas kernels for 23%

profile of v16, /device:TPU:0, one launch (start us, length us, event | category | flops | bytes accessed | tf_op | source)
XLA Modules:
  0.0 33.5 jit_solution(7143516771682396576)
XLA Ops:
  0.0 0.5 %collective-permute-start = (bf16[2,8,16,3,2,256]{5,4,3,2,1,0:T(2,128)(2,1)}, bf16[2,8,16,3,2,256]{5,4,3,2,1,0:T(2,128)(2,1)S(1)}, u32[]{:S(2)}, u32[]{:S(2)}) collective-permute-start(bf16[2,8,16,3,2,256]{5,4,3,2,1,0:T(2,128)(2,1)} %bitcast.11), channel_id=1, source_target_pairs={{1,0},{0,1},{3,2},{2,3},{5,4},{4,5},{7,6},{6,7},{9,8},{8,9},{11,10... | collective-permute-start | bytes 2359304 | tf_op jit(solution)/shard_map/ppermute | solution.py:14
  0.5 1.4 %shard_map.37 = (bf16[2,16,3,2,256]{4,3,2,1,0:T(2,128)(2,1)S(1)}, bf16[2,19,3,2,256]{4,3,2,1,0:T(2,128)(2,1)S(1)}, bf16[2,8,16,3,2,256]{5,4,3,2,1,0:T(2,128)(2,1...) custom-call(bf16[2,8,16,3,2,256]{5,4,3,2,1,0:T(2,128)(2,1)} %bitcast, ...), custom_call_target="tpu_custom_call" | custom-call | tf_op jit(solution)/shard_map/pallas_call | solution.py:19
  1.8 2.6 %collective-permute-start.3 = (bf16[2,19,3,2,256]{4,3,2,1,0:T(2,128)(2,1)S(1)}, bf16[2,19,3,2,256]{4,3,2,1,0:T(2,128)(2,1)S(1)}, u32[]{:S(2)}, u32[]{:S(2)}) collective-permute-start(bf16[2,19,3,2,256]{4,3,2,1,0:T(2,128)(2,1)S(1)} %get-tuple-element.70), channel_id=1, source_target_pairs={{12,0},{0,4},{4,8},{8,12},{13,1},{1,5},{5,9},{9,13},{14,2},{2,6},{... | collective-permute-start | bytes 350216 | tf_op jit(solution)/shard_map/ppermute | solution.py:14
  4.4 2.1 %collective-permute-start.2 = (bf16[2,16,3,2,256]{4,3,2,1,0:T(2,128)(2,1)S(1)}, bf16[2,16,3,2,256]{4,3,2,1,0:T(2,128)(2,1)S(1)}, u32[]{:S(2)}, u32[]{:S(2)}) collective-permute-start(bf16[2,16,3,2,256]{4,3,2,1,0:T(2,128)(2,1)S(1)} %get-tuple-element.69), channel_id=1, source_target_pairs={{4,0},{8,4},{12,8},{0,12},{5,1},{9,5},{13,9},{1,13},{6,2},{10,6},{... | collective-permute-start | bytes 294920 | tf_op jit(solution)/shard_map/ppermute | solution.py:14
  6.5 0.7 %shard_map.38 = (bf16[8,192,256]{2,1,0:T(8,128)(2,1)S(1)}, bf16[8,32,256]{2,1,0:T(8,128)(2,1)S(1)}, f32[8,8,256]{2,1,0:T(8,128)S(1)}, f32[8,8,256]{2,1,0:T(8,128...) custom-call(bf16[2,8,16,3,2,256]{5,4,3,2,1,0:T(2,128)(2,1)S(1)} %get-tuple-element.54.raw_ref, ...), custom_call_target="tpu_custom_call" | custom-call | tf_op jit(solution)/shard_map/pallas_call | solution.py:19
  7.3 1.7 %collective-permute-start.1 = (bf16[8,32,256]{2,1,0:T(8,128)(2,1)S(1)}, bf16[8,32,256]{2,1,0:T(8,128)(2,1)S(1)}, u32[]{:S(2)}, u32[]{:S(2)}) collective-permute-start(bf16[8,32,256]{2,1,0:T(8,128)(2,1)S(1)} %get-tuple-element.68), channel_id=1, source_target_pairs={{2,0},{0,2},{3,1},{1,3},{6,4},{4,6},{7,5},{5,7},{10,8},{8,10},{11,... | collective-permute-start | bytes 393224 | tf_op jit(solution)/shard_map/ppermute | solution.py:14
  8.9 0.5 %shard_map.39 = (bf16[1152,512]{1,0:T(8,128)(2,1)S(1)}, bf16[256,1536]{1,0:T(8,128)(2,1)S(1)}, bf16[192,192]{1,0:T(8,128)(2,1)S(1)}, f32[192,256]{1,0:T(8,128)S(1)}, f32[192,256]{1,0:T(8,128)S(1)}) custom-call(bf16[8,192,256]{2,1,0:T(8,128)(2,1)S(1)} %get-tuple-element.58.refs_0_, f32[8,8,256]{2,1,0:T(8,128)S(1)} %get-tuple-element.59.refs_1_, ...), custom_call_target="tpu_custom_call" | custom-call | flops 150994944 | tf_op jit(solution)/shard_map/pallas_call | solution.py:19
  9.5 0.0 collective-permute-done.raw_ref
  9.5 0.3 shard_map.40
  9.8 0.6 %shard_map.41.refs_0_ = f32[2,8,192,256]{3,2,1,0:T(8,128)S(1)} custom-call(bf16[8,192,256]{2,1,0:T(8,128)(2,1)S(1)} %get-tuple-element.58.refs_0_, bf16[1,8,192,256]{3,2,1,0:T(8,128)(2,1)S(1)} %bitcast.9, f32[8,8,256]{2,1,0:T(8,128)S(1)} %get-tuple-element.64.refs_2_.refs_3_, f32[8,8,256]{2,1,0:T(8,128)S(1)} %get-tuple-element.65.refs_3_), custom_call_target="tpu_custom_call" | custom-call | flops 150994944 | tf_op jit(solution)/shard_map/pallas_call | solution.py:19
  10.4 0.8 %shard_map.42.refs_8_.begun_ref = f32[2,256,512]{2,1,0:T(8,128)S(1)} custom-call(bf16[256,1536]{1,0:T(8,128)(2,1)S(1)} %get-tuple-element.61.own_ref.refs_6_, bf16[1,256,1536]{2,1,0:T(8,128)(2,1)S(1)} %bitcast.6, bf16[1152,512]{1,0:T(8,128)(2,1)S(1)} %get-tuple-element.66.right_ref), custom_call_target="tpu_custom_call" | custom-call | flops 402653184 | tf_op jit(solution)/shard_map/pallas_call | solution.py:19
  11.2 0.7 %collective-permute-done.2.refs_0_ = bf16[2,16,3,2,256]{4,3,2,1,0:T(2,128)(2,1)S(1)} collective-permute-done((bf16[2,16,3,2,256]{4,3,2,1,0:T(2,128)(2,1)S(1)}, bf16[2,16,3,2,256]{4,3,2,1,0:T(2,128)(2,1)S(1)}, u32[]{:S(2)}, u32[]{:S(2)}) %collective-permute-start.2) | collective-permute-done | bytes 98336 | tf_op jit(solution)/shard_map/ppermute | solution.py:14
  11.9 0.0 collective-permute-done.3.refs_1_
  11.9 0.8 %shard_map.43 = (f32[2,2,64,256]{3,2,1,0:T(8,128)S(1)}, bf16[2,2,64,256]{3,2,1,0:T(8,128)(2,1)S(1)}, bf16[384,512]{1,0:T(8,128)(2,1)S(1)}) custom-call(bf16[2,16,3,2,256]{4,3,2,1,0:T(2,128)(2,1)S(1)} %collective-permute-done.2.refs_0_, bf16[2,19,3,2,256]{4,3,2,1,0:T(2,128)(2,1)S(1)} %collective-permute-done.3.refs_1_, ...), custom_call_target="tpu_custom_call" | custom-call | flops 402653184 | tf_op jit(solution)/shard_map/pallas_call | solution.py:19
  12.6 0.3 collective-permute-done.1.refs_1_
  12.9 0.1 collective-permute-start.4
  13.0 1.6 %collective-permute-start.7 = (bf16[2,2,64,256]{3,2,1,0:T(8,128)(2,1)S(1)}, bf16[2,2,64,256]{3,2,1,0:T(8,128)(2,1)S(1)}, u32[]{:S(2)}, u32[]{:S(2)}) collective-permute-start(bf16[2,2,64,256]{3,2,1,0:T(8,128)(2,1)S(1)} %get-tuple-element.87), channel_id=1, source_target_pairs={{0,2},{1,5},{2,0},{3,7},{4,6},{5,1},{6,4},{7,3},{8,10},{9,13},{10,... | collective-permute-start | bytes 393224 | tf_op jit(solution)/shard_map/ppermute | solution.py:418
  14.6 0.0 collective-permute-done.4
  14.6 0.6 %shard_map.44.lefts_ref = bf16[2,256,1536]{2,1,0:T(8,128)(2,1)S(1)} custom-call(f32[2,8,192,256]{3,2,1,0:T(8,128)S(1)} %shard_map.41.refs_0_, bf16[8,32,256]{2,1,0:T(8,128)(2,1)S(1)} %collective-permute-done.1.refs_1_, bf16[1,8,24,256]{3,2,1,0:T(8,128)(2,1)S(1)} %bitcast.10, f32[8,8,256]{2,1,0:T(8,128)S(1)} %get-tuple-element.64.refs_2_.refs_3_), custom_call_target="tpu_custom_call" | custom-call | flops 150994944 | tf_op jit(solution)/shard_map/pallas_call | solution.py:19
  15.2 0.7 %shard_map.45 = (f32[2,2,64,256]{3,2,1,0:T(8,128)S(1)}, bf16[2,2,64,256]{3,2,1,0:T(8,128)(2,1)S(1)}) custom-call(bf16[2,256,1536]{2,1,0:T(8,128)(2,1)S(1)} %shard_map.44.lefts_ref, bf16[1152,512]{1,0:T(8,128)(2,1)S(1)} %get-tuple-element.66.right_ref, bf16[384,512]{1,0:T(8,128)(2,1)S(1)} %get-tuple-element.80.edge_ref.right_ref), custom_call_target="tpu_custom_call" | custom-call | flops 3221225472 | tf_op jit(solution)/shard_map/pallas_call | solution.py:19
  15.9 1.3 %collective-permute-start.6 = (bf16[2,2,64,256]{3,2,1,0:T(8,128)(2,1)S(1)}, bf16[2,2,64,256]{3,2,1,0:T(8,128)(2,1)S(1)}, u32[]{:S(2)}, u32[]{:S(2)}) collective-permute-start(bf16[2,2,64,256]{3,2,1,0:T(8,128)(2,1)S(1)} %get-tuple-element.85), channel_id=1, source_target_pairs={{0,2},{1,5},{2,0},{3,7},{4,6},{5,1},{6,4},{7,3},{8,10},{9,13},{10,... | collective-permute-start | bytes 393224 | tf_op jit(solution)/shard_map/ppermute | solution.py:418
  17.2 0.4 %shard_map.46 = (f32[2,2,64,256]{3,2,1,0:T(8,128)S(1)}, bf16[2,2,64,256]{3,2,1,0:T(8,128)(2,1)S(1)}) custom-call(bf16[256,1536]{1,0:T(8,128)(2,1)S(1)} %get-tuple-element.61.own_ref.refs_6_, bf16[1,256,1536]{2,1,0:T(8,128)(2,1)S(1)} %bitcast.8, f32[2,256,512]{2,1,0:T(8,128)S(1)} %shard_map.42.refs_8_.begun_ref, ...), custom_call_target="tpu_custom_call" | custom-call | tf_op jit(solution)/shard_map/pallas_call | solution.py:19
  17.6 0.7 %shard_map.47 = (f32[2,2,64,256]{3,2,1,0:T(8,128)S(1)}, bf16[4,2,64,256]{3,2,1,0:T(8,128)(2,1)S(1)}) custom-call(bf16[2,256,1536]{2,1,0:T(8,128)(2,1)S(1)} %shard_map.44.lefts_ref, bf16[1152,512]{1,0:T(8,128)(2,1)S(1)} %get-tuple-element.66.right_ref, bf16[384,512]{1,0:T(8,128)(2,1)S(1)} %get-tuple-element.80.edge_ref.right_ref, ...), custom_call_target="tpu_custom_call" | custom-call | tf_op jit(solution)/shard_map/pallas_call | solution.py:19
  18.3 0.9 %collective-permute-start.5 = (bf16[4,2,64,256]{3,2,1,0:T(8,128)(2,1)S(1)}, bf16[4,2,64,256]{3,2,1,0:T(8,128)(2,1)S(1)}, u32[]{:S(2)}, u32[]{:S(2)}) collective-permute-start(bf16[4,2,64,256]{3,2,1,0:T(8,128)(2,1)S(1)} %get-tuple-element.83), channel_id=1, source_target_pairs={{0,2},{1,5},{2,0},{3,7},{4,6},{5,1},{6,4},{7,3},{8,10},{9,13},{10,... | collective-permute-start | bytes 786440 | tf_op jit(solution)/shard_map/ppermute | solution.py:418
  19.1 0.0 collective-permute-done.7.refs_1_
  19.2 0.9 %collective-permute-start.9 = (bf16[2,1,64,256]{3,2,1,0:T(8,128)(2,1)S(1)}, bf16[2,1,64,256]{3,2,1,0:T(8,128)(2,1)S(1)}, u32[]{:S(2)}, u32[]{:S(2)}) collective-permute-start(bf16[2,1,64,256]{3,2,1,0:T(8,128)(2,1)S(1)} %get-tuple-element.94), channel_id=1, source_target_pairs={{0,4},{1,3},{2,6},{3,1},{4,0},{5,7},{6,2},{7,5},{8,12},{9,11},{10,... | collective-permute-start | bytes 196616 | tf_op jit(solution)/shard_map/ppermute | solution.py:418
  20.1 0.8 %collective-permute-done.6.refs_1_ = bf16[2,2,64,256]{3,2,1,0:T(8,128)(2,1)S(1)} collective-permute-done((bf16[2,2,64,256]{3,2,1,0:T(8,128)(2,1)S(1)}, bf16[2,2,64,256]{3,2,1,0:T(8,128)(2,1)S(1)}, u32[]{:S(2)}, u32[]{:S(2)}) %collective-permute-start.6) | collective-permute-done | bytes 131104 | tf_op jit(solution)/shard_map/ppermute | solution.py:418
  21.0 0.9 %collective-permute-start.8 = (bf16[2,1,64,256]{3,2,1,0:T(8,128)(2,1)S(1)}, bf16[2,1,64,256]{3,2,1,0:T(8,128)(2,1)S(1)}, u32[]{:S(2)}, u32[]{:S(2)}) collective-permute-start(bf16[2,1,64,256]{3,2,1,0:T(8,128)(2,1)S(1)} %get-tuple-element.93), channel_id=1, source_target_pairs={{0,4},{1,3},{2,6},{3,1},{4,0},{5,7},{6,2},{7,5},{8,12},{9,11},{10,... | collective-permute-start | bytes 196616 | tf_op jit(solution)/shard_map/ppermute | solution.py:418
  21.9 1.8 %collective-permute-done.9.came_ref = bf16[2,1,64,256]{3,2,1,0:T(8,128)(2,1)S(1)} collective-permute-done((bf16[2,1,64,256]{3,2,1,0:T(8,128)(2,1)S(1)}, bf16[2,1,64,256]{3,2,1,0:T(8,128)(2,1)S(1)}, u32[]{:S(2)}, u32[]{:S(2)}) %collective-permute-start.9) | collective-permute-done | bytes 65568 | tf_op jit(solution)/shard_map/ppermute | solution.py:418
  23.7 1.7 %collective-permute-start.12 = (bf16[2,1,64,256]{3,2,1,0:T(8,128)(2,1)S(1)}, bf16[2,1,64,256]{3,2,1,0:T(8,128)(2,1)S(1)}, u32[]{:S(2)}, u32[]{:S(2)}) collective-permute-start(bf16[2,1,64,256]{3,2,1,0:T(8,128)(2,1)S(1)} %shard_map.50), channel_id=1, source_target_pairs={{0,8},{1,9},{2,10},{3,11},{4,12},{5,13},{6,14},{7,15},{8,0},{9,1},... | collective-permute-start | bytes 196616 | tf_op jit(solution)/shard_map/ppermute | solution.py:418
  25.4 0.0 collective-permute-done.8.came_ref
  25.4 1.4 %collective-permute-start.11 = (bf16[2,1,64,256]{3,2,1,0:T(8,128)(2,1)S(1)}, bf16[2,1,64,256]{3,2,1,0:T(8,128)(2,1)S(1)}, u32[]{:S(2)}, u32[]{:S(2)}) collective-permute-start(bf16[2,1,64,256]{3,2,1,0:T(8,128)(2,1)S(1)} %shard_map.51), channel_id=1, source_target_pairs={{0,8},{1,9},{2,10},{3,11},{4,12},{5,13},{6,14},{7,15},{8,0},{9,1},... | collective-permute-start | bytes 196616 | tf_op jit(solution)/shard_map/ppermute | solution.py:418
  26.8 0.0 collective-permute-done.5.refs_1_.refs_3_
  26.8 0.1 shard_map.52
  26.9 1.3 %collective-permute-start.10 = (bf16[4,1,64,256]{3,2,1,0:T(8,128)(2,1)S(1)}, bf16[4,1,64,256]{3,2,1,0:T(8,128)(2,1)S(1)}, u32[]{:S(2)}, u32[]{:S(2)}) collective-permute-start(bf16[4,1,64,256]{3,2,1,0:T(8,128)(2,1)S(1)} %get-tuple-element.98), channel_id=1, source_target_pairs={{0,4},{1,3},{2,6},{3,1},{4,0},{5,7},{6,2},{7,5},{8,12},{9,11},{10,... | collective-permute-start | bytes 393224 | tf_op jit(solution)/shard_map/ppermute | solution.py:418
  28.2 3.2 %collective-permute-done.12.refs_1_ = bf16[2,1,64,256]{3,2,1,0:T(8,128)(2,1)S(1)} collective-permute-done((bf16[2,1,64,256]{3,2,1,0:T(8,128)(2,1)S(1)}, bf16[2,1,64,256]{3,2,1,0:T(8,128)(2,1)S(1)}, u32[]{:S(2)}, u32[]{:S(2)}) %collective-permute-start.12) | collective-permute-done | bytes 65568 | tf_op jit(solution)/shard_map/ppermute | solution.py:418
  31.4 0.7 %collective-permute-done.11.refs_1_ = bf16[2,1,64,256]{3,2,1,0:T(8,128)(2,1)S(1)} collective-permute-done((bf16[2,1,64,256]{3,2,1,0:T(8,128)(2,1)S(1)}, bf16[2,1,64,256]{3,2,1,0:T(8,128)(2,1)S(1)}, u32[]{:S(2)}, u32[]{:S(2)}) %collective-permute-start.11) | collective-permute-done | bytes 65568 | tf_op jit(solution)/shard_map/ppermute | solution.py:418
  32.1 0.7 %collective-permute-done.10.came_ref = bf16[4,1,64,256]{3,2,1,0:T(8,128)(2,1)S(1)} collective-permute-done((bf16[4,1,64,256]{3,2,1,0:T(8,128)(2,1)S(1)}, bf16[4,1,64,256]{3,2,1,0:T(8,128)(2,1)S(1)}, u32[]{:S(2)}, u32[]{:S(2)}) %collective-permute-start.10) | collective-permute-done | bytes 131104 | tf_op jit(solution)/shard_map/ppermute | solution.py:418
  32.7 0.7 %shard_map.55 = f32[2,2,64,256]{3,2,1,0:T(8,128)} custom-call(bf16[4,1,64,256]{3,2,1,0:T(8,128)(2,1)S(1)} %collective-permute-done.10.came_ref, f32[2,1,64,256]{3,2,1,0:T(8,128)S(1)} %shard_map.53.refs_0_, f32[2,1,64,256]{3,2,1,0:T(8,128)S(1)} %shard_map.54.refs_1_), custom_call_target="tpu_custom_call" | custom-call | tf_op jit(solution)/shard_map/pallas_call | solution.py:19
  (7 shorter events, 0.1 us)
Async XLA Ops:
  0.0 9.5 %collective-permute-start = (bf16[2,8,16,3,2,256]{5,4,3,2,1,0:T(2,128)(2,1)}, bf16[2,8,16,3,2,256]{5,4,3,2,1,0:T(2,128)(2,1)S(1)}, u32[]{:S(2)}, u32[]{:S(2)}) collective-permute-start(bf16[2,8,16,3,2,256]{5,4,3,2,1,0:T(2,128)(2,1)} %bitcast.11), channel_id=1, source_target_pairs={{1,0},{0,1},{3,2},{2,3},{5,4},{4,5},{7,6},{6,7},{9,8},{8,9},{11,10... | collective-permute-start | bytes 2359304 | tf_op jit(solution)/shard_map/ppermute | solution.py:14
  1.8 10.1 %collective-permute-start.3 = (bf16[2,19,3,2,256]{4,3,2,1,0:T(2,128)(2,1)S(1)}, bf16[2,19,3,2,256]{4,3,2,1,0:T(2,128)(2,1)S(1)}, u32[]{:S(2)}, u32[]{:S(2)}) collective-permute-start(bf16[2,19,3,2,256]{4,3,2,1,0:T(2,128)(2,1)S(1)} %get-tuple-element.70), channel_id=1, source_target_pairs={{12,0},{0,4},{4,8},{8,12},{13,1},{1,5},{5,9},{9,13},{14,2},{2,6},{... | collective-permute-start | bytes 350216 | tf_op jit(solution)/shard_map/ppermute | solution.py:14
  4.4 7.4 %collective-permute-start.2 = (bf16[2,16,3,2,256]{4,3,2,1,0:T(2,128)(2,1)S(1)}, bf16[2,16,3,2,256]{4,3,2,1,0:T(2,128)(2,1)S(1)}, u32[]{:S(2)}, u32[]{:S(2)}) collective-permute-start(bf16[2,16,3,2,256]{4,3,2,1,0:T(2,128)(2,1)S(1)} %get-tuple-element.69), channel_id=1, source_target_pairs={{4,0},{8,4},{12,8},{0,12},{5,1},{9,5},{13,9},{1,13},{6,2},{10,6},{... | collective-permute-start | bytes 294920 | tf_op jit(solution)/shard_map/ppermute | solution.py:14
  7.3 5.6 %collective-permute-start.1 = (bf16[8,32,256]{2,1,0:T(8,128)(2,1)S(1)}, bf16[8,32,256]{2,1,0:T(8,128)(2,1)S(1)}, u32[]{:S(2)}, u32[]{:S(2)}) collective-permute-start(bf16[8,32,256]{2,1,0:T(8,128)(2,1)S(1)} %get-tuple-element.68), channel_id=1, source_target_pairs={{2,0},{0,2},{3,1},{1,3},{6,4},{4,6},{7,5},{5,7},{10,8},{8,10},{11,... | collective-permute-start | bytes 393224 | tf_op jit(solution)/shard_map/ppermute | solution.py:14
  12.9 1.6 %collective-permute-start.4 = (bf16[8,24,256]{2,1,0:T(8,128)(2,1)S(1)}, bf16[8,24,256]{2,1,0:T(8,128)(2,1)S(1)}, u32[]{:S(2)}, u32[]{:S(2)}) collective-permute-start(bf16[8,24,256]{2,1,0:T(8,128)(2,1)S(1)} %slice.3), channel_id=1, source_target_pairs={{1,0},{0,1},{3,2},{2,3},{5,4},{4,5},{7,6},{6,7},{9,8},{8,9},{11,10... | collective-permute-start | bytes 294920 | tf_op jit(solution)/shard_map/ppermute | solution.py:14
  13.0 6.1 %collective-permute-start.7 = (bf16[2,2,64,256]{3,2,1,0:T(8,128)(2,1)S(1)}, bf16[2,2,64,256]{3,2,1,0:T(8,128)(2,1)S(1)}, u32[]{:S(2)}, u32[]{:S(2)}) collective-permute-start(bf16[2,2,64,256]{3,2,1,0:T(8,128)(2,1)S(1)} %get-tuple-element.87), channel_id=1, source_target_pairs={{0,2},{1,5},{2,0},{3,7},{4,6},{5,1},{6,4},{7,3},{8,10},{9,13},{10,... | collective-permute-start | bytes 393224 | tf_op jit(solution)/shard_map/ppermute | solution.py:418
  15.9 5.0 %collective-permute-start.6 = (bf16[2,2,64,256]{3,2,1,0:T(8,128)(2,1)S(1)}, bf16[2,2,64,256]{3,2,1,0:T(8,128)(2,1)S(1)}, u32[]{:S(2)}, u32[]{:S(2)}) collective-permute-start(bf16[2,2,64,256]{3,2,1,0:T(8,128)(2,1)S(1)} %get-tuple-element.85), channel_id=1, source_target_pairs={{0,2},{1,5},{2,0},{3,7},{4,6},{5,1},{6,4},{7,3},{8,10},{9,13},{10,... | collective-permute-start | bytes 393224 | tf_op jit(solution)/shard_map/ppermute | solution.py:418
  18.3 8.5 %collective-permute-start.5 = (bf16[4,2,64,256]{3,2,1,0:T(8,128)(2,1)S(1)}, bf16[4,2,64,256]{3,2,1,0:T(8,128)(2,1)S(1)}, u32[]{:S(2)}, u32[]{:S(2)}) collective-permute-start(bf16[4,2,64,256]{3,2,1,0:T(8,128)(2,1)S(1)} %get-tuple-element.83), channel_id=1, source_target_pairs={{0,2},{1,5},{2,0},{3,7},{4,6},{5,1},{6,4},{7,3},{8,10},{9,13},{10,... | collective-permute-start | bytes 786440 | tf_op jit(solution)/shard_map/ppermute | solution.py:418
  19.2 4.5 %collective-permute-start.9 = (bf16[2,1,64,256]{3,2,1,0:T(8,128)(2,1)S(1)}, bf16[2,1,64,256]{3,2,1,0:T(8,128)(2,1)S(1)}, u32[]{:S(2)}, u32[]{:S(2)}) collective-permute-start(bf16[2,1,64,256]{3,2,1,0:T(8,128)(2,1)S(1)} %get-tuple-element.94), channel_id=1, source_target_pairs={{0,4},{1,3},{2,6},{3,1},{4,0},{5,7},{6,2},{7,5},{8,12},{9,11},{10,... | collective-permute-start | bytes 196616 | tf_op jit(solution)/shard_map/ppermute | solution.py:418
  21.0 4.4 %collective-permute-start.8 = (bf16[2,1,64,256]{3,2,1,0:T(8,128)(2,1)S(1)}, bf16[2,1,64,256]{3,2,1,0:T(8,128)(2,1)S(1)}, u32[]{:S(2)}, u32[]{:S(2)}) collective-permute-start(bf16[2,1,64,256]{3,2,1,0:T(8,128)(2,1)S(1)} %get-tuple-element.93), channel_id=1, source_target_pairs={{0,4},{1,3},{2,6},{3,1},{4,0},{5,7},{6,2},{7,5},{8,12},{9,11},{10,... | collective-permute-start | bytes 196616 | tf_op jit(solution)/shard_map/ppermute | solution.py:418
  23.7 7.6 %collective-permute-start.12 = (bf16[2,1,64,256]{3,2,1,0:T(8,128)(2,1)S(1)}, bf16[2,1,64,256]{3,2,1,0:T(8,128)(2,1)S(1)}, u32[]{:S(2)}, u32[]{:S(2)}) collective-permute-start(bf16[2,1,64,256]{3,2,1,0:T(8,128)(2,1)S(1)} %shard_map.50), channel_id=1, source_target_pairs={{0,8},{1,9},{2,10},{3,11},{4,12},{5,13},{6,14},{7,15},{8,0},{9,1},... | collective-permute-start | bytes 196616 | tf_op jit(solution)/shard_map/ppermute | solution.py:418
  25.4 6.6 %collective-permute-start.11 = (bf16[2,1,64,256]{3,2,1,0:T(8,128)(2,1)S(1)}, bf16[2,1,64,256]{3,2,1,0:T(8,128)(2,1)S(1)}, u32[]{:S(2)}, u32[]{:S(2)}) collective-permute-start(bf16[2,1,64,256]{3,2,1,0:T(8,128)(2,1)S(1)} %shard_map.51), channel_id=1, source_target_pairs={{0,8},{1,9},{2,10},{3,11},{4,12},{5,13},{6,14},{7,15},{8,0},{9,1},... | collective-permute-start | bytes 196616 | tf_op jit(solution)/shard_map/ppermute | solution.py:418
  26.9 5.9 %collective-permute-start.10 = (bf16[4,1,64,256]{3,2,1,0:T(8,128)(2,1)S(1)}, bf16[4,1,64,256]{3,2,1,0:T(8,128)(2,1)S(1)}, u32[]{:S(2)}, u32[]{:S(2)}) collective-permute-start(bf16[4,1,64,256]{3,2,1,0:T(8,128)(2,1)S(1)} %get-tuple-element.98), channel_id=1, source_target_pairs={{0,4},{1,3},{2,6},{3,1},{4,0},{5,7},{6,2},{7,5},{8,12},{9,11},{10,... | collective-permute-start | bytes 393224 | tf_op jit(solution)/shard_map/ppermute | solution.py:418

commit v17 on v15

--- a/solution.py
+++ b/solution.py
@@ -576,19 +576,24 @@
         second_own_kernel, (kept_shape, shape(2 * parts, pieces, rows, width)), 0,
         [lefts, right, right_edge, sent_own], [total],
     )
-    came_own = exchange(sent_own, plan[0])
-    staying = [(own_first, came_own, slice(0, parts)), (own_second, came_own, slice(parts, 2 * parts))]
     crossing = [(kept_first, came_first), (kept_second, came_second)]
     after = own_second
+    staying = None
     for step in plan[1:]:
         for d, (kept, came) in enumerate(crossing):
             came, after = lax.optimization_barrier((came, after))
-            crossing[d] = halve([(kept, came, None)], step, 4 * project_flops if d else 0)
+            crossing[d] = halve([(kept, came, None)], step)
             after = crossing[d][0]
+            if staying is None:
+                sent_own, after = lax.optimization_barrier((sent_own, after))
+                came_own = exchange(sent_own, plan[0])
+                staying = [
+                    (own_first, came_own, slice(0, parts)), (own_second, came_own, slice(parts, 2 * parts))
+                ]
     crossed = []
     for kept, came in crossing:
         came, after = lax.optimization_barrier((came, after))
-        after = call(sum_kernel, pltpu.VMEM(kept.shape, bf16), 0, [kept, came])
+        after = call(sum_kernel, pltpu.VMEM(kept.shape, bf16), 8 * project_flops, [kept, came])
         crossed.append(exchange(after, (top, top)))
     for step in plan[1:]:
         kept, came, which = staying[0]

time: 33.2 us -> 33.3 us (level)
  transfers between devices with their start and end apart: 13 -> 13, of which waited for: 7 -> 10; matrix products, arithmetic and copies ran while one was open for 0% -> 0% of each run, Pallas kernels for 23% -> 23%
where the time goes in v17:
time: 33.3 us; the launch traced here: 33.2 us
  starting transfers between devices  17.5 us (53%)
  Pallas kernels  8.39 us (25%)
  waiting for transfers between devices  7.14 us (21%)
    ppermute x8, starting transfers between devices, exchange(): return lax.ppermute(block, axes, route)  10.6 us
    pallas_call x19, Pallas kernels, call(): pl.pallas_call(body, out_shape=out_shape, in_specs=[pl.BlockSpec(memory_s...  8.39 us
    ppermute x5, starting transfers between devices, shifted(): return lax.ppermute(block, axis, route)  6.9 us
    ppermute x8, waiting for transfers between devices, exchange(): return lax.ppermute(block, axes, route)  5.84 us
    ppermute x5, waiting for transfers between devices, shifted(): return lax.ppermute(block, axis, route)  1.3 us
  transfers between devices with their start and end apart: 13, of which 10 were waited for; matrix products, arithmetic and copies ran while one was open for 0% of the time, Pallas kernels for 23%

profile of v17, /device:TPU:0, one launch (start us, length us, event | category | flops | bytes accessed | tf_op | source)
XLA Modules:
  0.0 33.2 jit_solution(16118711765284603306)
XLA Ops:
  0.0 0.5 %collective-permute-start = (bf16[2,8,16,3,2,256]{5,4,3,2,1,0:T(2,128)(2,1)}, bf16[2,8,16,3,2,256]{5,4,3,2,1,0:T(2,128)(2,1)S(1)}, u32[]{:S(2)}, u32[]{:S(2)}) collective-permute-start(bf16[2,8,16,3,2,256]{5,4,3,2,1,0:T(2,128)(2,1)} %bitcast.11), channel_id=1, source_target_pairs={{1,0},{0,1},{3,2},{2,3},{5,4},{4,5},{7,6},{6,7},{9,8},{8,9},{11,10... | collective-permute-start | bytes 2359304 | tf_op jit(solution)/shard_map/ppermute | solution.py:14
  0.5 1.4 %shard_map.37 = (bf16[2,16,3,2,256]{4,3,2,1,0:T(2,128)(2,1)S(1)}, bf16[2,19,3,2,256]{4,3,2,1,0:T(2,128)(2,1)S(1)}, bf16[2,8,16,3,2,256]{5,4,3,2,1,0:T(2,128)(2,1...) custom-call(bf16[2,8,16,3,2,256]{5,4,3,2,1,0:T(2,128)(2,1)} %bitcast, ...), custom_call_target="tpu_custom_call" | custom-call | tf_op jit(solution)/shard_map/pallas_call | solution.py:19
  1.8 2.6 %collective-permute-start.3 = (bf16[2,19,3,2,256]{4,3,2,1,0:T(2,128)(2,1)S(1)}, bf16[2,19,3,2,256]{4,3,2,1,0:T(2,128)(2,1)S(1)}, u32[]{:S(2)}, u32[]{:S(2)}) collective-permute-start(bf16[2,19,3,2,256]{4,3,2,1,0:T(2,128)(2,1)S(1)} %get-tuple-element.70), channel_id=1, source_target_pairs={{12,0},{0,4},{4,8},{8,12},{13,1},{1,5},{5,9},{9,13},{14,2},{2,6},{... | collective-permute-start | bytes 350216 | tf_op jit(solution)/shard_map/ppermute | solution.py:14
  4.4 2.1 %collective-permute-start.2 = (bf16[2,16,3,2,256]{4,3,2,1,0:T(2,128)(2,1)S(1)}, bf16[2,16,3,2,256]{4,3,2,1,0:T(2,128)(2,1)S(1)}, u32[]{:S(2)}, u32[]{:S(2)}) collective-permute-start(bf16[2,16,3,2,256]{4,3,2,1,0:T(2,128)(2,1)S(1)} %get-tuple-element.69), channel_id=1, source_target_pairs={{4,0},{8,4},{12,8},{0,12},{5,1},{9,5},{13,9},{1,13},{6,2},{10,6},{... | collective-permute-start | bytes 294920 | tf_op jit(solution)/shard_map/ppermute | solution.py:14
  6.5 0.7 %shard_map.38 = (bf16[8,192,256]{2,1,0:T(8,128)(2,1)S(1)}, bf16[8,32,256]{2,1,0:T(8,128)(2,1)S(1)}, f32[8,8,256]{2,1,0:T(8,128)S(1)}, f32[8,8,256]{2,1,0:T(8,128...) custom-call(bf16[2,8,16,3,2,256]{5,4,3,2,1,0:T(2,128)(2,1)S(1)} %get-tuple-element.54.raw_ref, ...), custom_call_target="tpu_custom_call" | custom-call | tf_op jit(solution)/shard_map/pallas_call | solution.py:19
  7.3 1.7 %collective-permute-start.1 = (bf16[8,32,256]{2,1,0:T(8,128)(2,1)S(1)}, bf16[8,32,256]{2,1,0:T(8,128)(2,1)S(1)}, u32[]{:S(2)}, u32[]{:S(2)}) collective-permute-start(bf16[8,32,256]{2,1,0:T(8,128)(2,1)S(1)} %get-tuple-element.68), channel_id=1, source_target_pairs={{2,0},{0,2},{3,1},{1,3},{6,4},{4,6},{7,5},{5,7},{10,8},{8,10},{11,... | collective-permute-start | bytes 393224 | tf_op jit(solution)/shard_map/ppermute | solution.py:14
  8.9 0.5 %shard_map.39 = (bf16[1152,512]{1,0:T(8,128)(2,1)S(1)}, bf16[256,1536]{1,0:T(8,128)(2,1)S(1)}, bf16[192,192]{1,0:T(8,128)(2,1)S(1)}, f32[192,256]{1,0:T(8,128)S(1)}, f32[192,256]{1,0:T(8,128)S(1)}) custom-call(bf16[8,192,256]{2,1,0:T(8,128)(2,1)S(1)} %get-tuple-element.58.refs_0_, f32[8,8,256]{2,1,0:T(8,128)S(1)} %get-tuple-element.59.refs_1_, ...), custom_call_target="tpu_custom_call" | custom-call | flops 150994944 | tf_op jit(solution)/shard_map/pallas_call | solution.py:19
  9.5 0.0 collective-permute-done.raw_ref
  9.5 0.3 shard_map.40
  9.8 0.6 %shard_map.41.refs_0_ = f32[2,8,192,256]{3,2,1,0:T(8,128)S(1)} custom-call(bf16[8,192,256]{2,1,0:T(8,128)(2,1)S(1)} %get-tuple-element.58.refs_0_, bf16[1,8,192,256]{3,2,1,0:T(8,128)(2,1)S(1)} %bitcast.9, f32[8,8,256]{2,1,0:T(8,128)S(1)} %get-tuple-element.64.refs_2_.refs_3_, f32[8,8,256]{2,1,0:T(8,128)S(1)} %get-tuple-element.65.refs_3_), custom_call_target="tpu_custom_call" | custom-call | flops 150994944 | tf_op jit(solution)/shard_map/pallas_call | solution.py:19
  10.4 0.8 %shard_map.42.refs_8_.begun_ref = f32[2,256,512]{2,1,0:T(8,128)S(1)} custom-call(bf16[256,1536]{1,0:T(8,128)(2,1)S(1)} %get-tuple-element.61.own_ref.refs_6_, bf16[1,256,1536]{2,1,0:T(8,128)(2,1)S(1)} %bitcast.6, bf16[1152,512]{1,0:T(8,128)(2,1)S(1)} %get-tuple-element.66.right_ref), custom_call_target="tpu_custom_call" | custom-call | flops 402653184 | tf_op jit(solution)/shard_map/pallas_call | solution.py:19
  11.2 0.7 %collective-permute-done.2.refs_0_ = bf16[2,16,3,2,256]{4,3,2,1,0:T(2,128)(2,1)S(1)} collective-permute-done((bf16[2,16,3,2,256]{4,3,2,1,0:T(2,128)(2,1)S(1)}, bf16[2,16,3,2,256]{4,3,2,1,0:T(2,128)(2,1)S(1)}, u32[]{:S(2)}, u32[]{:S(2)}) %collective-permute-start.2) | collective-permute-done | bytes 98336 | tf_op jit(solution)/shard_map/ppermute | solution.py:14
  11.9 0.0 collective-permute-done.3.refs_1_
  11.9 0.8 %shard_map.43 = (f32[2,2,64,256]{3,2,1,0:T(8,128)S(1)}, bf16[2,2,64,256]{3,2,1,0:T(8,128)(2,1)S(1)}, bf16[384,512]{1,0:T(8,128)(2,1)S(1)}) custom-call(bf16[2,16,3,2,256]{4,3,2,1,0:T(2,128)(2,1)S(1)} %collective-permute-done.2.refs_0_, bf16[2,19,3,2,256]{4,3,2,1,0:T(2,128)(2,1)S(1)} %collective-permute-done.3.refs_1_, ...), custom_call_target="tpu_custom_call" | custom-call | flops 402653184 | tf_op jit(solution)/shard_map/pallas_call | solution.py:19
  12.7 0.3 collective-permute-done.1.refs_1_
  12.9 0.1 collective-permute-start.4
  13.0 0.9 %collective-permute-start.5 = (bf16[2,2,64,256]{3,2,1,0:T(8,128)(2,1)S(1)}, bf16[2,2,64,256]{3,2,1,0:T(8,128)(2,1)S(1)}, u32[]{:S(2)}, u32[]{:S(2)}) collective-permute-start(bf16[2,2,64,256]{3,2,1,0:T(8,128)(2,1)S(1)} %get-tuple-element.85), channel_id=1, source_target_pairs={{0,4},{1,3},{2,6},{3,1},{4,0},{5,7},{6,2},{7,5},{8,12},{9,11},{10,... | collective-permute-start | bytes 393224 | tf_op jit(solution)/shard_map/ppermute | solution.py:418
  14.0 0.3 %collective-permute-done.4 = bf16[8,24,256]{2,1,0:T(8,128)(2,1)S(1)} collective-permute-done((bf16[8,24,256]{2,1,0:T(8,128)(2,1)S(1)}, bf16[8,24,256]{2,1,0:T(8,128)(2,1)S(1)}, u32[]{:S(2)}, u32[]{:S(2)}) %collective-permute-start.4) | collective-permute-done | bytes 98336 | tf_op jit(solution)/shard_map/ppermute | solution.py:14
  14.3 0.6 %shard_map.44.lefts_ref = bf16[2,256,1536]{2,1,0:T(8,128)(2,1)S(1)} custom-call(f32[2,8,192,256]{3,2,1,0:T(8,128)S(1)} %shard_map.41.refs_0_, bf16[8,32,256]{2,1,0:T(8,128)(2,1)S(1)} %collective-permute-done.1.refs_1_, bf16[1,8,24,256]{3,2,1,0:T(8,128)(2,1)S(1)} %bitcast.10, f32[8,8,256]{2,1,0:T(8,128)S(1)} %get-tuple-element.64.refs_2_.refs_3_), custom_call_target="tpu_custom_call" | custom-call | flops 150994944 | tf_op jit(solution)/shard_map/pallas_call | solution.py:19
  15.0 0.7 %shard_map.45 = (f32[2,2,64,256]{3,2,1,0:T(8,128)S(1)}, bf16[2,2,64,256]{3,2,1,0:T(8,128)(2,1)S(1)}) custom-call(bf16[2,256,1536]{2,1,0:T(8,128)(2,1)S(1)} %shard_map.44.lefts_ref, bf16[1152,512]{1,0:T(8,128)(2,1)S(1)} %get-tuple-element.66.right_ref, bf16[384,512]{1,0:T(8,128)(2,1)S(1)} %get-tuple-element.80.edge_ref.right_ref), custom_call_target="tpu_custom_call" | custom-call | flops 3221225472 | tf_op jit(solution)/shard_map/pallas_call | solution.py:19
  15.6 0.9 %collective-permute-start.7 = (bf16[2,2,64,256]{3,2,1,0:T(8,128)(2,1)S(1)}, bf16[2,2,64,256]{3,2,1,0:T(8,128)(2,1)S(1)}, u32[]{:S(2)}, u32[]{:S(2)}) collective-permute-start(bf16[2,2,64,256]{3,2,1,0:T(8,128)(2,1)S(1)} %get-tuple-element.91), channel_id=1, source_target_pairs={{0,4},{1,3},{2,6},{3,1},{4,0},{5,7},{6,2},{7,5},{8,12},{9,11},{10,... | collective-permute-start | bytes 393224 | tf_op jit(solution)/shard_map/ppermute | solution.py:418
  16.6 0.4 %shard_map.46 = (f32[2,2,64,256]{3,2,1,0:T(8,128)S(1)}, bf16[2,2,64,256]{3,2,1,0:T(8,128)(2,1)S(1)}) custom-call(bf16[256,1536]{1,0:T(8,128)(2,1)S(1)} %get-tuple-element.61.own_ref.refs_6_, bf16[1,256,1536]{2,1,0:T(8,128)(2,1)S(1)} %bitcast.8, f32[2,256,512]{2,1,0:T(8,128)S(1)} %shard_map.42.refs_8_.begun_ref, ...), custom_call_target="tpu_custom_call" | custom-call | tf_op jit(solution)/shard_map/pallas_call | solution.py:19
  17.0 0.7 %shard_map.47 = (f32[2,2,64,256]{3,2,1,0:T(8,128)S(1)}, bf16[4,2,64,256]{3,2,1,0:T(8,128)(2,1)S(1)}) custom-call(bf16[2,256,1536]{2,1,0:T(8,128)(2,1)S(1)} %shard_map.44.lefts_ref, bf16[1152,512]{1,0:T(8,128)(2,1)S(1)} %get-tuple-element.66.right_ref, bf16[384,512]{1,0:T(8,128)(2,1)S(1)} %get-tuple-element.80.edge_ref.right_ref, ...), custom_call_target="tpu_custom_call" | custom-call | tf_op jit(solution)/shard_map/pallas_call | solution.py:19
  17.6 0.4 %collective-permute-done.5.refs_1_ = bf16[2,2,64,256]{3,2,1,0:T(8,128)(2,1)S(1)} collective-permute-done((bf16[2,2,64,256]{3,2,1,0:T(8,128)(2,1)S(1)}, bf16[2,2,64,256]{3,2,1,0:T(8,128)(2,1)S(1)}, u32[]{:S(2)}, u32[]{:S(2)}) %collective-permute-start.5) | collective-permute-done | bytes 131104 | tf_op jit(solution)/shard_map/ppermute | solution.py:418
  18.1 1.6 %collective-permute-start.9 = (bf16[2,1,64,256]{3,2,1,0:T(8,128)(2,1)S(1)}, bf16[2,1,64,256]{3,2,1,0:T(8,128)(2,1)S(1)}, u32[]{:S(2)}, u32[]{:S(2)}) collective-permute-start(bf16[2,1,64,256]{3,2,1,0:T(8,128)(2,1)S(1)} %get-tuple-element.94), channel_id=1, source_target_pairs={{0,2},{1,5},{2,0},{3,7},{4,6},{5,1},{6,4},{7,3},{8,10},{9,13},{10,... | collective-permute-start | bytes 196616 | tf_op jit(solution)/shard_map/ppermute | solution.py:418
  19.6 0.9 %collective-permute-start.6 = (bf16[4,2,64,256]{3,2,1,0:T(8,128)(2,1)S(1)}, bf16[4,2,64,256]{3,2,1,0:T(8,128)(2,1)S(1)}, u32[]{:S(2)}, u32[]{:S(2)}) collective-permute-start(bf16[4,2,64,256]{3,2,1,0:T(8,128)(2,1)S(1)} %get-tuple-element.89), channel_id=1, source_target_pairs={{0,4},{1,3},{2,6},{3,1},{4,0},{5,7},{6,2},{7,5},{8,12},{9,11},{10,... | collective-permute-start | bytes 786440 | tf_op jit(solution)/shard_map/ppermute | solution.py:418
  20.5 0.2 collective-permute-done.7.refs_1_
  20.7 1.9 %collective-permute-start.8 = (bf16[2,1,64,256]{3,2,1,0:T(8,128)(2,1)S(1)}, bf16[2,1,64,256]{3,2,1,0:T(8,128)(2,1)S(1)}, u32[]{:S(2)}, u32[]{:S(2)}) collective-permute-start(bf16[2,1,64,256]{3,2,1,0:T(8,128)(2,1)S(1)} %get-tuple-element.93), channel_id=1, source_target_pairs={{0,2},{1,5},{2,0},{3,7},{4,6},{5,1},{6,4},{7,3},{8,10},{9,13},{10,... | collective-permute-start | bytes 196616 | tf_op jit(solution)/shard_map/ppermute | solution.py:418
  22.6 0.5 %collective-permute-done.9.came_ref = bf16[2,1,64,256]{3,2,1,0:T(8,128)(2,1)S(1)} collective-permute-done((bf16[2,1,64,256]{3,2,1,0:T(8,128)(2,1)S(1)}, bf16[2,1,64,256]{3,2,1,0:T(8,128)(2,1)S(1)}, u32[]{:S(2)}, u32[]{:S(2)}) %collective-permute-start.9) | collective-permute-done | bytes 65568 | tf_op jit(solution)/shard_map/ppermute | solution.py:418
  23.1 1.3 %collective-permute-start.12 = (bf16[2,1,64,256]{3,2,1,0:T(8,128)(2,1)S(1)}, bf16[2,1,64,256]{3,2,1,0:T(8,128)(2,1)S(1)}, u32[]{:S(2)}, u32[]{:S(2)}) collective-permute-start(bf16[2,1,64,256]{3,2,1,0:T(8,128)(2,1)S(1)} %shard_map.50), channel_id=1, source_target_pairs={{0,8},{1,9},{2,10},{3,11},{4,12},{5,13},{6,14},{7,15},{8,0},{9,1},... | collective-permute-start | bytes 196616 | tf_op jit(solution)/shard_map/ppermute | solution.py:418
  24.5 1.2 %collective-permute-done.8.came_ref = bf16[2,1,64,256]{3,2,1,0:T(8,128)(2,1)S(1)} collective-permute-done((bf16[2,1,64,256]{3,2,1,0:T(8,128)(2,1)S(1)}, bf16[2,1,64,256]{3,2,1,0:T(8,128)(2,1)S(1)}, u32[]{:S(2)}, u32[]{:S(2)}) %collective-permute-start.8) | collective-permute-done | bytes 65568 | tf_op jit(solution)/shard_map/ppermute | solution.py:418
  25.7 1.7 %collective-permute-start.11 = (bf16[2,1,64,256]{3,2,1,0:T(8,128)(2,1)S(1)}, bf16[2,1,64,256]{3,2,1,0:T(8,128)(2,1)S(1)}, u32[]{:S(2)}, u32[]{:S(2)}) collective-permute-start(bf16[2,1,64,256]{3,2,1,0:T(8,128)(2,1)S(1)} %shard_map.51), channel_id=1, source_target_pairs={{0,8},{1,9},{2,10},{3,11},{4,12},{5,13},{6,14},{7,15},{8,0},{9,1},... | collective-permute-start | bytes 196616 | tf_op jit(solution)/shard_map/ppermute | solution.py:418
  27.4 0.0 collective-permute-done.6.refs_1_.refs_3_
  27.4 0.1 shard_map.52
  27.4 1.4 %collective-permute-start.10 = (bf16[4,1,64,256]{3,2,1,0:T(8,128)(2,1)S(1)}, bf16[4,1,64,256]{3,2,1,0:T(8,128)(2,1)S(1)}, u32[]{:S(2)}, u32[]{:S(2)}) collective-permute-start(bf16[4,1,64,256]{3,2,1,0:T(8,128)(2,1)S(1)} %get-tuple-element.98), channel_id=1, source_target_pairs={{0,2},{1,5},{2,0},{3,7},{4,6},{5,1},{6,4},{7,3},{8,10},{9,13},{10,... | collective-permute-start | bytes 393224 | tf_op jit(solution)/shard_map/ppermute | solution.py:418
  28.9 1.6 %collective-permute-done.12.refs_1_ = bf16[2,1,64,256]{3,2,1,0:T(8,128)(2,1)S(1)} collective-permute-done((bf16[2,1,64,256]{3,2,1,0:T(8,128)(2,1)S(1)}, bf16[2,1,64,256]{3,2,1,0:T(8,128)(2,1)S(1)}, u32[]{:S(2)}, u32[]{:S(2)}) %collective-permute-start.12) | collective-permute-done | bytes 65568 | tf_op jit(solution)/shard_map/ppermute | solution.py:418
  30.5 1.4 %collective-permute-done.11.refs_1_ = bf16[2,1,64,256]{3,2,1,0:T(8,128)(2,1)S(1)} collective-permute-done((bf16[2,1,64,256]{3,2,1,0:T(8,128)(2,1)S(1)}, bf16[2,1,64,256]{3,2,1,0:T(8,128)(2,1)S(1)}, u32[]{:S(2)}, u32[]{:S(2)}) %collective-permute-start.11) | collective-permute-done | bytes 65568 | tf_op jit(solution)/shard_map/ppermute | solution.py:418
  31.9 0.5 %collective-permute-done.10.came_ref = bf16[4,1,64,256]{3,2,1,0:T(8,128)(2,1)S(1)} collective-permute-done((bf16[4,1,64,256]{3,2,1,0:T(8,128)(2,1)S(1)}, bf16[4,1,64,256]{3,2,1,0:T(8,128)(2,1)S(1)}, u32[]{:S(2)}, u32[]{:S(2)}) %collective-permute-start.10) | collective-permute-done | bytes 131104 | tf_op jit(solution)/shard_map/ppermute | solution.py:418
  32.5 0.7 %shard_map.55 = f32[2,2,64,256]{3,2,1,0:T(8,128)} custom-call(bf16[4,1,64,256]{3,2,1,0:T(8,128)(2,1)S(1)} %collective-permute-done.10.came_ref, f32[2,1,64,256]{3,2,1,0:T(8,128)S(1)} %shard_map.53.refs_0_, f32[2,1,64,256]{3,2,1,0:T(8,128)S(1)} %shard_map.54.refs_1_), custom_call_target="tpu_custom_call" | custom-call | tf_op jit(solution)/shard_map/pallas_call | solution.py:19
  (7 shorter events, 0.1 us)
Async XLA Ops:
  0.0 9.5 %collective-permute-start = (bf16[2,8,16,3,2,256]{5,4,3,2,1,0:T(2,128)(2,1)}, bf16[2,8,16,3,2,256]{5,4,3,2,1,0:T(2,128)(2,1)S(1)}, u32[]{:S(2)}, u32[]{:S(2)}) collective-permute-start(bf16[2,8,16,3,2,256]{5,4,3,2,1,0:T(2,128)(2,1)} %bitcast.11), channel_id=1, source_target_pairs={{1,0},{0,1},{3,2},{2,3},{5,4},{4,5},{7,6},{6,7},{9,8},{8,9},{11,10... | collective-permute-start | bytes 2359304 | tf_op jit(solution)/shard_map/ppermute | solution.py:14
  1.8 10.1 %collective-permute-start.3 = (bf16[2,19,3,2,256]{4,3,2,1,0:T(2,128)(2,1)S(1)}, bf16[2,19,3,2,256]{4,3,2,1,0:T(2,128)(2,1)S(1)}, u32[]{:S(2)}, u32[]{:S(2)}) collective-permute-start(bf16[2,19,3,2,256]{4,3,2,1,0:T(2,128)(2,1)S(1)} %get-tuple-element.70), channel_id=1, source_target_pairs={{12,0},{0,4},{4,8},{8,12},{13,1},{1,5},{5,9},{9,13},{14,2},{2,6},{... | collective-permute-start | bytes 350216 | tf_op jit(solution)/shard_map/ppermute | solution.py:14
  4.4 7.4 %collective-permute-start.2 = (bf16[2,16,3,2,256]{4,3,2,1,0:T(2,128)(2,1)S(1)}, bf16[2,16,3,2,256]{4,3,2,1,0:T(2,128)(2,1)S(1)}, u32[]{:S(2)}, u32[]{:S(2)}) collective-permute-start(bf16[2,16,3,2,256]{4,3,2,1,0:T(2,128)(2,1)S(1)} %get-tuple-element.69), channel_id=1, source_target_pairs={{4,0},{8,4},{12,8},{0,12},{5,1},{9,5},{13,9},{1,13},{6,2},{10,6},{... | collective-permute-start | bytes 294920 | tf_op jit(solution)/shard_map/ppermute | solution.py:14
  7.3 5.6 %collective-permute-start.1 = (bf16[8,32,256]{2,1,0:T(8,128)(2,1)S(1)}, bf16[8,32,256]{2,1,0:T(8,128)(2,1)S(1)}, u32[]{:S(2)}, u32[]{:S(2)}) collective-permute-start(bf16[8,32,256]{2,1,0:T(8,128)(2,1)S(1)} %get-tuple-element.68), channel_id=1, source_target_pairs={{2,0},{0,2},{3,1},{1,3},{6,4},{4,6},{7,5},{5,7},{10,8},{8,10},{11,... | collective-permute-start | bytes 393224 | tf_op jit(solution)/shard_map/ppermute | solution.py:14
  12.9 1.4 %collective-permute-start.4 = (bf16[8,24,256]{2,1,0:T(8,128)(2,1)S(1)}, bf16[8,24,256]{2,1,0:T(8,128)(2,1)S(1)}, u32[]{:S(2)}, u32[]{:S(2)}) collective-permute-start(bf16[8,24,256]{2,1,0:T(8,128)(2,1)S(1)} %slice.3), channel_id=1, source_target_pairs={{1,0},{0,1},{3,2},{2,3},{5,4},{4,5},{7,6},{6,7},{9,8},{8,9},{11,10... | collective-permute-start | bytes 294920 | tf_op jit(solution)/shard_map/ppermute | solution.py:14
  13.0 5.0 %collective-permute-start.5 = (bf16[2,2,64,256]{3,2,1,0:T(8,128)(2,1)S(1)}, bf16[2,2,64,256]{3,2,1,0:T(8,128)(2,1)S(1)}, u32[]{:S(2)}, u32[]{:S(2)}) collective-permute-start(bf16[2,2,64,256]{3,2,1,0:T(8,128)(2,1)S(1)} %get-tuple-element.85), channel_id=1, source_target_pairs={{0,4},{1,3},{2,6},{3,1},{4,0},{5,7},{6,2},{7,5},{8,12},{9,11},{10,... | collective-permute-start | bytes 393224 | tf_op jit(solution)/shard_map/ppermute | solution.py:418
  15.6 5.0 %collective-permute-start.7 = (bf16[2,2,64,256]{3,2,1,0:T(8,128)(2,1)S(1)}, bf16[2,2,64,256]{3,2,1,0:T(8,128)(2,1)S(1)}, u32[]{:S(2)}, u32[]{:S(2)}) collective-permute-start(bf16[2,2,64,256]{3,2,1,0:T(8,128)(2,1)S(1)} %get-tuple-element.91), channel_id=1, source_target_pairs={{0,4},{1,3},{2,6},{3,1},{4,0},{5,7},{6,2},{7,5},{8,12},{9,11},{10,... | collective-permute-start | bytes 393224 | tf_op jit(solution)/shard_map/ppermute | solution.py:418
  18.1 5.0 %collective-permute-start.9 = (bf16[2,1,64,256]{3,2,1,0:T(8,128)(2,1)S(1)}, bf16[2,1,64,256]{3,2,1,0:T(8,128)(2,1)S(1)}, u32[]{:S(2)}, u32[]{:S(2)}) collective-permute-start(bf16[2,1,64,256]{3,2,1,0:T(8,128)(2,1)S(1)} %get-tuple-element.94), channel_id=1, source_target_pairs={{0,2},{1,5},{2,0},{3,7},{4,6},{5,1},{6,4},{7,3},{8,10},{9,13},{10,... | collective-permute-start | bytes 196616 | tf_op jit(solution)/shard_map/ppermute | solution.py:418
  19.6 7.7 %collective-permute-start.6 = (bf16[4,2,64,256]{3,2,1,0:T(8,128)(2,1)S(1)}, bf16[4,2,64,256]{3,2,1,0:T(8,128)(2,1)S(1)}, u32[]{:S(2)}, u32[]{:S(2)}) collective-permute-start(bf16[4,2,64,256]{3,2,1,0:T(8,128)(2,1)S(1)} %get-tuple-element.89), channel_id=1, source_target_pairs={{0,4},{1,3},{2,6},{3,1},{4,0},{5,7},{6,2},{7,5},{8,12},{9,11},{10,... | collective-permute-start | bytes 786440 | tf_op jit(solution)/shard_map/ppermute | solution.py:418
  20.7 4.9 %collective-permute-start.8 = (bf16[2,1,64,256]{3,2,1,0:T(8,128)(2,1)S(1)}, bf16[2,1,64,256]{3,2,1,0:T(8,128)(2,1)S(1)}, u32[]{:S(2)}, u32[]{:S(2)}) collective-permute-start(bf16[2,1,64,256]{3,2,1,0:T(8,128)(2,1)S(1)} %get-tuple-element.93), channel_id=1, source_target_pairs={{0,2},{1,5},{2,0},{3,7},{4,6},{5,1},{6,4},{7,3},{8,10},{9,13},{10,... | collective-permute-start | bytes 196616 | tf_op jit(solution)/shard_map/ppermute | solution.py:418
  23.1 7.3 %collective-permute-start.12 = (bf16[2,1,64,256]{3,2,1,0:T(8,128)(2,1)S(1)}, bf16[2,1,64,256]{3,2,1,0:T(8,128)(2,1)S(1)}, u32[]{:S(2)}, u32[]{:S(2)}) collective-permute-start(bf16[2,1,64,256]{3,2,1,0:T(8,128)(2,1)S(1)} %shard_map.50), channel_id=1, source_target_pairs={{0,8},{1,9},{2,10},{3,11},{4,12},{5,13},{6,14},{7,15},{8,0},{9,1},... | collective-permute-start | bytes 196616 | tf_op jit(solution)/shard_map/ppermute | solution.py:418
  25.7 6.3 %collective-permute-start.11 = (bf16[2,1,64,256]{3,2,1,0:T(8,128)(2,1)S(1)}, bf16[2,1,64,256]{3,2,1,0:T(8,128)(2,1)S(1)}, u32[]{:S(2)}, u32[]{:S(2)}) collective-permute-start(bf16[2,1,64,256]{3,2,1,0:T(8,128)(2,1)S(1)} %shard_map.51), channel_id=1, source_target_pairs={{0,8},{1,9},{2,10},{3,11},{4,12},{5,13},{6,14},{7,15},{8,0},{9,1},... | collective-permute-start | bytes 196616 | tf_op jit(solution)/shard_map/ppermute | solution.py:418
  27.4 5.0 %collective-permute-start.10 = (bf16[4,1,64,256]{3,2,1,0:T(8,128)(2,1)S(1)}, bf16[4,1,64,256]{3,2,1,0:T(8,128)(2,1)S(1)}, u32[]{:S(2)}, u32[]{:S(2)}) collective-permute-start(bf16[4,1,64,256]{3,2,1,0:T(8,128)(2,1)S(1)} %get-tuple-element.98), channel_id=1, source_target_pairs={{0,2},{1,5},{2,0},{3,7},{4,6},{5,1},{6,4},{7,3},{8,10},{9,13},{10,... | collective-permute-start | bytes 393224 | tf_op jit(solution)/shard_map/ppermute | solution.py:418

commit v18 on v15

--- a/solution.py
+++ b/solution.py
@@ -14,7 +14,7 @@
     return lax.ppermute(block, axis, route)
 
 
-def call(body, out_shape, flops, operands, scratch=(), places=None):
+def call(body, out_shape, flops, operands, scratch=(), places=None, **more):
     places = places or [pltpu.VMEM] * len(operands)
     return pl.pallas_call(
         body,
@@ -23,6 +23,7 @@
         scratch_shapes=scratch,
         cost_estimate=pl.CostEstimate(flops=flops // 2, bytes_accessed=0, transcendentals=0),
         compiler_params=pltpu.CompilerParams(vmem_limit_bytes=VMEM_LIMIT),
+        **more,
     )(*(pltpu.with_memory_space_constraint(a, place) for a, place in zip(operands, places)))
 
 
@@ -454,10 +455,16 @@
 
 
 def finish_kernel(came_ref, *refs):
-    *kept_refs, out_ref = refs
-    parts = out_ref.shape[1]
+    *kept_refs, out_hbm, sum_ref, left = refs
+    parts = sum_ref.shape[1]
+    copies = []
     for d, kept_ref in enumerate(kept_refs):
-        out_ref[d] = kept_ref[:, 0] + came_ref[d * parts : (d + 1) * parts, 0].astype(jnp.float32)
+        for p in range(parts):
+            sum_ref[d, p] = kept_ref[p, 0] + came_ref[d * parts + p, 0].astype(jnp.float32)
+            copies.append(pltpu.make_async_copy(sum_ref.at[d, p], out_hbm.at[d, p], left.at[d * parts + p]))
+            copies[-1].start()
+    for copy in copies:
+        copy.wait()
 
 
 def local(eigen_modes, links_first, links_second):
@@ -607,8 +614,11 @@
         after = call(cross, shape(*block.shape, dtype=f32), 4 * project_flops, [kept, block])
         totals.append(after)
     came, after = lax.optimization_barrier((came, after))
+    result = (2, parts, rows, width)
     return call(
-        finish_kernel, jax.ShapeDtypeStruct((2, parts, rows, width), f32), 0, [came, *totals]
+        finish_kernel, jax.ShapeDtypeStruct(result, f32), 0, [came, *totals],
+        [pltpu.VMEM(result, f32), pltpu.SemaphoreType.DMA((2 * parts,))],
+        out_specs=pl.BlockSpec(memory_space=pltpu.HBM),
     )
 
 

time: 33.2 us -> 33.2 us (level)
  no operation moved by 1% of the time
where the time goes in v18:
time: 33.2 us; the launch traced here: 33.1 us
  starting transfers between devices  17.3 us (52%)
  Pallas kernels  8.4 us (25%)
  waiting for transfers between devices  7.21 us (22%)
    ppermute x8, starting transfers between devices, exchange(): return lax.ppermute(block, axes, route)  10.4 us
    pallas_call x19, Pallas kernels, call(): pl.pallas_call(body, out_shape=out_shape, in_specs=[pl.BlockSpec(memory_s...  8.4 us
    ppermute x5, starting transfers between devices, shifted(): return lax.ppermute(block, axis, route)  6.9 us
    ppermute x8, waiting for transfers between devices, exchange(): return lax.ppermute(block, axes, route)  5.91 us
    ppermute x5, waiting for transfers between devices, shifted(): return lax.ppermute(block, axis, route)  1.3 us
  transfers between devices with their start and end apart: 13, of which 7 were waited for; matrix products, arithmetic and copies ran while one was open for 0% of the time, Pallas kernels for 23%

profile of v18, /device:TPU:0, one launch (start us, length us, event | category | flops | bytes accessed | tf_op | source)
XLA Modules:
  0.0 33.1 jit_solution(1523156027827729441)
XLA Ops:
  0.0 0.5 %collective-permute-start = (bf16[2,8,16,3,2,256]{5,4,3,2,1,0:T(2,128)(2,1)}, bf16[2,8,16,3,2,256]{5,4,3,2,1,0:T(2,128)(2,1)S(1)}, u32[]{:S(2)}, u32[]{:S(2)}) collective-permute-start(bf16[2,8,16,3,2,256]{5,4,3,2,1,0:T(2,128)(2,1)} %bitcast.11), channel_id=1, source_target_pairs={{1,0},{0,1},{3,2},{2,3},{5,4},{4,5},{7,6},{6,7},{9,8},{8,9},{11,10... | collective-permute-start | bytes 2359304 | tf_op jit(solution)/shard_map/ppermute | solution.py:14
  0.5 1.4 %shard_map.37 = (bf16[2,16,3,2,256]{4,3,2,1,0:T(2,128)(2,1)S(1)}, bf16[2,19,3,2,256]{4,3,2,1,0:T(2,128)(2,1)S(1)}, bf16[2,8,16,3,2,256]{5,4,3,2,1,0:T(2,128)(2,1...) custom-call(bf16[2,8,16,3,2,256]{5,4,3,2,1,0:T(2,128)(2,1)} %bitcast, ...), custom_call_target="tpu_custom_call" | custom-call | tf_op jit(solution)/shard_map/pallas_call | solution.py:19
  1.8 2.6 %collective-permute-start.3 = (bf16[2,19,3,2,256]{4,3,2,1,0:T(2,128)(2,1)S(1)}, bf16[2,19,3,2,256]{4,3,2,1,0:T(2,128)(2,1)S(1)}, u32[]{:S(2)}, u32[]{:S(2)}) collective-permute-start(bf16[2,19,3,2,256]{4,3,2,1,0:T(2,128)(2,1)S(1)} %get-tuple-element.70), channel_id=1, source_target_pairs={{12,0},{0,4},{4,8},{8,12},{13,1},{1,5},{5,9},{9,13},{14,2},{2,6},{... | collective-permute-start | bytes 350216 | tf_op jit(solution)/shard_map/ppermute | solution.py:14
  4.4 2.1 %collective-permute-start.2 = (bf16[2,16,3,2,256]{4,3,2,1,0:T(2,128)(2,1)S(1)}, bf16[2,16,3,2,256]{4,3,2,1,0:T(2,128)(2,1)S(1)}, u32[]{:S(2)}, u32[]{:S(2)}) collective-permute-start(bf16[2,16,3,2,256]{4,3,2,1,0:T(2,128)(2,1)S(1)} %get-tuple-element.69), channel_id=1, source_target_pairs={{4,0},{8,4},{12,8},{0,12},{5,1},{9,5},{13,9},{1,13},{6,2},{10,6},{... | collective-permute-start | bytes 294920 | tf_op jit(solution)/shard_map/ppermute | solution.py:14
  6.5 0.7 %shard_map.38 = (bf16[8,192,256]{2,1,0:T(8,128)(2,1)S(1)}, bf16[8,32,256]{2,1,0:T(8,128)(2,1)S(1)}, f32[8,8,256]{2,1,0:T(8,128)S(1)}, f32[8,8,256]{2,1,0:T(8,128...) custom-call(bf16[2,8,16,3,2,256]{5,4,3,2,1,0:T(2,128)(2,1)S(1)} %get-tuple-element.54.raw_ref, ...), custom_call_target="tpu_custom_call" | custom-call | tf_op jit(solution)/shard_map/pallas_call | solution.py:19
  7.3 1.7 %collective-permute-start.1 = (bf16[8,32,256]{2,1,0:T(8,128)(2,1)S(1)}, bf16[8,32,256]{2,1,0:T(8,128)(2,1)S(1)}, u32[]{:S(2)}, u32[]{:S(2)}) collective-permute-start(bf16[8,32,256]{2,1,0:T(8,128)(2,1)S(1)} %get-tuple-element.68), channel_id=1, source_target_pairs={{2,0},{0,2},{3,1},{1,3},{6,4},{4,6},{7,5},{5,7},{10,8},{8,10},{11,... | collective-permute-start | bytes 393224 | tf_op jit(solution)/shard_map/ppermute | solution.py:14
  8.9 0.5 %shard_map.39 = (bf16[1152,512]{1,0:T(8,128)(2,1)S(1)}, bf16[256,1536]{1,0:T(8,128)(2,1)S(1)}, bf16[192,192]{1,0:T(8,128)(2,1)S(1)}, f32[192,256]{1,0:T(8,128)S(1)}, f32[192,256]{1,0:T(8,128)S(1)}) custom-call(bf16[8,192,256]{2,1,0:T(8,128)(2,1)S(1)} %get-tuple-element.58.refs_0_, f32[8,8,256]{2,1,0:T(8,128)S(1)} %get-tuple-element.59.refs_1_, ...), custom_call_target="tpu_custom_call" | custom-call | flops 150994944 | tf_op jit(solution)/shard_map/pallas_call | solution.py:19
  9.5 0.0 collective-permute-done.raw_ref
  9.5 0.3 shard_map.40
  9.8 0.6 %shard_map.41.refs_0_ = f32[2,8,192,256]{3,2,1,0:T(8,128)S(1)} custom-call(bf16[8,192,256]{2,1,0:T(8,128)(2,1)S(1)} %get-tuple-element.58.refs_0_, bf16[1,8,192,256]{3,2,1,0:T(8,128)(2,1)S(1)} %bitcast.9, f32[8,8,256]{2,1,0:T(8,128)S(1)} %get-tuple-element.64.refs_2_.refs_3_, f32[8,8,256]{2,1,0:T(8,128)S(1)} %get-tuple-element.65.refs_3_), custom_call_target="tpu_custom_call" | custom-call | flops 150994944 | tf_op jit(solution)/shard_map/pallas_call | solution.py:19
  10.4 0.8 %shard_map.42.refs_8_.begun_ref = f32[2,256,512]{2,1,0:T(8,128)S(1)} custom-call(bf16[256,1536]{1,0:T(8,128)(2,1)S(1)} %get-tuple-element.61.own_ref.refs_6_, bf16[1,256,1536]{2,1,0:T(8,128)(2,1)S(1)} %bitcast.6, bf16[1152,512]{1,0:T(8,128)(2,1)S(1)} %get-tuple-element.66.right_ref), custom_call_target="tpu_custom_call" | custom-call | flops 402653184 | tf_op jit(solution)/shard_map/pallas_call | solution.py:19
  11.2 0.7 %collective-permute-done.2.refs_0_ = bf16[2,16,3,2,256]{4,3,2,1,0:T(2,128)(2,1)S(1)} collective-permute-done((bf16[2,16,3,2,256]{4,3,2,1,0:T(2,128)(2,1)S(1)}, bf16[2,16,3,2,256]{4,3,2,1,0:T(2,128)(2,1)S(1)}, u32[]{:S(2)}, u32[]{:S(2)}) %collective-permute-start.2) | collective-permute-done | bytes 98336 | tf_op jit(solution)/shard_map/ppermute | solution.py:14
  11.9 0.0 collective-permute-done.3.refs_1_
  11.9 0.8 %shard_map.43 = (f32[2,2,64,256]{3,2,1,0:T(8,128)S(1)}, bf16[2,2,64,256]{3,2,1,0:T(8,128)(2,1)S(1)}, bf16[384,512]{1,0:T(8,128)(2,1)S(1)}) custom-call(bf16[2,16,3,2,256]{4,3,2,1,0:T(2,128)(2,1)S(1)} %collective-permute-done.2.refs_0_, bf16[2,19,3,2,256]{4,3,2,1,0:T(2,128)(2,1)S(1)} %collective-permute-done.3.refs_1_, ...), custom_call_target="tpu_custom_call" | custom-call | flops 402653184 | tf_op jit(solution)/shard_map/pallas_call | solution.py:19
  12.7 0.3 collective-permute-done.1.refs_1_
  12.9 0.1 collective-permute-start.4
  13.0 0.9 %collective-permute-start.7 = (bf16[2,2,64,256]{3,2,1,0:T(8,128)(2,1)S(1)}, bf16[2,2,64,256]{3,2,1,0:T(8,128)(2,1)S(1)}, u32[]{:S(2)}, u32[]{:S(2)}) collective-permute-start(bf16[2,2,64,256]{3,2,1,0:T(8,128)(2,1)S(1)} %get-tuple-element.87), channel_id=1, source_target_pairs={{0,4},{1,3},{2,6},{3,1},{4,0},{5,7},{6,2},{7,5},{8,12},{9,11},{10,... | collective-permute-start | bytes 393224 | tf_op jit(solution)/shard_map/ppermute | solution.py:419
  14.0 0.3 %collective-permute-done.4 = bf16[8,24,256]{2,1,0:T(8,128)(2,1)S(1)} collective-permute-done((bf16[8,24,256]{2,1,0:T(8,128)(2,1)S(1)}, bf16[8,24,256]{2,1,0:T(8,128)(2,1)S(1)}, u32[]{:S(2)}, u32[]{:S(2)}) %collective-permute-start.4) | collective-permute-done | bytes 98336 | tf_op jit(solution)/shard_map/ppermute | solution.py:14
  14.3 0.6 %shard_map.44.lefts_ref = bf16[2,256,1536]{2,1,0:T(8,128)(2,1)S(1)} custom-call(f32[2,8,192,256]{3,2,1,0:T(8,128)S(1)} %shard_map.41.refs_0_, bf16[8,32,256]{2,1,0:T(8,128)(2,1)S(1)} %collective-permute-done.1.refs_1_, bf16[1,8,24,256]{3,2,1,0:T(8,128)(2,1)S(1)} %bitcast.10, f32[8,8,256]{2,1,0:T(8,128)S(1)} %get-tuple-element.64.refs_2_.refs_3_), custom_call_target="tpu_custom_call" | custom-call | flops 150994944 | tf_op jit(solution)/shard_map/pallas_call | solution.py:19
  15.0 0.7 %shard_map.45 = (f32[2,2,64,256]{3,2,1,0:T(8,128)S(1)}, bf16[2,2,64,256]{3,2,1,0:T(8,128)(2,1)S(1)}) custom-call(bf16[2,256,1536]{2,1,0:T(8,128)(2,1)S(1)} %shard_map.44.lefts_ref, bf16[1152,512]{1,0:T(8,128)(2,1)S(1)} %get-tuple-element.66.right_ref, bf16[384,512]{1,0:T(8,128)(2,1)S(1)} %get-tuple-element.80.edge_ref.right_ref), custom_call_target="tpu_custom_call" | custom-call | flops 3221225472 | tf_op jit(solution)/shard_map/pallas_call | solution.py:19
  15.6 0.9 %collective-permute-start.6 = (bf16[2,2,64,256]{3,2,1,0:T(8,128)(2,1)S(1)}, bf16[2,2,64,256]{3,2,1,0:T(8,128)(2,1)S(1)}, u32[]{:S(2)}, u32[]{:S(2)}) collective-permute-start(bf16[2,2,64,256]{3,2,1,0:T(8,128)(2,1)S(1)} %get-tuple-element.85), channel_id=1, source_target_pairs={{0,4},{1,3},{2,6},{3,1},{4,0},{5,7},{6,2},{7,5},{8,12},{9,11},{10,... | collective-permute-start | bytes 393224 | tf_op jit(solution)/shard_map/ppermute | solution.py:419
  16.6 0.4 %shard_map.46 = (f32[2,2,64,256]{3,2,1,0:T(8,128)S(1)}, bf16[2,2,64,256]{3,2,1,0:T(8,128)(2,1)S(1)}) custom-call(bf16[256,1536]{1,0:T(8,128)(2,1)S(1)} %get-tuple-element.61.own_ref.refs_6_, bf16[1,256,1536]{2,1,0:T(8,128)(2,1)S(1)} %bitcast.8, f32[2,256,512]{2,1,0:T(8,128)S(1)} %shard_map.42.refs_8_.begun_ref, ...), custom_call_target="tpu_custom_call" | custom-call | tf_op jit(solution)/shard_map/pallas_call | solution.py:19
  17.0 0.7 %shard_map.47 = (f32[2,2,64,256]{3,2,1,0:T(8,128)S(1)}, bf16[4,2,64,256]{3,2,1,0:T(8,128)(2,1)S(1)}) custom-call(bf16[2,256,1536]{2,1,0:T(8,128)(2,1)S(1)} %shard_map.44.lefts_ref, bf16[1152,512]{1,0:T(8,128)(2,1)S(1)} %get-tuple-element.66.right_ref, bf16[384,512]{1,0:T(8,128)(2,1)S(1)} %get-tuple-element.80.edge_ref.right_ref, ...), custom_call_target="tpu_custom_call" | custom-call | tf_op jit(solution)/shard_map/pallas_call | solution.py:19
  17.6 1.2 %collective-permute-start.5 = (bf16[4,2,64,256]{3,2,1,0:T(8,128)(2,1)S(1)}, bf16[4,2,64,256]{3,2,1,0:T(8,128)(2,1)S(1)}, u32[]{:S(2)}, u32[]{:S(2)}) collective-permute-start(bf16[4,2,64,256]{3,2,1,0:T(8,128)(2,1)S(1)} %get-tuple-element.83), channel_id=1, source_target_pairs={{0,4},{1,3},{2,6},{3,1},{4,0},{5,7},{6,2},{7,5},{8,12},{9,11},{10,... | collective-permute-start | bytes 786440 | tf_op jit(solution)/shard_map/ppermute | solution.py:419
  18.9 0.0 collective-permute-done.7.refs_1_
  18.9 1.6 %collective-permute-start.9 = (bf16[2,1,64,256]{3,2,1,0:T(8,128)(2,1)S(1)}, bf16[2,1,64,256]{3,2,1,0:T(8,128)(2,1)S(1)}, u32[]{:S(2)}, u32[]{:S(2)}) collective-permute-start(bf16[2,1,64,256]{3,2,1,0:T(8,128)(2,1)S(1)} %get-tuple-element.94), channel_id=1, source_target_pairs={{0,2},{1,5},{2,0},{3,7},{4,6},{5,1},{6,4},{7,3},{8,10},{9,13},{10,... | collective-permute-start | bytes 196616 | tf_op jit(solution)/shard_map/ppermute | solution.py:419
  20.5 0.2 collective-permute-done.6.refs_1_
  20.7 1.6 %collective-permute-start.8 = (bf16[2,1,64,256]{3,2,1,0:T(8,128)(2,1)S(1)}, bf16[2,1,64,256]{3,2,1,0:T(8,128)(2,1)S(1)}, u32[]{:S(2)}, u32[]{:S(2)}) collective-permute-start(bf16[2,1,64,256]{3,2,1,0:T(8,128)(2,1)S(1)} %get-tuple-element.93), channel_id=1, source_target_pairs={{0,2},{1,5},{2,0},{3,7},{4,6},{5,1},{6,4},{7,3},{8,10},{9,13},{10,... | collective-permute-start | bytes 196616 | tf_op jit(solution)/shard_map/ppermute | solution.py:419
  22.3 1.7 %collective-permute-done.9.came_ref = bf16[2,1,64,256]{3,2,1,0:T(8,128)(2,1)S(1)} collective-permute-done((bf16[2,1,64,256]{3,2,1,0:T(8,128)(2,1)S(1)}, bf16[2,1,64,256]{3,2,1,0:T(8,128)(2,1)S(1)}, u32[]{:S(2)}, u32[]{:S(2)}) %collective-permute-start.9) | collective-permute-done | bytes 65568 | tf_op jit(solution)/shard_map/ppermute | solution.py:419
  24.0 1.4 %collective-permute-start.12 = (bf16[2,1,64,256]{3,2,1,0:T(8,128)(2,1)S(1)}, bf16[2,1,64,256]{3,2,1,0:T(8,128)(2,1)S(1)}, u32[]{:S(2)}, u32[]{:S(2)}) collective-permute-start(bf16[2,1,64,256]{3,2,1,0:T(8,128)(2,1)S(1)} %shard_map.50), channel_id=1, source_target_pairs={{0,8},{1,9},{2,10},{3,11},{4,12},{5,13},{6,14},{7,15},{8,0},{9,1},... | collective-permute-start | bytes 196616 | tf_op jit(solution)/shard_map/ppermute | solution.py:419
  25.4 0.0 collective-permute-done.8.came_ref
  25.4 1.7 %collective-permute-start.11 = (bf16[2,1,64,256]{3,2,1,0:T(8,128)(2,1)S(1)}, bf16[2,1,64,256]{3,2,1,0:T(8,128)(2,1)S(1)}, u32[]{:S(2)}, u32[]{:S(2)}) collective-permute-start(bf16[2,1,64,256]{3,2,1,0:T(8,128)(2,1)S(1)} %shard_map.51), channel_id=1, source_target_pairs={{0,8},{1,9},{2,10},{3,11},{4,12},{5,13},{6,14},{7,15},{8,0},{9,1},... | collective-permute-start | bytes 196616 | tf_op jit(solution)/shard_map/ppermute | solution.py:419
  27.1 0.0 collective-permute-done.5.refs_1_.refs_3_
  27.1 0.1 shard_map.52
  27.2 1.2 %collective-permute-start.10 = (bf16[4,1,64,256]{3,2,1,0:T(8,128)(2,1)S(1)}, bf16[4,1,64,256]{3,2,1,0:T(8,128)(2,1)S(1)}, u32[]{:S(2)}, u32[]{:S(2)}) collective-permute-start(bf16[4,1,64,256]{3,2,1,0:T(8,128)(2,1)S(1)} %get-tuple-element.98), channel_id=1, source_target_pairs={{0,2},{1,5},{2,0},{3,7},{4,6},{5,1},{6,4},{7,3},{8,10},{9,13},{10,... | collective-permute-start | bytes 393224 | tf_op jit(solution)/shard_map/ppermute | solution.py:419
  28.3 2.7 %collective-permute-done.12.refs_1_ = bf16[2,1,64,256]{3,2,1,0:T(8,128)(2,1)S(1)} collective-permute-done((bf16[2,1,64,256]{3,2,1,0:T(8,128)(2,1)S(1)}, bf16[2,1,64,256]{3,2,1,0:T(8,128)(2,1)S(1)}, u32[]{:S(2)}, u32[]{:S(2)}) %collective-permute-start.12) | collective-permute-done | bytes 65568 | tf_op jit(solution)/shard_map/ppermute | solution.py:419
  31.1 1.2 %collective-permute-done.11.refs_1_ = bf16[2,1,64,256]{3,2,1,0:T(8,128)(2,1)S(1)} collective-permute-done((bf16[2,1,64,256]{3,2,1,0:T(8,128)(2,1)S(1)}, bf16[2,1,64,256]{3,2,1,0:T(8,128)(2,1)S(1)}, u32[]{:S(2)}, u32[]{:S(2)}) %collective-permute-start.11) | collective-permute-done | bytes 65568 | tf_op jit(solution)/shard_map/ppermute | solution.py:419
  32.3 0.0 collective-permute-done.10.came_ref
  32.3 0.7 %shard_map.55 = f32[2,2,64,256]{3,2,1,0:T(8,128)} custom-call(bf16[4,1,64,256]{3,2,1,0:T(8,128)(2,1)S(1)} %collective-permute-done.10.came_ref, f32[2,1,64,256]{3,2,1,0:T(8,128)S(1)} %shard_map.53.refs_0_, f32[2,1,64,256]{3,2,1,0:T(8,128)S(1)} %shard_map.54.refs_1_), custom_call_target="tpu_custom_call" | custom-call | tf_op jit(solution)/shard_map/pallas_call | solution.py:19
  (7 shorter events, 0.1 us)
Async XLA Ops:
  0.0 9.5 %collective-permute-start = (bf16[2,8,16,3,2,256]{5,4,3,2,1,0:T(2,128)(2,1)}, bf16[2,8,16,3,2,256]{5,4,3,2,1,0:T(2,128)(2,1)S(1)}, u32[]{:S(2)}, u32[]{:S(2)}) collective-permute-start(bf16[2,8,16,3,2,256]{5,4,3,2,1,0:T(2,128)(2,1)} %bitcast.11), channel_id=1, source_target_pairs={{1,0},{0,1},{3,2},{2,3},{5,4},{4,5},{7,6},{6,7},{9,8},{8,9},{11,10... | collective-permute-start | bytes 2359304 | tf_op jit(solution)/shard_map/ppermute | solution.py:14
  1.8 10.1 %collective-permute-start.3 = (bf16[2,19,3,2,256]{4,3,2,1,0:T(2,128)(2,1)S(1)}, bf16[2,19,3,2,256]{4,3,2,1,0:T(2,128)(2,1)S(1)}, u32[]{:S(2)}, u32[]{:S(2)}) collective-permute-start(bf16[2,19,3,2,256]{4,3,2,1,0:T(2,128)(2,1)S(1)} %get-tuple-element.70), channel_id=1, source_target_pairs={{12,0},{0,4},{4,8},{8,12},{13,1},{1,5},{5,9},{9,13},{14,2},{2,6},{... | collective-permute-start | bytes 350216 | tf_op jit(solution)/shard_map/ppermute | solution.py:14
  4.4 7.4 %collective-permute-start.2 = (bf16[2,16,3,2,256]{4,3,2,1,0:T(2,128)(2,1)S(1)}, bf16[2,16,3,2,256]{4,3,2,1,0:T(2,128)(2,1)S(1)}, u32[]{:S(2)}, u32[]{:S(2)}) collective-permute-start(bf16[2,16,3,2,256]{4,3,2,1,0:T(2,128)(2,1)S(1)} %get-tuple-element.69), channel_id=1, source_target_pairs={{4,0},{8,4},{12,8},{0,12},{5,1},{9,5},{13,9},{1,13},{6,2},{10,6},{... | collective-permute-start | bytes 294920 | tf_op jit(solution)/shard_map/ppermute | solution.py:14
  7.3 5.6 %collective-permute-start.1 = (bf16[8,32,256]{2,1,0:T(8,128)(2,1)S(1)}, bf16[8,32,256]{2,1,0:T(8,128)(2,1)S(1)}, u32[]{:S(2)}, u32[]{:S(2)}) collective-permute-start(bf16[8,32,256]{2,1,0:T(8,128)(2,1)S(1)} %get-tuple-element.68), channel_id=1, source_target_pairs={{2,0},{0,2},{3,1},{1,3},{6,4},{4,6},{7,5},{5,7},{10,8},{8,10},{11,... | collective-permute-start | bytes 393224 | tf_op jit(solution)/shard_map/ppermute | solution.py:14
  12.9 1.4 %collective-permute-start.4 = (bf16[8,24,256]{2,1,0:T(8,128)(2,1)S(1)}, bf16[8,24,256]{2,1,0:T(8,128)(2,1)S(1)}, u32[]{:S(2)}, u32[]{:S(2)}) collective-permute-start(bf16[8,24,256]{2,1,0:T(8,128)(2,1)S(1)} %slice.3), channel_id=1, source_target_pairs={{1,0},{0,1},{3,2},{2,3},{5,4},{4,5},{7,6},{6,7},{9,8},{8,9},{11,10... | collective-permute-start | bytes 294920 | tf_op jit(solution)/shard_map/ppermute | solution.py:14
  13.0 5.9 %collective-permute-start.7 = (bf16[2,2,64,256]{3,2,1,0:T(8,128)(2,1)S(1)}, bf16[2,2,64,256]{3,2,1,0:T(8,128)(2,1)S(1)}, u32[]{:S(2)}, u32[]{:S(2)}) collective-permute-start(bf16[2,2,64,256]{3,2,1,0:T(8,128)(2,1)S(1)} %get-tuple-element.87), channel_id=1, source_target_pairs={{0,4},{1,3},{2,6},{3,1},{4,0},{5,7},{6,2},{7,5},{8,12},{9,11},{10,... | collective-permute-start | bytes 393224 | tf_op jit(solution)/shard_map/ppermute | solution.py:419
  15.6 5.0 %collective-permute-start.6 = (bf16[2,2,64,256]{3,2,1,0:T(8,128)(2,1)S(1)}, bf16[2,2,64,256]{3,2,1,0:T(8,128)(2,1)S(1)}, u32[]{:S(2)}, u32[]{:S(2)}) collective-permute-start(bf16[2,2,64,256]{3,2,1,0:T(8,128)(2,1)S(1)} %get-tuple-element.85), channel_id=1, source_target_pairs={{0,4},{1,3},{2,6},{3,1},{4,0},{5,7},{6,2},{7,5},{8,12},{9,11},{10,... | collective-permute-start | bytes 393224 | tf_op jit(solution)/shard_map/ppermute | solution.py:419
  17.6 9.5 %collective-permute-start.5 = (bf16[4,2,64,256]{3,2,1,0:T(8,128)(2,1)S(1)}, bf16[4,2,64,256]{3,2,1,0:T(8,128)(2,1)S(1)}, u32[]{:S(2)}, u32[]{:S(2)}) collective-permute-start(bf16[4,2,64,256]{3,2,1,0:T(8,128)(2,1)S(1)} %get-tuple-element.83), channel_id=1, source_target_pairs={{0,4},{1,3},{2,6},{3,1},{4,0},{5,7},{6,2},{7,5},{8,12},{9,11},{10,... | collective-permute-start | bytes 786440 | tf_op jit(solution)/shard_map/ppermute | solution.py:419
  18.9 5.1 %collective-permute-start.9 = (bf16[2,1,64,256]{3,2,1,0:T(8,128)(2,1)S(1)}, bf16[2,1,64,256]{3,2,1,0:T(8,128)(2,1)S(1)}, u32[]{:S(2)}, u32[]{:S(2)}) collective-permute-start(bf16[2,1,64,256]{3,2,1,0:T(8,128)(2,1)S(1)} %get-tuple-element.94), channel_id=1, source_target_pairs={{0,2},{1,5},{2,0},{3,7},{4,6},{5,1},{6,4},{7,3},{8,10},{9,13},{10,... | collective-permute-start | bytes 196616 | tf_op jit(solution)/shard_map/ppermute | solution.py:419
  20.7 4.7 %collective-permute-start.8 = (bf16[2,1,64,256]{3,2,1,0:T(8,128)(2,1)S(1)}, bf16[2,1,64,256]{3,2,1,0:T(8,128)(2,1)S(1)}, u32[]{:S(2)}, u32[]{:S(2)}) collective-permute-start(bf16[2,1,64,256]{3,2,1,0:T(8,128)(2,1)S(1)} %get-tuple-element.93), channel_id=1, source_target_pairs={{0,2},{1,5},{2,0},{3,7},{4,6},{5,1},{6,4},{7,3},{8,10},{9,13},{10,... | collective-permute-start | bytes 196616 | tf_op jit(solution)/shard_map/ppermute | solution.py:419
  24.0 7.0 %collective-permute-start.12 = (bf16[2,1,64,256]{3,2,1,0:T(8,128)(2,1)S(1)}, bf16[2,1,64,256]{3,2,1,0:T(8,128)(2,1)S(1)}, u32[]{:S(2)}, u32[]{:S(2)}) collective-permute-start(bf16[2,1,64,256]{3,2,1,0:T(8,128)(2,1)S(1)} %shard_map.50), channel_id=1, source_target_pairs={{0,8},{1,9},{2,10},{3,11},{4,12},{5,13},{6,14},{7,15},{8,0},{9,1},... | collective-permute-start | bytes 196616 | tf_op jit(solution)/shard_map/ppermute | solution.py:419
  25.4 6.9 %collective-permute-start.11 = (bf16[2,1,64,256]{3,2,1,0:T(8,128)(2,1)S(1)}, bf16[2,1,64,256]{3,2,1,0:T(8,128)(2,1)S(1)}, u32[]{:S(2)}, u32[]{:S(2)}) collective-permute-start(bf16[2,1,64,256]{3,2,1,0:T(8,128)(2,1)S(1)} %shard_map.51), channel_id=1, source_target_pairs={{0,8},{1,9},{2,10},{3,11},{4,12},{5,13},{6,14},{7,15},{8,0},{9,1},... | collective-permute-start | bytes 196616 | tf_op jit(solution)/shard_map/ppermute | solution.py:419
  27.2 5.2 %collective-permute-start.10 = (bf16[4,1,64,256]{3,2,1,0:T(8,128)(2,1)S(1)}, bf16[4,1,64,256]{3,2,1,0:T(8,128)(2,1)S(1)}, u32[]{:S(2)}, u32[]{:S(2)}) collective-permute-start(bf16[4,1,64,256]{3,2,1,0:T(8,128)(2,1)S(1)} %get-tuple-element.98), channel_id=1, source_target_pairs={{0,2},{1,5},{2,0},{3,7},{4,6},{5,1},{6,4},{7,3},{8,10},{9,13},{10,... | collective-permute-start | bytes 393224 | tf_op jit(solution)/shard_map/ppermute | solution.py:419

commit v19 on v15

--- a/solution.py
+++ b/solution.py
@@ -172,14 +172,9 @@
 
 
 def prepare_kernel(
-    raw_ref, links_x_ref, links_y_ref, maps_ref,
-    rows_ref, ends_ref, ahead_x_ref, back_x_ref, ahead_y_ref, back_y_ref,
+    raw_ref, links_x_ref, links_y_ref, maps_ref, ends_ref, ahead_x_ref, back_x_ref, ahead_y_ref, back_y_ref
 ):
-    planes, depth, width = rows_ref.shape
-    zs = raw_ref.shape[4]
-    ys = raw_ref.shape[2]
-    sites = ys * zs
-    row_size = depth // sites * zs
+    parts, planes, ys, colours, zs, width = raw_ref.shape
     lanes = ahead_y_ref.shape[2]
     ahead_x, ahead_y, back_x, back_y = coefficients(
         links_x_ref[...].reshape(-1, ys), links_y_ref[...].reshape(-1, ys), maps_ref, planes
@@ -188,18 +183,13 @@
     back_x_ref[...] = back_x
     ahead_y_ref[...] = ahead_y
     back_y_ref[...] = back_y
-
-    row, lane = iotas((2 * row_size, depth))
-    spot = row % row_size
-    wanted = (spot // zs) * sites + spot % zs + jnp.where(row < row_size, 0, sites - zs)
-    ends = (lane == wanted).astype(jnp.bfloat16)
     filler = jnp.zeros((8, width - 128), jnp.float32)
-    spare = ends_ref.shape[1] - 2 * row_size - 8
+    spare = ends_ref.shape[1] - 2 * parts * colours * zs - 8
     for x in range(planes):
-        plane = plane_rows(raw_ref.at[:, x], ys)
-        rows_ref[place_of(x, planes)] = plane
-        tail = jnp.concatenate([back_y[x, :, lanes - 128 :], filler], axis=1)
-        pieces = [dot(ends, plane), tail]
+        pieces = [
+            raw_ref[p, x, y].astype(jnp.float32).reshape(colours * zs, width) for y in (0, ys - 1) for p in range(parts)
+        ]
+        pieces.append(jnp.concatenate([back_y[x, :, lanes - 128 :], filler], axis=1))
         if spare:
             pieces.append(jnp.zeros((spare, width), jnp.float32))
         ends_ref[x] = jnp.concatenate(pieces, axis=0).astype(jnp.bfloat16)
@@ -235,9 +225,11 @@
 
 
 def inner_kernel(
-    sites, rows_ref, ahead_ref, back_ref, right_ref, turned_ref, matrix_ref, ahead_part_ref, back_part_ref
+    sites, raw_ref, ahead_ref, back_ref, rows_ref, right_ref, turned_ref, matrix_ref, ahead_part_ref, back_part_ref
 ):
     planes, depth, width = rows_ref.shape
+    for x in range(planes):
+        rows_ref[place_of(x, planes)] = plane_rows(raw_ref.at[:, x], raw_ref.shape[2])
     same = same_site(sites, depth)
     for x in range(1, planes - 1):
         above = rows_ref[place_of(x + 1, planes)]
@@ -502,9 +494,9 @@
     )
     low = shifted(last_plane, "gx", 1)
     high = shifted(first_plane, "gx", -1)
-    field, ends, ahead_x, back_x, ahead_y, back_y = call(
+    ends, ahead_x, back_x, ahead_y, back_y = call(
         prepare_kernel,
-        (field_shape, shape(planes, edge, width), link_shape, link_shape, link_shape, link_shape),
+        (shape(planes, edge, width), link_shape, link_shape, link_shape, link_shape),
         0,
         inputs,
     )
@@ -531,14 +523,14 @@
     def move_y(*refs):
         move_y_kernel(sites, zs, *refs)
 
-    right, own, matrix, ahead_part, back_part = call(
+    field, right, own, matrix, ahead_part, back_part = call(
         inner,
         (
-            shape(inner_depth, parts * width), turned_shape, shape(depth, depth),
+            field_shape, shape(inner_depth, parts * width), turned_shape, shape(depth, depth),
             shape(depth, width, dtype=f32), shape(depth, width, dtype=f32),
         ),
         2 * step_flops,
-        [field, ahead_x, back_x],
+        [inputs[0], ahead_x, back_x],
     )
     turned = [call(turn_kernel, (field_shape, turned_shape), step_flops // 4, [r]) for r in raw_others]
     fields = jnp.stack([t[0] for t in turned])

time: 33.2 us -> 33.1 us (level)
  no operation moved by 1% of the time
where the time goes in v19:
time: 33.1 us; the launch traced here: 32.9 us
  starting transfers between devices  17.5 us (53%)
  Pallas kernels  8.35 us (25%)
  waiting for transfers between devices  6.95 us (21%)
    ppermute x8, starting transfers between devices, exchange(): return lax.ppermute(block, axes, route)  10.5 us
    pallas_call x19, Pallas kernels, call(): pl.pallas_call(body, out_shape=out_shape, in_specs=[pl.BlockSpec(memory_s...  8.35 us
    ppermute x5, starting transfers between devices, shifted(): return lax.ppermute(block, axis, route)  6.96 us
    ppermute x8, waiting for transfers between devices, exchange(): return lax.ppermute(block, axes, route)  5.93 us
    ppermute x5, waiting for transfers between devices, shifted(): return lax.ppermute(block, axis, route)  1.03 us
  transfers between devices with their start and end apart: 13, of which 7 were waited for; matrix products, arithmetic and copies ran while one was open for 0% of the time, Pallas kernels for 23%

profile of v19, /device:TPU:0, one launch (start us, length us, event | category | flops | bytes accessed | tf_op | source)
XLA Modules:
  0.0 32.9 jit_solution(6942787205618374716)
XLA Ops:
  0.0 0.5 %collective-permute-start = (bf16[2,8,16,3,2,256]{5,4,3,2,1,0:T(2,128)(2,1)}, bf16[2,8,16,3,2,256]{5,4,3,2,1,0:T(2,128)(2,1)S(1)}, u32[]{:S(2)}, u32[]{:S(2)}) collective-permute-start(bf16[2,8,16,3,2,256]{5,4,3,2,1,0:T(2,128)(2,1)} %bitcast.11), channel_id=1, source_target_pairs={{1,0},{0,1},{3,2},{2,3},{5,4},{4,5},{7,6},{6,7},{9,8},{8,9},{11,10... | collective-permute-start | bytes 2359304 | tf_op jit(solution)/shard_map/ppermute | solution.py:14
  0.5 1.4 %shard_map.37 = (bf16[2,16,3,2,256]{4,3,2,1,0:T(2,128)(2,1)S(1)}, bf16[2,19,3,2,256]{4,3,2,1,0:T(2,128)(2,1)S(1)}, bf16[2,8,16,3,2,256]{5,4,3,2,1,0:T(2,128)(2,1...) custom-call(bf16[2,8,16,3,2,256]{5,4,3,2,1,0:T(2,128)(2,1)} %bitcast, ...), custom_call_target="tpu_custom_call" | custom-call | tf_op jit(solution)/shard_map/pallas_call | solution.py:19
  1.8 2.6 %collective-permute-start.3 = (bf16[2,19,3,2,256]{4,3,2,1,0:T(2,128)(2,1)S(1)}, bf16[2,19,3,2,256]{4,3,2,1,0:T(2,128)(2,1)S(1)}, u32[]{:S(2)}, u32[]{:S(2)}) collective-permute-start(bf16[2,19,3,2,256]{4,3,2,1,0:T(2,128)(2,1)S(1)} %get-tuple-element.70), channel_id=1, source_target_pairs={{12,0},{0,4},{4,8},{8,12},{13,1},{1,5},{5,9},{9,13},{14,2},{2,6},{... | collective-permute-start | bytes 350216 | tf_op jit(solution)/shard_map/ppermute | solution.py:14
  4.4 2.1 %collective-permute-start.2 = (bf16[2,16,3,2,256]{4,3,2,1,0:T(2,128)(2,1)S(1)}, bf16[2,16,3,2,256]{4,3,2,1,0:T(2,128)(2,1)S(1)}, u32[]{:S(2)}, u32[]{:S(2)}) collective-permute-start(bf16[2,16,3,2,256]{4,3,2,1,0:T(2,128)(2,1)S(1)} %get-tuple-element.69), channel_id=1, source_target_pairs={{4,0},{8,4},{12,8},{0,12},{5,1},{9,5},{13,9},{1,13},{6,2},{10,6},{... | collective-permute-start | bytes 294920 | tf_op jit(solution)/shard_map/ppermute | solution.py:14
  6.5 0.6 %shard_map.38 = (bf16[8,32,256]{2,1,0:T(8,128)(2,1)S(1)}, f32[8,8,256]{2,1,0:T(8,128)S(1)}, f32[8,8,256]{2,1,0:T(8,128)S(1)}, f32[8,8,256]{2,1,0:T(8,128)S(1)}, f32[8,8,256]{2,1,0:T(8,128)S(1)}) custom-call(bf16[2,8,16,3,2,256]{5,4,3,2,1,0:T(2,128)(2,1)S(1)} %get-tuple-element.54.raw_ref.refs_0_, ...), custom_call_target="tpu_custom_call" | custom-call | tf_op jit(solution)/shard_map/pallas_call | solution.py:19
  7.1 1.7 %collective-permute-start.1 = (bf16[8,32,256]{2,1,0:T(8,128)(2,1)S(1)}, bf16[8,32,256]{2,1,0:T(8,128)(2,1)S(1)}, u32[]{:S(2)}, u32[]{:S(2)}) collective-permute-start(bf16[8,32,256]{2,1,0:T(8,128)(2,1)S(1)} %get-tuple-element.68), channel_id=1, source_target_pairs={{2,0},{0,2},{3,1},{1,3},{6,4},{4,6},{7,5},{5,7},{10,8},{8,10},{11,... | collective-permute-start | bytes 393224 | tf_op jit(solution)/shard_map/ppermute | solution.py:14
  8.8 0.7 %shard_map.39 = (bf16[8,192,256]{2,1,0:T(8,128)(2,1)S(1)}, bf16[1152,512]{1,0:T(8,128)(2,1)S(1)}, bf16[256,1536]{1,0:T(8,128)(2,1)S(1)}, bf16[192,192]{1,0:T(8,1...) custom-call(bf16[2,8,16,3,2,256]{5,4,3,2,1,0:T(2,128)(2,1)S(1)} %get-tuple-element.54.raw_ref.refs_0_, ...), custom_call_target="tpu_custom_call" | custom-call | flops 150994944 | tf_op jit(solution)/shard_map/pallas_call | solution.py:19
  9.5 0.0 collective-permute-done.raw_ref
  9.5 0.3 shard_map.40
  9.8 0.6 %shard_map.41.refs_0_ = f32[2,8,192,256]{3,2,1,0:T(8,128)S(1)} custom-call(bf16[8,192,256]{2,1,0:T(8,128)(2,1)S(1)} %get-tuple-element.62.refs_0_, bf16[1,8,192,256]{3,2,1,0:T(8,128)(2,1)S(1)} %bitcast.9, f32[8,8,256]{2,1,0:T(8,128)S(1)} %get-tuple-element.64.refs_2_.refs_3_, f32[8,8,256]{2,1,0:T(8,128)S(1)} %get-tuple-element.65.refs_3_), custom_call_target="tpu_custom_call" | custom-call | flops 150994944 | tf_op jit(solution)/shard_map/pallas_call | solution.py:19
  10.4 0.8 %shard_map.42.refs_8_.begun_ref = f32[2,256,512]{2,1,0:T(8,128)S(1)} custom-call(bf16[256,1536]{1,0:T(8,128)(2,1)S(1)} %get-tuple-element.60.own_ref.refs_6_, bf16[1,256,1536]{2,1,0:T(8,128)(2,1)S(1)} %bitcast.6, bf16[1152,512]{1,0:T(8,128)(2,1)S(1)} %get-tuple-element.66.right_ref), custom_call_target="tpu_custom_call" | custom-call | flops 402653184 | tf_op jit(solution)/shard_map/pallas_call | solution.py:19
  11.2 0.7 %collective-permute-done.2.refs_0_ = bf16[2,16,3,2,256]{4,3,2,1,0:T(2,128)(2,1)S(1)} collective-permute-done((bf16[2,16,3,2,256]{4,3,2,1,0:T(2,128)(2,1)S(1)}, bf16[2,16,3,2,256]{4,3,2,1,0:T(2,128)(2,1)S(1)}, u32[]{:S(2)}, u32[]{:S(2)}) %collective-permute-start.2) | collective-permute-done | bytes 98336 | tf_op jit(solution)/shard_map/ppermute | solution.py:14
  11.9 0.0 collective-permute-done.3.refs_1_
  11.9 0.8 %shard_map.43 = (f32[2,2,64,256]{3,2,1,0:T(8,128)S(1)}, bf16[2,2,64,256]{3,2,1,0:T(8,128)(2,1)S(1)}, bf16[384,512]{1,0:T(8,128)(2,1)S(1)}) custom-call(bf16[2,16,3,2,256]{4,3,2,1,0:T(2,128)(2,1)S(1)} %collective-permute-done.2.refs_0_, bf16[2,19,3,2,256]{4,3,2,1,0:T(2,128)(2,1)S(1)} %collective-permute-done.3.refs_1_, ...), custom_call_target="tpu_custom_call" | custom-call | flops 402653184 | tf_op jit(solution)/shard_map/pallas_call | solution.py:19
  12.7 0.1 collective-permute-done.1.refs_1_
  12.8 0.1 collective-permute-start.4
  12.9 1.1 %collective-permute-start.7 = (bf16[2,2,64,256]{3,2,1,0:T(8,128)(2,1)S(1)}, bf16[2,2,64,256]{3,2,1,0:T(8,128)(2,1)S(1)}, u32[]{:S(2)}, u32[]{:S(2)}) collective-permute-start(bf16[2,2,64,256]{3,2,1,0:T(8,128)(2,1)S(1)} %get-tuple-element.87), channel_id=1, source_target_pairs={{0,4},{1,3},{2,6},{3,1},{4,0},{5,7},{6,2},{7,5},{8,12},{9,11},{10,... | collective-permute-start | bytes 393224 | tf_op jit(solution)/shard_map/ppermute | solution.py:410
  14.0 0.2 collective-permute-done.4
  14.2 0.6 %shard_map.44.lefts_ref = bf16[2,256,1536]{2,1,0:T(8,128)(2,1)S(1)} custom-call(f32[2,8,192,256]{3,2,1,0:T(8,128)S(1)} %shard_map.41.refs_0_, bf16[8,32,256]{2,1,0:T(8,128)(2,1)S(1)} %collective-permute-done.1.refs_1_, bf16[1,8,24,256]{3,2,1,0:T(8,128)(2,1)S(1)} %bitcast.10, f32[8,8,256]{2,1,0:T(8,128)S(1)} %get-tuple-element.64.refs_2_.refs_3_), custom_call_target="tpu_custom_call" | custom-call | flops 150994944 | tf_op jit(solution)/shard_map/pallas_call | solution.py:19
  14.8 0.7 %shard_map.45 = (f32[2,2,64,256]{3,2,1,0:T(8,128)S(1)}, bf16[2,2,64,256]{3,2,1,0:T(8,128)(2,1)S(1)}) custom-call(bf16[2,256,1536]{2,1,0:T(8,128)(2,1)S(1)} %shard_map.44.lefts_ref, bf16[1152,512]{1,0:T(8,128)(2,1)S(1)} %get-tuple-element.66.right_ref, bf16[384,512]{1,0:T(8,128)(2,1)S(1)} %get-tuple-element.80.edge_ref.right_ref), custom_call_target="tpu_custom_call" | custom-call | flops 3221225472 | tf_op jit(solution)/shard_map/pallas_call | solution.py:19
  15.5 1.1 %collective-permute-start.6 = (bf16[2,2,64,256]{3,2,1,0:T(8,128)(2,1)S(1)}, bf16[2,2,64,256]{3,2,1,0:T(8,128)(2,1)S(1)}, u32[]{:S(2)}, u32[]{:S(2)}) collective-permute-start(bf16[2,2,64,256]{3,2,1,0:T(8,128)(2,1)S(1)} %get-tuple-element.85), channel_id=1, source_target_pairs={{0,4},{1,3},{2,6},{3,1},{4,0},{5,7},{6,2},{7,5},{8,12},{9,11},{10,... | collective-permute-start | bytes 393224 | tf_op jit(solution)/shard_map/ppermute | solution.py:410
  16.6 0.4 %shard_map.46 = (f32[2,2,64,256]{3,2,1,0:T(8,128)S(1)}, bf16[2,2,64,256]{3,2,1,0:T(8,128)(2,1)S(1)}) custom-call(bf16[256,1536]{1,0:T(8,128)(2,1)S(1)} %get-tuple-element.60.own_ref.refs_6_, bf16[1,256,1536]{2,1,0:T(8,128)(2,1)S(1)} %bitcast.8, f32[2,256,512]{2,1,0:T(8,128)S(1)} %shard_map.42.refs_8_.begun_ref, ...), custom_call_target="tpu_custom_call" | custom-call | tf_op jit(solution)/shard_map/pallas_call | solution.py:19
  16.9 0.7 %shard_map.47 = (f32[2,2,64,256]{3,2,1,0:T(8,128)S(1)}, bf16[4,2,64,256]{3,2,1,0:T(8,128)(2,1)S(1)}) custom-call(bf16[2,256,1536]{2,1,0:T(8,128)(2,1)S(1)} %shard_map.44.lefts_ref, bf16[1152,512]{1,0:T(8,128)(2,1)S(1)} %get-tuple-element.66.right_ref, bf16[384,512]{1,0:T(8,128)(2,1)S(1)} %get-tuple-element.80.edge_ref.right_ref, ...), custom_call_target="tpu_custom_call" | custom-call | tf_op jit(solution)/shard_map/pallas_call | solution.py:19
  17.6 1.1 %collective-permute-start.5 = (bf16[4,2,64,256]{3,2,1,0:T(8,128)(2,1)S(1)}, bf16[4,2,64,256]{3,2,1,0:T(8,128)(2,1)S(1)}, u32[]{:S(2)}, u32[]{:S(2)}) collective-permute-start(bf16[4,2,64,256]{3,2,1,0:T(8,128)(2,1)S(1)} %get-tuple-element.83), channel_id=1, source_target_pairs={{0,4},{1,3},{2,6},{3,1},{4,0},{5,7},{6,2},{7,5},{8,12},{9,11},{10,... | collective-permute-start | bytes 786440 | tf_op jit(solution)/shard_map/ppermute | solution.py:410
  18.7 0.0 collective-permute-done.7.refs_1_
  18.8 1.5 %collective-permute-start.9 = (bf16[2,1,64,256]{3,2,1,0:T(8,128)(2,1)S(1)}, bf16[2,1,64,256]{3,2,1,0:T(8,128)(2,1)S(1)}, u32[]{:S(2)}, u32[]{:S(2)}) collective-permute-start(bf16[2,1,64,256]{3,2,1,0:T(8,128)(2,1)S(1)} %get-tuple-element.94), channel_id=1, source_target_pairs={{0,2},{1,5},{2,0},{3,7},{4,6},{5,1},{6,4},{7,3},{8,10},{9,13},{10,... | collective-permute-start | bytes 196616 | tf_op jit(solution)/shard_map/ppermute | solution.py:410
  20.3 0.2 collective-permute-done.6.refs_1_
  20.6 1.5 %collective-permute-start.8 = (bf16[2,1,64,256]{3,2,1,0:T(8,128)(2,1)S(1)}, bf16[2,1,64,256]{3,2,1,0:T(8,128)(2,1)S(1)}, u32[]{:S(2)}, u32[]{:S(2)}) collective-permute-start(bf16[2,1,64,256]{3,2,1,0:T(8,128)(2,1)S(1)} %get-tuple-element.93), channel_id=1, source_target_pairs={{0,2},{1,5},{2,0},{3,7},{4,6},{5,1},{6,4},{7,3},{8,10},{9,13},{10,... | collective-permute-start | bytes 196616 | tf_op jit(solution)/shard_map/ppermute | solution.py:410
  22.1 1.7 %collective-permute-done.9.came_ref = bf16[2,1,64,256]{3,2,1,0:T(8,128)(2,1)S(1)} collective-permute-done((bf16[2,1,64,256]{3,2,1,0:T(8,128)(2,1)S(1)}, bf16[2,1,64,256]{3,2,1,0:T(8,128)(2,1)S(1)}, u32[]{:S(2)}, u32[]{:S(2)}) %collective-permute-start.9) | collective-permute-done | bytes 65568 | tf_op jit(solution)/shard_map/ppermute | solution.py:410
  23.9 1.5 %collective-permute-start.12 = (bf16[2,1,64,256]{3,2,1,0:T(8,128)(2,1)S(1)}, bf16[2,1,64,256]{3,2,1,0:T(8,128)(2,1)S(1)}, u32[]{:S(2)}, u32[]{:S(2)}) collective-permute-start(bf16[2,1,64,256]{3,2,1,0:T(8,128)(2,1)S(1)} %shard_map.50), channel_id=1, source_target_pairs={{0,8},{1,9},{2,10},{3,11},{4,12},{5,13},{6,14},{7,15},{8,0},{9,1},... | collective-permute-start | bytes 196616 | tf_op jit(solution)/shard_map/ppermute | solution.py:410
  25.4 0.0 collective-permute-done.8.came_ref
  25.4 1.5 %collective-permute-start.11 = (bf16[2,1,64,256]{3,2,1,0:T(8,128)(2,1)S(1)}, bf16[2,1,64,256]{3,2,1,0:T(8,128)(2,1)S(1)}, u32[]{:S(2)}, u32[]{:S(2)}) collective-permute-start(bf16[2,1,64,256]{3,2,1,0:T(8,128)(2,1)S(1)} %shard_map.51), channel_id=1, source_target_pairs={{0,8},{1,9},{2,10},{3,11},{4,12},{5,13},{6,14},{7,15},{8,0},{9,1},... | collective-permute-start | bytes 196616 | tf_op jit(solution)/shard_map/ppermute | solution.py:410
  27.0 0.0 collective-permute-done.5.refs_1_.refs_3_
  27.0 0.1 shard_map.52
  27.0 1.2 %collective-permute-start.10 = (bf16[4,1,64,256]{3,2,1,0:T(8,128)(2,1)S(1)}, bf16[4,1,64,256]{3,2,1,0:T(8,128)(2,1)S(1)}, u32[]{:S(2)}, u32[]{:S(2)}) collective-permute-start(bf16[4,1,64,256]{3,2,1,0:T(8,128)(2,1)S(1)} %get-tuple-element.98), channel_id=1, source_target_pairs={{0,2},{1,5},{2,0},{3,7},{4,6},{5,1},{6,4},{7,3},{8,10},{9,13},{10,... | collective-permute-start | bytes 393224 | tf_op jit(solution)/shard_map/ppermute | solution.py:410
  28.2 2.6 %collective-permute-done.12.refs_1_ = bf16[2,1,64,256]{3,2,1,0:T(8,128)(2,1)S(1)} collective-permute-done((bf16[2,1,64,256]{3,2,1,0:T(8,128)(2,1)S(1)}, bf16[2,1,64,256]{3,2,1,0:T(8,128)(2,1)S(1)}, u32[]{:S(2)}, u32[]{:S(2)}) %collective-permute-start.12) | collective-permute-done | bytes 65568 | tf_op jit(solution)/shard_map/ppermute | solution.py:410
  30.8 1.4 %collective-permute-done.11.refs_1_ = bf16[2,1,64,256]{3,2,1,0:T(8,128)(2,1)S(1)} collective-permute-done((bf16[2,1,64,256]{3,2,1,0:T(8,128)(2,1)S(1)}, bf16[2,1,64,256]{3,2,1,0:T(8,128)(2,1)S(1)}, u32[]{:S(2)}, u32[]{:S(2)}) %collective-permute-start.11) | collective-permute-done | bytes 65568 | tf_op jit(solution)/shard_map/ppermute | solution.py:410
  32.2 0.0 collective-permute-done.10.came_ref
  32.2 0.7 %shard_map.55 = f32[2,2,64,256]{3,2,1,0:T(8,128)} custom-call(bf16[4,1,64,256]{3,2,1,0:T(8,128)(2,1)S(1)} %collective-permute-done.10.came_ref, f32[2,1,64,256]{3,2,1,0:T(8,128)S(1)} %shard_map.53.refs_0_, f32[2,1,64,256]{3,2,1,0:T(8,128)S(1)} %shard_map.54.refs_1_), custom_call_target="tpu_custom_call" | custom-call | tf_op jit(solution)/shard_map/pallas_call | solution.py:19
  (7 shorter events, 0.1 us)
Async XLA Ops:
  0.0 9.5 %collective-permute-start = (bf16[2,8,16,3,2,256]{5,4,3,2,1,0:T(2,128)(2,1)}, bf16[2,8,16,3,2,256]{5,4,3,2,1,0:T(2,128)(2,1)S(1)}, u32[]{:S(2)}, u32[]{:S(2)}) collective-permute-start(bf16[2,8,16,3,2,256]{5,4,3,2,1,0:T(2,128)(2,1)} %bitcast.11), channel_id=1, source_target_pairs={{1,0},{0,1},{3,2},{2,3},{5,4},{4,5},{7,6},{6,7},{9,8},{8,9},{11,10... | collective-permute-start | bytes 2359304 | tf_op jit(solution)/shard_map/ppermute | solution.py:14
  1.8 10.1 %collective-permute-start.3 = (bf16[2,19,3,2,256]{4,3,2,1,0:T(2,128)(2,1)S(1)}, bf16[2,19,3,2,256]{4,3,2,1,0:T(2,128)(2,1)S(1)}, u32[]{:S(2)}, u32[]{:S(2)}) collective-permute-start(bf16[2,19,3,2,256]{4,3,2,1,0:T(2,128)(2,1)S(1)} %get-tuple-element.70), channel_id=1, source_target_pairs={{12,0},{0,4},{4,8},{8,12},{13,1},{1,5},{5,9},{9,13},{14,2},{2,6},{... | collective-permute-start | bytes 350216 | tf_op jit(solution)/shard_map/ppermute | solution.py:14
  4.4 7.4 %collective-permute-start.2 = (bf16[2,16,3,2,256]{4,3,2,1,0:T(2,128)(2,1)S(1)}, bf16[2,16,3,2,256]{4,3,2,1,0:T(2,128)(2,1)S(1)}, u32[]{:S(2)}, u32[]{:S(2)}) collective-permute-start(bf16[2,16,3,2,256]{4,3,2,1,0:T(2,128)(2,1)S(1)} %get-tuple-element.69), channel_id=1, source_target_pairs={{4,0},{8,4},{12,8},{0,12},{5,1},{9,5},{13,9},{1,13},{6,2},{10,6},{... | collective-permute-start | bytes 294920 | tf_op jit(solution)/shard_map/ppermute | solution.py:14
  7.1 5.7 %collective-permute-start.1 = (bf16[8,32,256]{2,1,0:T(8,128)(2,1)S(1)}, bf16[8,32,256]{2,1,0:T(8,128)(2,1)S(1)}, u32[]{:S(2)}, u32[]{:S(2)}) collective-permute-start(bf16[8,32,256]{2,1,0:T(8,128)(2,1)S(1)} %get-tuple-element.68), channel_id=1, source_target_pairs={{2,0},{0,2},{3,1},{1,3},{6,4},{4,6},{7,5},{5,7},{10,8},{8,10},{11,... | collective-permute-start | bytes 393224 | tf_op jit(solution)/shard_map/ppermute | solution.py:14
  12.8 1.4 %collective-permute-start.4 = (bf16[8,24,256]{2,1,0:T(8,128)(2,1)S(1)}, bf16[8,24,256]{2,1,0:T(8,128)(2,1)S(1)}, u32[]{:S(2)}, u32[]{:S(2)}) collective-permute-start(bf16[8,24,256]{2,1,0:T(8,128)(2,1)S(1)} %slice.3), channel_id=1, source_target_pairs={{1,0},{0,1},{3,2},{2,3},{5,4},{4,5},{7,6},{6,7},{9,8},{8,9},{11,10... | collective-permute-start | bytes 294920 | tf_op jit(solution)/shard_map/ppermute | solution.py:14
  12.9 5.9 %collective-permute-start.7 = (bf16[2,2,64,256]{3,2,1,0:T(8,128)(2,1)S(1)}, bf16[2,2,64,256]{3,2,1,0:T(8,128)(2,1)S(1)}, u32[]{:S(2)}, u32[]{:S(2)}) collective-permute-start(bf16[2,2,64,256]{3,2,1,0:T(8,128)(2,1)S(1)} %get-tuple-element.87), channel_id=1, source_target_pairs={{0,4},{1,3},{2,6},{3,1},{4,0},{5,7},{6,2},{7,5},{8,12},{9,11},{10,... | collective-permute-start | bytes 393224 | tf_op jit(solution)/shard_map/ppermute | solution.py:410
  15.5 5.0 %collective-permute-start.6 = (bf16[2,2,64,256]{3,2,1,0:T(8,128)(2,1)S(1)}, bf16[2,2,64,256]{3,2,1,0:T(8,128)(2,1)S(1)}, u32[]{:S(2)}, u32[]{:S(2)}) collective-permute-start(bf16[2,2,64,256]{3,2,1,0:T(8,128)(2,1)S(1)} %get-tuple-element.85), channel_id=1, source_target_pairs={{0,4},{1,3},{2,6},{3,1},{4,0},{5,7},{6,2},{7,5},{8,12},{9,11},{10,... | collective-permute-start | bytes 393224 | tf_op jit(solution)/shard_map/ppermute | solution.py:410
  17.6 9.3 %collective-permute-start.5 = (bf16[4,2,64,256]{3,2,1,0:T(8,128)(2,1)S(1)}, bf16[4,2,64,256]{3,2,1,0:T(8,128)(2,1)S(1)}, u32[]{:S(2)}, u32[]{:S(2)}) collective-permute-start(bf16[4,2,64,256]{3,2,1,0:T(8,128)(2,1)S(1)} %get-tuple-element.83), channel_id=1, source_target_pairs={{0,4},{1,3},{2,6},{3,1},{4,0},{5,7},{6,2},{7,5},{8,12},{9,11},{10,... | collective-permute-start | bytes 786440 | tf_op jit(solution)/shard_map/ppermute | solution.py:410
  18.8 5.1 %collective-permute-start.9 = (bf16[2,1,64,256]{3,2,1,0:T(8,128)(2,1)S(1)}, bf16[2,1,64,256]{3,2,1,0:T(8,128)(2,1)S(1)}, u32[]{:S(2)}, u32[]{:S(2)}) collective-permute-start(bf16[2,1,64,256]{3,2,1,0:T(8,128)(2,1)S(1)} %get-tuple-element.94), channel_id=1, source_target_pairs={{0,2},{1,5},{2,0},{3,7},{4,6},{5,1},{6,4},{7,3},{8,10},{9,13},{10,... | collective-permute-start | bytes 196616 | tf_op jit(solution)/shard_map/ppermute | solution.py:410
  20.6 4.8 %collective-permute-start.8 = (bf16[2,1,64,256]{3,2,1,0:T(8,128)(2,1)S(1)}, bf16[2,1,64,256]{3,2,1,0:T(8,128)(2,1)S(1)}, u32[]{:S(2)}, u32[]{:S(2)}) collective-permute-start(bf16[2,1,64,256]{3,2,1,0:T(8,128)(2,1)S(1)} %get-tuple-element.93), channel_id=1, source_target_pairs={{0,2},{1,5},{2,0},{3,7},{4,6},{5,1},{6,4},{7,3},{8,10},{9,13},{10,... | collective-permute-start | bytes 196616 | tf_op jit(solution)/shard_map/ppermute | solution.py:410
  23.9 6.9 %collective-permute-start.12 = (bf16[2,1,64,256]{3,2,1,0:T(8,128)(2,1)S(1)}, bf16[2,1,64,256]{3,2,1,0:T(8,128)(2,1)S(1)}, u32[]{:S(2)}, u32[]{:S(2)}) collective-permute-start(bf16[2,1,64,256]{3,2,1,0:T(8,128)(2,1)S(1)} %shard_map.50), channel_id=1, source_target_pairs={{0,8},{1,9},{2,10},{3,11},{4,12},{5,13},{6,14},{7,15},{8,0},{9,1},... | collective-permute-start | bytes 196616 | tf_op jit(solution)/shard_map/ppermute | solution.py:410
  25.4 6.8 %collective-permute-start.11 = (bf16[2,1,64,256]{3,2,1,0:T(8,128)(2,1)S(1)}, bf16[2,1,64,256]{3,2,1,0:T(8,128)(2,1)S(1)}, u32[]{:S(2)}, u32[]{:S(2)}) collective-permute-start(bf16[2,1,64,256]{3,2,1,0:T(8,128)(2,1)S(1)} %shard_map.51), channel_id=1, source_target_pairs={{0,8},{1,9},{2,10},{3,11},{4,12},{5,13},{6,14},{7,15},{8,0},{9,1},... | collective-permute-start | bytes 196616 | tf_op jit(solution)/shard_map/ppermute | solution.py:410
  27.0 5.2 %collective-permute-start.10 = (bf16[4,1,64,256]{3,2,1,0:T(8,128)(2,1)S(1)}, bf16[4,1,64,256]{3,2,1,0:T(8,128)(2,1)S(1)}, u32[]{:S(2)}, u32[]{:S(2)}) collective-permute-start(bf16[4,1,64,256]{3,2,1,0:T(8,128)(2,1)S(1)} %get-tuple-element.98), channel_id=1, source_target_pairs={{0,2},{1,5},{2,0},{3,7},{4,6},{5,1},{6,4},{7,3},{8,10},{9,13},{10,... | collective-permute-start | bytes 393224 | tf_op jit(solution)/shard_map/ppermute | solution.py:410

commit v20 on v19

--- a/solution.py
+++ b/solution.py
@@ -140,11 +140,13 @@
 
 def edges_kernel(
     raw_hbm, links_x_hbm, links_y_hbm,
-    first_ref, last_ref, raw_ref, links_x_ref, links_y_ref, maps_ref, past_maps_ref, arrived,
+    first_ref, last_ref, rows_y_ref, links_x_ref, links_y_ref, maps_ref, past_maps_ref, arrived,
 ):
     parts, planes, ys, colours, zs, _ = raw_hbm.shape
-    sources = (raw_hbm.at[:, planes - 1], raw_hbm.at[:, 0], links_x_hbm, links_y_hbm, raw_hbm)
-    targets = (last_ref.at[:, :ys], first_ref, links_x_ref, links_y_ref, raw_ref)
+    sources = (raw_hbm.at[:, planes - 1], raw_hbm.at[:, 0], links_x_hbm, links_y_hbm) + tuple(
+        raw_hbm.at[:, :, y] for y in (0, ys - 1)
+    )
+    targets = (last_ref.at[:, :ys], first_ref, links_x_ref, links_y_ref, rows_y_ref.at[0], rows_y_ref.at[1])
     copies = [
         pltpu.make_async_copy(source, target, arrived.at[i])
         for i, (source, target) in enumerate(zip(sources, targets))
@@ -172,9 +174,10 @@
 
 
 def prepare_kernel(
-    raw_ref, links_x_ref, links_y_ref, maps_ref, ends_ref, ahead_x_ref, back_x_ref, ahead_y_ref, back_y_ref
+    rows_y_ref, links_x_ref, links_y_ref, maps_ref, ends_ref, ahead_x_ref, back_x_ref, ahead_y_ref, back_y_ref
 ):
-    parts, planes, ys, colours, zs, width = raw_ref.shape
+    _, parts, planes, colours, zs, width = rows_y_ref.shape
+    ys = links_x_ref.shape[5]
     lanes = ahead_y_ref.shape[2]
     ahead_x, ahead_y, back_x, back_y = coefficients(
         links_x_ref[...].reshape(-1, ys), links_y_ref[...].reshape(-1, ys), maps_ref, planes
@@ -187,7 +190,9 @@
     spare = ends_ref.shape[1] - 2 * parts * colours * zs - 8
     for x in range(planes):
         pieces = [
-            raw_ref[p, x, y].astype(jnp.float32).reshape(colours * zs, width) for y in (0, ys - 1) for p in range(parts)
+            rows_y_ref[side, p, x].astype(jnp.float32).reshape(colours * zs, width)
+            for side in range(2)
+            for p in range(parts)
         ]
         pieces.append(jnp.concatenate([back_y[x, :, lanes - 128 :], filler], axis=1))
         if spare:
@@ -225,8 +230,12 @@
 
 
 def inner_kernel(
-    sites, raw_ref, ahead_ref, back_ref, rows_ref, right_ref, turned_ref, matrix_ref, ahead_part_ref, back_part_ref
+    sites, raw_hbm, ahead_ref, back_ref, rows_ref, right_ref, turned_ref, matrix_ref, ahead_part_ref, back_part_ref,
+    raw_ref, arrived,
 ):
+    copy = pltpu.make_async_copy(raw_hbm, raw_ref, arrived)
+    copy.start()
+    copy.wait()
     planes, depth, width = rows_ref.shape
     for x in range(planes):
         rows_ref[place_of(x, planes)] = plane_rows(raw_ref.at[:, x], raw_ref.shape[2])
@@ -483,13 +492,14 @@
         edges_kernel,
         (
             shape(parts, ys, colours, zs, width), shape(parts, ys + colours, colours, zs, width),
-            *(shape(*a.shape) for a in inputs),
+            shape(2, parts, planes, colours, zs, width),
+            *(shape(*a.shape) for a in inputs[1:]),
             shape(map_rows(parts, colours, planes, ys, zs)[-1], 2 * lanes, dtype=f32),
             shape(map_rows(parts, colours, 1, ys, zs)[-1], 2 * lanes, dtype=f32),
         ),
         0,
         inputs,
-        [pltpu.SemaphoreType.DMA((5,))],
+        [pltpu.SemaphoreType.DMA((6,))],
         [pltpu.HBM] * len(inputs),
     )
     low = shifted(last_plane, "gx", 1)
@@ -530,7 +540,9 @@
             shape(depth, width, dtype=f32), shape(depth, width, dtype=f32),
         ),
         2 * step_flops,
-        [inputs[0], ahead_x, back_x],
+        [raw, ahead_x, back_x],
+        [pltpu.VMEM(raw.shape, bf16), pltpu.SemaphoreType.DMA],
+        [pltpu.HBM, pltpu.VMEM, pltpu.VMEM],
     )
     turned = [call(turn_kernel, (field_shape, turned_shape), step_flops // 4, [r]) for r in raw_others]
     fields = jnp.stack([t[0] for t in turned])

time: 33.1 us -> 33 us (level)
  starting transfers between devices: 17.5 us -> 16.3 us
  Pallas kernels: 8.35 us -> 9.15 us
    ppermute x8, starting transfers between devices: 10.5 us -> 9.33 us  [exchange(): return lax.ppermute(block, axes, route)]
    pallas_call x19, Pallas kernels: 8.35 us -> 9.15 us  [call(): pl.pallas_call(body, out_shape=out_shape, in_specs=[pl.BlockSpec(memory_s...]
    ppermute x8, waiting for transfers between devices: 5.93 us -> 6.66 us  [exchange(): return lax.ppermute(block, axes, route)]
    ppermute x5, waiting for transfers between devices: 1.03 us -> 0.56 us  [shifted(): return lax.ppermute(block, axis, route)]
  transfers between devices with their start and end apart: 13 -> 13, of which waited for: 7 -> 6; matrix products, arithmetic and copies ran while one was open for 0% -> 0% of each run, Pallas kernels for 23% -> 26%
where the time goes in v20:
time: 33 us; the launch traced here: 32.8 us
  starting transfers between devices  16.3 us (49%)
  Pallas kernels  9.15 us (28%)
  waiting for transfers between devices  7.22 us (22%)
    ppermute x8, starting transfers between devices, exchange(): return lax.ppermute(block, axes, route)  9.33 us
    pallas_call x19, Pallas kernels, call(): pl.pallas_call(body, out_shape=out_shape, in_specs=[pl.BlockSpec(memory_s...  9.15 us
    ppermute x5, starting transfers between devices, shifted(): return lax.ppermute(block, axis, route)  6.96 us
    ppermute x8, waiting for transfers between devices, exchange(): return lax.ppermute(block, axes, route)  6.66 us
  transfers between devices with their start and end apart: 13, of which 6 were waited for; matrix products, arithmetic and copies ran while one was open for 0% of the time, Pallas kernels for 26%

profile of v20, /device:TPU:0, one launch (start us, length us, event | category | flops | bytes accessed | tf_op | source)
XLA Modules:
  0.0 32.8 jit_solution(1365078884179700265)
XLA Ops:
  0.0 0.5 %collective-permute-start = (bf16[2,8,16,3,2,256]{5,4,3,2,1,0:T(2,128)(2,1)}, bf16[2,8,16,3,2,256]{5,4,3,2,1,0:T(2,128)(2,1)S(1)}, u32[]{:S(2)}, u32[]{:S(2)}) collective-permute-start(bf16[2,8,16,3,2,256]{5,4,3,2,1,0:T(2,128)(2,1)} %bitcast.11), channel_id=1, source_target_pairs={{1,0},{0,1},{3,2},{2,3},{5,4},{4,5},{7,6},{6,7},{9,8},{8,9},{11,10... | collective-permute-start | bytes 2359304 | tf_op jit(solution)/shard_map/ppermute | solution.py:14
  0.5 1.1 %shard_map.37 = (bf16[2,16,3,2,256]{4,3,2,1,0:T(2,128)(2,1)S(1)}, bf16[2,19,3,2,256]{4,3,2,1,0:T(2,128)(2,1)S(1)}, bf16[2,2,8,3,2,256]{5,4,3,2,1,0:T(2,128)(2,1)...) custom-call(bf16[2,8,16,3,2,256]{5,4,3,2,1,0:T(2,128)(2,1)} %bitcast, ...), custom_call_target="tpu_custom_call" | custom-call | tf_op jit(solution)/shard_map/pallas_call | solution.py:19
  1.5 2.6 %collective-permute-start.3 = (bf16[2,19,3,2,256]{4,3,2,1,0:T(2,128)(2,1)S(1)}, bf16[2,19,3,2,256]{4,3,2,1,0:T(2,128)(2,1)S(1)}, u32[]{:S(2)}, u32[]{:S(2)}) collective-permute-start(bf16[2,19,3,2,256]{4,3,2,1,0:T(2,128)(2,1)S(1)} %get-tuple-element.70), channel_id=1, source_target_pairs={{12,0},{0,4},{4,8},{8,12},{13,1},{1,5},{5,9},{9,13},{14,2},{2,6},{... | collective-permute-start | bytes 350216 | tf_op jit(solution)/shard_map/ppermute | solution.py:14
  4.2 2.1 %collective-permute-start.2 = (bf16[2,16,3,2,256]{4,3,2,1,0:T(2,128)(2,1)S(1)}, bf16[2,16,3,2,256]{4,3,2,1,0:T(2,128)(2,1)S(1)}, u32[]{:S(2)}, u32[]{:S(2)}) collective-permute-start(bf16[2,16,3,2,256]{4,3,2,1,0:T(2,128)(2,1)S(1)} %get-tuple-element.69), channel_id=1, source_target_pairs={{4,0},{8,4},{12,8},{0,12},{5,1},{9,5},{13,9},{1,13},{6,2},{10,6},{... | collective-permute-start | bytes 294920 | tf_op jit(solution)/shard_map/ppermute | solution.py:14
  6.3 0.6 %shard_map.38 = (bf16[8,32,256]{2,1,0:T(8,128)(2,1)S(1)}, f32[8,8,256]{2,1,0:T(8,128)S(1)}, f32[8,8,256]{2,1,0:T(8,128)S(1)}, f32[8,8,256]{2,1,0:T(8,128)S(1)}, f32[8,8,256]{2,1,0:T(8,128)S(1)}) custom-call(bf16[2,2,8,3,2,256]{5,4,3,2,1,0:T(2,128)(2,1)S(1)} %get-tuple-element.54.rows_y_ref, bf16[2,3,3,8,2,16]{5,4,3,2,1,0:T(2,128)(2,1)S(1)} %get-tuple-element.55.links_x_ref, ...), custom_call_target="tpu_custom_call" | custom-call | tf_op jit(solution)/shard_map/pallas_call | solution.py:19
  6.8 1.7 %collective-permute-start.1 = (bf16[8,32,256]{2,1,0:T(8,128)(2,1)S(1)}, bf16[8,32,256]{2,1,0:T(8,128)(2,1)S(1)}, u32[]{:S(2)}, u32[]{:S(2)}) collective-permute-start(bf16[8,32,256]{2,1,0:T(8,128)(2,1)S(1)} %get-tuple-element.68), channel_id=1, source_target_pairs={{2,0},{0,2},{3,1},{1,3},{6,4},{4,6},{7,5},{5,7},{10,8},{8,10},{11,... | collective-permute-start | bytes 393224 | tf_op jit(solution)/shard_map/ppermute | solution.py:14
  8.5 1.8 %shard_map.39 = (bf16[8,192,256]{2,1,0:T(8,128)(2,1)S(1)}, bf16[1152,512]{1,0:T(8,128)(2,1)S(1)}, bf16[256,1536]{1,0:T(8,128)(2,1)S(1)}, bf16[192,192]{1,0:T(8,1...) custom-call(bf16[2,8,16,3,2,256]{5,4,3,2,1,0:T(2,128)(2,1)} %bitcast.13, ...), custom_call_target="tpu_custom_call" | custom-call | flops 150994944 | tf_op jit(solution)/shard_map/pallas_call | solution.py:19
  10.3 0.0 collective-permute-done.raw_ref
  10.3 0.3 shard_map.40
  10.6 0.6 %shard_map.41.refs_0_ = f32[2,8,192,256]{3,2,1,0:T(8,128)S(1)} custom-call(bf16[8,192,256]{2,1,0:T(8,128)(2,1)S(1)} %get-tuple-element.62.refs_0_, bf16[1,8,192,256]{3,2,1,0:T(8,128)(2,1)S(1)} %bitcast.9, f32[8,8,256]{2,1,0:T(8,128)S(1)} %get-tuple-element.64.refs_2_.refs_3_, f32[8,8,256]{2,1,0:T(8,128)S(1)} %get-tuple-element.65.refs_3_), custom_call_target="tpu_custom_call" | custom-call | flops 150994944 | tf_op jit(solution)/shard_map/pallas_call | solution.py:19
  11.2 0.8 %shard_map.42.refs_8_.begun_ref = f32[2,256,512]{2,1,0:T(8,128)S(1)} custom-call(bf16[256,1536]{1,0:T(8,128)(2,1)S(1)} %get-tuple-element.60.own_ref.refs_6_, bf16[1,256,1536]{2,1,0:T(8,128)(2,1)S(1)} %bitcast.6, bf16[1152,512]{1,0:T(8,128)(2,1)S(1)} %get-tuple-element.66.right_ref), custom_call_target="tpu_custom_call" | custom-call | flops 402653184 | tf_op jit(solution)/shard_map/pallas_call | solution.py:19
  12.0 0.0 collective-permute-done.2.refs_0_
  12.0 0.0 collective-permute-done.3.refs_1_
  12.0 0.8 %shard_map.43 = (f32[2,2,64,256]{3,2,1,0:T(8,128)S(1)}, bf16[2,2,64,256]{3,2,1,0:T(8,128)(2,1)S(1)}, bf16[384,512]{1,0:T(8,128)(2,1)S(1)}) custom-call(bf16[2,16,3,2,256]{4,3,2,1,0:T(2,128)(2,1)S(1)} %collective-permute-done.2.refs_0_, bf16[2,19,3,2,256]{4,3,2,1,0:T(2,128)(2,1)S(1)} %collective-permute-done.3.refs_1_, ...), custom_call_target="tpu_custom_call" | custom-call | flops 402653184 | tf_op jit(solution)/shard_map/pallas_call | solution.py:19
  12.8 0.0 collective-permute-done.1.refs_1_
  12.8 0.1 collective-permute-start.4
  12.9 0.7 %collective-permute-start.7 = (bf16[2,2,64,256]{3,2,1,0:T(8,128)(2,1)S(1)}, bf16[2,2,64,256]{3,2,1,0:T(8,128)(2,1)S(1)}, u32[]{:S(2)}, u32[]{:S(2)}) collective-permute-start(bf16[2,2,64,256]{3,2,1,0:T(8,128)(2,1)S(1)} %get-tuple-element.87), channel_id=1, source_target_pairs={{0,4},{1,3},{2,6},{3,1},{4,0},{5,7},{6,2},{7,5},{8,12},{9,11},{10,... | collective-permute-start | bytes 393224 | tf_op jit(solution)/shard_map/ppermute | solution.py:419
  13.7 0.5 %collective-permute-done.4 = bf16[8,24,256]{2,1,0:T(8,128)(2,1)S(1)} collective-permute-done((bf16[8,24,256]{2,1,0:T(8,128)(2,1)S(1)}, bf16[8,24,256]{2,1,0:T(8,128)(2,1)S(1)}, u32[]{:S(2)}, u32[]{:S(2)}) %collective-permute-start.4) | collective-permute-done | bytes 98336 | tf_op jit(solution)/shard_map/ppermute | solution.py:14
  14.2 0.6 %shard_map.44.lefts_ref = bf16[2,256,1536]{2,1,0:T(8,128)(2,1)S(1)} custom-call(f32[2,8,192,256]{3,2,1,0:T(8,128)S(1)} %shard_map.41.refs_0_, bf16[8,32,256]{2,1,0:T(8,128)(2,1)S(1)} %collective-permute-done.1.refs_1_, bf16[1,8,24,256]{3,2,1,0:T(8,128)(2,1)S(1)} %bitcast.10, f32[8,8,256]{2,1,0:T(8,128)S(1)} %get-tuple-element.64.refs_2_.refs_3_), custom_call_target="tpu_custom_call" | custom-call | flops 150994944 | tf_op jit(solution)/shard_map/pallas_call | solution.py:19
  14.9 0.7 %shard_map.45 = (f32[2,2,64,256]{3,2,1,0:T(8,128)S(1)}, bf16[2,2,64,256]{3,2,1,0:T(8,128)(2,1)S(1)}) custom-call(bf16[2,256,1536]{2,1,0:T(8,128)(2,1)S(1)} %shard_map.44.lefts_ref, bf16[1152,512]{1,0:T(8,128)(2,1)S(1)} %get-tuple-element.66.right_ref, bf16[384,512]{1,0:T(8,128)(2,1)S(1)} %get-tuple-element.80.edge_ref.right_ref), custom_call_target="tpu_custom_call" | custom-call | flops 3221225472 | tf_op jit(solution)/shard_map/pallas_call | solution.py:19
  15.6 0.9 %collective-permute-start.6 = (bf16[2,2,64,256]{3,2,1,0:T(8,128)(2,1)S(1)}, bf16[2,2,64,256]{3,2,1,0:T(8,128)(2,1)S(1)}, u32[]{:S(2)}, u32[]{:S(2)}) collective-permute-start(bf16[2,2,64,256]{3,2,1,0:T(8,128)(2,1)S(1)} %get-tuple-element.85), channel_id=1, source_target_pairs={{0,4},{1,3},{2,6},{3,1},{4,0},{5,7},{6,2},{7,5},{8,12},{9,11},{10,... | collective-permute-start | bytes 393224 | tf_op jit(solution)/shard_map/ppermute | solution.py:419
  16.4 0.4 %shard_map.46 = (f32[2,2,64,256]{3,2,1,0:T(8,128)S(1)}, bf16[2,2,64,256]{3,2,1,0:T(8,128)(2,1)S(1)}) custom-call(bf16[256,1536]{1,0:T(8,128)(2,1)S(1)} %get-tuple-element.60.own_ref.refs_6_, bf16[1,256,1536]{2,1,0:T(8,128)(2,1)S(1)} %bitcast.8, f32[2,256,512]{2,1,0:T(8,128)S(1)} %shard_map.42.refs_8_.begun_ref, ...), custom_call_target="tpu_custom_call" | custom-call | tf_op jit(solution)/shard_map/pallas_call | solution.py:19
  16.8 0.7 %shard_map.47 = (f32[2,2,64,256]{3,2,1,0:T(8,128)S(1)}, bf16[4,2,64,256]{3,2,1,0:T(8,128)(2,1)S(1)}) custom-call(bf16[2,256,1536]{2,1,0:T(8,128)(2,1)S(1)} %shard_map.44.lefts_ref, bf16[1152,512]{1,0:T(8,128)(2,1)S(1)} %get-tuple-element.66.right_ref, bf16[384,512]{1,0:T(8,128)(2,1)S(1)} %get-tuple-element.80.edge_ref.right_ref, ...), custom_call_target="tpu_custom_call" | custom-call | tf_op jit(solution)/shard_map/pallas_call | solution.py:19
  17.5 1.3 %collective-permute-start.5 = (bf16[4,2,64,256]{3,2,1,0:T(8,128)(2,1)S(1)}, bf16[4,2,64,256]{3,2,1,0:T(8,128)(2,1)S(1)}, u32[]{:S(2)}, u32[]{:S(2)}) collective-permute-start(bf16[4,2,64,256]{3,2,1,0:T(8,128)(2,1)S(1)} %get-tuple-element.83), channel_id=1, source_target_pairs={{0,4},{1,3},{2,6},{3,1},{4,0},{5,7},{6,2},{7,5},{8,12},{9,11},{10,... | collective-permute-start | bytes 786440 | tf_op jit(solution)/shard_map/ppermute | solution.py:419
  18.8 0.0 collective-permute-done.7.refs_1_
  18.8 1.2 %collective-permute-start.9 = (bf16[2,1,64,256]{3,2,1,0:T(8,128)(2,1)S(1)}, bf16[2,1,64,256]{3,2,1,0:T(8,128)(2,1)S(1)}, u32[]{:S(2)}, u32[]{:S(2)}) collective-permute-start(bf16[2,1,64,256]{3,2,1,0:T(8,128)(2,1)S(1)} %get-tuple-element.94), channel_id=1, source_target_pairs={{0,2},{1,5},{2,0},{3,7},{4,6},{5,1},{6,4},{7,3},{8,10},{9,13},{10,... | collective-permute-start | bytes 196616 | tf_op jit(solution)/shard_map/ppermute | solution.py:419
  20.0 0.5 %collective-permute-done.6.refs_1_ = bf16[2,2,64,256]{3,2,1,0:T(8,128)(2,1)S(1)} collective-permute-done((bf16[2,2,64,256]{3,2,1,0:T(8,128)(2,1)S(1)}, bf16[2,2,64,256]{3,2,1,0:T(8,128)(2,1)S(1)}, u32[]{:S(2)}, u32[]{:S(2)}) %collective-permute-start.6) | collective-permute-done | bytes 131104 | tf_op jit(solution)/shard_map/ppermute | solution.py:419
  20.6 1.2 %collective-permute-start.8 = (bf16[2,1,64,256]{3,2,1,0:T(8,128)(2,1)S(1)}, bf16[2,1,64,256]{3,2,1,0:T(8,128)(2,1)S(1)}, u32[]{:S(2)}, u32[]{:S(2)}) collective-permute-start(bf16[2,1,64,256]{3,2,1,0:T(8,128)(2,1)S(1)} %get-tuple-element.93), channel_id=1, source_target_pairs={{0,2},{1,5},{2,0},{3,7},{4,6},{5,1},{6,4},{7,3},{8,10},{9,13},{10,... | collective-permute-start | bytes 196616 | tf_op jit(solution)/shard_map/ppermute | solution.py:419
  21.9 2.0 %collective-permute-done.9.came_ref = bf16[2,1,64,256]{3,2,1,0:T(8,128)(2,1)S(1)} collective-permute-done((bf16[2,1,64,256]{3,2,1,0:T(8,128)(2,1)S(1)}, bf16[2,1,64,256]{3,2,1,0:T(8,128)(2,1)S(1)}, u32[]{:S(2)}, u32[]{:S(2)}) %collective-permute-start.9) | collective-permute-done | bytes 65568 | tf_op jit(solution)/shard_map/ppermute | solution.py:419
  23.9 1.2 %collective-permute-start.12 = (bf16[2,1,64,256]{3,2,1,0:T(8,128)(2,1)S(1)}, bf16[2,1,64,256]{3,2,1,0:T(8,128)(2,1)S(1)}, u32[]{:S(2)}, u32[]{:S(2)}) collective-permute-start(bf16[2,1,64,256]{3,2,1,0:T(8,128)(2,1)S(1)} %shard_map.50), channel_id=1, source_target_pairs={{0,8},{1,9},{2,10},{3,11},{4,12},{5,13},{6,14},{7,15},{8,0},{9,1},... | collective-permute-start | bytes 196616 | tf_op jit(solution)/shard_map/ppermute | solution.py:419
  25.1 0.0 collective-permute-done.8.came_ref
  25.2 1.8 %collective-permute-start.11 = (bf16[2,1,64,256]{3,2,1,0:T(8,128)(2,1)S(1)}, bf16[2,1,64,256]{3,2,1,0:T(8,128)(2,1)S(1)}, u32[]{:S(2)}, u32[]{:S(2)}) collective-permute-start(bf16[2,1,64,256]{3,2,1,0:T(8,128)(2,1)S(1)} %shard_map.51), channel_id=1, source_target_pairs={{0,8},{1,9},{2,10},{3,11},{4,12},{5,13},{6,14},{7,15},{8,0},{9,1},... | collective-permute-start | bytes 196616 | tf_op jit(solution)/shard_map/ppermute | solution.py:419
  27.0 0.0 collective-permute-done.5.refs_1_.refs_3_
  27.0 0.1 shard_map.52
  27.1 0.9 %collective-permute-start.10 = (bf16[4,1,64,256]{3,2,1,0:T(8,128)(2,1)S(1)}, bf16[4,1,64,256]{3,2,1,0:T(8,128)(2,1)S(1)}, u32[]{:S(2)}, u32[]{:S(2)}) collective-permute-start(bf16[4,1,64,256]{3,2,1,0:T(8,128)(2,1)S(1)} %get-tuple-element.98), channel_id=1, source_target_pairs={{0,2},{1,5},{2,0},{3,7},{4,6},{5,1},{6,4},{7,3},{8,10},{9,13},{10,... | collective-permute-start | bytes 393224 | tf_op jit(solution)/shard_map/ppermute | solution.py:419
  28.0 2.7 %collective-permute-done.12.refs_1_ = bf16[2,1,64,256]{3,2,1,0:T(8,128)(2,1)S(1)} collective-permute-done((bf16[2,1,64,256]{3,2,1,0:T(8,128)(2,1)S(1)}, bf16[2,1,64,256]{3,2,1,0:T(8,128)(2,1)S(1)}, u32[]{:S(2)}, u32[]{:S(2)}) %collective-permute-start.12) | collective-permute-done | bytes 65568 | tf_op jit(solution)/shard_map/ppermute | solution.py:419
  30.7 1.3 %collective-permute-done.11.refs_1_ = bf16[2,1,64,256]{3,2,1,0:T(8,128)(2,1)S(1)} collective-permute-done((bf16[2,1,64,256]{3,2,1,0:T(8,128)(2,1)S(1)}, bf16[2,1,64,256]{3,2,1,0:T(8,128)(2,1)S(1)}, u32[]{:S(2)}, u32[]{:S(2)}) %collective-permute-start.11) | collective-permute-done | bytes 65568 | tf_op jit(solution)/shard_map/ppermute | solution.py:419
  32.0 0.1 collective-permute-done.10.came_ref
  32.1 0.7 %shard_map.55 = f32[2,2,64,256]{3,2,1,0:T(8,128)} custom-call(bf16[4,1,64,256]{3,2,1,0:T(8,128)(2,1)S(1)} %collective-permute-done.10.came_ref, f32[2,1,64,256]{3,2,1,0:T(8,128)S(1)} %shard_map.53.refs_0_, f32[2,1,64,256]{3,2,1,0:T(8,128)S(1)} %shard_map.54.refs_1_), custom_call_target="tpu_custom_call" | custom-call | tf_op jit(solution)/shard_map/pallas_call | solution.py:19
  (7 shorter events, 0.1 us)
Async XLA Ops:
  0.0 10.3 %collective-permute-start = (bf16[2,8,16,3,2,256]{5,4,3,2,1,0:T(2,128)(2,1)}, bf16[2,8,16,3,2,256]{5,4,3,2,1,0:T(2,128)(2,1)S(1)}, u32[]{:S(2)}, u32[]{:S(2)}) collective-permute-start(bf16[2,8,16,3,2,256]{5,4,3,2,1,0:T(2,128)(2,1)} %bitcast.11), channel_id=1, source_target_pairs={{1,0},{0,1},{3,2},{2,3},{5,4},{4,5},{7,6},{6,7},{9,8},{8,9},{11,10... | collective-permute-start | bytes 2359304 | tf_op jit(solution)/shard_map/ppermute | solution.py:14
  1.5 10.5 %collective-permute-start.3 = (bf16[2,19,3,2,256]{4,3,2,1,0:T(2,128)(2,1)S(1)}, bf16[2,19,3,2,256]{4,3,2,1,0:T(2,128)(2,1)S(1)}, u32[]{:S(2)}, u32[]{:S(2)}) collective-permute-start(bf16[2,19,3,2,256]{4,3,2,1,0:T(2,128)(2,1)S(1)} %get-tuple-element.70), channel_id=1, source_target_pairs={{12,0},{0,4},{4,8},{8,12},{13,1},{1,5},{5,9},{9,13},{14,2},{2,6},{... | collective-permute-start | bytes 350216 | tf_op jit(solution)/shard_map/ppermute | solution.py:14
  4.2 7.9 %collective-permute-start.2 = (bf16[2,16,3,2,256]{4,3,2,1,0:T(2,128)(2,1)S(1)}, bf16[2,16,3,2,256]{4,3,2,1,0:T(2,128)(2,1)S(1)}, u32[]{:S(2)}, u32[]{:S(2)}) collective-permute-start(bf16[2,16,3,2,256]{4,3,2,1,0:T(2,128)(2,1)S(1)} %get-tuple-element.69), channel_id=1, source_target_pairs={{4,0},{8,4},{12,8},{0,12},{5,1},{9,5},{13,9},{1,13},{6,2},{10,6},{... | collective-permute-start | bytes 294920 | tf_op jit(solution)/shard_map/ppermute | solution.py:14
  6.8 6.0 %collective-permute-start.1 = (bf16[8,32,256]{2,1,0:T(8,128)(2,1)S(1)}, bf16[8,32,256]{2,1,0:T(8,128)(2,1)S(1)}, u32[]{:S(2)}, u32[]{:S(2)}) collective-permute-start(bf16[8,32,256]{2,1,0:T(8,128)(2,1)S(1)} %get-tuple-element.68), channel_id=1, source_target_pairs={{2,0},{0,2},{3,1},{1,3},{6,4},{4,6},{7,5},{5,7},{10,8},{8,10},{11,... | collective-permute-start | bytes 393224 | tf_op jit(solution)/shard_map/ppermute | solution.py:14
  12.8 1.4 %collective-permute-start.4 = (bf16[8,24,256]{2,1,0:T(8,128)(2,1)S(1)}, bf16[8,24,256]{2,1,0:T(8,128)(2,1)S(1)}, u32[]{:S(2)}, u32[]{:S(2)}) collective-permute-start(bf16[8,24,256]{2,1,0:T(8,128)(2,1)S(1)} %slice.3), channel_id=1, source_target_pairs={{1,0},{0,1},{3,2},{2,3},{5,4},{4,5},{7,6},{6,7},{9,8},{8,9},{11,10... | collective-permute-start | bytes 294920 | tf_op jit(solution)/shard_map/ppermute | solution.py:14
  12.9 5.9 %collective-permute-start.7 = (bf16[2,2,64,256]{3,2,1,0:T(8,128)(2,1)S(1)}, bf16[2,2,64,256]{3,2,1,0:T(8,128)(2,1)S(1)}, u32[]{:S(2)}, u32[]{:S(2)}) collective-permute-start(bf16[2,2,64,256]{3,2,1,0:T(8,128)(2,1)S(1)} %get-tuple-element.87), channel_id=1, source_target_pairs={{0,4},{1,3},{2,6},{3,1},{4,0},{5,7},{6,2},{7,5},{8,12},{9,11},{10,... | collective-permute-start | bytes 393224 | tf_op jit(solution)/shard_map/ppermute | solution.py:419
  15.6 5.0 %collective-permute-start.6 = (bf16[2,2,64,256]{3,2,1,0:T(8,128)(2,1)S(1)}, bf16[2,2,64,256]{3,2,1,0:T(8,128)(2,1)S(1)}, u32[]{:S(2)}, u32[]{:S(2)}) collective-permute-start(bf16[2,2,64,256]{3,2,1,0:T(8,128)(2,1)S(1)} %get-tuple-element.85), channel_id=1, source_target_pairs={{0,4},{1,3},{2,6},{3,1},{4,0},{5,7},{6,2},{7,5},{8,12},{9,11},{10,... | collective-permute-start | bytes 393224 | tf_op jit(solution)/shard_map/ppermute | solution.py:419
  17.5 9.5 %collective-permute-start.5 = (bf16[4,2,64,256]{3,2,1,0:T(8,128)(2,1)S(1)}, bf16[4,2,64,256]{3,2,1,0:T(8,128)(2,1)S(1)}, u32[]{:S(2)}, u32[]{:S(2)}) collective-permute-start(bf16[4,2,64,256]{3,2,1,0:T(8,128)(2,1)S(1)} %get-tuple-element.83), channel_id=1, source_target_pairs={{0,4},{1,3},{2,6},{3,1},{4,0},{5,7},{6,2},{7,5},{8,12},{9,11},{10,... | collective-permute-start | bytes 786440 | tf_op jit(solution)/shard_map/ppermute | solution.py:419
  18.8 5.1 %collective-permute-start.9 = (bf16[2,1,64,256]{3,2,1,0:T(8,128)(2,1)S(1)}, bf16[2,1,64,256]{3,2,1,0:T(8,128)(2,1)S(1)}, u32[]{:S(2)}, u32[]{:S(2)}) collective-permute-start(bf16[2,1,64,256]{3,2,1,0:T(8,128)(2,1)S(1)} %get-tuple-element.94), channel_id=1, source_target_pairs={{0,2},{1,5},{2,0},{3,7},{4,6},{5,1},{6,4},{7,3},{8,10},{9,13},{10,... | collective-permute-start | bytes 196616 | tf_op jit(solution)/shard_map/ppermute | solution.py:419
  20.6 4.5 %collective-permute-start.8 = (bf16[2,1,64,256]{3,2,1,0:T(8,128)(2,1)S(1)}, bf16[2,1,64,256]{3,2,1,0:T(8,128)(2,1)S(1)}, u32[]{:S(2)}, u32[]{:S(2)}) collective-permute-start(bf16[2,1,64,256]{3,2,1,0:T(8,128)(2,1)S(1)} %get-tuple-element.93), channel_id=1, source_target_pairs={{0,2},{1,5},{2,0},{3,7},{4,6},{5,1},{6,4},{7,3},{8,10},{9,13},{10,... | collective-permute-start | bytes 196616 | tf_op jit(solution)/shard_map/ppermute | solution.py:419
  23.9 6.8 %collective-permute-start.12 = (bf16[2,1,64,256]{3,2,1,0:T(8,128)(2,1)S(1)}, bf16[2,1,64,256]{3,2,1,0:T(8,128)(2,1)S(1)}, u32[]{:S(2)}, u32[]{:S(2)}) collective-permute-start(bf16[2,1,64,256]{3,2,1,0:T(8,128)(2,1)S(1)} %shard_map.50), channel_id=1, source_target_pairs={{0,8},{1,9},{2,10},{3,11},{4,12},{5,13},{6,14},{7,15},{8,0},{9,1},... | collective-permute-start | bytes 196616 | tf_op jit(solution)/shard_map/ppermute | solution.py:419
  25.2 6.8 %collective-permute-start.11 = (bf16[2,1,64,256]{3,2,1,0:T(8,128)(2,1)S(1)}, bf16[2,1,64,256]{3,2,1,0:T(8,128)(2,1)S(1)}, u32[]{:S(2)}, u32[]{:S(2)}) collective-permute-start(bf16[2,1,64,256]{3,2,1,0:T(8,128)(2,1)S(1)} %shard_map.51), channel_id=1, source_target_pairs={{0,8},{1,9},{2,10},{3,11},{4,12},{5,13},{6,14},{7,15},{8,0},{9,1},... | collective-permute-start | bytes 196616 | tf_op jit(solution)/shard_map/ppermute | solution.py:419
  27.1 5.0 %collective-permute-start.10 = (bf16[4,1,64,256]{3,2,1,0:T(8,128)(2,1)S(1)}, bf16[4,1,64,256]{3,2,1,0:T(8,128)(2,1)S(1)}, u32[]{:S(2)}, u32[]{:S(2)}) collective-permute-start(bf16[4,1,64,256]{3,2,1,0:T(8,128)(2,1)S(1)} %get-tuple-element.98), channel_id=1, source_target_pairs={{0,2},{1,5},{2,0},{3,7},{4,6},{5,1},{6,4},{7,3},{8,10},{9,13},{10,... | collective-permute-start | bytes 393224 | tf_op jit(solution)/shard_map/ppermute | solution.py:419

commit v21 on v19

--- a/solution.py
+++ b/solution.py
@@ -568,19 +568,24 @@
         second_own_kernel, (kept_shape, shape(2 * parts, pieces, rows, width)), 0,
         [lefts, right, right_edge, sent_own], [total],
     )
-    came_own = exchange(sent_own, plan[0])
-    staying = [(own_first, came_own, slice(0, parts)), (own_second, came_own, slice(parts, 2 * parts))]
     crossing = [(kept_first, came_first), (kept_second, came_second)]
     after = own_second
+    staying = None
     for step in plan[1:]:
         for d, (kept, came) in enumerate(crossing):
             came, after = lax.optimization_barrier((came, after))
-            crossing[d] = halve([(kept, came, None)], step, 4 * project_flops if d else 0)
+            crossing[d] = halve([(kept, came, None)], step)
             after = crossing[d][0]
+            if staying is None:
+                sent_own, after = lax.optimization_barrier((sent_own, after))
+                came_own = exchange(sent_own, plan[0])
+                staying = [
+                    (own_first, came_own, slice(0, parts)), (own_second, came_own, slice(parts, 2 * parts))
+                ]
     crossed = []
     for kept, came in crossing:
         came, after = lax.optimization_barrier((came, after))
-        after = call(sum_kernel, pltpu.VMEM(kept.shape, bf16), 0, [kept, came])
+        after = call(sum_kernel, pltpu.VMEM(kept.shape, bf16), 8 * project_flops, [kept, came])
         crossed.append(exchange(after, (top, top)))
     for step in plan[1:]:
         kept, came, which = staying[0]

time: 33.1 us -> 33.3 us (level)
  starting transfers between devices: 17.5 us -> 18.1 us
    ppermute x8, starting transfers between devices: 10.5 us -> 11.1 us  [exchange(): return lax.ppermute(block, axes, route)]
  transfers between devices with their start and end apart: 13 -> 13, of which waited for: 7 -> 9; matrix products, arithmetic and copies ran while one was open for 0% -> 0% of each run, Pallas kernels for 23% -> 23%
where the time goes in v21:
time: 33.3 us; the launch traced here: 33.2 us
  starting transfers between devices  18.1 us (54%)
  Pallas kernels  8.34 us (25%)
  waiting for transfers between devices  6.63 us (20%)
    ppermute x8, starting transfers between devices, exchange(): return lax.ppermute(block, axes, route)  11.1 us
    pallas_call x19, Pallas kernels, call(): pl.pallas_call(body, out_shape=out_shape, in_specs=[pl.BlockSpec(memory_s...  8.34 us
    ppermute x5, starting transfers between devices, shifted(): return lax.ppermute(block, axis, route)  6.96 us
    ppermute x8, waiting for transfers between devices, exchange(): return lax.ppermute(block, axes, route)  5.6 us
    ppermute x5, waiting for transfers between devices, shifted(): return lax.ppermute(block, axis, route)  1.03 us
  transfers between devices with their start and end apart: 13, of which 9 were waited for; matrix products, arithmetic and copies ran while one was open for 0% of the time, Pallas kernels for 23%

profile of v21, /device:TPU:0, one launch (start us, length us, event | category | flops | bytes accessed | tf_op | source)
XLA Modules:
  0.0 33.2 jit_solution(8880038755774136081)
XLA Ops:
  0.0 0.5 %collective-permute-start = (bf16[2,8,16,3,2,256]{5,4,3,2,1,0:T(2,128)(2,1)}, bf16[2,8,16,3,2,256]{5,4,3,2,1,0:T(2,128)(2,1)S(1)}, u32[]{:S(2)}, u32[]{:S(2)}) collective-permute-start(bf16[2,8,16,3,2,256]{5,4,3,2,1,0:T(2,128)(2,1)} %bitcast.11), channel_id=1, source_target_pairs={{1,0},{0,1},{3,2},{2,3},{5,4},{4,5},{7,6},{6,7},{9,8},{8,9},{11,10... | collective-permute-start | bytes 2359304 | tf_op jit(solution)/shard_map/ppermute | solution.py:14
  0.5 1.4 %shard_map.37 = (bf16[2,16,3,2,256]{4,3,2,1,0:T(2,128)(2,1)S(1)}, bf16[2,19,3,2,256]{4,3,2,1,0:T(2,128)(2,1)S(1)}, bf16[2,8,16,3,2,256]{5,4,3,2,1,0:T(2,128)(2,1...) custom-call(bf16[2,8,16,3,2,256]{5,4,3,2,1,0:T(2,128)(2,1)} %bitcast, ...), custom_call_target="tpu_custom_call" | custom-call | tf_op jit(solution)/shard_map/pallas_call | solution.py:19
  1.8 2.6 %collective-permute-start.3 = (bf16[2,19,3,2,256]{4,3,2,1,0:T(2,128)(2,1)S(1)}, bf16[2,19,3,2,256]{4,3,2,1,0:T(2,128)(2,1)S(1)}, u32[]{:S(2)}, u32[]{:S(2)}) collective-permute-start(bf16[2,19,3,2,256]{4,3,2,1,0:T(2,128)(2,1)S(1)} %get-tuple-element.70), channel_id=1, source_target_pairs={{12,0},{0,4},{4,8},{8,12},{13,1},{1,5},{5,9},{9,13},{14,2},{2,6},{... | collective-permute-start | bytes 350216 | tf_op jit(solution)/shard_map/ppermute | solution.py:14
  4.4 2.1 %collective-permute-start.2 = (bf16[2,16,3,2,256]{4,3,2,1,0:T(2,128)(2,1)S(1)}, bf16[2,16,3,2,256]{4,3,2,1,0:T(2,128)(2,1)S(1)}, u32[]{:S(2)}, u32[]{:S(2)}) collective-permute-start(bf16[2,16,3,2,256]{4,3,2,1,0:T(2,128)(2,1)S(1)} %get-tuple-element.69), channel_id=1, source_target_pairs={{4,0},{8,4},{12,8},{0,12},{5,1},{9,5},{13,9},{1,13},{6,2},{10,6},{... | collective-permute-start | bytes 294920 | tf_op jit(solution)/shard_map/ppermute | solution.py:14
  6.5 0.6 %shard_map.38 = (bf16[8,32,256]{2,1,0:T(8,128)(2,1)S(1)}, f32[8,8,256]{2,1,0:T(8,128)S(1)}, f32[8,8,256]{2,1,0:T(8,128)S(1)}, f32[8,8,256]{2,1,0:T(8,128)S(1)}, f32[8,8,256]{2,1,0:T(8,128)S(1)}) custom-call(bf16[2,8,16,3,2,256]{5,4,3,2,1,0:T(2,128)(2,1)S(1)} %get-tuple-element.54.raw_ref.refs_0_, ...), custom_call_target="tpu_custom_call" | custom-call | tf_op jit(solution)/shard_map/pallas_call | solution.py:19
  7.1 1.7 %collective-permute-start.1 = (bf16[8,32,256]{2,1,0:T(8,128)(2,1)S(1)}, bf16[8,32,256]{2,1,0:T(8,128)(2,1)S(1)}, u32[]{:S(2)}, u32[]{:S(2)}) collective-permute-start(bf16[8,32,256]{2,1,0:T(8,128)(2,1)S(1)} %get-tuple-element.68), channel_id=1, source_target_pairs={{2,0},{0,2},{3,1},{1,3},{6,4},{4,6},{7,5},{5,7},{10,8},{8,10},{11,... | collective-permute-start | bytes 393224 | tf_op jit(solution)/shard_map/ppermute | solution.py:14
  8.8 0.7 %shard_map.39 = (bf16[8,192,256]{2,1,0:T(8,128)(2,1)S(1)}, bf16[1152,512]{1,0:T(8,128)(2,1)S(1)}, bf16[256,1536]{1,0:T(8,128)(2,1)S(1)}, bf16[192,192]{1,0:T(8,1...) custom-call(bf16[2,8,16,3,2,256]{5,4,3,2,1,0:T(2,128)(2,1)S(1)} %get-tuple-element.54.raw_ref.refs_0_, ...), custom_call_target="tpu_custom_call" | custom-call | flops 150994944 | tf_op jit(solution)/shard_map/pallas_call | solution.py:19
  9.5 0.0 collective-permute-done.raw_ref
  9.5 0.3 shard_map.40
  9.8 0.6 %shard_map.41.refs_0_ = f32[2,8,192,256]{3,2,1,0:T(8,128)S(1)} custom-call(bf16[8,192,256]{2,1,0:T(8,128)(2,1)S(1)} %get-tuple-element.62.refs_0_, bf16[1,8,192,256]{3,2,1,0:T(8,128)(2,1)S(1)} %bitcast.9, f32[8,8,256]{2,1,0:T(8,128)S(1)} %get-tuple-element.64.refs_2_.refs_3_, f32[8,8,256]{2,1,0:T(8,128)S(1)} %get-tuple-element.65.refs_3_), custom_call_target="tpu_custom_call" | custom-call | flops 150994944 | tf_op jit(solution)/shard_map/pallas_call | solution.py:19
  10.4 0.8 %shard_map.42.refs_8_.begun_ref = f32[2,256,512]{2,1,0:T(8,128)S(1)} custom-call(bf16[256,1536]{1,0:T(8,128)(2,1)S(1)} %get-tuple-element.60.own_ref.refs_6_, bf16[1,256,1536]{2,1,0:T(8,128)(2,1)S(1)} %bitcast.6, bf16[1152,512]{1,0:T(8,128)(2,1)S(1)} %get-tuple-element.66.right_ref), custom_call_target="tpu_custom_call" | custom-call | flops 402653184 | tf_op jit(solution)/shard_map/pallas_call | solution.py:19
  11.2 0.7 %collective-permute-done.2.refs_0_ = bf16[2,16,3,2,256]{4,3,2,1,0:T(2,128)(2,1)S(1)} collective-permute-done((bf16[2,16,3,2,256]{4,3,2,1,0:T(2,128)(2,1)S(1)}, bf16[2,16,3,2,256]{4,3,2,1,0:T(2,128)(2,1)S(1)}, u32[]{:S(2)}, u32[]{:S(2)}) %collective-permute-start.2) | collective-permute-done | bytes 98336 | tf_op jit(solution)/shard_map/ppermute | solution.py:14
  11.9 0.0 collective-permute-done.3.refs_1_
  11.9 0.8 %shard_map.43 = (f32[2,2,64,256]{3,2,1,0:T(8,128)S(1)}, bf16[2,2,64,256]{3,2,1,0:T(8,128)(2,1)S(1)}, bf16[384,512]{1,0:T(8,128)(2,1)S(1)}) custom-call(bf16[2,16,3,2,256]{4,3,2,1,0:T(2,128)(2,1)S(1)} %collective-permute-done.2.refs_0_, bf16[2,19,3,2,256]{4,3,2,1,0:T(2,128)(2,1)S(1)} %collective-permute-done.3.refs_1_, ...), custom_call_target="tpu_custom_call" | custom-call | flops 402653184 | tf_op jit(solution)/shard_map/pallas_call | solution.py:19
  12.7 0.1 collective-permute-done.1.refs_1_
  12.8 0.1 collective-permute-start.4
  12.9 1.1 %collective-permute-start.5 = (bf16[2,2,64,256]{3,2,1,0:T(8,128)(2,1)S(1)}, bf16[2,2,64,256]{3,2,1,0:T(8,128)(2,1)S(1)}, u32[]{:S(2)}, u32[]{:S(2)}) collective-permute-start(bf16[2,2,64,256]{3,2,1,0:T(8,128)(2,1)S(1)} %get-tuple-element.85), channel_id=1, source_target_pairs={{0,4},{1,3},{2,6},{3,1},{4,0},{5,7},{6,2},{7,5},{8,12},{9,11},{10,... | collective-permute-start | bytes 393224 | tf_op jit(solution)/shard_map/ppermute | solution.py:410
  14.0 0.2 collective-permute-done.4
  14.2 0.6 %shard_map.44.lefts_ref = bf16[2,256,1536]{2,1,0:T(8,128)(2,1)S(1)} custom-call(f32[2,8,192,256]{3,2,1,0:T(8,128)S(1)} %shard_map.41.refs_0_, bf16[8,32,256]{2,1,0:T(8,128)(2,1)S(1)} %collective-permute-done.1.refs_1_, bf16[1,8,24,256]{3,2,1,0:T(8,128)(2,1)S(1)} %bitcast.10, f32[8,8,256]{2,1,0:T(8,128)S(1)} %get-tuple-element.64.refs_2_.refs_3_), custom_call_target="tpu_custom_call" | custom-call | flops 150994944 | tf_op jit(solution)/shard_map/pallas_call | solution.py:19
  14.8 0.7 %shard_map.45 = (f32[2,2,64,256]{3,2,1,0:T(8,128)S(1)}, bf16[2,2,64,256]{3,2,1,0:T(8,128)(2,1)S(1)}) custom-call(bf16[2,256,1536]{2,1,0:T(8,128)(2,1)S(1)} %shard_map.44.lefts_ref, bf16[1152,512]{1,0:T(8,128)(2,1)S(1)} %get-tuple-element.66.right_ref, bf16[384,512]{1,0:T(8,128)(2,1)S(1)} %get-tuple-element.80.edge_ref.right_ref), custom_call_target="tpu_custom_call" | custom-call | flops 3221225472 | tf_op jit(solution)/shard_map/pallas_call | solution.py:19
  15.5 1.1 %collective-permute-start.7 = (bf16[2,2,64,256]{3,2,1,0:T(8,128)(2,1)S(1)}, bf16[2,2,64,256]{3,2,1,0:T(8,128)(2,1)S(1)}, u32[]{:S(2)}, u32[]{:S(2)}) collective-permute-start(bf16[2,2,64,256]{3,2,1,0:T(8,128)(2,1)S(1)} %get-tuple-element.91), channel_id=1, source_target_pairs={{0,4},{1,3},{2,6},{3,1},{4,0},{5,7},{6,2},{7,5},{8,12},{9,11},{10,... | collective-permute-start | bytes 393224 | tf_op jit(solution)/shard_map/ppermute | solution.py:410
  16.6 0.4 %shard_map.46 = (f32[2,2,64,256]{3,2,1,0:T(8,128)S(1)}, bf16[2,2,64,256]{3,2,1,0:T(8,128)(2,1)S(1)}) custom-call(bf16[256,1536]{1,0:T(8,128)(2,1)S(1)} %get-tuple-element.60.own_ref.refs_6_, bf16[1,256,1536]{2,1,0:T(8,128)(2,1)S(1)} %bitcast.8, f32[2,256,512]{2,1,0:T(8,128)S(1)} %shard_map.42.refs_8_.begun_ref, ...), custom_call_target="tpu_custom_call" | custom-call | tf_op jit(solution)/shard_map/pallas_call | solution.py:19
  16.9 0.7 %shard_map.47 = (f32[2,2,64,256]{3,2,1,0:T(8,128)S(1)}, bf16[4,2,64,256]{3,2,1,0:T(8,128)(2,1)S(1)}) custom-call(bf16[2,256,1536]{2,1,0:T(8,128)(2,1)S(1)} %shard_map.44.lefts_ref, bf16[1152,512]{1,0:T(8,128)(2,1)S(1)} %get-tuple-element.66.right_ref, bf16[384,512]{1,0:T(8,128)(2,1)S(1)} %get-tuple-element.80.edge_ref.right_ref, ...), custom_call_target="tpu_custom_call" | custom-call | tf_op jit(solution)/shard_map/pallas_call | solution.py:19
  17.6 0.3 collective-permute-done.5.refs_1_
  18.0 1.6 %collective-permute-start.9 = (bf16[2,1,64,256]{3,2,1,0:T(8,128)(2,1)S(1)}, bf16[2,1,64,256]{3,2,1,0:T(8,128)(2,1)S(1)}, u32[]{:S(2)}, u32[]{:S(2)}) collective-permute-start(bf16[2,1,64,256]{3,2,1,0:T(8,128)(2,1)S(1)} %get-tuple-element.94), channel_id=1, source_target_pairs={{0,2},{1,5},{2,0},{3,7},{4,6},{5,1},{6,4},{7,3},{8,10},{9,13},{10,... | collective-permute-start | bytes 196616 | tf_op jit(solution)/shard_map/ppermute | solution.py:410
  19.5 1.0 %collective-permute-start.6 = (bf16[4,2,64,256]{3,2,1,0:T(8,128)(2,1)S(1)}, bf16[4,2,64,256]{3,2,1,0:T(8,128)(2,1)S(1)}, u32[]{:S(2)}, u32[]{:S(2)}) collective-permute-start(bf16[4,2,64,256]{3,2,1,0:T(8,128)(2,1)S(1)} %get-tuple-element.89), channel_id=1, source_target_pairs={{0,4},{1,3},{2,6},{3,1},{4,0},{5,7},{6,2},{7,5},{8,12},{9,11},{10,... | collective-permute-start | bytes 786440 | tf_op jit(solution)/shard_map/ppermute | solution.py:410
  20.5 0.0 collective-permute-done.7.refs_1_
  20.6 1.9 %collective-permute-start.8 = (bf16[2,1,64,256]{3,2,1,0:T(8,128)(2,1)S(1)}, bf16[2,1,64,256]{3,2,1,0:T(8,128)(2,1)S(1)}, u32[]{:S(2)}, u32[]{:S(2)}) collective-permute-start(bf16[2,1,64,256]{3,2,1,0:T(8,128)(2,1)S(1)} %get-tuple-element.93), channel_id=1, source_target_pairs={{0,2},{1,5},{2,0},{3,7},{4,6},{5,1},{6,4},{7,3},{8,10},{9,13},{10,... | collective-permute-start | bytes 196616 | tf_op jit(solution)/shard_map/ppermute | solution.py:410
  22.5 0.5 %collective-permute-done.9.came_ref = bf16[2,1,64,256]{3,2,1,0:T(8,128)(2,1)S(1)} collective-permute-done((bf16[2,1,64,256]{3,2,1,0:T(8,128)(2,1)S(1)}, bf16[2,1,64,256]{3,2,1,0:T(8,128)(2,1)S(1)}, u32[]{:S(2)}, u32[]{:S(2)}) %collective-permute-start.9) | collective-permute-done | bytes 65568 | tf_op jit(solution)/shard_map/ppermute | solution.py:410
  23.0 1.4 %collective-permute-start.12 = (bf16[2,1,64,256]{3,2,1,0:T(8,128)(2,1)S(1)}, bf16[2,1,64,256]{3,2,1,0:T(8,128)(2,1)S(1)}, u32[]{:S(2)}, u32[]{:S(2)}) collective-permute-start(bf16[2,1,64,256]{3,2,1,0:T(8,128)(2,1)S(1)} %shard_map.50), channel_id=1, source_target_pairs={{0,8},{1,9},{2,10},{3,11},{4,12},{5,13},{6,14},{7,15},{8,0},{9,1},... | collective-permute-start | bytes 196616 | tf_op jit(solution)/shard_map/ppermute | solution.py:410
  24.5 1.2 %collective-permute-done.8.came_ref = bf16[2,1,64,256]{3,2,1,0:T(8,128)(2,1)S(1)} collective-permute-done((bf16[2,1,64,256]{3,2,1,0:T(8,128)(2,1)S(1)}, bf16[2,1,64,256]{3,2,1,0:T(8,128)(2,1)S(1)}, u32[]{:S(2)}, u32[]{:S(2)}) %collective-permute-start.8) | collective-permute-done | bytes 65568 | tf_op jit(solution)/shard_map/ppermute | solution.py:410
  25.7 1.7 %collective-permute-start.11 = (bf16[2,1,64,256]{3,2,1,0:T(8,128)(2,1)S(1)}, bf16[2,1,64,256]{3,2,1,0:T(8,128)(2,1)S(1)}, u32[]{:S(2)}, u32[]{:S(2)}) collective-permute-start(bf16[2,1,64,256]{3,2,1,0:T(8,128)(2,1)S(1)} %shard_map.51), channel_id=1, source_target_pairs={{0,8},{1,9},{2,10},{3,11},{4,12},{5,13},{6,14},{7,15},{8,0},{9,1},... | collective-permute-start | bytes 196616 | tf_op jit(solution)/shard_map/ppermute | solution.py:410
  27.4 0.0 collective-permute-done.6.refs_1_.refs_3_
  27.4 0.1 shard_map.52
  27.4 1.4 %collective-permute-start.10 = (bf16[4,1,64,256]{3,2,1,0:T(8,128)(2,1)S(1)}, bf16[4,1,64,256]{3,2,1,0:T(8,128)(2,1)S(1)}, u32[]{:S(2)}, u32[]{:S(2)}) collective-permute-start(bf16[4,1,64,256]{3,2,1,0:T(8,128)(2,1)S(1)} %get-tuple-element.98), channel_id=1, source_target_pairs={{0,2},{1,5},{2,0},{3,7},{4,6},{5,1},{6,4},{7,3},{8,10},{9,13},{10,... | collective-permute-start | bytes 393224 | tf_op jit(solution)/shard_map/ppermute | solution.py:410
  28.9 1.5 %collective-permute-done.12.refs_1_ = bf16[2,1,64,256]{3,2,1,0:T(8,128)(2,1)S(1)} collective-permute-done((bf16[2,1,64,256]{3,2,1,0:T(8,128)(2,1)S(1)}, bf16[2,1,64,256]{3,2,1,0:T(8,128)(2,1)S(1)}, u32[]{:S(2)}, u32[]{:S(2)}) %collective-permute-start.12) | collective-permute-done | bytes 65568 | tf_op jit(solution)/shard_map/ppermute | solution.py:410
  30.3 1.5 %collective-permute-done.11.refs_1_ = bf16[2,1,64,256]{3,2,1,0:T(8,128)(2,1)S(1)} collective-permute-done((bf16[2,1,64,256]{3,2,1,0:T(8,128)(2,1)S(1)}, bf16[2,1,64,256]{3,2,1,0:T(8,128)(2,1)S(1)}, u32[]{:S(2)}, u32[]{:S(2)}) %collective-permute-start.11) | collective-permute-done | bytes 65568 | tf_op jit(solution)/shard_map/ppermute | solution.py:410
  31.8 0.7 %collective-permute-done.10.came_ref = bf16[4,1,64,256]{3,2,1,0:T(8,128)(2,1)S(1)} collective-permute-done((bf16[4,1,64,256]{3,2,1,0:T(8,128)(2,1)S(1)}, bf16[4,1,64,256]{3,2,1,0:T(8,128)(2,1)S(1)}, u32[]{:S(2)}, u32[]{:S(2)}) %collective-permute-start.10) | collective-permute-done | bytes 131104 | tf_op jit(solution)/shard_map/ppermute | solution.py:410
  32.5 0.7 %shard_map.55 = f32[2,2,64,256]{3,2,1,0:T(8,128)} custom-call(bf16[4,1,64,256]{3,2,1,0:T(8,128)(2,1)S(1)} %collective-permute-done.10.came_ref, f32[2,1,64,256]{3,2,1,0:T(8,128)S(1)} %shard_map.53.refs_0_, f32[2,1,64,256]{3,2,1,0:T(8,128)S(1)} %shard_map.54.refs_1_), custom_call_target="tpu_custom_call" | custom-call | tf_op jit(solution)/shard_map/pallas_call | solution.py:19
  (7 shorter events, 0.1 us)
Async XLA Ops:
  0.0 9.5 %collective-permute-start = (bf16[2,8,16,3,2,256]{5,4,3,2,1,0:T(2,128)(2,1)}, bf16[2,8,16,3,2,256]{5,4,3,2,1,0:T(2,128)(2,1)S(1)}, u32[]{:S(2)}, u32[]{:S(2)}) collective-permute-start(bf16[2,8,16,3,2,256]{5,4,3,2,1,0:T(2,128)(2,1)} %bitcast.11), channel_id=1, source_target_pairs={{1,0},{0,1},{3,2},{2,3},{5,4},{4,5},{7,6},{6,7},{9,8},{8,9},{11,10... | collective-permute-start | bytes 2359304 | tf_op jit(solution)/shard_map/ppermute | solution.py:14
  1.8 10.1 %collective-permute-start.3 = (bf16[2,19,3,2,256]{4,3,2,1,0:T(2,128)(2,1)S(1)}, bf16[2,19,3,2,256]{4,3,2,1,0:T(2,128)(2,1)S(1)}, u32[]{:S(2)}, u32[]{:S(2)}) collective-permute-start(bf16[2,19,3,2,256]{4,3,2,1,0:T(2,128)(2,1)S(1)} %get-tuple-element.70), channel_id=1, source_target_pairs={{12,0},{0,4},{4,8},{8,12},{13,1},{1,5},{5,9},{9,13},{14,2},{2,6},{... | collective-permute-start | bytes 350216 | tf_op jit(solution)/shard_map/ppermute | solution.py:14
  4.4 7.4 %collective-permute-start.2 = (bf16[2,16,3,2,256]{4,3,2,1,0:T(2,128)(2,1)S(1)}, bf16[2,16,3,2,256]{4,3,2,1,0:T(2,128)(2,1)S(1)}, u32[]{:S(2)}, u32[]{:S(2)}) collective-permute-start(bf16[2,16,3,2,256]{4,3,2,1,0:T(2,128)(2,1)S(1)} %get-tuple-element.69), channel_id=1, source_target_pairs={{4,0},{8,4},{12,8},{0,12},{5,1},{9,5},{13,9},{1,13},{6,2},{10,6},{... | collective-permute-start | bytes 294920 | tf_op jit(solution)/shard_map/ppermute | solution.py:14
  7.1 5.7 %collective-permute-start.1 = (bf16[8,32,256]{2,1,0:T(8,128)(2,1)S(1)}, bf16[8,32,256]{2,1,0:T(8,128)(2,1)S(1)}, u32[]{:S(2)}, u32[]{:S(2)}) collective-permute-start(bf16[8,32,256]{2,1,0:T(8,128)(2,1)S(1)} %get-tuple-element.68), channel_id=1, source_target_pairs={{2,0},{0,2},{3,1},{1,3},{6,4},{4,6},{7,5},{5,7},{10,8},{8,10},{11,... | collective-permute-start | bytes 393224 | tf_op jit(solution)/shard_map/ppermute | solution.py:14
  12.8 1.4 %collective-permute-start.4 = (bf16[8,24,256]{2,1,0:T(8,128)(2,1)S(1)}, bf16[8,24,256]{2,1,0:T(8,128)(2,1)S(1)}, u32[]{:S(2)}, u32[]{:S(2)}) collective-permute-start(bf16[8,24,256]{2,1,0:T(8,128)(2,1)S(1)} %slice.3), channel_id=1, source_target_pairs={{1,0},{0,1},{3,2},{2,3},{5,4},{4,5},{7,6},{6,7},{9,8},{8,9},{11,10... | collective-permute-start | bytes 294920 | tf_op jit(solution)/shard_map/ppermute | solution.py:14
  12.9 5.0 %collective-permute-start.5 = (bf16[2,2,64,256]{3,2,1,0:T(8,128)(2,1)S(1)}, bf16[2,2,64,256]{3,2,1,0:T(8,128)(2,1)S(1)}, u32[]{:S(2)}, u32[]{:S(2)}) collective-permute-start(bf16[2,2,64,256]{3,2,1,0:T(8,128)(2,1)S(1)} %get-tuple-element.85), channel_id=1, source_target_pairs={{0,4},{1,3},{2,6},{3,1},{4,0},{5,7},{6,2},{7,5},{8,12},{9,11},{10,... | collective-permute-start | bytes 393224 | tf_op jit(solution)/shard_map/ppermute | solution.py:410
  15.5 5.0 %collective-permute-start.7 = (bf16[2,2,64,256]{3,2,1,0:T(8,128)(2,1)S(1)}, bf16[2,2,64,256]{3,2,1,0:T(8,128)(2,1)S(1)}, u32[]{:S(2)}, u32[]{:S(2)}) collective-permute-start(bf16[2,2,64,256]{3,2,1,0:T(8,128)(2,1)S(1)} %get-tuple-element.91), channel_id=1, source_target_pairs={{0,4},{1,3},{2,6},{3,1},{4,0},{5,7},{6,2},{7,5},{8,12},{9,11},{10,... | collective-permute-start | bytes 393224 | tf_op jit(solution)/shard_map/ppermute | solution.py:410
  18.0 5.0 %collective-permute-start.9 = (bf16[2,1,64,256]{3,2,1,0:T(8,128)(2,1)S(1)}, bf16[2,1,64,256]{3,2,1,0:T(8,128)(2,1)S(1)}, u32[]{:S(2)}, u32[]{:S(2)}) collective-permute-start(bf16[2,1,64,256]{3,2,1,0:T(8,128)(2,1)S(1)} %get-tuple-element.94), channel_id=1, source_target_pairs={{0,2},{1,5},{2,0},{3,7},{4,6},{5,1},{6,4},{7,3},{8,10},{9,13},{10,... | collective-permute-start | bytes 196616 | tf_op jit(solution)/shard_map/ppermute | solution.py:410
  19.5 7.9 %collective-permute-start.6 = (bf16[4,2,64,256]{3,2,1,0:T(8,128)(2,1)S(1)}, bf16[4,2,64,256]{3,2,1,0:T(8,128)(2,1)S(1)}, u32[]{:S(2)}, u32[]{:S(2)}) collective-permute-start(bf16[4,2,64,256]{3,2,1,0:T(8,128)(2,1)S(1)} %get-tuple-element.89), channel_id=1, source_target_pairs={{0,4},{1,3},{2,6},{3,1},{4,0},{5,7},{6,2},{7,5},{8,12},{9,11},{10,... | collective-permute-start | bytes 786440 | tf_op jit(solution)/shard_map/ppermute | solution.py:410
  20.6 5.1 %collective-permute-start.8 = (bf16[2,1,64,256]{3,2,1,0:T(8,128)(2,1)S(1)}, bf16[2,1,64,256]{3,2,1,0:T(8,128)(2,1)S(1)}, u32[]{:S(2)}, u32[]{:S(2)}) collective-permute-start(bf16[2,1,64,256]{3,2,1,0:T(8,128)(2,1)S(1)} %get-tuple-element.93), channel_id=1, source_target_pairs={{0,2},{1,5},{2,0},{3,7},{4,6},{5,1},{6,4},{7,3},{8,10},{9,13},{10,... | collective-permute-start | bytes 196616 | tf_op jit(solution)/shard_map/ppermute | solution.py:410
  23.0 7.3 %collective-permute-start.12 = (bf16[2,1,64,256]{3,2,1,0:T(8,128)(2,1)S(1)}, bf16[2,1,64,256]{3,2,1,0:T(8,128)(2,1)S(1)}, u32[]{:S(2)}, u32[]{:S(2)}) collective-permute-start(bf16[2,1,64,256]{3,2,1,0:T(8,128)(2,1)S(1)} %shard_map.50), channel_id=1, source_target_pairs={{0,8},{1,9},{2,10},{3,11},{4,12},{5,13},{6,14},{7,15},{8,0},{9,1},... | collective-permute-start | bytes 196616 | tf_op jit(solution)/shard_map/ppermute | solution.py:410
  25.7 6.1 %collective-permute-start.11 = (bf16[2,1,64,256]{3,2,1,0:T(8,128)(2,1)S(1)}, bf16[2,1,64,256]{3,2,1,0:T(8,128)(2,1)S(1)}, u32[]{:S(2)}, u32[]{:S(2)}) collective-permute-start(bf16[2,1,64,256]{3,2,1,0:T(8,128)(2,1)S(1)} %shard_map.51), channel_id=1, source_target_pairs={{0,8},{1,9},{2,10},{3,11},{4,12},{5,13},{6,14},{7,15},{8,0},{9,1},... | collective-permute-start | bytes 196616 | tf_op jit(solution)/shard_map/ppermute | solution.py:410
  27.4 5.0 %collective-permute-start.10 = (bf16[4,1,64,256]{3,2,1,0:T(8,128)(2,1)S(1)}, bf16[4,1,64,256]{3,2,1,0:T(8,128)(2,1)S(1)}, u32[]{:S(2)}, u32[]{:S(2)}) collective-permute-start(bf16[4,1,64,256]{3,2,1,0:T(8,128)(2,1)S(1)} %get-tuple-element.98), channel_id=1, source_target_pairs={{0,2},{1,5},{2,0},{3,7},{4,6},{5,1},{6,4},{7,3},{8,10},{9,13},{10,... | collective-permute-start | bytes 393224 | tf_op jit(solution)/shard_map/ppermute | solution.py:410
